TPU v7x, 32 devices: a whole 2x2x4 slice. The times are simulated.
32 devices in a mesh: dp: 8 (over y, x, core), mp: 4 (over z).
Axes of the slice: x: 2, y: 2, z: 4, core: 2. Of those that a mesh axis runs over, the one named last changes fastest.
Arguments:
- patches: bfloat16 [3, 12288, 441], P(None, ('dp', 'mp')), may hold values from -6 to 6
- clip_len: int32 [8, 5], P('dp'), may hold values from 768 to 1536, as said below
- box_count: int32 [8, 3], P('dp'), may hold values from 1 to 8, as said below
- box_bounds: int32 [8, 3, 8, 2], P('dp'), may hold values from 0 to 64, as said below
- box_labels: int32 [8, 3, 8, 80], P('dp'), may hold values 0 or 1
- memory: bfloat16 [2, 2, 3072, 768], P(None, None, 'dp', 'mp'), may hold values from -6 to 6
- up_weight: float32 [768, 5376], P('dp', 'mp'), may hold values from -0.21875 to 0.21875
- down_weight: float32 [768, 3840], P('dp', 'mp'), may hold values from -0.21875 to 0.21875
- embed_weight: float32 [441, 768], P(None, ('dp', 'mp')), may hold values from -0.25 to 0.25
- head_weight: float32 [80, 768], P(None, ('dp', 'mp')), may hold values from -0.21875 to 0.21875
- vector_weight: float32 [7, 768], P(None, ('dp', 'mp'))
- conv_weight: float32 [2, 6, 768], P(None, None, 'mp'), may hold values from 0.15 to 0.6
- position_bias: float32 [12, 3], P('mp'), may hold values from -3 to 3
- up_moment: float32 [768, 5376], P('dp', 'mp'), may hold values from -0.00010681152 to 0.00010681152
- down_moment: float32 [768, 3840], P('dp', 'mp'), may hold values from -0.00010681152 to 0.00010681152
- embed_moment: float32 [441, 768], P(None, ('dp', 'mp')), may hold values from -0.00010681152 to 0.00010681152
- head_moment: float32 [80, 768], P(None, ('dp', 'mp')), may hold values from -0.00010681152 to 0.00010681152
- vector_moment: float32 [7, 768], P(None, ('dp', 'mp')), may hold values from -0.0004272461 to 0.0004272461
- conv_moment: float32 [2, 6, 768], P(None, None, 'mp'), may hold values from -0.0004272461 to 0.0004272461
- position_moment: float32 [12, 3], P('mp'), may hold values from -0.0004272461 to 0.0004272461
- up_average: float32 [768, 5376], P('dp', 'mp'), may hold values from -0.21875 to 0.21875
- down_average: float32 [768, 3840], P('dp', 'mp'), may hold values from -0.21875 to 0.21875
- embed_average: float32 [441, 768], P(None, ('dp', 'mp')), may hold values from -0.25 to 0.25
- head_average: float32 [80, 768], P(None, ('dp', 'mp')), may hold values from -0.21875 to 0.21875
- vector_average: float32 [7, 768], P(None, ('dp', 'mp')), may hold values from 0.3 to 1.2
- conv_average: float32 [2, 6, 768], P(None, None, 'mp'), may hold values from 0.15 to 0.6
- position_average: float32 [12, 3], P('mp'), may hold values from -3 to 3
Outputs:
- loss_sum: float32 [], replicated
- box_total: float32 [], replicated
- grad_norm: float32 [], replicated
- new_memory: bfloat16 [2, 2, 3072, 768], P(None, None, 'dp', 'mp')
- up_new: float32 [768, 5376], P('dp', 'mp')
- down_new: float32 [768, 3840], P('dp', 'mp')
- embed_new: float32 [441, 768], P(None, ('dp', 'mp'))
- head_new: float32 [80, 768], P(None, ('dp', 'mp'))
- vector_new: float32 [7, 768], P(None, ('dp', 'mp'))
- conv_new: float32 [2, 6, 768], P(None, None, 'mp')
- position_new: float32 [12, 3], P('mp')
- up_moment_new: float32 [768, 5376], P('dp', 'mp')
- down_moment_new: float32 [768, 3840], P('dp', 'mp')
- embed_moment_new: float32 [441, 768], P(None, ('dp', 'mp'))
- head_moment_new: float32 [80, 768], P(None, ('dp', 'mp'))
- vector_moment_new: float32 [7, 768], P(None, ('dp', 'mp'))
- conv_moment_new: float32 [2, 6, 768], P(None, None, 'mp')
- position_moment_new: float32 [12, 3], P('mp')
- up_average_new: float32 [768, 5376], P('dp', 'mp')
- down_average_new: float32 [768, 3840], P('dp', 'mp')
- embed_average_new: float32 [441, 768], P(None, ('dp', 'mp'))
- head_average_new: float32 [80, 768], P(None, ('dp', 'mp'))
- vector_average_new: float32 [7, 768], P(None, ('dp', 'mp'))
- conv_average_new: float32 [2, 6, 768], P(None, None, 'mp')
- position_average_new: float32 [12, 3], P('mp')
- up_copy: bfloat16 [768, 5376], P('dp', 'mp')
- down_copy: bfloat16 [768, 3840], P('dp', 'mp')
Inputs may be any that keep to these rules, and one draw needn't show every extreme that they name: `clip_len`: each entry is 1536 or 768; columns 0 and 1 are the older and the newer memory clip, column 2 + m the clip of micro-step m. `box_count`: boxes that count in each clip of each micro-step. `box_bounds`: each box is a pair start < end of positions within a frame.
All inputs are finite; a program needn't handle non-finite values. No bound on the sum of `box_labels` on one device may be relied on, other than what follows from the above.
Results may differ from a plain program's by a relative error of at most 0.0075.
Values may be sent and summed in bfloat16 or wider, within the bound.
No kernel may reach another device: no remote copies, remote signals or barrier semaphores. Data moves between devices by JAX's collectives and lax.ppermute only.
A program may use at most 256 MiB of HBM per device.

v0:
```python
import jax
import jax.numpy as jnp
from jax import lax
from jax.sharding import PartitionSpec as P

MICRO = 3
FRAME = 64


EPSILON = 1e-06
LEARNING = 300.0
VECTOR_LEARNING = 6000.0
MOMENTUM = 0.5
AVERAGING = 0.5
THRESHOLD = 0.05
PRECISE = lax.Precision.HIGHEST


def norm_rows(inputs, gain_row, shift_row):
    row_mean = jnp.mean(inputs, axis=-1, keepdims=True)
    centered = inputs - row_mean
    variance = jnp.mean(centered * centered, axis=-1, keepdims=True)
    return centered * lax.rsqrt(variance + EPSILON) * gain_row + shift_row


def gelu_exact(inputs):
    return jax.nn.gelu(inputs, approximate=False)


def pool_taps(inputs, conv_taps):
    channels = inputs.shape[-1]
    return jnp.sum(inputs.reshape(-1, conv_taps.shape[0], channels) * conv_taps, axis=1)


def unpool_taps(gradient, conv_taps, inputs):
    tap_count = conv_taps.shape[0]
    channels = inputs.shape[-1]
    spread = gradient[:, None, :] * conv_taps
    tap_grad = jnp.sum(gradient[:, None, :] * inputs.reshape(-1, tap_count, channels), axis=0)
    return (spread.reshape(-1, channels), tap_grad)


def product(first_operand, second_operand):
    return jnp.dot(first_operand, second_operand, preferred_element_type=jnp.float32)


def contract_last(first_operand, second_operand):
    return lax.dot_general(
        first_operand, second_operand, (((1,), (1,)), ((), ())), preferred_element_type=jnp.float32
    )


def contract_rows(first_operand, second_operand):
    return lax.dot_general(
        first_operand, second_operand, (((0,), (0,)), ((), ())), preferred_element_type=jnp.float32
    )


def apply_update(weight, gradient, moment, average, rate):
    moment = MOMENTUM * moment + gradient
    updated = weight - rate * (gradient + MOMENTUM * moment)
    return (updated, moment, AVERAGING * average + (1.0 - AVERAGING) * updated)


def gather_rows(inputs):
    return lax.all_gather(inputs, "mp", axis=0, tiled=True)


def sum_rows(inputs):
    return lax.psum_scatter(
        inputs.astype(jnp.bfloat16), "mp", scatter_dimension=0, tiled=True
    ).astype(jnp.float32)


def gather_grads(inputs):
    return lax.all_gather(inputs, "mp", axis=0, tiled=True)


def sum_grads(inputs):
    return lax.psum_scatter(
        inputs.astype(jnp.bfloat16), "mp", scatter_dimension=0, tiled=True
    ).astype(jnp.float32)


def closing_sum(inputs):
    return lax.psum(inputs, ("dp", "mp"))


def key_layout(rel_bias, lengths, pooled):
    position = jnp.arange(2 * pooled)
    offset = (position >= pooled).astype(jnp.int32) + (position >= pooled + pooled // 2).astype(
        jnp.int32
    )
    key_limit = jnp.where(
        offset == 0, lengths[0] // 4, jnp.where(offset == 1, lengths[1] // 8, lengths[2] // 8)
    )
    key_local = position - jnp.where(
        offset == 0, 0, jnp.where(offset == 1, pooled, pooled + pooled // 2)
    )
    group_table = (offset[:, None] == jnp.arange(3)[None, :]).astype(jnp.float32)
    key_bias = jnp.dot(rel_bias, group_table.T, precision=PRECISE)
    return (key_bias, key_local < key_limit, group_table)


def block_scores(query_block, key_rows, key_bias, key_valid):
    scaling = query_block.shape[-1] ** (-0.5)
    scores = (
        jnp.einsum("qhd,khd->hqk", query_block, key_rows, preferred_element_type=jnp.float32)
        * scaling
        + key_bias[:, None, :]
    )
    return jnp.where(key_valid[None, None, :], scores, -1e30)


def split_blocks(inputs):
    block_rows = min(512, inputs.shape[0])
    return inputs.reshape((inputs.shape[0] // block_rows, block_rows) + inputs.shape[1:])


def attend(query_rows, key_rows, value_rows, key_bias, key_valid):

    def one_block(query_block):
        scores = block_scores(query_block, key_rows, key_bias, key_valid)
        row_max = jnp.max(scores, axis=-1, keepdims=True)
        exponent = jnp.exp(scores - row_max)
        row_total = jnp.sum(exponent, axis=-1, keepdims=True)
        prob_rows = (exponent / row_total).astype(jnp.bfloat16)
        attended = jnp.einsum(
            "hqk,khd->qhd", prob_rows, value_rows, preferred_element_type=jnp.float32
        )
        return (attended, (row_max + jnp.log(row_total))[..., 0])

    attended, log_total = lax.map(one_block, split_blocks(query_rows))
    return (attended.reshape(query_rows.shape), log_total)


def attend_back(query_rows, key_rows, value_rows, key_bias, key_valid, log_total, grad_out):
    scaling = query_rows.shape[-1] ** (-0.5)

    def one_block(inputs):
        query_block, grad_block, total_block = inputs
        scores = block_scores(query_block, key_rows, key_bias, key_valid)
        prob_rows = jnp.exp(scores - total_block[..., None])
        grad_prob = jnp.einsum(
            "qhd,khd->hqk", grad_block, value_rows, preferred_element_type=jnp.float32
        )
        grad_score = (
            prob_rows * (grad_prob - jnp.sum(prob_rows * grad_prob, axis=-1, keepdims=True))
        ).astype(jnp.bfloat16)
        grad_query = (
            jnp.einsum("hqk,khd->qhd", grad_score, key_rows, preferred_element_type=jnp.float32)
            * scaling
        )
        grad_keys = (
            jnp.einsum("hqk,qhd->khd", grad_score, query_block, preferred_element_type=jnp.float32)
            * scaling
        )
        grad_values = jnp.einsum(
            "hqk,qhd->khd",
            prob_rows.astype(jnp.bfloat16),
            grad_block,
            preferred_element_type=jnp.float32,
        )
        return (grad_query, grad_keys, grad_values, jnp.sum(grad_score.astype(jnp.float32), axis=1))

    grad_query, grad_keys, grad_values, grad_bias = lax.map(
        one_block, (split_blocks(query_rows), split_blocks(grad_out), log_total)
    )
    return (
        grad_query.reshape(query_rows.shape),
        jnp.sum(grad_keys, axis=0),
        jnp.sum(grad_values, axis=0),
        jnp.sum(grad_bias, axis=0),
    )


def box_select(bounds, clip_length, mp_index, tok_rows):
    position = mp_index * tok_rows + jnp.arange(tok_rows)
    within = position % FRAME
    inside = (
        (within[None, :] >= bounds[:, 0:1])
        & (within[None, :] < bounds[:, 1:2])
        & (position[None, :] < clip_length)
    )
    denominator = ((bounds[:, 1] - bounds[:, 0]) * (clip_length // FRAME)).astype(jnp.float32)
    return inside.astype(jnp.float32) / denominator[:, None]


def layer_forward(
    weights, patch_rows, lengths, mem_newer, mem_older, bounds, labels_row, box_number, mp_index
):
    embed_low, head_low, vectors, w_qkv, w_hidden, w_out, w_back, conv_all, rel_bias = weights
    head_cols = conv_all.shape[2]
    head_count = rel_bias.shape[0]
    shape_heads = (-1, head_count, head_cols // head_count)
    embedded = product(patch_rows, embed_low) + vectors[0]
    normed_all = gather_rows(norm_rows(embedded, vectors[1], vectors[2]).astype(jnp.bfloat16))
    projected = product(normed_all, w_qkv)
    clip_rows = projected.shape[0]
    query_rows = projected[:, :head_cols].astype(jnp.bfloat16)
    pool_key = pool_taps(projected[:, head_cols : 2 * head_cols], conv_all[0, :4]).astype(
        jnp.bfloat16
    )
    pool_value = pool_taps(projected[:, 2 * head_cols : 3 * head_cols], conv_all[1, :4]).astype(
        jnp.bfloat16
    )
    pooled = pool_key.shape[0]
    key_rows = jnp.concatenate(
        [
            pool_key,
            pool_taps(mem_newer[0].astype(jnp.float32), conv_all[0, 4:]).astype(jnp.bfloat16),
            pool_taps(mem_older[0].astype(jnp.float32), conv_all[0, 4:]).astype(jnp.bfloat16),
        ],
        axis=0,
    )
    value_rows = jnp.concatenate(
        [
            pool_value,
            pool_taps(mem_newer[1].astype(jnp.float32), conv_all[1, 4:]).astype(jnp.bfloat16),
            pool_taps(mem_older[1].astype(jnp.float32), conv_all[1, 4:]).astype(jnp.bfloat16),
        ],
        axis=0,
    )
    key_bias, key_valid, group_table = key_layout(rel_bias, lengths, pooled)
    attended, log_total = attend(
        query_rows.reshape(shape_heads),
        key_rows.reshape(shape_heads),
        value_rows.reshape(shape_heads),
        key_bias,
        key_valid,
    )
    attended = (attended.reshape(clip_rows, head_cols) + query_rows.astype(jnp.float32)).astype(
        jnp.bfloat16
    )
    first_res = embedded + sum_rows(contract_last(attended, w_out))
    normed_mlp = gather_rows(norm_rows(first_res, vectors[3], vectors[4]).astype(jnp.bfloat16))
    hidden = product(normed_mlp, w_hidden)
    active = gelu_exact(hidden).astype(jnp.bfloat16)
    second_res = first_res + sum_rows(contract_last(active, w_back))
    final_rows = norm_rows(second_res, vectors[5], vectors[6])
    select = box_select(bounds, lengths[0], mp_index, patch_rows.shape[0])
    feature = lax.psum(jnp.dot(select, final_rows, precision=PRECISE), "mp")
    logits = contract_last(feature.astype(jnp.bfloat16), head_low)
    target = labels_row.astype(jnp.float32)
    box_keep = (jnp.arange(bounds.shape[0]) < box_number).astype(jnp.float32)[:, None]
    loss_part = jnp.sum((jax.nn.softplus(logits) - target * logits) * box_keep)
    grad_logits = ((jax.nn.sigmoid(logits) - target) * box_keep).astype(jnp.bfloat16)
    kept_state = (
        embedded,
        first_res,
        second_res,
        normed_all,
        normed_mlp,
        projected,
        query_rows,
        key_rows,
        value_rows,
        key_bias,
        key_valid,
        group_table,
        log_total,
        attended,
        hidden,
        active,
        select,
        feature,
        grad_logits,
    )
    pooled_now = jnp.stack([key_rows[:pooled], value_rows[:pooled]])
    return (loss_part, pooled_now, kept_state)


def layer_backward(weights, kept_state, patch_rows, mem_newer, mem_older, lead_flag):
    embed_low, head_low, vectors, w_qkv, w_hidden, w_out, w_back, conv_all, rel_bias = weights
    (
        embedded,
        first_res,
        second_res,
        normed_all,
        normed_mlp,
        projected,
        query_rows,
        key_rows,
        value_rows,
        key_bias,
        key_valid,
        group_table,
        log_total,
        attended,
        hidden,
        active,
        select,
        feature,
        grad_logits,
    ) = kept_state
    head_cols = conv_all.shape[2]
    head_count = rel_bias.shape[0]
    shape_heads = (-1, head_count, head_cols // head_count)
    pooled = key_rows.shape[0] // 2
    half_pool = pooled // 2
    grad_head = contract_rows(grad_logits, feature.astype(jnp.bfloat16)) * lead_flag
    grad_final = jnp.dot(select.T, product(grad_logits, head_low), precision=PRECISE)
    grad_second, grad_gain3, grad_shift3 = jax.vjp(norm_rows, second_res, vectors[5], vectors[6])[
        1
    ](grad_final)
    grad_branch = gather_grads(grad_second.astype(jnp.bfloat16))
    grad_back = contract_rows(grad_branch, active)
    grad_active = product(grad_branch, w_back)
    grad_hidden = jax.vjp(gelu_exact, hidden)[1](grad_active)[0].astype(jnp.bfloat16)
    grad_w_hidden = contract_rows(normed_mlp, grad_hidden)
    grad_normed = sum_grads(contract_last(grad_hidden, w_hidden))
    grad_first, grad_gain2, grad_shift2 = jax.vjp(norm_rows, first_res, vectors[3], vectors[4])[1](
        grad_normed
    )
    grad_first = grad_first + grad_second
    grad_attn = gather_grads(grad_first.astype(jnp.bfloat16))
    grad_out = contract_rows(grad_attn, attended)
    grad_attended = product(grad_attn, w_out).astype(jnp.bfloat16)
    grad_query, grad_keys, grad_values, grad_bias = attend_back(
        query_rows.reshape(shape_heads),
        key_rows.reshape(shape_heads),
        value_rows.reshape(shape_heads),
        key_bias,
        key_valid,
        log_total,
        grad_attended.reshape(shape_heads),
    )
    grad_keys = grad_keys.reshape(-1, head_cols)
    grad_values = grad_values.reshape(-1, head_cols)
    grad_key_pool = grad_keys[:pooled]
    grad_value_pool = grad_values[:pooled]
    grad_key_raw, key_taps = unpool_taps(
        grad_key_pool, conv_all[0, :4], projected[:, head_cols : 2 * head_cols]
    )
    grad_value_raw, value_taps = unpool_taps(
        grad_value_pool, conv_all[1, :4], projected[:, 2 * head_cols : 3 * head_cols]
    )
    memory_taps = []
    for channel, rows_grad in ((0, grad_keys), (1, grad_values)):
        newer_taps = unpool_taps(
            rows_grad[pooled : pooled + half_pool],
            conv_all[channel, 4:],
            mem_newer[channel].astype(jnp.float32),
        )[1]
        older_taps = unpool_taps(
            rows_grad[pooled + half_pool :],
            conv_all[channel, 4:],
            mem_older[channel].astype(jnp.float32),
        )[1]
        memory_taps.append(newer_taps + older_taps)
    grad_conv = jnp.stack(
        [
            jnp.concatenate([key_taps, memory_taps[0]], axis=0),
            jnp.concatenate([value_taps, memory_taps[1]], axis=0),
        ]
    )
    grad_rel = jnp.dot(grad_bias, group_table, precision=PRECISE)
    grad_projected = jnp.concatenate(
        [
            grad_query.reshape(-1, head_cols) + grad_attended.astype(jnp.float32),
            grad_key_raw,
            grad_value_raw,
        ],
        axis=1,
    ).astype(jnp.bfloat16)
    grad_qkv = contract_rows(normed_all, grad_projected)
    grad_normed_in = sum_grads(contract_last(grad_projected, w_qkv))
    grad_embedded, grad_gain1, grad_shift1 = jax.vjp(norm_rows, embedded, vectors[1], vectors[2])[
        1
    ](grad_normed_in)
    grad_embedded = (grad_embedded + grad_first).astype(jnp.bfloat16)
    grad_embed = contract_rows(patch_rows, grad_embedded)
    grad_vectors = jnp.stack(
        [
            jnp.sum(grad_embedded.astype(jnp.float32), axis=0),
            grad_gain1,
            grad_shift1,
            grad_gain2,
            grad_shift2,
            grad_gain3,
            grad_shift3,
        ]
    )
    return (
        jnp.concatenate([grad_qkv, grad_w_hidden], axis=1),
        jnp.concatenate([grad_out, grad_back], axis=1),
        grad_embed,
        grad_head,
        grad_vectors,
        grad_conv,
        grad_rel,
    )


def shards(
    patches,
    clip_len,
    box_count,
    box_bounds,
    box_labels,
    memory,
    up_weight,
    down_weight,
    embed_weight,
    head_weight,
    vector_weight,
    conv_weight,
    position_bias,
    up_moment,
    down_moment,
    embed_moment,
    head_moment,
    vector_moment,
    conv_moment,
    position_moment,
    up_average,
    down_average,
    embed_average,
    head_average,
    vector_average,
    conv_average,
    position_average,
):
    up_all, down_all = (
        lax.all_gather(up_weight.astype(jnp.bfloat16), "dp", axis=0, tiled=True),
        lax.all_gather(down_weight.astype(jnp.bfloat16), "dp", axis=0, tiled=True),
    )
    embed_all, head_all, vectors = (
        lax.all_gather(embed_weight, ("dp", "mp"), axis=1, tiled=True),
        lax.all_gather(head_weight, ("dp", "mp"), axis=1, tiled=True),
        lax.all_gather(vector_weight, ("dp", "mp"), axis=1, tiled=True),
    )
    head_local = conv_weight.shape[2]
    mp_index = lax.axis_index("mp")
    lead_flag = (mp_index == 0).astype(jnp.float32)
    weights = (
        embed_all.astype(jnp.bfloat16),
        head_all.astype(jnp.bfloat16),
        vectors,
        up_all[:, : 3 * head_local],
        up_all[:, 3 * head_local :],
        down_all[:, :head_local],
        down_all[:, head_local:],
        conv_weight,
        position_bias,
    )
    lengths_all = clip_len[0]
    memories = [memory[0], memory[1]]
    totals = None
    loss_local = jnp.zeros((), jnp.float32)
    loss_global = jnp.zeros((), jnp.float32)
    for micro_step in range(MICRO):
        lengths = jnp.stack(
            [lengths_all[2 + micro_step], lengths_all[1 + micro_step], lengths_all[micro_step]]
        )
        loss_part, pooled_now, kept_state = layer_forward(
            weights,
            patches[micro_step],
            lengths,
            memories[-1],
            memories[-2],
            box_bounds[0, micro_step],
            box_labels[0, micro_step],
            box_count[0, micro_step],
            mp_index,
        )
        memories.append(pooled_now)
        loss_local = loss_local + loss_part
        loss_global = loss_global + lax.psum(loss_part, "dp")
        gradients = layer_backward(
            weights, kept_state, patches[micro_step], memories[-2], memories[-3], lead_flag
        )
        totals = (
            gradients
            if totals is None
            else tuple((earlier + later for earlier, later in zip(totals, gradients)))
        )
    totals = (
        tuple(
            (
                lax.psum_scatter(
                    totals[0].astype(jnp.bfloat16), "dp", scatter_dimension=0, tiled=True
                ).astype(jnp.float32),
                lax.psum_scatter(
                    totals[1].astype(jnp.bfloat16), "dp", scatter_dimension=0, tiled=True
                ).astype(jnp.float32),
            )
        )
        + totals[2:]
    )
    embed_grad, vector_grad, head_grad = (
        lax.psum_scatter(totals[2], ("dp", "mp"), scatter_dimension=1, tiled=True),
        lax.psum_scatter(totals[4], ("dp", "mp"), scatter_dimension=1, tiled=True),
        lax.psum_scatter(totals[3], ("dp", "mp"), scatter_dimension=1, tiled=True),
    )
    conv_grad, position_grad = lax.psum((totals[5], totals[6]), "dp")
    reduced = (totals[0], totals[1], embed_grad, head_grad, vector_grad, conv_grad, position_grad)
    squares = sum((jnp.sum(gradient * gradient) for gradient in reduced[:5]))
    squares = squares + (
        jnp.sum(conv_grad * conv_grad) + jnp.sum(position_grad * position_grad)
    ) / lax.axis_size("dp")
    count_local = jnp.sum(box_count).astype(jnp.float32) * lead_flag
    box_total, square_total = closing_sum((count_local, squares))
    grad_norm = jnp.sqrt(square_total) / box_total
    scaling = jnp.minimum(1.0, THRESHOLD / grad_norm) / box_total
    masters = (
        up_weight,
        down_weight,
        embed_weight,
        head_weight,
        vector_weight,
        conv_weight,
        position_bias,
    )
    moments = (
        up_moment,
        down_moment,
        embed_moment,
        head_moment,
        vector_moment,
        conv_moment,
        position_moment,
    )
    averages = (
        up_average,
        down_average,
        embed_average,
        head_average,
        vector_average,
        conv_average,
        position_average,
    )
    rates = (
        LEARNING,
        LEARNING,
        LEARNING,
        LEARNING,
        VECTOR_LEARNING,
        VECTOR_LEARNING,
        VECTOR_LEARNING,
    )
    results = [
        apply_update(weight, gradient * scaling, moment, average, rate)
        for weight, gradient, moment, average, rate in zip(
            masters, reduced, moments, averages, rates
        )
    ]
    new_memory = jnp.stack([memories[-2], memories[-1]])
    return (
        loss_global,
        box_total,
        grad_norm,
        new_memory,
        results[0][0],
        results[1][0],
        results[2][0],
        results[3][0],
        results[4][0],
        results[5][0],
        results[6][0],
        results[0][1],
        results[1][1],
        results[2][1],
        results[3][1],
        results[4][1],
        results[5][1],
        results[6][1],
        results[0][2],
        results[1][2],
        results[2][2],
        results[3][2],
        results[4][2],
        results[5][2],
        results[6][2],
        results[0][0].astype(jnp.bfloat16),
        results[1][0].astype(jnp.bfloat16),
    )


def solution(mesh):
    placed = (
        P(None, ("dp", "mp"), None),
        P("dp", None),
        P("dp", None),
        P("dp", None, None, None),
        P("dp", None, None, None),
        P(None, None, "dp", "mp"),
        P("dp", "mp"),
        P("dp", "mp"),
        P(None, ("dp", "mp")),
        P(None, ("dp", "mp")),
        P(None, ("dp", "mp")),
        P(None, None, "mp"),
        P("mp", None),
        P("dp", "mp"),
        P("dp", "mp"),
        P(None, ("dp", "mp")),
        P(None, ("dp", "mp")),
        P(None, ("dp", "mp")),
        P(None, None, "mp"),
        P("mp", None),
        P("dp", "mp"),
        P("dp", "mp"),
        P(None, ("dp", "mp")),
        P(None, ("dp", "mp")),
        P(None, ("dp", "mp")),
        P(None, None, "mp"),
        P("mp", None),
    )
    return jax.shard_map(
        shards,
        mesh=mesh,
        in_specs=placed,
        out_specs=(
            P(),
            P(),
            P(),
            P(None, None, "dp", "mp"),
            P("dp", "mp"),
            P("dp", "mp"),
            P(None, ("dp", "mp")),
            P(None, ("dp", "mp")),
            P(None, ("dp", "mp")),
            P(None, None, "mp"),
            P("mp", None),
            P("dp", "mp"),
            P("dp", "mp"),
            P(None, ("dp", "mp")),
            P(None, ("dp", "mp")),
            P(None, ("dp", "mp")),
            P(None, None, "mp"),
            P("mp", None),
            P("dp", "mp"),
            P("dp", "mp"),
            P(None, ("dp", "mp")),
            P(None, ("dp", "mp")),
            P(None, ("dp", "mp")),
            P(None, None, "mp"),
            P("mp", None),
            P("dp", "mp"),
            P("dp", "mp"),
        ),
        check_vma=False,
    )
```

profile of v0, /device:TPU:0, one launch (start us, length us, event | category | flops | bytes accessed | tf_op | source)
XLA Modules:
  0.0 2006.6 jit_solution(18045697881722455078)
XLA Ops:
  7.3 71.0 %all-gather = f32[32,24,7]{1,2,0:T(8,128)S(1)} all-gather(f32[1,24,7]{1,2,0:T(8,128)} %bitcast.595), channel_id=1, replica_groups=mesh['dp'=8,'mp'=4] {'dp','mp'}, dimensions={0}, use_global_device_ids=true | all-gather | bytes 22176 | tf_op jit(solution)/shard_map/all_gather | solution.py:431
  79.9 71.1 %all_gather.51 = bf16[441,768]{0,1:T(8,128)(2,1)S(1)} all-gather(bf16[441,24]{0,1:T(8,128)(2,1)S(1)} %convert.102), channel_id=1, replica_groups=mesh['dp'=8,'mp'=4] {'dp','mp'}, dimensions={1}, use_global_device_ids=true | all-gather | bytes 698544 | tf_op jit(solution)/shard_map/all_gather | solution.py:429
  179.3 24.9 %all-gather.28.cloned.1.call-done = bf16[1536,768]{1,0:T(8,128)(2,1)} async-done(((bf16[384,768]{1,0:T(8,128)(2,1)}), bf16[1536,768]{1,0:T(8,128)(2,1)}) %all-gather.28.cloned.1.call-update) | async-done | bytes 2359312 | tf_op jit(solution)/shard_map/all_gather | solution.py:66
  204.2 29.5 %all-gather.18.cloned.1.call-done = bf16[768,1344]{1,0:T(8,128)(2,1)} async-done(((bf16[96,1344]{1,0:T(8,128)(2,1)}), bf16[768,1344]{1,0:T(8,128)(2,1)}) %all-gather.18.cloned.1.call-update) | async-done | bytes 2064400 | tf_op jit(solution)/shard_map/all_gather | solution.py:425
  240.4 45.4 %all-gather.24.cloned.1.call-done = bf16[1536,768]{1,0:T(8,128)(2,1)} async-done(((bf16[384,768]{1,0:T(8,128)(2,1)}), bf16[1536,768]{1,0:T(8,128)(2,1)}) %all-gather.24.cloned.1.call-update) | async-done | bytes 2359312 | tf_op jit(solution)/shard_map/all_gather | solution.py:66
  295.2 41.9 %all-gather.16.cloned.1.call-done = bf16[1536,768]{1,0:T(8,128)(2,1)} async-done(((bf16[384,768]{1,0:T(8,128)(2,1)}), bf16[1536,768]{1,0:T(8,128)(2,1)}) %all-gather.16.cloned.1.call-update) | async-done | bytes 2359312 | tf_op jit(solution)/shard_map/all_gather | solution.py:66
  348.9 5.6 multiply_reduce_fusion.10
  374.8 5.6 multiply_reduce_fusion.9
  405.6 38.5 %while.91 = (s32[]{:T(128)}, f32[3,512,3,64]{1,0,3,2:T(4,128)}, f32[3,3,512]{2,1,0:T(4,128)S(1)}, bf16[3,512,3,64]{1,3,2,0:T(8,128)(2,1)S(1)}, bf16[768,3,64]{0,...) while((s32[]{:T(128)}, f32[3,512,3,64]{1,0,3,2:T(4,128)}, ...), condition=%wide.region_30.31_spmd.clone, body=%wide.region_27.30_spmd.clone.sunk | while | flops 319693056 | bytes 16997780 | solution.py:133
  409.9 8.6 dynamic_update_slice.109
  422.7 8.6 dynamic_update_slice.109
  435.5 8.6 dynamic_update_slice.109
  457.8 38.6 %while.92 = (s32[]{:T(128)}, f32[3,512,3,64]{1,0,3,2:T(4,128)}, f32[3,3,512]{2,1,0:T(4,128)S(1)}, bf16[3,512,3,64]{1,3,2,0:T(8,128)(2,1)S(1)}, bf16[768,3,64]{0,...) while((s32[]{:T(128)}, f32[3,512,3,64]{1,0,3,2:T(4,128)}, ...), condition=%wide.region_49.50_spmd.clone, body=%wide.region_46.49_spmd.clone.sunk | while | flops 319693056 | bytes 16997780 | solution.py:133
  462.2 8.6 dynamic_update_slice.111
  475.0 8.6 dynamic_update_slice.111
  487.8 8.6 dynamic_update_slice.111
  507.9 38.4 %while.90 = (s32[]{:T(128)}, f32[3,512,3,64]{1,0,3,2:T(4,128)}, f32[3,3,512]{2,1,0:T(4,128)S(1)}, bf16[3,512,3,64]{1,3,2,0:T(8,128)(2,1)S(1)}, bf16[768,3,64]{0,...) while((s32[]{:T(128)}, f32[3,512,3,64]{1,0,3,2:T(4,128)}, ...), condition=%wide.region_11.12_spmd.clone, body=%wide.region_8.11_spmd.clone.sunk | while | flops 319693056 | bytes 16997780 | solution.py:133
  512.0 8.6 dynamic_update_slice.107
  524.8 8.6 dynamic_update_slice.107
  537.6 8.6 dynamic_update_slice.107
  560.5 42.8 %reduce-scatter.26.cloned.1.call-done = bf16[384,768]{1,0:T(8,128)(2,1)} async-done(((bf16[1536,768]{1,0:T(8,128)(2,1)}), bf16[384,768]{1,0:T(8,128)(2,1)}) %reduce-scatter.26.cloned.1.call-update) | async-done | bytes 589840 | tf_op jit(solution)/shard_map/reduce_scatter | solution.py:70
  609.5 48.7 %all-gather.30.cloned.1.call-done = bf16[1536,768]{1,0:T(8,128)(2,1)} async-done(((bf16[384,768]{1,0:T(8,128)(2,1)}), bf16[1536,768]{1,0:T(8,128)(2,1)}) %all-gather.30.cloned.1.call-update) | async-done | bytes 2359312 | tf_op jit(solution)/shard_map/all_gather | solution.py:66
  658.3 15.5 multiply_convert_fusion.3
  678.9 30.1 %all-gather.22.cloned.1.call-done = bf16[1536,768]{1,0:T(8,128)(2,1)} async-done(((bf16[384,768]{1,0:T(8,128)(2,1)}), bf16[1536,768]{1,0:T(8,128)(2,1)}) %all-gather.22.cloned.1.call-update) | async-done | bytes 2359312 | tf_op jit(solution)/shard_map/all_gather | solution.py:66
  709.0 15.5 multiply_convert_fusion.5
  729.8 30.7 %all-gather.26.cloned.1.call-done = bf16[1536,768]{1,0:T(8,128)(2,1)} async-done(((bf16[384,768]{1,0:T(8,128)(2,1)}), bf16[1536,768]{1,0:T(8,128)(2,1)}) %all-gather.26.cloned.1.call-update) | async-done | bytes 2359312 | tf_op jit(solution)/shard_map/all_gather | solution.py:66
  760.5 15.5 multiply_convert_fusion.4
  782.3 77.4 %all_gather.57 = bf16[80,768]{0,1:T(8,128)(2,1)} all-gather(bf16[80,24]{0,1:T(8,128)(2,1)} %convert.101), channel_id=1, replica_groups=mesh['dp'=8,'mp'=4] {'dp','mp'}, dimensions={1}, use_global_device_ids=true | all-gather | bytes 126720 | tf_op jit(solution)/shard_map/all_gather | solution.py:430
  875.9 36.3 %reduce-scatter.32.cloned.1.call-done = bf16[384,768]{1,0:T(8,128)(2,1)} async-done(((bf16[1536,768]{1,0:T(8,128)(2,1)}), bf16[384,768]{1,0:T(8,128)(2,1)}) %reduce-scatter.32.cloned.1.call-update) | async-done | bytes 589840 | tf_op jit(solution)/shard_map/reduce_scatter | solution.py:70
  919.4 19.7 all-reduce.4
  964.5 43.3 %all-gather.40.cloned.1.call-done = bf16[1536,768]{1,0:T(8,128)(2,1)} async-done(((bf16[384,768]{1,0:T(8,128)(2,1)}), bf16[1536,768]{1,0:T(8,128)(2,1)}) %all-gather.40.cloned.1.call-update) | async-done | bytes 2359312 | tf_op jit(solution)/shard_map/all_gather | solution.py:76
  1007.8 8.3 add_convert_fusion
  1021.3 37.2 %all-gather.32.cloned.1.call-done = bf16[1536,768]{1,0:T(8,128)(2,1)} async-done(((bf16[384,768]{1,0:T(8,128)(2,1)}), bf16[1536,768]{1,0:T(8,128)(2,1)}) %all-gather.32.cloned.1.call-update) | async-done | bytes 2359312 | tf_op jit(solution)/shard_map/all_gather | solution.py:76
  1058.5 8.3 add_convert_fusion.2
  1071.8 37.4 %all-gather.36.cloned.1.call-done = bf16[1536,768]{1,0:T(8,128)(2,1)} async-done(((bf16[384,768]{1,0:T(8,128)(2,1)}), bf16[1536,768]{1,0:T(8,128)(2,1)}) %all-gather.36.cloned.1.call-update) | async-done | bytes 2359312 | tf_op jit(solution)/shard_map/all_gather | solution.py:76
  1109.2 8.3 add_convert_fusion.1
  1122.6 35.7 %reduce-scatter.42.cloned.1.call-done = bf16[384,768]{1,0:T(8,128)(2,1)} async-done(((bf16[1536,768]{1,0:T(8,128)(2,1)}), bf16[384,768]{1,0:T(8,128)(2,1)}) %reduce-scatter.42.cloned.1.call-update) | async-done | bytes 589840 | tf_op jit(solution)/shard_map/reduce_scatter | solution.py:80
  1158.3 49.8 %reduce-scatter.38.cloned.1.call-done = bf16[384,768]{1,0:T(8,128)(2,1)} async-done(((bf16[1536,768]{1,0:T(8,128)(2,1)}), bf16[384,768]{1,0:T(8,128)(2,1)}) %reduce-scatter.38.cloned.1.call-update) | async-done | bytes 589840 | tf_op jit(solution)/shard_map/reduce_scatter | solution.py:80
  1208.1 49.7 %reduce-scatter.40.cloned.1.call-done = bf16[384,768]{1,0:T(8,128)(2,1)} async-done(((bf16[1536,768]{1,0:T(8,128)(2,1)}), bf16[384,768]{1,0:T(8,128)(2,1)}) %reduce-scatter.40.cloned.1.call-update) | async-done | bytes 589840 | tf_op jit(solution)/shard_map/reduce_scatter | solution.py:80
  1275.6 44.1 %all-gather.38.cloned.1.call-done = bf16[1536,768]{1,0:T(8,128)(2,1)} async-done(((bf16[384,768]{1,0:T(8,128)(2,1)}), bf16[1536,768]{1,0:T(8,128)(2,1)}) %all-gather.38.cloned.1.call-update) | async-done | bytes 2359312 | tf_op jit(solution)/shard_map/all_gather | solution.py:76
  1328.6 67.9 %while.94 = (s32[]{:T(128)}, f32[3,512,3,64]{1,0,3,2:T(4,128)}, f32[3,768,3,64]{1,3,2,0:T(8,128)}, f32[3,768,3,64]{1,3,2,0:T(8,128)}, f32[3,3,768]{2,1,0:T(4,128...) while((s32[]{:T(128)}, f32[3,512,3,64]{1,0,3,2:T(4,128)}, ...), condition=%wide.region_80.81_spmd.clone, body=%wide.region_77.80_spmd.clone.sunk | while | flops 769382400 | bytes 63876880 | solution.py:166
  1336.4 8.6 dynamic_update_slice.119
  1359.0 8.6 dynamic_update_slice.119
  1381.6 8.6 dynamic_update_slice.119
  1404.9 68.0 %while.93 = (s32[]{:T(128)}, f32[3,512,3,64]{1,0,3,2:T(4,128)}, f32[3,768,3,64]{1,3,2,0:T(8,128)}, f32[3,768,3,64]{1,3,2,0:T(8,128)}, f32[3,3,768]{2,1,0:T(4,128...) while((s32[]{:T(128)}, f32[3,512,3,64]{1,0,3,2:T(4,128)}, ...), condition=%wide.region_69.70_spmd.clone, body=%wide.region_66.69_spmd.clone.sunk | while | flops 769382400 | bytes 63876880 | solution.py:166
  1412.7 8.7 dynamic_update_slice.115
  1435.3 8.7 dynamic_update_slice.115
  1458.0 8.7 dynamic_update_slice.115
  1481.8 69.9 %while.95 = (s32[]{:T(128)}, f32[3,512,3,64]{1,0,3,2:T(4,128)}, f32[3,768,3,64]{1,3,2,0:T(8,128)}, f32[3,768,3,64]{1,3,2,0:T(8,128)}, f32[3,3,768]{2,1,0:T(4,128...) while((s32[]{:T(128)}, f32[3,512,3,64]{1,0,3,2:T(4,128)}, ...), condition=%wide.region_91.92_spmd.clone, body=%wide.region_88.91_spmd.clone.sunk | while | flops 769382400 | bytes 63873808 | solution.py:166
  1489.7 8.7 dynamic_update_slice.123
  1513.0 8.7 dynamic_update_slice.123
  1536.2 8.7 dynamic_update_slice.123
  1575.6 5.2 multiply_convert_fusion.6
  1585.5 4.8 multiply_convert_fusion.7
  1594.0 4.9 convolution_convert_fusion.1
  1626.4 6.0 fusion.405
  1642.5 6.0 fusion.407
  1708.8 4.9 fusion.145
  1738.4 7.2 reduce-scatter.44.cloned.1.call-done
  1760.6 24.6 %all-reduce.3 = (f32[]{:T(128)}, f32[2,6,192]{2,1,0:T(8,128)S(1)}, f32[3,3]{1,0:T(4,128)S(1)}) all-reduce(f32[]{:T(128)S(6)} %add.709, f32[2,6,192]{2,1,0:T(8,128)S(1)} %fusion.271, f32[3,3]{1,0:T(4,128)S(1)} %convolution_add_fusion.7), channel_id=1, replica_groups=mesh['dp'=8,'mp'=4] {'dp'}, use_global_device_ids=true, to_apply=%region_20.21 | all-reduce | flops 2314 | bytes 18512 | tf_op jit(solution)/shard_map/psum | solution.py:469
  1789.6 43.2 %reduce-scatter.50.cloned.1.call-done = bf16[96,1344]{1,0:T(8,128)(2,1)} async-done(((bf16[768,1344]{1,0:T(8,128)(2,1)}), bf16[96,1344]{1,0:T(8,128)(2,1)}) %reduce-scatter.50.cloned.1.call-update) | async-done | bytes 258064
  1836.5 39.5 %all-reduce.1 = f32[7,768]{1,0:T(8,128)S(1)} all-reduce(f32[7,768]{1,0:T(8,128)S(1)} %add_add_fusion.12), channel_id=18, replica_groups=mesh['dp'=8,'mp'=4] {'dp','mp'}, use_global_device_ids=true, to_apply=%region_132.133.clone | all-reduce | flops 5376 | bytes 43008
  1876.7 58.2 %reduce-scatter.54.cloned.1.call-done = f32[24,441]{1,0:T(8,128)} async-done(((f32[768,441]{1,0:T(8,128)}), f32[24,441]{1,0:T(8,128)}) %reduce-scatter.54.cloned.1.call-update) | async-done | bytes 42352
  1939.6 40.2 %all-reduce.2 = (f32[]{:T(128)}, f32[]{:T(128)}) all-reduce(f32[]{:T(128)S(6)} %mul.1444, f32[]{:T(128)S(6)} %add.748), channel_id=1, replica_groups=mesh['dp'=8,'mp'=4] {'dp','mp'}, use_global_device_ids=true, to_apply=%region_60.61 | all-reduce | flops 2 | bytes 16 | tf_op jit(solution)/shard_map/psum | solution.py:86
  (1372 shorter events, 611.9 us)
Async XLA Ops:
  7.2 145.4 %copy-start.94 = (bf16[3,384,441]{1,2,0:T(8,128)(2,1)S(1)}, bf16[3,384,441]{1,2,0:T(8,128)(2,1)}, u32[]{:S(2)}) copy-start(bf16[3,384,441]{1,2,0:T(8,128)(2,1)} %param.39) | copy-start | bytes 3048196
  7.2 197.0 %all-gather.28.cloned.1.call-start = ((), (), s32[]{:S(2)}) async-start(), calls=%async_computation.26 | async-start | bytes 2949120 | tf_op jit(solution)/shard_map/all_gather | solution.py:66
  79.1 76.2 %copy-start.186 = (f32[768]{0:T(1024)}, f32[768]{0:T(1024)S(1)}, u32[]{:S(2)}) copy-start(f32[768]{0:T(1024)S(1)} %get-tuple-element.1180) | copy-start | bytes 9220
  157.2 76.5 %all-gather.18.cloned.1.call-start = ((), (), s32[]{:S(2)}) async-start(), calls=%async_computation.17 | async-start | bytes 2433024 | tf_op jit(solution)/shard_map/all_gather | solution.py:425
  158.0 127.8 %all-gather.24.cloned.1.call-start = ((), (), s32[]{:S(2)}) async-start(), calls=%async_computation.22 | async-start | bytes 2949120 | tf_op jit(solution)/shard_map/all_gather | solution.py:66
  158.8 178.4 %all-gather.16.cloned.1.call-start = ((), (), s32[]{:S(2)}) async-start(), calls=%async_computation.16 | async-start | bytes 2949120 | tf_op jit(solution)/shard_map/all_gather | solution.py:66
  159.3 293.0 %all-gather.20.cloned.1.call-start = ((), (), s32[]{:S(2)}) async-start(), calls=%async_computation.18 | async-start | bytes 1769472 | tf_op jit(solution)/shard_map/all_gather | solution.py:426
  160.1 393.7 %reduce-scatter.30.cloned.1.call-start = ((), (), s32[]{:S(2)}) async-start(), calls=%async_computation.23 | async-start | bytes 2949120 | tf_op jit(solution)/shard_map/reduce_scatter | solution.py:70
  175.4 213.3 %copy-start.99 = (f32[192,2,192]{2,1,0:T(2,128)}, f32[192,2,192]{2,1,0:T(2,128)S(1)}, u32[]{:S(2)}) copy-start(f32[192,2,192]{2,1,0:T(2,128)S(1)} %reshape.846) | copy-start | bytes 884740
  178.4 170.5 %copy-start.220 = (f32[4,192]{1,0:T(4,128)}, f32[4,192]{1,0:T(4,128)S(1)}, u32[]{:S(2)}) copy-start(f32[4,192]{1,0:T(4,128)S(1)} %get-tuple-element.1548) | copy-start | bytes 9220
  240.4 108.5 %copy-start.37 = (f32[384,4,192]{2,1,0:T(4,128)}, f32[384,4,192]{2,1,0:T(4,128)S(1)}, u32[]{:S(2)}) copy-start(f32[384,4,192]{2,1,0:T(4,128)S(1)} %reshape.826) | copy-start | bytes 3538948
  295.2 53.7 %copy-start.39 = (f32[384,4,192]{2,1,0:T(4,128)}, f32[384,4,192]{2,1,0:T(4,128)S(1)}, u32[]{:S(2)}) copy-start(f32[384,4,192]{2,1,0:T(4,128)S(1)} %reshape.824) | copy-start | bytes 3538948
  456.4 100.3 %reduce-scatter.34.cloned.1.call-start = ((), (), s32[]{:S(2)}) async-start(), calls=%async_computation.27 | async-start | bytes 2949120 | tf_op jit(solution)/shard_map/reduce_scatter | solution.py:70
  506.4 97.0 %reduce-scatter.26.cloned.1.call-start = ((), (), s32[]{:S(2)}) async-start(), calls=%async_computation.19 | async-start | bytes 2949120 | tf_op jit(solution)/shard_map/reduce_scatter | solution.py:70
  553.3 104.9 %all-gather.30.cloned.1.call-start = ((), (), s32[]{:S(2)}) async-start(), calls=%async_computation.28 | async-start | bytes 2949120 | tf_op jit(solution)/shard_map/all_gather | solution.py:66
  608.1 100.9 %all-gather.22.cloned.1.call-start = ((), (), s32[]{:S(2)}) async-start(), calls=%async_computation.20 | async-start | bytes 2949120 | tf_op jit(solution)/shard_map/all_gather | solution.py:66
  608.7 151.8 %all-gather.26.cloned.1.call-start = ((), (), s32[]{:S(2)}) async-start(), calls=%async_computation.24 | async-start | bytes 2949120 | tf_op jit(solution)/shard_map/all_gather | solution.py:66
  609.5 259.5 %reduce-scatter.36.cloned.1.call-start = ((), (), s32[]{:S(2)}) async-start(), calls=%async_computation.29 | async-start | bytes 2949120 | tf_op jit(solution)/shard_map/reduce_scatter | solution.py:70
  678.9 193.2 %reduce-scatter.28.cloned.1.call-start = ((), (), s32[]{:S(2)}) async-start(), calls=%async_computation.21 | async-start | bytes 2949120 | tf_op jit(solution)/shard_map/reduce_scatter | solution.py:70
  729.5 182.6 %reduce-scatter.32.cloned.1.call-start = ((), (), s32[]{:S(2)}) async-start(), calls=%async_computation.25 | async-start | bytes 2949120 | tf_op jit(solution)/shard_map/reduce_scatter | solution.py:70
  781.0 78.7 %copy-start.333 = (s32[1,3]{1,0:T(1,128)S(1)}, s32[1,3]{1,0:T(1,128)}, u32[]{:S(2)}) copy-start(s32[1,3]{1,0:T(1,128)} %param.41) | copy-start | bytes 40
  781.0 91.0 %copy-start.15 = (f32[384,768]{1,0:T(8,128)S(1)}, f32[384,768]{1,0:T(8,128)}, u32[]{:S(2)}) copy-start(f32[384,768]{1,0:T(8,128)} %copy-done.14) | copy-start | bytes 3538948
  781.1 226.7 %all-gather.40.cloned.1.call-start = ((), (), s32[]{:S(2)}) async-start(), calls=%async_computation.36 | async-start | bytes 2949120 | tf_op jit(solution)/shard_map/all_gather | solution.py:76
  866.4 51.4 %copy-start.229 = (s32[384]{0:T(512)}, s32[384]{0:T(512)S(1)}, u32[]{:S(2)}) copy-start(s32[384]{0:T(512)S(1)} %add_select_fusion.3) | copy-start | bytes 4612
  958.6 99.9 %all-gather.32.cloned.1.call-start = ((), (), s32[]{:S(2)}) async-start(), calls=%async_computation.30 | async-start | bytes 2949120 | tf_op jit(solution)/shard_map/all_gather | solution.py:76
  961.5 147.7 %all-gather.36.cloned.1.call-start = ((), (), s32[]{:S(2)}) async-start(), calls=%async_computation.33 | async-start | bytes 2949120 | tf_op jit(solution)/shard_map/all_gather | solution.py:76
  964.4 193.9 %reduce-scatter.42.cloned.1.call-start = ((), (), s32[]{:S(2)}) async-start(), calls=%async_computation.37 | async-start | bytes 2949120 | tf_op jit(solution)/shard_map/reduce_scatter | solution.py:80
  1021.1 187.1 %reduce-scatter.38.cloned.1.call-start = ((), (), s32[]{:S(2)}) async-start(), calls=%async_computation.31 | async-start | bytes 2949120 | tf_op jit(solution)/shard_map/reduce_scatter | solution.py:80
  1071.8 186.1 %reduce-scatter.40.cloned.1.call-start = ((), (), s32[]{:S(2)}) async-start(), calls=%async_computation.34 | async-start | bytes 2949120 | tf_op jit(solution)/shard_map/reduce_scatter | solution.py:80
  1122.5 135.4 %copy-start.202 = (f32[768]{0:T(1024)S(1)}, f32[768]{0:T(1024)}, u32[]{:S(2)}) copy-start(f32[768]{0:T(1024)} %get-tuple-element.1178) | copy-start | bytes 9220
  1122.5 135.4 %copy-start.204 = (f32[384]{0:T(512)S(1)}, f32[384]{0:T(512)}, u32[]{:S(2)}) copy-start(f32[384]{0:T(512)} %copy-done.203) | copy-start | bytes 4612
  1122.5 135.4 %copy-start.206 = (f32[384]{0:T(512)S(1)}, f32[384]{0:T(512)}, u32[]{:S(2)}) copy-start(f32[384]{0:T(512)} %copy-done.205) | copy-start | bytes 4612
  1122.5 135.4 %copy-start.208 = (f32[384]{0:T(512)S(1)}, f32[384]{0:T(512)}, u32[]{:S(2)}) copy-start(f32[384]{0:T(512)} %copy-done.207) | copy-start | bytes 4612
  1122.5 197.2 %all-gather.38.cloned.1.call-start = ((), (), s32[]{:S(2)}) async-start(), calls=%async_computation.35 | async-start | bytes 2949120 | tf_op jit(solution)/shard_map/all_gather | solution.py:76
  1269.6 126.9 %all-gather.34.cloned.1.call-start = ((), (), s32[]{:S(2)}) async-start(), calls=%async_computation.32 | async-start | bytes 2949120 | tf_op jit(solution)/shard_map/all_gather | solution.py:76
  1272.7 200.2 %all-gather.42.cloned.1.call-start = ((), (), s32[]{:S(2)}) async-start(), calls=%async_computation.38 | async-start | bytes 2949120 | tf_op jit(solution)/shard_map/all_gather | solution.py:76
  1273.9 351.1 %reduce-scatter.56.cloned.1.call-start = ((), (), s32[]{:S(2)}) async-start(), calls=%async_computation.45 | async-start | bytes 405504
  1275.6 459.5 %reduce-scatter.46.cloned.1.call-start = ((), (), s32[]{:S(2)}) async-start(), calls=%async_computation.40 | async-start | bytes 2949120 | tf_op jit(solution)/shard_map/reduce_scatter | solution.py:80
  1598.9 139.5 %reduce-scatter.48.cloned.1.call-start = ((), (), s32[]{:S(2)}) async-start(), calls=%async_computation.41 | async-start | bytes 2949120 | tf_op jit(solution)/shard_map/reduce_scatter | solution.py:80
  1610.0 135.6 %reduce-scatter.44.cloned.1.call-start = ((), (), s32[]{:S(2)}) async-start(), calls=%async_computation.39 | async-start | bytes 2949120 | tf_op jit(solution)/shard_map/reduce_scatter | solution.py:80
  1642.3 145.5 %reduce-scatter.52.cloned.1.call-start = ((), (), s32[]{:S(2)}) async-start(), calls=%async_computation.43 | async-start | bytes 1769472
  1695.1 137.7 %reduce-scatter.50.cloned.1.call-start = ((), (), s32[]{:S(2)}) async-start(), calls=%async_computation.42 | async-start | bytes 2433024
  1734.8 200.1 %reduce-scatter.54.cloned.1.call-start = ((), (), s32[]{:S(2)}) async-start(), calls=%async_computation.44 | async-start | bytes 1622016
  1759.2 76.9 %copy-start.288 = (f32[768]{0:T(1024)S(1)}, f32[768]{0:T(1024)}, u32[]{:S(2)}) copy-start(f32[768]{0:T(1024)} %get-tuple-element.1379) | copy-start | bytes 9220
  1759.2 76.9 %copy-start.287 = (f32[768]{0:T(1024)S(1)}, f32[768]{0:T(1024)}, u32[]{:S(2)}) copy-start(f32[768]{0:T(1024)} %get-tuple-element.1147) | copy-start | bytes 9220
  1759.2 76.9 %copy-start.298 = (f32[768]{0:T(1024)S(1)}, f32[768]{0:T(1024)}, u32[]{:S(2)}) copy-start(f32[768]{0:T(1024)} %get-tuple-element.1165) | copy-start | bytes 9220
  1759.2 77.0 %copy-start.297 = (f32[768]{0:T(1024)S(1)}, f32[768]{0:T(1024)}, u32[]{:S(2)}) copy-start(f32[768]{0:T(1024)} %get-tuple-element.1486) | copy-start | bytes 9220
  1759.2 77.0 %copy-start.286 = (f32[768]{0:T(1024)S(1)}, f32[768]{0:T(1024)}, u32[]{:S(2)}) copy-start(f32[768]{0:T(1024)} %get-tuple-element.1481) | copy-start | bytes 9220
  1759.2 77.0 %copy-start.296 = (f32[768]{0:T(1024)S(1)}, f32[768]{0:T(1024)}, u32[]{:S(2)}) copy-start(f32[768]{0:T(1024)} %get-tuple-element.1484) | copy-start | bytes 9220
  1759.2 77.0 %copy-start.285 = (f32[768]{0:T(1024)S(1)}, f32[768]{0:T(1024)}, u32[]{:S(2)}) copy-start(f32[768]{0:T(1024)} %get-tuple-element.1159) | copy-start | bytes 9220
  1759.2 77.0 %copy-start.306 = (f32[1,768]{1,0:T(1,128)S(1)}, f32[1,768]{1,0:T(1,128)}, u32[]{:S(2)}) copy-start(f32[1,768]{1,0:T(1,128)} %reshape.844) | copy-start | bytes 9220
  1759.2 77.0 %copy-start.307 = (f32[1,768]{1,0:T(1,128)S(1)}, f32[1,768]{1,0:T(1,128)}, u32[]{:S(2)}) copy-start(f32[1,768]{1,0:T(1,128)} %reshape.845) | copy-start | bytes 9220
  1759.2 77.0 %copy-start.311 = (f32[1,768]{1,0:T(1,128)S(1)}, f32[1,768]{1,0:T(1,128)}, u32[]{:S(2)}) copy-start(f32[1,768]{1,0:T(1,128)} %reshape.842) | copy-start | bytes 9220
  1759.2 77.0 %copy-start.312 = (f32[1,768]{1,0:T(1,128)S(1)}, f32[1,768]{1,0:T(1,128)}, u32[]{:S(2)}) copy-start(f32[1,768]{1,0:T(1,128)} %reshape.843) | copy-start | bytes 9220
  1759.2 77.0 %copy-start.304 = (f32[1,768]{1,0:T(1,128)S(1)}, f32[1,768]{1,0:T(1,128)}, u32[]{:S(2)}) copy-start(f32[1,768]{1,0:T(1,128)} %reshape.832) | copy-start | bytes 9220
  1759.3 77.0 %copy-start.305 = (f32[1,768]{1,0:T(1,128)S(1)}, f32[1,768]{1,0:T(1,128)}, u32[]{:S(2)}) copy-start(f32[1,768]{1,0:T(1,128)} %reshape.833) | copy-start | bytes 9220
  1759.3 77.0 %copy-start.309 = (f32[1,768]{1,0:T(1,128)S(1)}, f32[1,768]{1,0:T(1,128)}, u32[]{:S(2)}) copy-start(f32[1,768]{1,0:T(1,128)} %reshape.830) | copy-start | bytes 9220
  1759.3 77.0 %copy-start.310 = (f32[1,768]{1,0:T(1,128)S(1)}, f32[1,768]{1,0:T(1,128)}, u32[]{:S(2)}) copy-start(f32[1,768]{1,0:T(1,128)} %reshape.831) | copy-start | bytes 9220
  1759.3 77.1 %copy-start.302 = (f32[1,768]{1,0:T(1,128)S(1)}, f32[1,768]{1,0:T(1,128)}, u32[]{:S(2)}) copy-start(f32[1,768]{1,0:T(1,128)} %reshape.838) | copy-start | bytes 9220
  1759.3 77.1 %copy-start.303 = (f32[1,768]{1,0:T(1,128)S(1)}, f32[1,768]{1,0:T(1,128)}, u32[]{:S(2)}) copy-start(f32[1,768]{1,0:T(1,128)} %reshape.839) | copy-start | bytes 9220
  1759.3 77.1 %copy-start.308 = (f32[1,768]{1,0:T(1,128)S(1)}, f32[1,768]{1,0:T(1,128)}, u32[]{:S(2)}) copy-start(f32[1,768]{1,0:T(1,128)} %reshape.836) | copy-start | bytes 9220
  1759.3 179.2 %copy-start.116 = (bf16[2,2,384,192]{3,2,1,0:T(8,128)(2,1)S(1)}, bf16[2,2,384,192]{3,2,1,0:T(8,128)(2,1)}, u32[]{:S(2)}) copy-start(bf16[2,2,384,192]{3,2,1,0:T(8,128)(2,1)} %pad_maximum_fusion.3) | copy-start | bytes 1769476
  1759.3 223.2 %copy-start.124 = (f32[96,1344]{0,1:T(8,128)S(1)}, f32[96,1344]{0,1:T(8,128)}, u32[]{:S(2)}) copy-start(f32[96,1344]{0,1:T(8,128)} %copy.486) | copy-start | bytes 1548292
  1759.4 223.2 %copy-start.125 = (f32[96,1344]{0,1:T(8,128)S(1)}, f32[96,1344]{0,1:T(8,128)}, u32[]{:S(2)}) copy-start(f32[96,1344]{0,1:T(8,128)} %copy.485) | copy-start | bytes 1548292
  (359 other events, 2057.6 us)
Sparse Core Ops, SparseCore 0:
  157.3 46.8 all-gather.27
  206.7 26.9 all-gather.17
  235.3 50.4 all-gather.23
  287.8 49.2 all-gather.15
  339.4 24.4 all-gather.19
  456.5 46.9 reduce-scatter.29
  506.5 46.9 reduce-scatter.33
  555.8 47.5 reduce-scatter.25
  608.3 49.9 all-gather.29
  659.7 49.2 all-gather.21
  711.2 49.2 all-gather.25
  762.6 48.0 reduce-scatter.35
  813.0 49.0 reduce-scatter.27
  864.3 47.7 reduce-scatter.31
  958.7 48.9 all-gather.39
  1009.2 49.2 all-gather.31
  1059.9 49.2 all-gather.35
  1111.4 46.8 reduce-scatter.41
  1160.6 47.4 reduce-scatter.37
  1210.3 47.5 reduce-scatter.39
  1269.8 49.9 all-gather.37
  1321.3 49.2 all-gather.33
  1372.2 49.2 all-gather.41
  1426.4 93.6 reduce-scatter.55
  1599.0 46.9 reduce-scatter.45
  1648.2 47.5 reduce-scatter.47
  1698.0 47.5 reduce-scatter.43
  1749.2 38.1 reduce-scatter.51
  1791.1 41.6 reduce-scatter.49
  1837.9 97.0 reduce-scatter.53
where the time goes:
time: 2020 us; the launch traced here: 2010 us
  waiting for transfers between devices  739 us (37%)
  local copies, waits for them, and re-layouts  398 us (20%)
  blocking collectives  344 us (17%)
  matrix products  324 us (16%)
  other arithmetic  154 us (8%)
  between operations  43.5 us (2%)
    all_gather x6, waiting for transfers between devices, gather_rows(): return lax.all_gather(inputs, 'mp', axis=0, tiled=True)  222 us
    dynamic_update_slice x36, local copies, waits for them, and re-layouts, attend(): attended, log_total = lax.map(one_block, split_blocks(query_rows))  163 us
    all_gather x6, waiting for transfers between devices, gather_grads(): return lax.all_gather(inputs, 'mp', axis=0, tiled=True)  162 us
    reduce_scatter x6, waiting for transfers between devices, sum_grads(): lax.psum_scatter(inputs.astype(jnp.bfloat16), 'mp', scatter_dimension=0,...  142 us
    unnamed x34, waiting for transfers between devices  104 us
    dot_general x18, matrix products, product(): jnp.dot(first_operand, second_operand, preferred_element_type=jnp.float32)  96 us
    reduce_scatter x6, waiting for transfers between devices, sum_rows(): lax.psum_scatter(inputs.astype(jnp.bfloat16), 'mp', scatter_dimension=0,...  79.1 us
    all_gather x1, blocking collectives, shards(): lax.all_gather(head_weight, ('dp', 'mp'), axis=1, tiled=True)  77.4 us
  transfers between devices with their start and end apart: 30, of which 19 were waited for; matrix products, arithmetic and copies ran while one was open for 38% of the time, Pallas kernels for 0%

commit v1 on v0

v1 whole, which is shorter than its diff:
```python
import functools

import jax
import jax.numpy as jnp
from jax import lax
from jax.experimental import pallas as pl
from jax.experimental.pallas import tpu as pltpu
from jax.sharding import PartitionSpec as P

MICRO = 3
FRAME = 64
EPSILON = 1e-06
LEARNING = 300.0
VECTOR_LEARNING = 6000.0
MOMENTUM = 0.5
AVERAGING = 0.5
THRESHOLD = 0.05
PRECISE = lax.Precision.HIGHEST
QUAD = 4
bf16 = jnp.bfloat16
f32 = jnp.float32


def norm_rows(inputs, gain_row, shift_row):
    row_mean = jnp.mean(inputs, axis=-1, keepdims=True)
    centered = inputs - row_mean
    variance = jnp.mean(centered * centered, axis=-1, keepdims=True)
    return centered * lax.rsqrt(variance + EPSILON) * gain_row + shift_row


def gelu_exact(inputs):
    return jax.nn.gelu(inputs, approximate=False)


def product(first_operand, second_operand):
    return jnp.dot(first_operand, second_operand, preferred_element_type=f32)


def contract_last(first_operand, second_operand):
    return lax.dot_general(
        first_operand, second_operand, (((1,), (1,)), ((), ())), preferred_element_type=f32
    )


def contract_rows(first_operand, second_operand):
    return lax.dot_general(
        first_operand, second_operand, (((0,), (0,)), ((), ())), preferred_element_type=f32
    )


def apply_update(weight, gradient, moment, average, rate):
    moment = MOMENTUM * moment + gradient
    updated = weight - rate * (gradient + MOMENTUM * moment)
    return (updated, moment, AVERAGING * average + (1.0 - AVERAGING) * updated)


def swap_dp(inputs, mask):
    size = lax.axis_size("dp")
    return lax.ppermute(inputs, "dp", [(i, i ^ mask) for i in range(size)])


def swap_mp(inputs, mask):
    size = lax.axis_size("mp")
    return lax.ppermute(inputs, "mp", [(i, i ^ mask) for i in range(size)])


def dp_bits():
    return lax.axis_size("dp").bit_length() - 1


def regroup(inputs):
    count = lax.axis_size("dp")
    pairs = []
    for d in range(count):
        for z in range(4):
            hi, x, k = d // 4, (d // 2) % 2, d % 2
            pairs.append((d * 4 + z, (hi * 4 + (z % 2) * 2 + z // 2) * 4 + 2 * k + x))
    return lax.ppermute(inputs, ("dp", "mp"), pairs)


def gather_mp(inputs):
    place = lax.axis_index("mp")
    pieces = jnp.stack([inputs] + [swap_mp(inputs, s) for s in (1, 2, 3)])
    return [lax.dynamic_index_in_dim(pieces, j ^ place, 0, keepdims=False) for j in range(4)]


def gather_dp(inputs, order):
    pieces = {0: inputs}
    rows = inputs.shape[0]
    for bit in order:
        keys = sorted(pieces)
        sent = jnp.concatenate([pieces[k] for k in keys]) if len(keys) > 1 else pieces[0]
        got = swap_dp(sent, 1 << bit)
        for i, k in enumerate(keys):
            pieces[k ^ (1 << bit)] = got[i * rows : (i + 1) * rows]
    return jnp.concatenate([pieces[k] for k in sorted(pieces)])


def scatter_dp(inputs, order):
    count = lax.axis_size("dp")
    rows = inputs.shape[0] // count
    pieces = {k: inputs[k * rows : (k + 1) * rows] for k in range(count)}
    for bit in order:
        mine = [k for k in sorted(pieces) if not (k >> bit) & 1]
        away = [k for k in sorted(pieces) if (k >> bit) & 1]
        sent = jnp.concatenate([pieces[k] for k in away]) if len(away) > 1 else pieces[away[0]]
        got = swap_dp(sent, 1 << bit)
        pieces = {
            k: (
                pieces[k].astype(f32) + got[i * rows : (i + 1) * rows].astype(f32)
            ).astype(inputs.dtype)
            for i, k in enumerate(mine)
        }
    return pieces[0]


def gather_split(inputs):
    half = inputs.shape[1] // 2
    up = list(range(1, dp_bits()))
    return jnp.concatenate(
        [
            gather_dp(inputs[:, :half], up + [0]),
            gather_dp(inputs[:, half:], up[::-1] + [0]),
        ],
        axis=1,
    )


def scatter_split(inputs):
    half = inputs.shape[1] // 2
    up = list(range(1, dp_bits()))
    return jnp.concatenate(
        [
            scatter_dp(inputs[:, :half], [0] + up),
            scatter_dp(inputs[:, half:], [0] + up[::-1]),
        ],
        axis=1,
    )


def scatter_mp(pieces):
    place = lax.axis_index("mp")
    stacked = jnp.stack(pieces)
    total = lax.dynamic_index_in_dim(stacked, place, 0, keepdims=False).astype(f32)
    for s in (1, 2, 3):
        total = total + swap_mp(
            lax.dynamic_index_in_dim(stacked, place ^ s, 0, keepdims=False), s
        ).astype(f32)
    return total


def sum_all(inputs):
    for bit in range(dp_bits()):
        inputs = inputs + swap_dp(inputs, 1 << bit)
    for mask in (1, 2):
        inputs = inputs + swap_mp(inputs, mask)
    return inputs


def group_gather(inputs):
    one = swap_dp(inputs, 1)
    two = swap_dp(inputs, 2)
    three = swap_dp(two, 1)
    return [inputs, one, two, three]


def group_scatter(parts):
    got = swap_dp(jnp.stack([parts[1], parts[3]]), 1)
    mine = parts[0].astype(f32) + got[0].astype(f32)
    far = (parts[2].astype(f32) + got[1].astype(f32)).astype(bf16)
    return mine + swap_dp(far, 2).astype(f32)


def group_sum_features(inputs):
    count = lax.axis_size("dp")
    width = inputs.shape[1] // count
    for mask in (1, 2):
        got = swap_dp(inputs, mask)
        blocks = [got[:, (b ^ mask) * width : ((b ^ mask) + 1) * width] for b in range(count)]
        inputs = inputs + jnp.concatenate(blocks, axis=1)
    return inputs


def attend_kernel(q_ref, k_ref, v_ref, bias_ref, out_ref, prob_ref):
    query = q_ref[...]
    rows, width = query.shape
    size = width // QUAD
    keys_t = k_ref[...].T
    values = v_ref[...]
    lane = lax.broadcasted_iota(jnp.int32, (rows, width), 1) // size
    scaled = query * (size**-0.5)
    total = query.astype(f32)
    for h in range(QUAD):
        own = jnp.where(lane == h, scaled, jnp.zeros_like(scaled))
        scores = jnp.dot(own, keys_t, preferred_element_type=f32) + bias_ref[0, h : h + 1, :]
        top = jnp.max(scores, axis=-1, keepdims=True)
        exponent = jnp.exp(scores - top)
        denominator = jnp.sum(exponent, axis=-1, keepdims=True)
        probs = (exponent * (1.0 / denominator)).astype(bf16)
        prob_ref[h] = probs
        mixed = jnp.dot(probs, values, preferred_element_type=f32)
        total = total + jnp.where(lane == h, mixed, 0.0)
    out_ref[...] = total.astype(bf16)


def attend(query, keys, values, bias):
    rows, width = query.shape
    count = keys.shape[0]
    heads = bias.shape[0] * QUAD
    block = width // bias.shape[0]
    return pl.pallas_call(
        attend_kernel,
        grid=(bias.shape[0],),
        in_specs=[
            pl.BlockSpec((rows, block), lambda i: (0, i)),
            pl.BlockSpec((count, block), lambda i: (0, i)),
            pl.BlockSpec((count, block), lambda i: (0, i)),
            pl.BlockSpec((1, QUAD, count), lambda i: (i, 0, 0)),
        ],
        out_specs=[
            pl.BlockSpec((rows, block), lambda i: (0, i)),
            pl.BlockSpec((QUAD, rows, count), lambda i: (i, 0, 0)),
        ],
        out_shape=[
            jax.ShapeDtypeStruct((rows, width), bf16),
            jax.ShapeDtypeStruct((heads, rows, count), bf16),
        ],
        compiler_params=pltpu.CompilerParams(vmem_limit_bytes=40 * 1024 * 1024),
        cost_estimate=pl.CostEstimate(
            flops=4 * rows * count * width * 4,
            bytes_accessed=heads * rows * count * 2,
            transcendentals=heads * rows * count,
        ),
    )(query, keys, values, bias)


def attend_back_kernel(q_ref, k_ref, v_ref, prob_ref, grad_ref, dq_ref, dk_ref, dv_ref, db_ref):
    query = q_ref[...]
    grad = grad_ref[...]
    rows, width = query.shape
    size = width // QUAD
    keys = k_ref[...]
    values_t = v_ref[...].T
    query_t = query.T
    grad_t = grad.T
    scaling = size**-0.5
    lane = lax.broadcasted_iota(jnp.int32, (rows, width), 1) // size
    total = jnp.zeros((rows, width), f32)
    ones = jnp.ones((16, rows), bf16)
    key_parts, value_parts = [], []
    for h in range(QUAD):
        own = jnp.where(lane == h, grad, jnp.zeros_like(grad))
        probs_low = prob_ref[h]
        probs = probs_low.astype(f32)
        pulled = probs * jnp.dot(own, values_t, preferred_element_type=f32)
        shift = jnp.sum(pulled, axis=-1, keepdims=True)
        score_grad = (pulled - probs * shift).astype(bf16)
        mixed = jnp.dot(score_grad, keys, preferred_element_type=f32)
        total = total + jnp.where(lane == h, mixed, 0.0)
        left = jnp.concatenate([query_t[h * size : (h + 1) * size], ones])
        found = jnp.dot(left, score_grad, preferred_element_type=f32)
        key_parts.append(found[:size])
        db_ref[0, h : h + 1, :] = found[size : size + 1]
        value_parts.append(
            jnp.dot(
                grad_t[h * size : (h + 1) * size], probs_low, preferred_element_type=f32
            )
        )
    dq_ref[...] = (total * scaling + grad.astype(f32)).astype(bf16)
    dk_ref[...] = jnp.concatenate(key_parts).T * scaling
    dv_ref[...] = jnp.concatenate(value_parts).T


def attend_back(query, keys, values, probs, grad):
    rows, width = query.shape
    count = keys.shape[0]
    heads = probs.shape[0]
    quads = heads // QUAD
    block = width // quads
    return pl.pallas_call(
        attend_back_kernel,
        grid=(quads,),
        in_specs=[
            pl.BlockSpec((rows, block), lambda i: (0, i)),
            pl.BlockSpec((count, block), lambda i: (0, i)),
            pl.BlockSpec((count, block), lambda i: (0, i)),
            pl.BlockSpec((QUAD, rows, count), lambda i: (i, 0, 0)),
            pl.BlockSpec((rows, block), lambda i: (0, i)),
        ],
        out_specs=[
            pl.BlockSpec((rows, block), lambda i: (0, i)),
            pl.BlockSpec((count, block), lambda i: (0, i)),
            pl.BlockSpec((count, block), lambda i: (0, i)),
            pl.BlockSpec((1, QUAD, count), lambda i: (i, 0, 0)),
        ],
        out_shape=[
            jax.ShapeDtypeStruct((rows, width), bf16),
            jax.ShapeDtypeStruct((count, width), f32),
            jax.ShapeDtypeStruct((count, width), f32),
            jax.ShapeDtypeStruct((quads, QUAD, count), f32),
        ],
        compiler_params=pltpu.CompilerParams(vmem_limit_bytes=40 * 1024 * 1024),
        cost_estimate=pl.CostEstimate(
            flops=8 * rows * count * width * 4,
            bytes_accessed=heads * rows * count * 2,
            transcendentals=0,
        ),
    )(query, keys, values, probs, grad)


def one_hot_rows(index, count):
    return (index[:, None] == jnp.arange(count)[None, :]).astype(bf16)


def shards(
    patches,
    clip_len,
    box_count,
    box_bounds,
    box_labels,
    memory,
    up_weight,
    down_weight,
    embed_weight,
    head_weight,
    vector_weight,
    conv_weight,
    position_bias,
    up_moment,
    down_moment,
    embed_moment,
    head_moment,
    vector_moment,
    conv_moment,
    position_moment,
    up_average,
    down_average,
    embed_average,
    head_average,
    vector_average,
    conv_average,
    position_average,
):
    dp_index = lax.axis_index("dp")
    mp_index = lax.axis_index("mp")
    dp_count = lax.axis_size("dp")
    across, core = (dp_index // 2) % 2, dp_index % 2
    quarter = 2 * core + across
    rows = patches.shape[1]
    eighth = rows // 8
    pooled = rows // 4
    head_cols = conv_weight.shape[2]
    width = 4 * head_cols
    sub = embed_weight.shape[1]
    patch = embed_weight.shape[0]
    classes = head_weight.shape[0]
    boxes = box_bounds.shape[2]
    heads = position_bias.shape[0] * 4

    ints = jnp.concatenate(
        [clip_len.reshape(-1), box_count.reshape(-1), box_bounds.reshape(-1), box_labels.reshape(-1)]
    )
    total_ints = ints.shape[0]
    ints = jnp.pad(ints, (0, -total_ints % 1024)).reshape(-1, 128)
    ints = regroup(ints).reshape(-1)
    patches = regroup(patches)
    memory_part = regroup(memory)
    lengths_all = ints[:5]
    counts = ints[5:8]
    bounds = ints[8 : 8 + MICRO * boxes * 2].reshape(MICRO, boxes, 2)
    labels = ints[8 + MICRO * boxes * 2 : total_ints].reshape(MICRO * boxes, classes)

    vec_hi = lax.reduce_precision(vector_weight, 8, 7)
    vec_mid = lax.reduce_precision(vector_weight - vec_hi, 8, 7)
    vec_lo = vector_weight - vec_hi - vec_mid
    small = jnp.concatenate(
        [embed_weight, head_weight, vec_hi, vec_mid, vec_lo], axis=0
    ).astype(bf16).T
    small = jnp.concatenate(gather_mp(small), axis=0)
    small = gather_dp(small, [1, 2] + list(range(3, dp_bits())) + [0])
    embed_t = small[:, :patch]
    head_t = small[:, patch : patch + classes]
    vec3 = small[:, patch + classes :].astype(f32)
    vectors = (vec3[:, :7] + vec3[:, 7:14] + vec3[:, 14:]).T

    taps_pos = jnp.concatenate(
        [
            conv_weight.reshape(12, head_cols),
            jnp.pad(position_bias.reshape(1, -1), ((0, 0), (0, head_cols - position_bias.size))),
        ]
    )
    taps_pos = gather_mp(taps_pos)
    conv_all = jnp.concatenate([t[:12] for t in taps_pos], axis=1).reshape(2, 6, width)
    rel_bias = jnp.concatenate(
        [t[12, : position_bias.size].reshape(position_bias.shape) for t in taps_pos], axis=0
    )

    up_low = up_weight.astype(bf16)
    down_low = down_weight.astype(bf16)
    qkv_pieces = gather_mp(up_low[:, : 3 * head_cols])
    qkv = jnp.concatenate(
        [p[:, j * head_cols : (j + 1) * head_cols] for j in range(3) for p in qkv_pieces], axis=1
    )
    qkv = gather_split(qkv)
    rest_pieces = gather_mp(jnp.concatenate([down_low, up_low[:, 3 * head_cols :]], axis=1))
    hidden_cols = up_weight.shape[1] - 3 * head_cols
    rest = jnp.concatenate(
        [p[:, :head_cols] for p in rest_pieces]
        + [p[:, head_cols : head_cols + hidden_cols] for p in rest_pieces]
        + [p[:, head_cols + hidden_cols :] for p in rest_pieces],
        axis=1,
    )
    rest = gather_split(rest)
    w_out = rest[:, :width]
    w_back = rest[:, width : width + 4 * hidden_cols]
    w_hidden = rest[:, width + 4 * hidden_cols :]

    place = jnp.arange(rows)
    token = 8 * (place % eighth) + 4 * ((place // eighth) % 2) + place // (2 * eighth)
    order = one_hot_rows(token, rows)
    patches = jnp.einsum("rt,mtc->mrc", order, patches, preferred_element_type=f32).astype(bf16)
    patches = patches.reshape(MICRO * rows, patch)
    mem_rows = memory_part.shape[2]
    mem_place = jnp.arange(mem_rows)
    mem_order = one_hot_rows(
        2 * (mem_place % (mem_rows // 2)) + mem_place // (mem_rows // 2), mem_rows
    )
    memory_part = jnp.einsum(
        "rt,abtc->abrc", mem_order, memory_part, preferred_element_type=f32
    ).astype(bf16)
    mem_parts = jnp.stack(group_gather(memory_part))
    part_of = [((q // 2) ^ core) + 2 * ((q % 2) ^ across) for q in range(4)]
    mem_full = jnp.concatenate(
        [lax.dynamic_index_in_dim(mem_parts, s, 0, keepdims=False) for s in part_of], axis=3
    )

    def compress(first, second, channel):
        return (
            first.astype(f32) * conv_all[channel, 4] + second.astype(f32) * conv_all[channel, 5]
        ).astype(bf16)

    half_mem = mem_rows // 2
    stored = []
    for m in range(2):
        stored.append(
            [
                (
                    mem_full[m, ch, :half_mem],
                    mem_full[m, ch, half_mem:],
                    compress(mem_full[m, ch, :half_mem], mem_full[m, ch, half_mem:], ch),
                )
                for ch in range(2)
            ]
        )

    embedded = contract_last(patches, embed_t) + vectors[0]
    normed = norm_rows(embedded, vectors[1], vectors[2]).astype(bf16)
    projected = product(normed, qkv)
    query = projected[:, :width].astype(bf16).reshape(MICRO, rows, width)
    raw = [
        projected[:, width * (1 + ch) : width * (2 + ch)].reshape(MICRO, 4, pooled, width)
        for ch in range(2)
    ]
    pools = [
        jnp.sum(raw[ch] * conv_all[ch, :4][None, :, None, :], axis=1).astype(bf16)
        for ch in range(2)
    ]
    gathered = [
        group_gather(jnp.stack([pools[0][m], pools[1][m]])) for m in range(MICRO)
    ]
    half_pool = pooled // 2
    for m in range(2):
        entry = []
        for ch in range(2):
            first = jnp.concatenate([g[ch, :half_pool] for g in gathered[m]])
            second = jnp.concatenate([g[ch, half_pool:] for g in gathered[m]])
            entry.append((first, second, compress(first, second, ch)))
        stored.append(entry)
    key_rows, value_rows = [], []
    for m in range(MICRO):
        for ch, out in ((0, key_rows), (1, value_rows)):
            out.append(
                jnp.concatenate(
                    [g[ch] for g in gathered[m]] + [stored[m + 1][ch][2], stored[m][ch][2]]
                )
            )

    part_quarter = [2 * (core ^ (s % 2)) + (across ^ (s // 2)) for s in range(4)]
    pool_place = jnp.arange(pooled)
    pool_token = 2 * (pool_place % half_pool) + pool_place // half_pool
    now_index = jnp.concatenate([pq * pooled + pool_token for pq in part_quarter])
    pool_index = jnp.concatenate([pq * half_pool + jnp.arange(half_pool) for pq in part_quarter])
    mem_index = jnp.arange(half_mem)

    def key_bias(m):
        newer_index = mem_index if m == 0 else pool_index
        older_index = mem_index if m < 2 else pool_index
        pieces = [
            (now_index, lengths_all[2 + m] // 4),
            (newer_index, lengths_all[1 + m] // 8),
            (older_index, lengths_all[m] // 8),
        ]
        return jnp.concatenate(
            [
                jnp.where((index < limit)[None, :], rel_bias[:, g : g + 1], -1e30)
                for g, (index, limit) in enumerate(pieces)
            ],
            axis=1,
        ).reshape(heads // QUAD, QUAD, -1)

    attended, probs = [], []
    for m in range(MICRO):
        out, prob = attend(query[m], key_rows[m], value_rows[m], key_bias(m))
        attended.append(out)
        probs.append(prob)
    attended_all = jnp.concatenate(attended)

    first_res = embedded + contract_last(attended_all, w_out)
    normed_mlp = norm_rows(first_res, vectors[3], vectors[4]).astype(bf16)
    hidden = product(normed_mlp, w_hidden)
    active = gelu_exact(hidden).astype(bf16)
    second_res = first_res + contract_last(active, w_back)
    final_rows = norm_rows(second_res, vectors[5], vectors[6])

    position = quarter * rows + token
    within = position % FRAME
    live = position[None, :] < lengths_all[2:, None]
    inside = (
        (within[None, None, :] >= bounds[:, :, 0:1])
        & (within[None, None, :] < bounds[:, :, 1:2])
        & live[:, None, :]
    )
    denominator = ((bounds[:, :, 1] - bounds[:, :, 0]) * (lengths_all[2:, None] // FRAME)).astype(
        f32
    )
    select = inside.astype(f32) / denominator[:, :, None]
    feature = jnp.einsum(
        "mbt,mtd->mbd", select, final_rows.reshape(MICRO, rows, width), precision=PRECISE
    ).reshape(MICRO * boxes, width)
    feature = group_sum_features(feature).astype(bf16)
    logits = product(feature, head_t)
    target = labels.astype(f32)
    keep = (jnp.arange(boxes)[None, :] < counts[:, None]).astype(f32).reshape(-1, 1)
    lead = (quarter == 0).astype(f32)
    loss_part = jnp.sum((jax.nn.softplus(logits) - target * logits) * keep) * lead
    grad_logits = ((jax.nn.sigmoid(logits) - target) * keep).astype(bf16)

    grad_head = contract_rows(feature, grad_logits) * lead
    grad_feature = contract_last(grad_logits, head_t).reshape(MICRO, boxes, width)
    grad_final = jnp.einsum("mbt,mbd->mtd", select, grad_feature, precision=PRECISE).reshape(
        MICRO * rows, width
    )
    grad_second, grad_gain3, grad_shift3 = jax.vjp(norm_rows, second_res, vectors[5], vectors[6])[
        1
    ](grad_final)
    grad_branch = grad_second.astype(bf16)
    grad_back = contract_rows(grad_branch, active)
    grad_active = product(grad_branch, w_back)
    grad_hidden = jax.vjp(gelu_exact, hidden)[1](grad_active)[0].astype(bf16)
    grad_w_hidden = contract_rows(normed_mlp, grad_hidden)
    rest_grad = scatter_split(
        jnp.concatenate([grad_back.astype(bf16), grad_w_hidden.astype(bf16)], axis=1)
    )
    grad_normed = contract_last(grad_hidden, w_hidden)
    grad_first, grad_gain2, grad_shift2 = jax.vjp(norm_rows, first_res, vectors[3], vectors[4])[1](
        grad_normed
    )
    grad_first = grad_first + grad_second
    grad_attn = grad_first.astype(bf16)
    grad_out = contract_rows(grad_attn, attended_all)
    grad_attended = product(grad_attn, w_out).astype(bf16).reshape(MICRO, rows, width)

    grad_query, pool_grads, bias_grads = [], [], []
    mem_taps = [jnp.zeros((2, width), f32), jnp.zeros((2, width), f32)]
    now = 4 * pooled
    for m in range(MICRO):
        dq, dk, dv, db = attend_back(
            query[m], key_rows[m], value_rows[m], probs[m], grad_attended[m]
        )
        grad_query.append(dq)
        bias_grads.append(db.reshape(heads, -1))
        low = jnp.stack([dk[:now].astype(bf16), dv[:now].astype(bf16)])
        pool_grads.append(
            group_scatter([low[:, s * pooled : (s + 1) * pooled] for s in range(4)])
        )
        for ch, grad in ((0, dk), (1, dv)):
            for which, start in ((m + 1, now), (m, now + half_mem)):
                part = grad[start : start + half_mem]
                mem_taps[ch] = mem_taps[ch] + jnp.stack(
                    [
                        jnp.sum(part * stored[which][ch][0].astype(f32), axis=0),
                        jnp.sum(part * stored[which][ch][1].astype(f32), axis=0),
                    ]
                )
    bias_total = bias_grads[0] + bias_grads[1] + bias_grads[2]
    grad_rel = jnp.stack(
        [
            jnp.sum(bias_total[:, :now], axis=1),
            jnp.sum(bias_total[:, now : now + half_mem], axis=1),
            jnp.sum(bias_total[:, now + half_mem :], axis=1),
        ],
        axis=1,
    )
    pool_grad = jnp.stack(pool_grads)
    raw_grads, taps_grads = [], []
    for ch in range(2):
        spread = pool_grad[:, ch][:, None] * conv_all[ch, :4][None, :, None, :]
        raw_grads.append(spread.astype(bf16).reshape(MICRO * rows, width))
        taps_grads.append(jnp.sum(pool_grad[:, ch][:, None] * raw[ch], axis=(0, 2)))
    grad_conv = jnp.stack(
        [jnp.concatenate([taps_grads[ch], mem_taps[ch]], axis=0) for ch in range(2)]
    )
    grad_projected = jnp.concatenate([jnp.concatenate(grad_query)] + raw_grads, axis=1)
    grad_qkv = contract_rows(normed, grad_projected)
    grad_normed_in = contract_last(grad_projected, qkv)
    grad_embedded, grad_gain1, grad_shift1 = jax.vjp(norm_rows, embedded, vectors[1], vectors[2])[
        1
    ](grad_normed_in)
    grad_embedded = (grad_embedded + grad_first).astype(bf16)
    grad_embed = contract_rows(grad_embedded, patches)
    grad_vectors = jnp.stack(
        [
            jnp.sum(grad_embedded.astype(f32), axis=0),
            grad_gain1,
            grad_shift1,
            grad_gain2,
            grad_shift2,
            grad_gain3,
            grad_shift3,
        ]
    )

    attn_grad = scatter_split(
        jnp.concatenate([grad_out.astype(bf16), grad_qkv.astype(bf16)], axis=1)
    )
    small_grad = scatter_dp(
        jnp.concatenate([grad_embed, grad_head, grad_vectors.T], axis=1),
        list(range(dp_bits())),
    )
    small_grad = scatter_mp([small_grad[j * sub : (j + 1) * sub] for j in range(4)]).T
    embed_grad = small_grad[:patch]
    head_grad = small_grad[patch : patch + classes]
    vector_grad = small_grad[patch + classes :]

    rest_mine = scatter_mp(
        [
            jnp.concatenate(
                [
                    rest_grad[:, j * hidden_cols : (j + 1) * hidden_cols],
                    rest_grad[:, (4 + j) * hidden_cols : (5 + j) * hidden_cols],
                ],
                axis=1,
            )
            for j in range(4)
        ]
    )
    attn_mine = scatter_mp(
        [
            jnp.concatenate(
                [
                    attn_grad[:, i * width + j * head_cols : i * width + (j + 1) * head_cols]
                    for i in range(4)
                ],
                axis=1,
            )
            for j in range(4)
        ]
    )
    down_grad = jnp.concatenate([attn_mine[:, :head_cols], rest_mine[:, :hidden_cols]], axis=1)
    up_grad = jnp.concatenate([attn_mine[:, head_cols:], rest_mine[:, hidden_cols:]], axis=1)

    count_local = jnp.sum(box_count).astype(f32) * (mp_index == 0).astype(f32)
    flat = jnp.concatenate(
        [grad_conv.reshape(-1), grad_rel.reshape(-1), loss_part[None], count_local[None]]
    )
    size = flat.shape[0]
    flat = sum_all(jnp.pad(flat, (0, -size % 1024)).reshape(-1, 128)).reshape(-1)
    conv_full = flat[: 12 * width].reshape(2, 6, 4, head_cols)
    conv_grad = lax.dynamic_index_in_dim(conv_full, mp_index, 2, keepdims=False)
    rel_full = flat[12 * width : 12 * width + heads * 3].reshape(4, heads // 4, 3)
    position_grad = lax.dynamic_index_in_dim(rel_full, mp_index, 0, keepdims=False)
    loss_global = flat[size - 2]
    box_total = flat[size - 1]

    reduced = (up_grad, down_grad, embed_grad, head_grad, vector_grad, conv_grad, position_grad)
    squares = sum((jnp.sum(gradient * gradient) for gradient in reduced[:5]))
    squares = squares + (
        jnp.sum(conv_grad * conv_grad) + jnp.sum(position_grad * position_grad)
    ) / dp_count
    square_total = sum_all(jnp.full((8, 128), squares, f32))[0, 0]
    grad_norm = jnp.sqrt(square_total) / box_total
    scaling = jnp.minimum(1.0, THRESHOLD / grad_norm) / box_total
    masters = (
        up_weight,
        down_weight,
        embed_weight,
        head_weight,
        vector_weight,
        conv_weight,
        position_bias,
    )
    moments = (
        up_moment,
        down_moment,
        embed_moment,
        head_moment,
        vector_moment,
        conv_moment,
        position_moment,
    )
    averages = (
        up_average,
        down_average,
        embed_average,
        head_average,
        vector_average,
        conv_average,
        position_average,
    )
    rates = (LEARNING,) * 4 + (VECTOR_LEARNING,) * 3
    results = [
        apply_update(weight, gradient * scaling, moment, average, rate)
        for weight, gradient, moment, average, rate in zip(
            masters, reduced, moments, averages, rates
        )
    ]

    kept = []
    for m in (1, 2):
        parts = jnp.stack(gathered[m]).reshape(4, 2, 2, half_pool, 4, head_cols)
        parts = lax.dynamic_index_in_dim(parts, quarter, 4, keepdims=False)
        ordered = jnp.stack(
            [lax.dynamic_index_in_dim(parts, s, 0, keepdims=False) for s in part_of], axis=1
        )
        kept.append(ordered.transpose(0, 1, 3, 2, 4).reshape(2, 4 * pooled, head_cols))
    new_memory = regroup(jnp.stack(kept))
    return (
        (loss_global, box_total, grad_norm, new_memory)
        + tuple(r[0] for r in results)
        + tuple(r[1] for r in results)
        + tuple(r[2] for r in results)
        + (results[0][0].astype(bf16), results[1][0].astype(bf16))
    )


def solution(mesh):
    both = ("dp", "mp")
    weight_specs = (
        P("dp", "mp"),
        P("dp", "mp"),
        P(None, both),
        P(None, both),
        P(None, both),
        P(None, None, "mp"),
        P("mp", None),
    )
    memory_spec = P(None, None, "dp", "mp")
    return jax.shard_map(
        shards,
        mesh=mesh,
        in_specs=(
            P(None, both, None),
            P("dp", None),
            P("dp", None),
            P("dp", None, None, None),
            P("dp", None, None, None),
            memory_spec,
        )
        + weight_specs * 3,
        out_specs=(P(), P(), P(), memory_spec)
        + weight_specs * 3
        + (P("dp", "mp"), P("dp", "mp")),
        check_vma=False,
    )
```

time: 2020 us -> 864 us (0.43)
  waiting for transfers between devices: 739 us -> 157 us
  blocking collectives: 344 us -> 0 us
  local copies, waits for them, and re-layouts: 398 us -> 210 us
  matrix products: 324 us -> 149 us
  starting transfers between devices: 2.48 us -> 124 us
  Pallas kernels: 0 us -> 60.7 us
  other arithmetic: 154 us -> 122 us
    all_gather x14 -> x0, waiting for transfers between devices: 413 us -> none  [the longest x6 222 us: gather_rows(): return lax.all_gather(inputs, 'mp', axis=0, tiled=True)]
    reduce_scatter x12 -> x0, waiting for transfers between devices: 222 us -> none  [the longest x6 142 us: sum_grads(): lax.psum_scatter(inputs.astype(jnp.bfloat16), 'mp', scatter_dimension=0,...]
    all_gather x3 -> x0, blocking collectives: 220 us -> none  [the longest x1 77.4 us: shards(): lax.all_gather(head_weight, ('dp', 'mp'), axis=1, tiled=True)]
    dynamic_update_slice x45 -> x0, local copies, waits for them, and re-layouts: 165 us -> none  [the longest x36 163 us: attend(): attended, log_total = lax.map(one_block, split_blocks(query_rows))]
    ppermute x0 -> x85, waiting for transfers between devices: none -> 157 us  [the longest x56 117 us: swap_dp(): return lax.ppermute(inputs, 'dp', [(i, i ^ mask) for i in range(size)])]
    dot_general x91 -> x9, matrix products: 226 us -> 82.2 us  [the longest x5 71.2 us: product(): return jnp.dot(first_operand, second_operand, preferred_element_type=f32)]
    ppermute x0 -> x85, starting transfers between devices: none -> 124 us  [the longest x25 56.3 us: swap_mp(): return lax.ppermute(inputs, 'mp', [(i, i ^ mask) for i in range(size)])]
    unnamed x34 -> x0, waiting for transfers between devices: 104 us -> none
  transfers between devices with their start and end apart: 30 -> 85, of which waited for: 19 -> 29; matrix products, arithmetic and copies ran while one was open for 38% -> 35% of each run, Pallas kernels for 0% -> 3%
where the time goes in v1:
time: 864 us; the launch traced here: 851 us
  local copies, waits for them, and re-layouts  210 us (24%)
  waiting for transfers between devices  157 us (18%)
  matrix products  149 us (17%)
  starting transfers between devices  124 us (14%)
  other arithmetic  122 us (14%)
  Pallas kernels  60.7 us (7%)
  between operations  27.6 us (3%)
    ppermute x56, waiting for transfers between devices, swap_dp(): return lax.ppermute(inputs, 'dp', [(i, i ^ mask) for i in range(size)])  117 us
    unnamed x558, local copies, waits for them, and re-layouts  88.3 us
    dot_general x5, matrix products, product(): return jnp.dot(first_operand, second_operand, preferred_element_type=f32)  71.2 us
    ppermute x25, starting transfers between devices, swap_mp(): return lax.ppermute(inputs, 'mp', [(i, i ^ mask) for i in range(size)])  56.3 us
    ppermute x56, starting transfers between devices, swap_dp(): return lax.ppermute(inputs, 'dp', [(i, i ^ mask) for i in range(size)])  50.1 us
    ppermute x25, waiting for transfers between devices, swap_mp(): return lax.ppermute(inputs, 'mp', [(i, i ^ mask) for i in range(size)])  39.9 us
    pallas_call x3, Pallas kernels, attend_back(): pl.pallas_call(attend_back_kernel, grid=(quads,), in_specs=[pl.BlockSpec(...  38 us
    dot_general x6, matrix products, contract_last(): lax.dot_general(first_operand, second_operand, (((1,), (1,)), ((), ())),...  35.3 us
  transfers between devices with their start and end apart: 85, of which 29 were waited for; matrix products, arithmetic and copies ran while one was open for 35% of the time, Pallas kernels for 3%

profile of v1, /device:TPU:0, one launch (start us, length us, event | category | flops | bytes accessed | tf_op | source)
XLA Modules:
  0.0 850.9 jit_solution(8972515852562157169)
XLA Ops:
  2.2 4.1 collective-permute-start.17
  13.5 3.2 collective-permute-start.2
  22.4 2.5 collective-permute-start.1
  44.4 2.6 collective-permute-start.7
  51.0 2.9 collective-permute-start.33
  56.6 7.4 collective-permute-start.35
  64.1 5.9 collective-permute-start.22
  72.2 2.7 collective-permute-done.4
  74.9 9.4 %collective-permute-start = (bf16[3,384,441]{1,2,0:T(8,128)(2,1)}, bf16[3,384,441]{1,2,0:T(8,128)(2,1)}, u32[]{:S(2)}, u32[]{:S(2)}) collective-permute-start(bf16[3,384,441]{1,2,0:T(8,128)(2,1)} %param.27), channel_id=1, source_target_pairs={{0,0},{1,8},{2,4},{3,12},{4,2},{5,10},{6,6},{7,14},{8,1},{9,9},{10... | collective-permute-start | bytes 3048200 | tf_op jit(solution)/shard_map/ppermute | solution.py:78
  87.2 14.0 %collective-permute-start.10 = (bf16[96,1152]{1,0:T(8,128)(2,1)S(1)}, bf16[96,1152]{1,0:T(8,128)(2,1)S(1)}, u32[]{:S(2)}, u32[]{:S(2)}) collective-permute-start(bf16[96,1152]{1,0:T(8,128)(2,1)S(1)} %concatenate.283), channel_id=1, source_target_pairs={{0,8},{4,12},{8,0},{12,4},{16,24},{20,28},{24,16},{28,20},{1,9},{5... | collective-permute-start | bytes 663560 | tf_op jit(solution)/shard_map/ppermute | solution.py:59
  106.9 5.4 collective-permute-done.10
  122.7 18.0 %collective-permute-done.11 = bf16[192,1152]{1,0:T(8,128)(2,1)S(1)} collective-permute-done((bf16[192,1152]{1,0:T(8,128)(2,1)S(1)}, bf16[192,1152]{1,0:T(8,128)(2,1)S(1)}, u32[]{:S(2)}, u32[]{:S(2)}) %collective-permute-start.11) | collective-permute-done | bytes 442400 | tf_op jit(solution)/shard_map/ppermute | solution.py:59
  141.8 5.5 collective-permute-done.14
  154.0 3.1 fusion.23
  158.9 2.8 fusion.223
  172.7 7.0 fusion.224
  208.6 4.3 pad_maximum_fusion.6
  222.0 3.5 collective-permute-done.28
  263.5 2.8 constant_dynamic-update-slice_fusion.44
  267.6 7.2 shard_map.466
  274.7 2.8 copy-done.19
  278.5 8.1 shard_map.467
  286.7 2.9 copy-done.18
  293.2 7.3 shard_map.468
  301.5 2.8 fusion.202
  304.3 3.1 pad_maximum_fusion.4
  316.4 3.2 fusion.225
  323.5 39.5 %multiply_convert_fusion = (bf16[1152,3072]{1,0:T(8,128)(2,1)}, f32[1152,3072]{1,0:T(8,128)}, f32[1152,3072]{1,0:T(8,128)}) fusion(bf16[768,3456]{1,0:T(8,128)(2,1)S(1)} %slice_dynamic-update-slice_fusion, f32[1152,768]{1,0:T(8,128)S(1)} %get-tuple-element.602, f32[768]{0:T(1024)S(1)} %get-tuple-element.263, f32[768]{0:T(1024)S(1)} %get-tuple-element.264, ...), kind=kOutput, calls=%fused_computation.3 | convolution fusion | flops 5670273024 | bytes 43671552 | tf_op jit(solution)/shard_map/dot_general | solution.py:36
  363.0 10.2 %fusion.226 = (f32[1152]{0:T(1024)S(1)}, f32[1152,768]{1,0:T(8,128)S(1)}) fusion(f32[1152,768]{1,0:T(8,128)S(1)} %get-tuple-element.602, bf16[1152,3072]{1,0:T(8,128)(2,1)} %get-tuple-element.308, bf16[768,3456]{1,0:T(8,128)(2,1)S(1)} %slice_dynamic-update-slice_fusion, bf16[768,3456]{1,0:T(8,128)(2,1)} %slice_dynamic-update-slice_fusion.4), kind=kOutput, calls=%fused_computation.818 | convolution fusion | flops 5447023616 | bytes 24777216 | tf_op jit(solution)/shard_map/dot_general | solution.py:40
  386.3 3.7 fusion.227
  393.3 8.3 convolution_convert_fusion.1
  401.7 18.7 %add_convert_fusion = bf16[1152,3072]{1,0:T(8,128)(2,1)} fusion(f32[1152,3072]{1,0:T(8,128)} %get-tuple-element.309, f32[1152,3072]{1,0:T(8,128)} %get-tuple-element.603, bf16[768,3456]{1,0:T(8,128)(2,1)} %copy-done.169, bf16[768,3456]{1,0:T(8,128)(2,1)} %slice_dynamic-update-slice_fusion.4, f32[1152,768]{1,0:T(8,128)} %copy-done.41, ...), kind=kOutput, calls=%fused_computation.2 | convolution fusion | flops 5496569856 | bytes 49549824 | tf_op jit(solution)/shard_map/dot_general | solution.py:36
  420.5 12.8 %multiply_reduce_fusion = (f32[768]{0:T(1024)}, f32[1152]{0:T(1024)S(1)}, f32[768]{0:T(1024)}, f32[1152,768]{1,0:T(8,128)S(1)}) fusion(f32[1152,768]{1,0:T(8,128)} %copy-done.37, f32[1152]{0:T(1024)S(1)} %fusion.145, f32[1152]{0:T(1024)S(1)} %broadcast_multiply_fusion.1, f32[768]{0:T(1024)S(1)} %copy-done.197, bf16[1152,3072]{1,0:T(8,128)(2,1)} %add_convert_fusion, ...), kind=kOutput, calls=%fused_computation.36 | convolution fusion | flops 5442892800 | bytes 18897408 | tf_op jit(solution)/shard_map/dot_general | solution.py:40
  433.2 9.4 %convolution_convert_fusion = bf16[768,3072]{1,0:T(8,128)(2,1)} fusion(bf16[1152,3072]{1,0:T(8,128)(2,1)S(1)} %copy-done.228, f32[1152,768]{1,0:T(8,128)S(1)} %copy-done.38, f32[768]{0:T(1024)S(1)} %copy-done.215, f32[768]{0:T(1024)S(1)} %copy-done.197, f32[1152]{0:T(1024)S(1)} %fusion.145, f32[1152]{0:T(1024)S(1)} %broadcast_multiply_fusion.1), kind=kOutput, calls=%fused_computation.21 | convolution fusion | flops 5442600960 | bytes 15350784 | tf_op jit(solution)/shard_map/dot_general | solution.py:46
  445.2 3.9 convolution_convert_fusion.3
  449.1 2.8 convolution_convert_fusion.4
  453.2 12.5 %shard_map.469 = (bf16[384,768]{1,0:T(8,128)(2,1)S(1)}, f32[768,768]{1,0:T(8,128)S(1)}, f32[768,768]{1,0:T(8,128)S(1)}, f32[3,4,768]{2,1,0:T(4,128)S(1)}) custom-call(bf16[384,768]{1,0:T(8,128)(2,1)S(1)} %get-tuple-element.330.q_ref, bf16[768,768]{1,0:T(8,128)(2,1)S(1)} %get-tuple-element.356.k_ref, bf16[768,768]{1,0:T(8,128)(2,1)S(1)} %copy-done.10, ...), custom_call_target="tpu_custom_call" | custom-call | flops 7247757312 | bytes 7077888 | tf_op jit(solution)/shard_map/pallas_call | solution.py:280
  468.6 13.2 %shard_map.470 = (bf16[384,768]{1,0:T(8,128)(2,1)S(1)}, f32[768,768]{1,0:T(8,128)S(1)}, f32[768,768]{1,0:T(8,128)S(1)}, f32[3,4,768]{2,1,0:T(4,128)S(1)}) custom-call(bf16[384,768]{1,0:T(8,128)(2,1)S(1)} %copy-done.8, bf16[768,768]{1,0:T(8,128)(2,1)S(1)} %copy-done.12, bf16[768,768]{1,0:T(8,128)(2,1)} %get-tuple-element.350.v_ref, ...), custom_call_target="tpu_custom_call" | custom-call | flops 7247757312 | bytes 7077888 | tf_op jit(solution)/shard_map/pallas_call | solution.py:280
  483.2 12.3 %shard_map.471 = (bf16[384,768]{1,0:T(8,128)(2,1)S(1)}, f32[768,768]{1,0:T(8,128)S(1)}, f32[768,768]{1,0:T(8,128)S(1)}, f32[3,4,768]{2,1,0:T(4,128)S(1)}) custom-call(bf16[384,768]{1,0:T(8,128)(2,1)S(1)} %copy-done.6, bf16[768,768]{1,0:T(8,128)(2,1)S(1)} %copy-done.14, bf16[768,768]{1,0:T(8,128)(2,1)S(1)} %copy-done.17, bf16[12,384,768]{2,1,0:T(8,128)(2,1)} %copy-done.20, ...), custom_call_target="tpu_custom_call" | custom-call | flops 7247757312 | bytes 7077888 | tf_op jit(solution)/shard_map/pallas_call | solution.py:280
  504.7 2.7 fusion.67
  523.8 2.6 copy.253
  552.4 5.5 collective-permute-done.45
  558.9 5.3 collective-permute-done.49
  565.2 4.8 collective-permute-done.47
  577.1 5.1 multiply_reduce_fusion.1
  582.3 7.1 convolution_convert_fusion.2
  604.6 10.4 %fusion.27 = bf16[384,1536]{1,0:T(8,128)(2,1)} fusion(bf16[768,2304]{1,0:T(8,128)(2,1)S(1)} %copy-done.23, bf16[768,768]{1,0:T(8,128)(2,1)S(1)} %copy-done.32), kind=kLoop, calls=%fused_computation.112 | loop fusion | flops 18874368 | bytes 5898240 | tf_op jit(solution)/shard_map/concatenate | solution.py:106
  615.1 8.0 collective-permute-start.53
  625.7 2.8 collective-permute-start.54
  679.9 12.3 %collective-permute-done.77 = f32[24,528]{0,1:T(8,128)} collective-permute-done((f32[24,528]{0,1:T(8,128)}, f32[24,528]{0,1:T(8,128)}, u32[]{:S(2)}, u32[]{:S(2)}) %collective-permute-start.77) | collective-permute-done | bytes 50720 | tf_op jit(solution)/shard_map/ppermute | solution.py:64
  699.0 9.5 %collective-permute-done.56 = bf16[192,1536]{1,0:T(8,128)(2,1)S(1)} collective-permute-done((bf16[192,1536]{1,0:T(8,128)(2,1)}, bf16[192,1536]{1,0:T(8,128)(2,1)S(1)}, u32[]{:S(2)}, u32[]{:S(2)}) %collective-permute-start.56) | collective-permute-done | bytes 589856 | tf_op jit(solution)/shard_map/ppermute | solution.py:59
  713.6 6.1 collective-permute-done.57
  719.7 10.9 %collective-permute-done.59 = bf16[192,1536]{1,0:T(8,128)(2,1)S(1)} collective-permute-done((bf16[192,1536]{1,0:T(8,128)(2,1)S(1)}, bf16[192,1536]{1,0:T(8,128)(2,1)S(1)}, u32[]{:S(2)}, u32[]{:S(2)}) %collective-permute-start.59) | collective-permute-done | bytes 589856 | tf_op jit(solution)/shard_map/ppermute | solution.py:59
  734.3 5.4 collective-permute-done.60
  742.3 3.0 collective-permute-start.63
  747.5 14.5 %collective-permute-done.68 = bf16[192,3072]{1,0:T(8,128)(2,1)S(1)} collective-permute-done((bf16[192,3072]{1,0:T(8,128)(2,1)S(1)}, bf16[192,3072]{1,0:T(8,128)(2,1)S(1)}, u32[]{:S(2)}, u32[]{:S(2)}) %collective-permute-start.68) | collective-permute-done | bytes 1179680 | tf_op jit(solution)/shard_map/ppermute | solution.py:59
  764.4 7.4 collective-permute-done.66
  775.4 2.7 collective-permute-start.72
  781.6 3.2 collective-permute-done.70
  784.8 7.5 collective-permute-done.72
  792.3 15.6 %collective-permute-done.71 = bf16[96,1536]{1,0:T(8,128)(2,1)S(1)} collective-permute-done((bf16[96,1536]{1,0:T(8,128)(2,1)S(1)}, bf16[96,1536]{1,0:T(8,128)(2,1)S(1)}, u32[]{:S(2)}, u32[]{:S(2)}) %collective-permute-start.71) | collective-permute-done | bytes 294944 | tf_op jit(solution)/shard_map/ppermute | solution.py:64
  815.2 2.6 collective-permute-done.80
  818.8 2.6 collective-permute-done.81
  825.8 3.2 collective-permute-start.83
  (1060 shorter events, 370.0 us)
Async XLA Ops:
  2.2 40.5 %collective-permute-start.17 = (f32[13,192]{1,0:T(8,128)S(1)}, f32[13,192]{1,0:T(8,128)S(1)}, u32[]{:S(2)}, u32[]{:S(2)}) collective-permute-start(f32[13,192]{1,0:T(8,128)S(1)} %select_maximum_fusion), channel_id=1, source_target_pairs={{0,2},{1,3},{2,0},{3,1},{4,6},{5,7},{6,4},{7,5},{8,10},{9,11},{10,... | collective-permute-start | bytes 29960 | tf_op jit(solution)/shard_map/ppermute | solution.py:64
  6.3 37.5 %collective-permute-start.16 = (f32[13,192]{1,0:T(8,128)S(1)}, f32[13,192]{1,0:T(8,128)S(1)}, u32[]{:S(2)}, u32[]{:S(2)}) collective-permute-start(f32[13,192]{1,0:T(8,128)S(1)} %select_maximum_fusion), channel_id=1, source_target_pairs={{0,1},{1,0},{2,3},{3,2},{4,5},{5,4},{6,7},{7,6},{8,9},{9,8},{10,11... | collective-permute-start | bytes 29960 | tf_op jit(solution)/shard_map/ppermute | solution.py:64
  7.9 36.6 %collective-permute-start.18 = (f32[13,192]{1,0:T(8,128)S(1)}, f32[13,192]{1,0:T(8,128)S(1)}, u32[]{:S(2)}, u32[]{:S(2)}) collective-permute-start(f32[13,192]{1,0:T(8,128)S(1)} %select_maximum_fusion), channel_id=1, source_target_pairs={{0,3},{1,2},{2,1},{3,0},{4,7},{5,6},{6,5},{7,4},{8,11},{9,10},{10,... | collective-permute-start | bytes 29960 | tf_op jit(solution)/shard_map/ppermute | solution.py:64
  10.3 12.2 %collective-permute-start.26 = (s32[16,128]{1,0:T(8,128)S(1)}, s32[16,128]{1,0:T(8,128)S(1)}, u32[]{:S(2)}, u32[]{:S(2)}) collective-permute-start(s32[16,128]{1,0:T(8,128)S(1)} %pad_bitcast_fusion.1), channel_id=1, source_target_pairs={{0,0},{1,8},{2,4},{3,12},{4,2},{5,10},{6,6},{7,14},{8,1},{9,9},{10... | collective-permute-start | bytes 24584 | tf_op jit(solution)/shard_map/ppermute | solution.py:78
  13.5 35.9 %collective-permute-start.2 = (bf16[24,542]{1,0:T(8,128)(2,1)S(1)}, bf16[24,542]{1,0:T(8,128)(2,1)S(1)}, u32[]{:S(2)}, u32[]{:S(2)}) collective-permute-start(bf16[24,542]{1,0:T(8,128)(2,1)S(1)} %bitcast.569), channel_id=1, source_target_pairs={{0,2},{1,3},{2,0},{3,1},{4,6},{5,7},{6,4},{7,5},{8,10},{9,11},{10,... | collective-permute-start | bytes 78056 | tf_op jit(solution)/shard_map/ppermute | solution.py:64
  22.4 28.2 %collective-permute-start.1 = (bf16[24,542]{1,0:T(8,128)(2,1)S(1)}, bf16[24,542]{1,0:T(8,128)(2,1)S(1)}, u32[]{:S(2)}, u32[]{:S(2)}) collective-permute-start(bf16[24,542]{1,0:T(8,128)(2,1)S(1)} %bitcast.570), channel_id=1, source_target_pairs={{0,1},{1,0},{2,3},{3,2},{4,5},{5,4},{6,7},{7,6},{8,9},{9,8},{10,11... | collective-permute-start | bytes 78056 | tf_op jit(solution)/shard_map/ppermute | solution.py:64
  43.8 12.8 %collective-permute-start.8 = (bf16[96,576]{1,0:T(8,128)(2,1)S(1)}, bf16[96,576]{1,0:T(8,128)(2,1)S(1)}, u32[]{:S(2)}, u32[]{:S(2)}) collective-permute-start(bf16[96,576]{1,0:T(8,128)(2,1)S(1)} %get-tuple-element.518), channel_id=1, source_target_pairs={{0,2},{1,3},{2,0},{3,1},{4,6},{5,7},{6,4},{7,5},{8,10},{9,11},{10,... | collective-permute-start | bytes 331784 | tf_op jit(solution)/shard_map/ppermute | solution.py:64
  44.4 19.6 %collective-permute-start.7 = (bf16[96,576]{1,0:T(8,128)(2,1)S(1)}, bf16[96,576]{1,0:T(8,128)(2,1)S(1)}, u32[]{:S(2)}, u32[]{:S(2)}) collective-permute-start(bf16[96,576]{1,0:T(8,128)(2,1)S(1)} %get-tuple-element.518), channel_id=1, source_target_pairs={{0,1},{1,0},{2,3},{3,2},{4,5},{5,4},{6,7},{7,6},{8,9},{9,8},{10,11... | collective-permute-start | bytes 331784 | tf_op jit(solution)/shard_map/ppermute | solution.py:64
  49.5 20.6 %collective-permute-start.9 = (bf16[96,576]{1,0:T(8,128)(2,1)S(1)}, bf16[96,576]{1,0:T(8,128)(2,1)S(1)}, u32[]{:S(2)}, u32[]{:S(2)}) collective-permute-start(bf16[96,576]{1,0:T(8,128)(2,1)S(1)} %get-tuple-element.518), channel_id=1, source_target_pairs={{0,3},{1,2},{2,1},{3,0},{4,7},{5,6},{6,5},{7,4},{8,11},{9,10},{10,... | collective-permute-start | bytes 331784 | tf_op jit(solution)/shard_map/ppermute | solution.py:64
  50.7 35.0 %collective-permute-start.34 = (bf16[96,1728]{1,0:T(8,128)(2,1)S(1)}, bf16[96,1728]{1,0:T(8,128)(2,1)S(1)}, u32[]{:S(2)}, u32[]{:S(2)}) collective-permute-start(bf16[96,1728]{1,0:T(8,128)(2,1)S(1)} %get-tuple-element.454), channel_id=1, source_target_pairs={{0,2},{1,3},{2,0},{3,1},{4,6},{5,7},{6,4},{7,5},{8,10},{9,11},{10,... | collective-permute-start | bytes 995336 | tf_op jit(solution)/shard_map/ppermute | solution.py:64
  51.0 36.2 %collective-permute-start.33 = (bf16[96,1728]{1,0:T(8,128)(2,1)S(1)}, bf16[96,1728]{1,0:T(8,128)(2,1)S(1)}, u32[]{:S(2)}, u32[]{:S(2)}) collective-permute-start(bf16[96,1728]{1,0:T(8,128)(2,1)S(1)} %get-tuple-element.454), channel_id=1, source_target_pairs={{0,1},{1,0},{2,3},{3,2},{4,5},{5,4},{6,7},{7,6},{8,9},{9,8},{10,11... | collective-permute-start | bytes 995336 | tf_op jit(solution)/shard_map/ppermute | solution.py:64
  56.6 44.6 %collective-permute-start.35 = (bf16[96,1728]{1,0:T(8,128)(2,1)S(1)}, bf16[96,1728]{1,0:T(8,128)(2,1)S(1)}, u32[]{:S(2)}, u32[]{:S(2)}) collective-permute-start(bf16[96,1728]{1,0:T(8,128)(2,1)S(1)} %get-tuple-element.454), channel_id=1, source_target_pairs={{0,3},{1,2},{2,1},{3,0},{4,7},{5,6},{6,5},{7,4},{8,11},{9,10},{10,... | collective-permute-start | bytes 995336 | tf_op jit(solution)/shard_map/ppermute | solution.py:64
  64.1 52.0 %collective-permute-start.22 = (bf16[2,2,384,192]{2,3,1,0:T(8,128)(2,1)}, bf16[2,2,384,192]{2,3,1,0:T(8,128)(2,1)}, u32[]{:S(2)}, u32[]{:S(2)}) collective-permute-start(bf16[2,2,384,192]{2,3,1,0:T(8,128)(2,1)} %param.32), channel_id=1, source_target_pairs={{0,0},{1,8},{2,4},{3,12},{4,2},{5,10},{6,6},{7,14},{8,1},{9,9},{10... | collective-permute-start | bytes 1769480 | tf_op jit(solution)/shard_map/ppermute | solution.py:78
  74.9 79.1 %collective-permute-start = (bf16[3,384,441]{1,2,0:T(8,128)(2,1)}, bf16[3,384,441]{1,2,0:T(8,128)(2,1)}, u32[]{:S(2)}, u32[]{:S(2)}) collective-permute-start(bf16[3,384,441]{1,2,0:T(8,128)(2,1)} %param.27), channel_id=1, source_target_pairs={{0,0},{1,8},{2,4},{3,12},{4,2},{5,10},{6,6},{7,14},{8,1},{9,9},{10... | collective-permute-start | bytes 3048200 | tf_op jit(solution)/shard_map/ppermute | solution.py:78
  85.7 30.2 %collective-permute-start.13 = (bf16[96,1152]{1,0:T(8,128)(2,1)S(1)}, bf16[96,1152]{1,0:T(8,128)(2,1)S(1)}, u32[]{:S(2)}, u32[]{:S(2)}) collective-permute-start(bf16[96,1152]{1,0:T(8,128)(2,1)S(1)} %concatenate.287), channel_id=1, source_target_pairs={{0,16},{4,20},{8,24},{12,28},{16,0},{20,4},{24,8},{28,12},{1,17},{... | collective-permute-start | bytes 663560 | tf_op jit(solution)/shard_map/ppermute | solution.py:59
  87.2 25.1 %collective-permute-start.10 = (bf16[96,1152]{1,0:T(8,128)(2,1)S(1)}, bf16[96,1152]{1,0:T(8,128)(2,1)S(1)}, u32[]{:S(2)}, u32[]{:S(2)}) collective-permute-start(bf16[96,1152]{1,0:T(8,128)(2,1)S(1)} %concatenate.283), channel_id=1, source_target_pairs={{0,8},{4,12},{8,0},{12,4},{16,24},{20,28},{24,16},{28,20},{1,9},{5... | collective-permute-start | bytes 663560 | tf_op jit(solution)/shard_map/ppermute | solution.py:59
  101.2 13.6 %collective-permute-start.5 = (bf16[192,542]{1,0:T(8,128)(2,1)}, bf16[192,542]{1,0:T(8,128)(2,1)S(1)}, u32[]{:S(2)}, u32[]{:S(2)}) collective-permute-start(bf16[192,542]{1,0:T(8,128)(2,1)} %copy-done.220), channel_id=1, source_target_pairs={{0,16},{4,20},{8,24},{12,28},{16,0},{20,4},{24,8},{28,12},{1,17},{... | collective-permute-start | bytes 624392 | tf_op jit(solution)/shard_map/ppermute | solution.py:59
  112.3 38.5 %collective-permute-start.36 = (bf16[96,3456]{1,0:T(8,128)(2,1)S(1)}, bf16[96,3456]{1,0:T(8,128)(2,1)S(1)}, u32[]{:S(2)}, u32[]{:S(2)}) collective-permute-start(bf16[96,3456]{1,0:T(8,128)(2,1)S(1)} %get-tuple-element.402), channel_id=1, source_target_pairs={{0,8},{4,12},{8,0},{12,4},{16,24},{20,28},{24,16},{28,20},{1,9},{5... | collective-permute-start | bytes 1990664 | tf_op jit(solution)/shard_map/ppermute | solution.py:59
  114.8 37.2 %collective-permute-start.39 = (bf16[96,3456]{1,0:T(8,128)(2,1)S(1)}, bf16[96,3456]{1,0:T(8,128)(2,1)S(1)}, u32[]{:S(2)}, u32[]{:S(2)}) collective-permute-start(bf16[96,3456]{1,0:T(8,128)(2,1)S(1)} %get-tuple-element.400), channel_id=1, source_target_pairs={{0,16},{4,20},{8,24},{12,28},{16,0},{20,4},{24,8},{28,12},{1,17},{... | collective-permute-start | bytes 1990664 | tf_op jit(solution)/shard_map/ppermute | solution.py:59
  116.1 31.2 %collective-permute-start.14 = (bf16[192,1152]{1,0:T(8,128)(2,1)S(1)}, bf16[192,1152]{1,0:T(8,128)(2,1)S(1)}, u32[]{:S(2)}, u32[]{:S(2)}) collective-permute-start(bf16[192,1152]{1,0:T(8,128)(2,1)S(1)} %pad_maximum_fusion.34), channel_id=1, source_target_pairs={{0,8},{4,12},{8,0},{12,4},{16,24},{20,28},{24,16},{28,20},{1,9},{5... | collective-permute-start | bytes 1327112 | tf_op jit(solution)/shard_map/ppermute | solution.py:59
  118.7 22.1 %collective-permute-start.11 = (bf16[192,1152]{1,0:T(8,128)(2,1)S(1)}, bf16[192,1152]{1,0:T(8,128)(2,1)S(1)}, u32[]{:S(2)}, u32[]{:S(2)}) collective-permute-start(bf16[192,1152]{1,0:T(8,128)(2,1)S(1)} %pad_maximum_fusion.33), channel_id=1, source_target_pairs={{0,16},{4,20},{8,24},{12,28},{16,0},{20,4},{24,8},{28,12},{1,17},{... | collective-permute-start | bytes 1327112 | tf_op jit(solution)/shard_map/ppermute | solution.py:59
  140.8 53.3 %collective-permute-start.23 = (bf16[2,2,384,192]{2,3,1,0:T(8,128)(2,1)}, bf16[2,2,384,192]{2,3,1,0:T(8,128)(2,1)}, u32[]{:S(2)}, u32[]{:S(2)}) collective-permute-start(bf16[2,2,384,192]{2,3,1,0:T(8,128)(2,1)} %bitcast.35), channel_id=1, source_target_pairs={{0,4},{4,0},{8,12},{12,8},{16,20},{20,16},{24,28},{28,24},{1,5},{5... | collective-permute-start | bytes 1769480 | tf_op jit(solution)/shard_map/ppermute | solution.py:59
  147.3 15.3 %collective-permute-start.24 = (bf16[2,2,384,192]{2,3,1,0:T(8,128)(2,1)}, bf16[2,2,384,192]{2,3,1,0:T(8,128)(2,1)}, u32[]{:S(2)}, u32[]{:S(2)}) collective-permute-start(bf16[2,2,384,192]{2,3,1,0:T(8,128)(2,1)} %bitcast.35), channel_id=1, source_target_pairs={{0,8},{4,12},{8,0},{12,4},{16,24},{20,28},{24,16},{28,20},{1,9},{5... | collective-permute-start | bytes 1769480 | tf_op jit(solution)/shard_map/ppermute | solution.py:59
  150.8 13.5 %collective-permute-start.12 = (bf16[384,1152]{1,0:T(8,128)(2,1)}, bf16[384,1152]{1,0:T(8,128)(2,1)}, u32[]{:S(2)}, u32[]{:S(2)}) collective-permute-start(bf16[384,1152]{1,0:T(8,128)(2,1)} %pad_maximum_fusion.20), channel_id=1, source_target_pairs={{0,4},{4,0},{8,12},{12,8},{16,20},{20,16},{24,28},{28,24},{1,5},{5... | collective-permute-start | bytes 2654216 | tf_op jit(solution)/shard_map/ppermute | solution.py:59
  152.0 16.4 %collective-permute-start.15 = (bf16[384,1152]{1,0:T(8,128)(2,1)}, bf16[384,1152]{1,0:T(8,128)(2,1)}, u32[]{:S(2)}, u32[]{:S(2)}) collective-permute-start(bf16[384,1152]{1,0:T(8,128)(2,1)} %pad_maximum_fusion.21), channel_id=1, source_target_pairs={{0,4},{4,0},{8,12},{12,8},{16,20},{20,16},{24,28},{28,24},{1,5},{5... | collective-permute-start | bytes 2654216 | tf_op jit(solution)/shard_map/ppermute | solution.py:59
  154.0 135.7 %collective-permute-start.37 = (bf16[192,3456]{1,0:T(8,128)(2,1)}, bf16[192,3456]{1,0:T(8,128)(2,1)}, u32[]{:S(2)}, u32[]{:S(2)}) collective-permute-start(bf16[192,3456]{1,0:T(8,128)(2,1)} %pad_maximum_fusion.14), channel_id=1, source_target_pairs={{0,16},{4,20},{8,24},{12,28},{16,0},{20,4},{24,8},{28,12},{1,17},{... | collective-permute-start | bytes 3981320 | tf_op jit(solution)/shard_map/ppermute | solution.py:59
  162.6 138.9 %collective-permute-start.40 = (bf16[192,3456]{1,0:T(8,128)(2,1)}, bf16[192,3456]{1,0:T(8,128)(2,1)}, u32[]{:S(2)}, u32[]{:S(2)}) collective-permute-start(bf16[192,3456]{1,0:T(8,128)(2,1)} %pad_maximum_fusion.15), channel_id=1, source_target_pairs={{0,8},{4,12},{8,0},{12,4},{16,24},{20,28},{24,16},{28,20},{1,9},{5... | collective-permute-start | bytes 3981320 | tf_op jit(solution)/shard_map/ppermute | solution.py:59
  164.3 30.2 %collective-permute-start.25 = (bf16[2,2,384,192]{2,3,1,0:T(8,128)(2,1)}, bf16[2,2,384,192]{2,3,1,0:T(8,128)(2,1)}, u32[]{:S(2)}, u32[]{:S(2)}) collective-permute-start(bf16[2,2,384,192]{2,3,1,0:T(8,128)(2,1)} %collective-permute-done.24), channel_id=1, source_target_pairs={{0,4},{4,0},{8,12},{12,8},{16,20},{20,16},{24,28},{28,24},{1,5},{5... | collective-permute-start | bytes 1769480 | tf_op jit(solution)/shard_map/ppermute | solution.py:59
  185.8 30.1 %collective-permute-start.31 = (bf16[2,96,768]{2,1,0:T(8,128)(2,1)}, bf16[2,96,768]{2,1,0:T(8,128)(2,1)}, u32[]{:S(2)}, u32[]{:S(2)}) collective-permute-start(bf16[2,96,768]{2,1,0:T(8,128)(2,1)} %pad_maximum_fusion.47), channel_id=1, source_target_pairs={{0,8},{4,12},{8,0},{12,4},{16,24},{20,28},{24,16},{28,20},{1,9},{5... | collective-permute-start | bytes 884744 | tf_op jit(solution)/shard_map/ppermute | solution.py:59
  194.1 18.8 %collective-permute-start.30 = (bf16[2,96,768]{2,1,0:T(8,128)(2,1)}, bf16[2,96,768]{2,1,0:T(8,128)(2,1)S(1)}, u32[]{:S(2)}, u32[]{:S(2)}) collective-permute-start(bf16[2,96,768]{2,1,0:T(8,128)(2,1)} %pad_maximum_fusion.47), channel_id=1, source_target_pairs={{0,4},{4,0},{8,12},{12,8},{16,20},{20,16},{24,28},{28,24},{1,5},{5... | collective-permute-start | bytes 884744 | tf_op jit(solution)/shard_map/ppermute | solution.py:59
  194.5 25.6 %collective-permute-start.20 = (bf16[2,96,768]{2,1,0:T(8,128)(2,1)}, bf16[2,96,768]{2,1,0:T(8,128)(2,1)}, u32[]{:S(2)}, u32[]{:S(2)}) collective-permute-start(bf16[2,96,768]{2,1,0:T(8,128)(2,1)} %pad_maximum_fusion.41), channel_id=1, source_target_pairs={{0,8},{4,12},{8,0},{12,4},{16,24},{20,28},{24,16},{28,20},{1,9},{5... | collective-permute-start | bytes 884744 | tf_op jit(solution)/shard_map/ppermute | solution.py:59
  212.9 18.5 %collective-permute-start.19 = (bf16[2,96,768]{2,1,0:T(8,128)(2,1)}, bf16[2,96,768]{2,1,0:T(8,128)(2,1)}, u32[]{:S(2)}, u32[]{:S(2)}) collective-permute-start(bf16[2,96,768]{2,1,0:T(8,128)(2,1)} %pad_maximum_fusion.41), channel_id=1, source_target_pairs={{0,4},{4,0},{8,12},{12,8},{16,20},{20,16},{24,28},{28,24},{1,5},{5... | collective-permute-start | bytes 884744 | tf_op jit(solution)/shard_map/ppermute | solution.py:59
  225.5 25.8 %collective-permute-start.21 = (bf16[2,96,768]{2,1,0:T(8,128)(2,1)}, bf16[2,96,768]{2,1,0:T(8,128)(2,1)}, u32[]{:S(2)}, u32[]{:S(2)}) collective-permute-start(bf16[2,96,768]{2,1,0:T(8,128)(2,1)} %collective-permute-done.20), channel_id=1, source_target_pairs={{0,4},{4,0},{8,12},{12,8},{16,20},{20,16},{24,28},{28,24},{1,5},{5... | collective-permute-start | bytes 884744 | tf_op jit(solution)/shard_map/ppermute | solution.py:59
  227.1 25.4 %collective-permute-start.29 = (bf16[2,96,768]{2,1,0:T(8,128)(2,1)}, bf16[2,96,768]{2,1,0:T(8,128)(2,1)S(1)}, u32[]{:S(2)}, u32[]{:S(2)}) collective-permute-start(bf16[2,96,768]{2,1,0:T(8,128)(2,1)} %copy-done.60), channel_id=1, source_target_pairs={{0,4},{4,0},{8,12},{12,8},{16,20},{20,16},{24,28},{28,24},{1,5},{5... | collective-permute-start | bytes 884744 | tf_op jit(solution)/shard_map/ppermute | solution.py:59
  231.5 14.6 %collective-permute-start.32 = (bf16[2,96,768]{2,1,0:T(8,128)(2,1)}, bf16[2,96,768]{2,1,0:T(8,128)(2,1)}, u32[]{:S(2)}, u32[]{:S(2)}) collective-permute-start(bf16[2,96,768]{2,1,0:T(8,128)(2,1)} %collective-permute-done.31), channel_id=1, source_target_pairs={{0,4},{4,0},{8,12},{12,8},{16,20},{20,16},{24,28},{28,24},{1,5},{5... | collective-permute-start | bytes 884744 | tf_op jit(solution)/shard_map/ppermute | solution.py:59
  291.4 16.4 %collective-permute-start.38 = (bf16[384,3456]{1,0:T(8,128)(2,1)S(1)}, bf16[384,3456]{1,0:T(8,128)(2,1)S(1)}, u32[]{:S(2)}, u32[]{:S(2)}) collective-permute-start(bf16[384,3456]{1,0:T(8,128)(2,1)S(1)} %pad_maximum_fusion.3), channel_id=1, source_target_pairs={{0,4},{4,0},{8,12},{12,8},{16,20},{20,16},{24,28},{28,24},{1,5},{5... | collective-permute-start | bytes 7962632 | tf_op jit(solution)/shard_map/ppermute | solution.py:59
  307.5 12.7 %collective-permute-start.41 = (bf16[384,3456]{1,0:T(8,128)(2,1)S(1)}, bf16[384,3456]{1,0:T(8,128)(2,1)S(1)}, u32[]{:S(2)}, u32[]{:S(2)}) collective-permute-start(bf16[384,3456]{1,0:T(8,128)(2,1)S(1)} %pad_maximum_fusion.4), channel_id=1, source_target_pairs={{0,4},{4,0},{8,12},{12,8},{16,20},{20,16},{24,28},{28,24},{1,5},{5... | collective-permute-start | bytes 7962632 | tf_op jit(solution)/shard_map/ppermute | solution.py:59
  513.7 33.2 %collective-permute-start.44 = (bf16[2,2,96,768]{3,2,1,0:T(8,128)(2,1)}, bf16[2,2,96,768]{3,2,1,0:T(8,128)(2,1)}, u32[]{:S(2)}, u32[]{:S(2)}) collective-permute-start(bf16[2,2,96,768]{3,2,1,0:T(8,128)(2,1)} %pad_maximum_fusion.24), channel_id=1, source_target_pairs={{0,4},{4,0},{8,12},{12,8},{16,20},{20,16},{24,28},{28,24},{1,5},{5... | collective-permute-start | bytes 1769480 | tf_op jit(solution)/shard_map/ppermute | solution.py:59
  514.6 34.4 %collective-permute-start.48 = (bf16[2,2,96,768]{3,2,1,0:T(8,128)(2,1)}, bf16[2,2,96,768]{3,2,1,0:T(8,128)(2,1)}, u32[]{:S(2)}, u32[]{:S(2)}) collective-permute-start(bf16[2,2,96,768]{3,2,1,0:T(8,128)(2,1)} %pad_maximum_fusion.26), channel_id=1, source_target_pairs={{0,4},{4,0},{8,12},{12,8},{16,20},{20,16},{24,28},{28,24},{1,5},{5... | collective-permute-start | bytes 1769480 | tf_op jit(solution)/shard_map/ppermute | solution.py:59
  517.1 178.6 %collective-permute-start.64 = (bf16[384,3072]{1,0:T(8,128)(2,1)}, bf16[384,3072]{1,0:T(8,128)(2,1)}, u32[]{:S(2)}, u32[]{:S(2)}) collective-permute-start(bf16[384,3072]{1,0:T(8,128)(2,1)} %pad_maximum_fusion.7), channel_id=1, source_target_pairs={{0,4},{4,0},{8,12},{12,8},{16,20},{20,16},{24,28},{28,24},{1,5},{5... | collective-permute-start | bytes 7077896 | tf_op jit(solution)/shard_map/ppermute | solution.py:59
  518.7 193.3 %collective-permute-start.67 = (bf16[384,3072]{1,0:T(8,128)(2,1)}, bf16[384,3072]{1,0:T(8,128)(2,1)}, u32[]{:S(2)}, u32[]{:S(2)}) collective-permute-start(bf16[384,3072]{1,0:T(8,128)(2,1)} %pad_maximum_fusion.8), channel_id=1, source_target_pairs={{0,4},{4,0},{8,12},{12,8},{16,20},{20,16},{24,28},{28,24},{1,5},{5... | collective-permute-start | bytes 7077896 | tf_op jit(solution)/shard_map/ppermute | solution.py:59
  550.1 14.0 %collective-permute-start.49 = (bf16[2,96,768]{2,1,0:T(8,128)(2,1)S(1)}, bf16[2,96,768]{2,1,0:T(8,128)(2,1)S(1)}, u32[]{:S(2)}, u32[]{:S(2)}) collective-permute-start(bf16[2,96,768]{2,1,0:T(8,128)(2,1)S(1)} %fusion.84), channel_id=1, source_target_pairs={{0,8},{4,12},{8,0},{12,4},{16,24},{20,28},{24,16},{28,20},{1,9},{5... | collective-permute-start | bytes 884744 | tf_op jit(solution)/shard_map/ppermute | solution.py:59
  551.3 18.7 %collective-permute-start.47 = (bf16[2,96,768]{2,1,0:T(8,128)(2,1)S(1)}, bf16[2,96,768]{2,1,0:T(8,128)(2,1)S(1)}, u32[]{:S(2)}, u32[]{:S(2)}) collective-permute-start(bf16[2,96,768]{2,1,0:T(8,128)(2,1)S(1)} %fusion.87), channel_id=1, source_target_pairs={{0,8},{4,12},{8,0},{12,4},{16,24},{20,28},{24,16},{28,20},{1,9},{5... | collective-permute-start | bytes 884744 | tf_op jit(solution)/shard_map/ppermute | solution.py:59
  599.3 29.2 %collective-permute-start.73 = (f32[384,528]{0,1:T(8,128)S(1)}, f32[384,528]{0,1:T(8,128)S(1)}, u32[]{:S(2)}, u32[]{:S(2)}) collective-permute-start(f32[384,528]{0,1:T(8,128)S(1)} %pad_maximum_fusion.22), channel_id=1, source_target_pairs={{0,4},{4,0},{8,12},{12,8},{16,20},{20,16},{24,28},{28,24},{1,5},{5... | collective-permute-start | bytes 2433032 | tf_op jit(solution)/shard_map/ppermute | solution.py:59
  602.6 12.4 %collective-permute-start.52 = (f32[80,128]{1,0:T(8,128)S(1)}, f32[80,128]{1,0:T(8,128)S(1)}, u32[]{:S(2)}, u32[]{:S(2)}) collective-permute-start(f32[80,128]{1,0:T(8,128)S(1)} %fusion.247), channel_id=1, source_target_pairs={{0,16},{4,20},{8,24},{12,28},{16,0},{20,4},{24,8},{28,12},{1,17},{... | collective-permute-start | bytes 122888 | tf_op jit(solution)/shard_map/ppermute | solution.py:59
  624.1 26.2 %collective-permute-start.55 = (bf16[384,1536]{1,0:T(8,128)(2,1)}, bf16[384,1536]{1,0:T(8,128)(2,1)}, u32[]{:S(2)}, u32[]{:S(2)}) collective-permute-start(bf16[384,1536]{1,0:T(8,128)(2,1)} %fusion.27), channel_id=1, source_target_pairs={{0,4},{4,0},{8,12},{12,8},{16,20},{20,16},{24,28},{28,24},{1,5},{5... | collective-permute-start | bytes 3538952 | tf_op jit(solution)/shard_map/ppermute | solution.py:59
  625.7 10.1 %collective-permute-start.54 = (f32[80,128]{1,0:T(8,128)}, f32[80,128]{1,0:T(8,128)}, u32[]{:S(2)}, u32[]{:S(2)}) collective-permute-start(f32[80,128]{1,0:T(8,128)} %add.1003), channel_id=1, source_target_pairs={{0,2},{1,3},{2,0},{3,1},{4,6},{5,7},{6,4},{7,5},{8,10},{9,11},{10,... | collective-permute-start | bytes 122888 | tf_op jit(solution)/shard_map/ppermute | solution.py:64
  632.5 11.1 %collective-permute-start.74 = (f32[192,528]{1,0:T(8,128)}, f32[192,528]{1,0:T(8,128)}, u32[]{:S(2)}, u32[]{:S(2)}) collective-permute-start(f32[192,528]{1,0:T(8,128)} %copy.254), channel_id=1, source_target_pairs={{0,8},{4,12},{8,0},{12,4},{16,24},{20,28},{24,16},{28,20},{1,9},{5... | collective-permute-start | bytes 1216520 | tf_op jit(solution)/shard_map/ppermute | solution.py:59
  672.0 20.1 %collective-permute-start.77 = (f32[24,528]{0,1:T(8,128)}, f32[24,528]{0,1:T(8,128)}, u32[]{:S(2)}, u32[]{:S(2)}) collective-permute-start(f32[24,528]{0,1:T(8,128)} %copy.263), channel_id=1, source_target_pairs={{0,2},{1,3},{2,0},{3,1},{4,6},{5,7},{6,4},{7,5},{8,10},{9,11},{10,... | collective-permute-start | bytes 152072 | tf_op jit(solution)/shard_map/ppermute | solution.py:64
  674.0 18.1 %collective-permute-start.78 = (f32[24,528]{0,1:T(8,128)}, f32[24,528]{0,1:T(8,128)}, u32[]{:S(2)}, u32[]{:S(2)}) collective-permute-start(f32[24,528]{0,1:T(8,128)} %copy.264), channel_id=1, source_target_pairs={{0,3},{1,2},{2,1},{3,0},{4,7},{5,6},{6,5},{7,4},{8,11},{9,10},{10,... | collective-permute-start | bytes 152072 | tf_op jit(solution)/shard_map/ppermute | solution.py:64
  676.3 16.9 %collective-permute-start.76 = (f32[24,528]{0,1:T(8,128)}, f32[24,528]{0,1:T(8,128)}, u32[]{:S(2)}, u32[]{:S(2)}) collective-permute-start(f32[24,528]{0,1:T(8,128)} %copy.261), channel_id=1, source_target_pairs={{0,1},{1,0},{2,3},{3,2},{4,5},{5,4},{6,7},{7,6},{8,9},{9,8},{10,11... | collective-permute-start | bytes 152072 | tf_op jit(solution)/shard_map/ppermute | solution.py:64
  692.1 16.3 %collective-permute-start.56 = (bf16[192,1536]{1,0:T(8,128)(2,1)}, bf16[192,1536]{1,0:T(8,128)(2,1)S(1)}, u32[]{:S(2)}, u32[]{:S(2)}) collective-permute-start(bf16[192,1536]{1,0:T(8,128)(2,1)} %pad_maximum_fusion.27), channel_id=1, source_target_pairs={{0,8},{4,12},{8,0},{12,4},{16,24},{20,28},{24,16},{28,20},{1,9},{5... | collective-permute-start | bytes 1769480 | tf_op jit(solution)/shard_map/ppermute | solution.py:59
  697.9 47.4 %collective-permute-start.65 = (bf16[192,3072]{1,0:T(8,128)(2,1)S(1)}, bf16[192,3072]{1,0:T(8,128)(2,1)S(1)}, u32[]{:S(2)}, u32[]{:S(2)}) collective-permute-start(bf16[192,3072]{1,0:T(8,128)(2,1)S(1)} %pad_maximum_fusion.17), channel_id=1, source_target_pairs={{0,8},{4,12},{8,0},{12,4},{16,24},{20,28},{24,16},{28,20},{1,9},{5... | collective-permute-start | bytes 3538952 | tf_op jit(solution)/shard_map/ppermute | solution.py:59
  709.7 10.0 %collective-permute-start.57 = (bf16[96,1536]{1,0:T(8,128)(2,1)S(1)}, bf16[96,1536]{1,0:T(8,128)(2,1)S(1)}, u32[]{:S(2)}, u32[]{:S(2)}) collective-permute-start(bf16[96,1536]{1,0:T(8,128)(2,1)S(1)} %get-tuple-element.343), channel_id=1, source_target_pairs={{0,16},{4,20},{8,24},{12,28},{16,0},{20,4},{24,8},{28,12},{1,17},{... | collective-permute-start | bytes 884744 | tf_op jit(solution)/shard_map/ppermute | solution.py:59
  710.8 19.8 %collective-permute-start.59 = (bf16[192,1536]{1,0:T(8,128)(2,1)S(1)}, bf16[192,1536]{1,0:T(8,128)(2,1)S(1)}, u32[]{:S(2)}, u32[]{:S(2)}) collective-permute-start(bf16[192,1536]{1,0:T(8,128)(2,1)S(1)} %pad_maximum_fusion.28), channel_id=1, source_target_pairs={{0,16},{4,20},{8,24},{12,28},{16,0},{20,4},{24,8},{28,12},{1,17},{... | collective-permute-start | bytes 1769480 | tf_op jit(solution)/shard_map/ppermute | solution.py:59
  733.1 29.0 %collective-permute-start.68 = (bf16[192,3072]{1,0:T(8,128)(2,1)S(1)}, bf16[192,3072]{1,0:T(8,128)(2,1)S(1)}, u32[]{:S(2)}, u32[]{:S(2)}) collective-permute-start(bf16[192,3072]{1,0:T(8,128)(2,1)S(1)} %pad_maximum_fusion.18), channel_id=1, source_target_pairs={{0,16},{4,20},{8,24},{12,28},{16,0},{20,4},{24,8},{28,12},{1,17},{... | collective-permute-start | bytes 3538952 | tf_op jit(solution)/shard_map/ppermute | solution.py:59
  740.6 37.5 %collective-permute-start.61 = (bf16[96,768]{1,0:T(8,128)(2,1)S(1)}, bf16[96,768]{1,0:T(8,128)(2,1)S(1)}, u32[]{:S(2)}, u32[]{:S(2)}) collective-permute-start(bf16[96,768]{1,0:T(8,128)(2,1)S(1)} %get-tuple-element.406), channel_id=1, source_target_pairs={{0,1},{1,0},{2,3},{3,2},{4,5},{5,4},{6,7},{7,6},{8,9},{9,8},{10,11... | collective-permute-start | bytes 442376 | tf_op jit(solution)/shard_map/ppermute | solution.py:64
  742.3 37.2 %collective-permute-start.63 = (bf16[96,768]{1,0:T(8,128)(2,1)S(1)}, bf16[96,768]{1,0:T(8,128)(2,1)S(1)}, u32[]{:S(2)}, u32[]{:S(2)}) collective-permute-start(bf16[96,768]{1,0:T(8,128)(2,1)S(1)} %get-tuple-element.407), channel_id=1, source_target_pairs={{0,3},{1,2},{2,1},{3,0},{4,7},{5,6},{6,5},{7,4},{8,11},{9,10},{10,... | collective-permute-start | bytes 442376 | tf_op jit(solution)/shard_map/ppermute | solution.py:64
  745.3 36.0 %collective-permute-start.62 = (bf16[96,768]{1,0:T(8,128)(2,1)S(1)}, bf16[96,768]{1,0:T(8,128)(2,1)S(1)}, u32[]{:S(2)}, u32[]{:S(2)}) collective-permute-start(bf16[96,768]{1,0:T(8,128)(2,1)S(1)} %get-tuple-element.408), channel_id=1, source_target_pairs={{0,2},{1,3},{2,0},{3,1},{4,6},{5,7},{6,4},{7,5},{8,10},{9,11},{10,... | collective-permute-start | bytes 442376 | tf_op jit(solution)/shard_map/ppermute | solution.py:64
  746.7 25.0 %collective-permute-start.66 = (bf16[96,3072]{1,0:T(8,128)(2,1)S(1)}, bf16[96,3072]{1,0:T(8,128)(2,1)S(1)}, u32[]{:S(2)}, u32[]{:S(2)}) collective-permute-start(bf16[96,3072]{1,0:T(8,128)(2,1)S(1)} %add_convert_fusion.13), channel_id=1, source_target_pairs={{0,16},{4,20},{8,24},{12,28},{16,0},{20,4},{24,8},{28,12},{1,17},{... | collective-permute-start | bytes 1769480 | tf_op jit(solution)/shard_map/ppermute | solution.py:59
  763.3 10.1 %collective-permute-start.69 = (bf16[96,3072]{1,0:T(8,128)(2,1)S(1)}, bf16[96,3072]{1,0:T(8,128)(2,1)S(1)}, u32[]{:S(2)}, u32[]{:S(2)}) collective-permute-start(bf16[96,3072]{1,0:T(8,128)(2,1)S(1)} %add_convert_fusion.6), channel_id=1, source_target_pairs={{0,8},{4,12},{8,0},{12,4},{16,24},{20,28},{24,16},{28,20},{1,9},{5... | collective-permute-start | bytes 1769480 | tf_op jit(solution)/shard_map/ppermute | solution.py:59
  775.4 17.0 %collective-permute-start.72 = (bf16[96,1536]{1,0:T(8,128)(2,1)S(1)}, bf16[96,1536]{1,0:T(8,128)(2,1)S(1)}, u32[]{:S(2)}, u32[]{:S(2)}) collective-permute-start(bf16[96,1536]{1,0:T(8,128)(2,1)S(1)} %get-tuple-element.388), channel_id=1, source_target_pairs={{0,3},{1,2},{2,1},{3,0},{4,7},{5,6},{6,5},{7,4},{8,11},{9,10},{10,... | collective-permute-start | bytes 884744 | tf_op jit(solution)/shard_map/ppermute | solution.py:64
  778.1 29.9 %collective-permute-start.71 = (bf16[96,1536]{1,0:T(8,128)(2,1)S(1)}, bf16[96,1536]{1,0:T(8,128)(2,1)S(1)}, u32[]{:S(2)}, u32[]{:S(2)}) collective-permute-start(bf16[96,1536]{1,0:T(8,128)(2,1)S(1)} %get-tuple-element.389), channel_id=1, source_target_pairs={{0,2},{1,3},{2,0},{3,1},{4,6},{5,7},{6,4},{7,5},{8,10},{9,11},{10,... | collective-permute-start | bytes 884744 | tf_op jit(solution)/shard_map/ppermute | solution.py:64
  779.5 45.4 %collective-permute-start.84 = (bf16[2,2,384,192]{2,3,1,0:T(8,128)(2,1)}, bf16[2,2,384,192]{2,3,1,0:T(8,128)(2,1)S(1)}, u32[]{:S(2)}, u32[]{:S(2)}) collective-permute-start(bf16[2,2,384,192]{2,3,1,0:T(8,128)(2,1)} %copy.276), channel_id=1, source_target_pairs={{0,0},{1,8},{2,4},{3,12},{4,2},{5,10},{6,6},{7,14},{8,1},{9,9},{10... | collective-permute-start | bytes 1769480 | tf_op jit(solution)/shard_map/ppermute | solution.py:78
  (260 other events, 2874.9 us)

commit v2 on v1

v2 whole, which is shorter than its diff:
```python
import functools

import jax
import jax.numpy as jnp
from jax import lax
from jax.experimental import pallas as pl
from jax.experimental.pallas import tpu as pltpu
from jax.sharding import PartitionSpec as P

MICRO = 3
FRAME = 64
EPSILON = 1e-06
LEARNING = 300.0
VECTOR_LEARNING = 6000.0
MOMENTUM = 0.5
AVERAGING = 0.5
THRESHOLD = 0.05
PRECISE = lax.Precision.HIGHEST
QUAD = 4
bf16 = jnp.bfloat16
f32 = jnp.float32


NEAR = 48 * 1024 * 1024


def product(first_operand, second_operand):
    return jnp.dot(first_operand, second_operand, preferred_element_type=f32)


def contract_last(first_operand, second_operand):
    return lax.dot_general(
        first_operand, second_operand, (((1,), (1,)), ((), ())), preferred_element_type=f32
    )


def contract_rows(first_operand, second_operand):
    return lax.dot_general(
        first_operand, second_operand, (((0,), (0,)), ((), ())), preferred_element_type=f32
    )


def apply_update(weight, gradient, moment, average, rate):
    moment = MOMENTUM * moment + gradient
    updated = weight - rate * (gradient + MOMENTUM * moment)
    return (updated, moment, AVERAGING * average + (1.0 - AVERAGING) * updated)


def swap_dp(inputs, mask):
    size = lax.axis_size("dp")
    return lax.ppermute(inputs, "dp", [(i, i ^ mask) for i in range(size)])


def swap_mp(inputs, mask):
    size = lax.axis_size("mp")
    return lax.ppermute(inputs, "mp", [(i, i ^ mask) for i in range(size)])


def dp_bits():
    return lax.axis_size("dp").bit_length() - 1


def regroup(inputs):
    count = lax.axis_size("dp")
    pairs = []
    for d in range(count):
        for z in range(4):
            hi, x, k = d // 4, (d // 2) % 2, d % 2
            pairs.append((d * 4 + z, (hi * 4 + (z % 2) * 2 + z // 2) * 4 + 2 * k + x))
    return lax.ppermute(inputs, ("dp", "mp"), pairs)


def gather_mp(inputs):
    return [inputs] + [swap_mp(inputs, s) for s in (1, 2, 3)]


def scatter_mp(pieces):
    total = pieces[0].astype(f32)
    for s in (1, 2, 3):
        total = total + swap_mp(pieces[s], s).astype(f32)
    return total


def gather_dp(inputs, order):
    pieces = {0: inputs}
    rows = inputs.shape[0]
    for bit in order:
        keys = sorted(pieces)
        sent = jnp.concatenate([pieces[k] for k in keys]) if len(keys) > 1 else inputs
        got = swap_dp(sent, 1 << bit)
        for i, k in enumerate(keys):
            pieces[k ^ (1 << bit)] = got[i * rows : (i + 1) * rows]
    near = jnp.concatenate([pieces[k] for k in sorted(pieces)])
    return near, swap_dp(near, 1)


def scatter_dp(near, far, order):
    got = swap_dp(far, 1)
    left = list(range(1, dp_bits()))
    rows = near.shape[0] >> len(left)
    columns = near.shape[1]
    kind = far.dtype
    for bit in order:
        at = left.index(bit)
        shape = (-1, 2, rows << at, columns)
        mine, other = near.reshape(shape), got.reshape(shape)
        away = (mine[:, 1].astype(f32) + other[:, 1].astype(f32)).astype(kind)
        near = (mine[:, 0].astype(f32) + other[:, 0].astype(f32)).astype(kind)
        near = near.reshape(-1, columns)
        got = swap_dp(away.reshape(-1, columns), 1 << bit)
        left.remove(bit)
    return (near.astype(f32) + got.astype(f32)).astype(kind)


def sum_dp(inputs):
    for bit in range(dp_bits()):
        inputs = inputs + swap_dp(inputs, 1 << bit)
    return inputs


def sum_all(inputs):
    inputs = sum_dp(inputs)
    for mask in (1, 2):
        inputs = inputs + swap_mp(inputs, mask)
    return inputs


def group_sum_features(inputs):
    count = lax.axis_size("dp")
    width = inputs.shape[1] // count
    order = [b for b in range(count) if b % 2 == 0] + [b for b in range(count) if b % 2]
    for mask in (1, 2):
        got = swap_dp(inputs, mask)
        at = [order.index(b ^ mask) for b in order]
        inputs = inputs + jnp.concatenate(
            [got[:, p * width : (p + 1) * width] for p in at], axis=1
        )
    return inputs


def call(body, grid, in_specs, out_specs, out_shape, operands, flops, scratch=(), alias=None):
    moved = sum(o.size * o.dtype.itemsize for o in operands)
    return pl.pallas_call(
        body,
        grid=grid,
        in_specs=in_specs,
        out_specs=out_specs,
        out_shape=out_shape,
        scratch_shapes=list(scratch),
        input_output_aliases=alias or {},
        compiler_params=pltpu.CompilerParams(vmem_limit_bytes=NEAR),
        cost_estimate=pl.CostEstimate(flops=flops, bytes_accessed=moved, transcendentals=0),
    )(*operands)


def whole(array):
    return pl.BlockSpec(array.shape, lambda *i, n=array.ndim: (0,) * n)


def fetch(pairs, sems):
    copies = [
        pltpu.make_async_copy(source, target, sems.at[i])
        for i, (source, target) in enumerate(pairs)
    ]
    for copy in copies:
        copy.start()
    for copy in copies:
        copy.wait()


def standard(inputs):
    centered = inputs - jnp.mean(inputs, axis=-1, keepdims=True)
    scale = lax.rsqrt(jnp.mean(centered * centered, axis=-1, keepdims=True) + EPSILON)
    return centered * scale, scale


def standard_back(grad, unit, scale):
    return scale * (
        grad
        - jnp.mean(grad, axis=-1, keepdims=True)
        - unit * jnp.mean(grad * unit, axis=-1, keepdims=True)
    )


def memory_in_kernel(index_ref, order_ref, one_ref, two_ref, three_ref, four_ref, out_ref):
    parts = [r[0, 0] for r in (one_ref, two_ref, three_ref, four_ref)]
    blocks = []
    for c in range(4):
        s = index_ref[c]
        chosen = parts[3]
        for p in (2, 1, 0):
            chosen = jnp.where(s == p, parts[p], chosen)
        blocks.append(chosen)
    out_ref[0, 0] = contract_last(order_ref[...], jnp.concatenate(blocks)).astype(bf16)


def memory_in(index, order, parts):
    _, _, columns, rows = parts[0].shape
    return call(
        memory_in_kernel,
        (2, 2),
        [pl.BlockSpec(memory_space=pltpu.SMEM), pl.BlockSpec((rows, rows), lambda i, j: (0, 0))]
        + [pl.BlockSpec((1, 1, columns, rows), lambda i, j: (i, j, 0, 0))] * 4,
        pl.BlockSpec((1, 1, rows, 4 * columns), lambda i, j: (i, j, 0, 0)),
        jax.ShapeDtypeStruct((2, 2, rows, 4 * columns), bf16),
        (index, order) + tuple(parts),
        8 * rows * rows * 4 * columns,
    )


def memory_out_kernel(index_ref, order_ref, *refs):
    out_ref = refs[-1]
    chosen = index_ref[0]
    for m in range(2):
        rows = jnp.concatenate([r[0, 0] for r in refs[4 * m : 4 * m + 4]])
        turned = contract_rows(rows, order_ref[...]).astype(bf16)
        columns = turned.shape[0] // 4
        blocks = [turned[c * columns : (c + 1) * columns] for c in range(4)]
        block = blocks[3]
        for c in (2, 1, 0):
            block = jnp.where(chosen == c, blocks[c], block)
        out_ref[m, 0] = block


def memory_out(index, order, parts):
    _, _, rows, width = parts[0][0].shape
    return call(
        memory_out_kernel,
        (2,),
        [
            pl.BlockSpec(memory_space=pltpu.SMEM),
            pl.BlockSpec((4 * rows, 4 * rows), lambda i: (0, 0)),
        ]
        + [pl.BlockSpec((1, 1, rows, width), lambda i, m=m: (m, i, 0, 0)) for _, m in parts],
        pl.BlockSpec((2, 1, width // 4, 4 * rows), lambda i: (0, i, 0, 0)),
        jax.ShapeDtypeStruct((2, 2, width // 4, 4 * rows), bf16),
        (index, order) + tuple(a for a, _ in parts),
        8 * (4 * rows) ** 2 * width,
    )


def embed_kernel(
    patch_ref, order_ref, embed_ref, vec_ref, taps_ref, qk0, qk1, vo0, vo1,
    sorted_ref, embedded_ref, normed_ref, query_ref, key_ref, value_ref, pool_ref,
    qk_s, v_s, sems,
):
    width = embedded_ref.shape[1]
    half = width // 2

    @pl.when(pl.program_id(0) == 0)
    def _():
        fetch(
            [
                (qk0, qk_s.at[:half]),
                (qk1, qk_s.at[half:]),
                (vo0.at[:, :width], v_s.at[:half]),
                (vo1.at[:, :width], v_s.at[half:]),
            ],
            sems,
        )

    patch = contract_last(order_ref[...], patch_ref[0]).astype(bf16)
    sorted_ref[...] = patch
    embedded = contract_last(patch, embed_ref[...]) + vec_ref[0:1]
    embedded_ref[...] = embedded
    unit, _ = standard(embedded)
    normed = (unit * vec_ref[1:2] + vec_ref[2:3]).astype(bf16)
    normed_ref[...] = normed
    query_ref[...] = product(normed, qk_s[:, :width]).astype(bf16)
    for ch, weight, raw_ref in ((0, qk_s[:, width:], key_ref), (1, v_s[...], value_ref)):
        raw = product(normed, weight)
        raw_ref[...] = raw.astype(bf16)
        rows = raw.shape[0] // 4
        pooled = raw[:rows] * taps_ref[ch, 0:1]
        for t in range(1, 4):
            pooled = pooled + raw[t * rows : (t + 1) * rows] * taps_ref[ch, t : t + 1]
        pool_ref[0, ch] = pooled.astype(bf16)


def embed(patches_t, order, embed_t, vec, taps, qk, vo):
    _, patch, rows = patches_t.shape
    width = vec.shape[1]
    total = MICRO * rows

    def tile(columns):
        return pl.BlockSpec((rows, columns), lambda i: (i, 0))

    anywhere = pl.BlockSpec(memory_space=pl.ANY)
    return call(
        embed_kernel,
        (MICRO,),
        [pl.BlockSpec((1, patch, rows), lambda i: (i, 0, 0))]
        + [whole(a) for a in (order, embed_t, vec, taps)]
        + [anywhere] * 4,
        [tile(patch), tile(width), tile(width), tile(width), tile(width), tile(width)]
        + [pl.BlockSpec((1, 2, rows // 4, width), lambda i: (i, 0, 0, 0))],
        [
            jax.ShapeDtypeStruct((total, patch), bf16),
            jax.ShapeDtypeStruct((total, width), f32),
        ]
        + [jax.ShapeDtypeStruct((total, width), bf16)] * 4
        + [jax.ShapeDtypeStruct((MICRO, 2, rows // 4, width), bf16)],
        (patches_t, order, embed_t, vec, taps) + qk + vo,
        2 * total * width * (patch + 3 * width),
        scratch=[
            pltpu.VMEM((width, 2 * width), bf16),
            pltpu.VMEM((width, width), bf16),
            pltpu.SemaphoreType.DMA((4,)),
        ],
    )


def attend_kernel(sources, q_ref, taps_ref, bias_ref, *refs):
    count = sum(sources)
    now, newer = refs[: sources[0]], refs[sources[0] : sources[0] + sources[1]]
    older = refs[sources[0] + sources[1] : count]
    out_ref, prob_ref, key_ref, value_ref = refs[-4:]
    query = q_ref[...]
    rows, width = query.shape
    size = width // QUAD
    for ch, target in ((0, key_ref), (1, value_ref)):
        at = 0
        for r in now:
            n = r.shape[2]
            target[at : at + n] = r[0, ch]
            at += n
        first, second = taps_ref[ch, 4:5], taps_ref[ch, 5:6]
        for r in newer + older:
            n = r.shape[2] // 2
            target[at : at + n] = (
                r[0, ch, :n].astype(f32) * first + r[0, ch, n:].astype(f32) * second
            ).astype(bf16)
            at += n
    keys_t = key_ref[...].T
    values = value_ref[...]
    lane = lax.broadcasted_iota(jnp.int32, (rows, width), 1) // size
    scaled = query * (size**-0.5)
    total = query.astype(f32)
    for h in range(QUAD):
        own = jnp.where(lane == h, scaled, jnp.zeros_like(scaled))
        scores = product(own, keys_t) + bias_ref[0, h : h + 1, :]
        top = jnp.max(scores, axis=-1, keepdims=True)
        exponent = jnp.exp(scores - top)
        denominator = jnp.sum(exponent, axis=-1, keepdims=True)
        probs = (exponent * (1.0 / denominator)).astype(bf16)
        prob_ref[h] = probs
        total = total + jnp.where(lane == h, product(probs, values), 0.0)
    out_ref[...] = total.astype(bf16)


def source_specs(entries, block):
    return [
        pl.BlockSpec((1, 2, a.shape[2], block), lambda i, m=m: (m, 0, 0, i)) for a, m in entries
    ]


def attend(micro, query, taps, bias, now, newer, older, before):
    rows = query.shape[0] // MICRO
    width = query.shape[1]
    count = bias.shape[2]
    quads = bias.shape[0]
    block = width // quads
    entries = now + newer + older
    operands = (query, taps, bias) + tuple(a for a, _ in entries)
    specs = [
        pl.BlockSpec((rows, block), lambda i: (micro, i)),
        pl.BlockSpec((2, 6, block), lambda i: (0, 0, i)),
        pl.BlockSpec((1, QUAD, count), lambda i: (i, 0, 0)),
    ] + source_specs(entries, block)
    alias = {}
    if before is not None:
        alias = {len(operands): 0}
        operands = operands + (before,)
        specs.append(pl.BlockSpec(memory_space=pl.ANY))
    return call(
        functools.partial(attend_kernel, (len(now), len(newer), len(older))),
        (quads,),
        specs,
        [
            pl.BlockSpec((rows, block), lambda i: (micro, i)),
            pl.BlockSpec((QUAD, rows, count), lambda i: (i, 0, 0)),
            pl.BlockSpec((count, block), lambda i: (0, i)),
            pl.BlockSpec((count, block), lambda i: (0, i)),
        ],
        [
            jax.ShapeDtypeStruct(query.shape, bf16),
            jax.ShapeDtypeStruct((quads * QUAD, rows, count), bf16),
            jax.ShapeDtypeStruct((count, width), bf16),
            jax.ShapeDtypeStruct((count, width), bf16),
        ],
        operands,
        4 * rows * count * width * 4,
        alias=alias,
    )


def attend_back_kernel(sources, q_ref, k_ref, v_ref, prob_ref, grad_ref, *refs):
    entries = refs[: sum(sources)]
    dq_ref, keep_ref, send_ref, taps_ref, bias_ref = refs[-5:]
    query = q_ref[...]
    grad = grad_ref[...]
    rows, width = query.shape
    size = width // QUAD
    keys = k_ref[...]
    count = keys.shape[0]
    values_t = v_ref[...].T
    query_t = query.T
    grad_t = grad.T
    scaling = size**-0.5
    lane = lax.broadcasted_iota(jnp.int32, (rows, width), 1) // size
    total = jnp.zeros((rows, width), f32)
    ones = jnp.ones((16, rows), bf16)
    half = count // 2
    spot = lax.broadcasted_iota(jnp.int32, (1, 128), 1)
    key_parts, value_parts = [], []
    for h in range(QUAD):
        own = jnp.where(lane == h, grad, jnp.zeros_like(grad))
        probs_low = prob_ref[h]
        probs = probs_low.astype(f32)
        pulled = probs * product(own, values_t)
        shift = jnp.sum(pulled, axis=-1, keepdims=True)
        score_grad = (pulled - probs * shift).astype(bf16)
        total = total + jnp.where(lane == h, product(score_grad, keys), 0.0)
        left = jnp.concatenate([query_t[h * size : (h + 1) * size], ones])
        found = product(left, score_grad)
        key_parts.append(found[:size])
        sums = found[size : size + 1]
        row = jnp.zeros((1, 128), f32)
        for g, (a, b) in enumerate(((0, half), (half, half + half // 2), (half + half // 2, count))):
            row = row + jnp.where(spot == g, jnp.sum(sums[:, a:b], axis=1, keepdims=True), 0.0)
        bias_ref[0, h : h + 1, :] = row
        value_parts.append(product(grad_t[h * size : (h + 1) * size], probs_low))
    dq_ref[...] = (total * scaling + grad.astype(f32)).astype(bf16)
    part = keep_ref.shape[2]
    for ch, parts, factor in ((0, key_parts, scaling), (1, value_parts, 1.0)):
        found = jnp.concatenate(parts).T * factor
        for s in range(4):
            target = send_ref if s % 2 else keep_ref
            target[ch, s // 2] = found[s * part : (s + 1) * part].astype(bf16)
        at = half
        first = jnp.zeros((1, width), f32)
        second = jnp.zeros((1, width), f32)
        for r in entries:
            n = r.shape[2] // 2
            piece = found[at : at + n]
            first = first + jnp.sum(piece * r[0, ch, :n].astype(f32), axis=0, keepdims=True)
            second = second + jnp.sum(piece * r[0, ch, n:].astype(f32), axis=0, keepdims=True)
            at += n
        taps_ref[ch, 0:1] = first
        taps_ref[ch, 1:2] = second


def attend_back(micro, query, keys, values, probs, grad, newer, older, before):
    heads, rows, count = probs.shape
    width = query.shape[1]
    quads = heads // QUAD
    block = width // quads
    entries = newer + older
    operands = (query, keys, values, probs, grad) + tuple(a for a, _ in entries)
    specs = [
        pl.BlockSpec((rows, block), lambda i: (micro, i)),
        pl.BlockSpec((count, block), lambda i: (0, i)),
        pl.BlockSpec((count, block), lambda i: (0, i)),
        pl.BlockSpec((QUAD, rows, count), lambda i: (i, 0, 0)),
        pl.BlockSpec((rows, block), lambda i: (micro, i)),
    ] + source_specs(entries, block)
    alias = {}
    if before is not None:
        alias = {len(operands): 0}
        operands = operands + (before,)
        specs.append(pl.BlockSpec(memory_space=pl.ANY))
    part = count // 8
    return call(
        functools.partial(attend_back_kernel, (len(newer), len(older))),
        (quads,),
        specs,
        [
            pl.BlockSpec((rows, block), lambda i: (micro, i)),
            pl.BlockSpec((2, 2, part, block), lambda i: (0, 0, 0, i)),
            pl.BlockSpec((2, 2, part, block), lambda i: (0, 0, 0, i)),
            pl.BlockSpec((2, 2, block), lambda i: (0, 0, i)),
            pl.BlockSpec((1, QUAD, 128), lambda i: (i, 0, 0)),
        ],
        [
            jax.ShapeDtypeStruct(query.shape, bf16),
            jax.ShapeDtypeStruct((2, 2, part, width), bf16),
            jax.ShapeDtypeStruct((2, 2, part, width), bf16),
            jax.ShapeDtypeStruct((2, 2, width), f32),
            jax.ShapeDtypeStruct((quads, QUAD, 128), f32),
        ],
        operands,
        8 * rows * count * width * 4,
        alias=alias,
    )


def gelu_pair(inputs):
    size = jnp.abs(inputs)
    t = 1.0 / (1.0 + (0.3275911 * 0.5**0.5) * size)
    bell = jnp.exp(-0.5 * inputs * inputs)
    tail = (
        t
        * (
            0.5 * 0.254829592
            + t
            * (
                0.5 * -0.284496736
                + t * (0.5 * 1.421413741 + t * (0.5 * -1.453152027 + t * (0.5 * 1.061405429)))
            )
        )
        * bell
    )
    share = jnp.where(inputs > 0.0, 1.0 - tail, tail)
    return inputs * share, share + inputs * bell * 0.3989422804014327


def mlp_kernel(
    attended_ref, embedded_ref, vec_ref, select_ref, vo0, vo1, wb0, wb1, wh0, wh1,
    first_ref, normed_ref, active_ref, slope_ref, second_ref, feature_ref,
    wo_s, wb_s, wh_s, sems,
):
    width = embedded_ref.shape[1]
    half = width // 2

    @pl.when(pl.program_id(0) == 0)
    def _():
        fetch(
            [
                (vo0.at[:, width:], wo_s.at[:half]),
                (vo1.at[:, width:], wo_s.at[half:]),
                (wh0, wh_s.at[:half]),
                (wh1, wh_s.at[half:]),
                (wb0, wb_s.at[:half]),
                (wb1, wb_s.at[half:]),
            ],
            sems,
        )

    first = embedded_ref[...] + contract_last(attended_ref[...], wo_s[...])
    first_ref[...] = first
    unit, _ = standard(first)
    normed = (unit * vec_ref[3:4] + vec_ref[4:5]).astype(bf16)
    normed_ref[...] = normed
    total = first
    chunk = 512
    for at in range(0, wh_s.shape[1], chunk):
        hidden = product(normed, wh_s[:, at : at + chunk])
        value, slope = gelu_pair(hidden)
        value = value.astype(bf16)
        active_ref[:, at : at + chunk] = value
        slope_ref[:, at : at + chunk] = slope.astype(bf16)
        total = total + contract_last(value, wb_s[:, at : at + chunk])
    second_ref[...] = total
    unit, _ = standard(total)
    final = unit * vec_ref[5:6] + vec_ref[6:7]
    feature_ref[0] = jnp.dot(
        select_ref[0], final, precision=PRECISE, preferred_element_type=f32
    )


def mlp(attended, embedded, vec, select, vo, wb, wh):
    total, width = embedded.shape
    rows = total // MICRO
    units = wb[0].shape[1]
    boxes = select.shape[1]

    def tile(columns):
        return pl.BlockSpec((rows, columns), lambda i: (i, 0))

    return call(
        mlp_kernel,
        (MICRO,),
        [
            tile(width),
            tile(width),
            whole(vec),
            pl.BlockSpec((1, boxes, rows), lambda i: (i, 0, 0)),
        ]
        + [pl.BlockSpec(memory_space=pl.ANY)] * 6,
        [tile(width), tile(width), tile(units), tile(units), tile(width)]
        + [pl.BlockSpec((1, boxes, width), lambda i: (i, 0, 0))],
        [
            jax.ShapeDtypeStruct((total, width), f32),
            jax.ShapeDtypeStruct((total, width), bf16),
            jax.ShapeDtypeStruct((total, units), bf16),
            jax.ShapeDtypeStruct((total, units), bf16),
            jax.ShapeDtypeStruct((total, width), f32),
            jax.ShapeDtypeStruct((MICRO, boxes, width), f32),
        ],
        (attended, embedded, vec, select) + vo + wb + wh,
        2 * total * width * (width + 2 * units),
        scratch=[
            pltpu.VMEM((width, width), bf16),
            pltpu.VMEM((width, units), bf16),
            pltpu.VMEM((width, units), bf16),
            pltpu.SemaphoreType.DMA((6,)),
        ],
    )


def mlp_back_kernel(
    pull_ref, select_ref, second_ref, first_ref, slope_ref, vec_ref, vo0, vo1, wb0, wb1, wh0, wh1,
    branch_ref, hidden_ref, attn_ref, first_grad_ref, attended_ref, sums_ref,
    wo_s, wb_s, wh_s, sems,
):
    width = second_ref.shape[1]
    half = width // 2

    @pl.when(pl.program_id(0) == 0)
    def _():
        sums_ref[...] = jnp.zeros_like(sums_ref)
        fetch(
            [
                (vo0.at[:, width:], wo_s.at[:half]),
                (vo1.at[:, width:], wo_s.at[half:]),
                (wh0, wh_s.at[:half]),
                (wh1, wh_s.at[half:]),
                (wb0, wb_s.at[:half]),
                (wb1, wb_s.at[half:]),
            ],
            sems,
        )

    pull = lax.dot_general(
        select_ref[0],
        pull_ref[0],
        (((0,), (0,)), ((), ())),
        precision=PRECISE,
        preferred_element_type=f32,
    )
    unit, scale = standard(second_ref[...])
    sums_ref[2:3] += jnp.sum(pull * unit, axis=0, keepdims=True)
    sums_ref[3:4] += jnp.sum(pull, axis=0, keepdims=True)
    second_grad = standard_back(pull * vec_ref[5:6], unit, scale)
    branch = second_grad.astype(bf16)
    branch_ref[...] = branch
    chunk = 512
    normed_grad = jnp.zeros(second_grad.shape, f32)
    for at in range(0, wh_s.shape[1], chunk):
        active_grad = product(branch, wb_s[:, at : at + chunk])
        hidden_grad = (active_grad * slope_ref[:, at : at + chunk].astype(f32)).astype(bf16)
        hidden_ref[:, at : at + chunk] = hidden_grad
        normed_grad = normed_grad + contract_last(hidden_grad, wh_s[:, at : at + chunk])
    unit, scale = standard(first_ref[...])
    sums_ref[0:1] += jnp.sum(normed_grad * unit, axis=0, keepdims=True)
    sums_ref[1:2] += jnp.sum(normed_grad, axis=0, keepdims=True)
    first_grad = standard_back(normed_grad * vec_ref[3:4], unit, scale) + second_grad
    first_grad_ref[...] = first_grad
    attn = first_grad.astype(bf16)
    attn_ref[...] = attn
    attended_ref[...] = product(attn, wo_s[...]).astype(bf16)


def mlp_back(pull, select, second, first, slope, vec, vo, wb, wh):
    total, width = second.shape
    rows = total // MICRO
    units = wb[0].shape[1]
    boxes = select.shape[1]

    def tile(columns):
        return pl.BlockSpec((rows, columns), lambda i: (i, 0))

    return call(
        mlp_back_kernel,
        (MICRO,),
        [
            pl.BlockSpec((1, boxes, width), lambda i: (i, 0, 0)),
            pl.BlockSpec((1, boxes, rows), lambda i: (i, 0, 0)),
            tile(width),
            tile(width),
            tile(units),
            whole(vec),
        ]
        + [pl.BlockSpec(memory_space=pl.ANY)] * 6,
        [tile(width), tile(units), tile(width), tile(width), tile(width)]
        + [pl.BlockSpec((8, width), lambda i: (0, 0))],
        [
            jax.ShapeDtypeStruct((total, width), bf16),
            jax.ShapeDtypeStruct((total, units), bf16),
            jax.ShapeDtypeStruct((total, width), bf16),
            jax.ShapeDtypeStruct((total, width), f32),
            jax.ShapeDtypeStruct((total, width), bf16),
            jax.ShapeDtypeStruct((8, width), f32),
        ],
        (pull, select, second, first, slope, vec) + vo + wb + wh,
        2 * total * width * (width + 2 * units),
        scratch=[
            pltpu.VMEM((width, width), bf16),
            pltpu.VMEM((width, units), bf16),
            pltpu.VMEM((width, units), bf16),
            pltpu.SemaphoreType.DMA((6,)),
        ],
    )


def embed_back_kernel(
    dq_ref, pool_ref, key_ref, value_ref, taps_ref, embedded_ref, first_ref, vec_ref,
    qk0, qk1, vo0, vo1,
    projected_ref, grad_ref, sums_ref, taps_out,
    qk_s, v_s, sems,
):
    width = embedded_ref.shape[1]
    half = width // 2

    @pl.when(pl.program_id(0) == 0)
    def _():
        sums_ref[...] = jnp.zeros_like(sums_ref)
        taps_out[...] = jnp.zeros_like(taps_out)
        fetch(
            [
                (qk0, qk_s.at[:half]),
                (qk1, qk_s.at[half:]),
                (vo0.at[:, :width], v_s.at[:half]),
                (vo1.at[:, :width], v_s.at[half:]),
            ],
            sems,
        )

    projected_ref[:, :width] = dq_ref[...]
    rows = pool_ref.shape[2]
    for ch, raw_ref in ((0, key_ref), (1, value_ref)):
        pool = pool_ref[0, ch]
        for t in range(4):
            projected_ref[t * rows : (t + 1) * rows, (1 + ch) * width : (2 + ch) * width] = (
                pool * taps_ref[ch, t : t + 1]
            ).astype(bf16)
            raw = raw_ref[t * rows : (t + 1) * rows].astype(f32)
            taps_out[4 * ch + t : 4 * ch + t + 1] += jnp.sum(pool * raw, axis=0, keepdims=True)
    normed_grad = contract_last(projected_ref[:, : 2 * width], qk_s[...])
    normed_grad = normed_grad + contract_last(projected_ref[:, 2 * width :], v_s[...])
    unit, scale = standard(embedded_ref[...])
    sums_ref[1:2] += jnp.sum(normed_grad * unit, axis=0, keepdims=True)
    sums_ref[2:3] += jnp.sum(normed_grad, axis=0, keepdims=True)
    grad = standard_back(normed_grad * vec_ref[1:2], unit, scale) + first_ref[...]
    grad = grad.astype(bf16)
    grad_ref[...] = grad
    sums_ref[0:1] += jnp.sum(grad.astype(f32), axis=0, keepdims=True)


def embed_back(dq, pool, keys, values, taps, embedded, first_grad, vec, qk, vo):
    total, width = embedded.shape
    rows = total // MICRO

    def tile(columns):
        return pl.BlockSpec((rows, columns), lambda i: (i, 0))

    return call(
        embed_back_kernel,
        (MICRO,),
        [
            tile(width),
            pl.BlockSpec((1, 2, rows // 4, width), lambda i: (i, 0, 0, 0)),
            tile(width),
            tile(width),
            whole(taps),
            tile(width),
            tile(width),
            whole(vec),
        ]
        + [pl.BlockSpec(memory_space=pl.ANY)] * 4,
        [
            tile(3 * width),
            tile(width),
            pl.BlockSpec((8, width), lambda i: (0, 0)),
            pl.BlockSpec((8, width), lambda i: (0, 0)),
        ],
        [
            jax.ShapeDtypeStruct((total, 3 * width), bf16),
            jax.ShapeDtypeStruct((total, width), bf16),
            jax.ShapeDtypeStruct((8, width), f32),
            jax.ShapeDtypeStruct((8, width), f32),
        ],
        (dq, pool, keys, values, taps, embedded, first_grad, vec) + qk + vo,
        2 * total * width * 3 * width,
        scratch=[
            pltpu.VMEM((width, 2 * width), bf16),
            pltpu.VMEM((width, width), bf16),
            pltpu.SemaphoreType.DMA((4,)),
        ],
    )


def one_hot_rows(index, count):
    return (index[:, None] == jnp.arange(count)[None, :]).astype(bf16)


def shards(
    patches,
    clip_len,
    box_count,
    box_bounds,
    box_labels,
    memory,
    up_weight,
    down_weight,
    embed_weight,
    head_weight,
    vector_weight,
    conv_weight,
    position_bias,
    up_moment,
    down_moment,
    embed_moment,
    head_moment,
    vector_moment,
    conv_moment,
    position_moment,
    up_average,
    down_average,
    embed_average,
    head_average,
    vector_average,
    conv_average,
    position_average,
):
    dp_index = lax.axis_index("dp")
    mp_index = lax.axis_index("mp")
    dp_count = lax.axis_size("dp")
    across, core = (dp_index // 2) % 2, dp_index % 2
    quarter = 2 * core + across
    rows = patches.shape[1]
    eighth = rows // 8
    pooled = rows // 4
    half_pool = pooled // 2
    head_cols = conv_weight.shape[2]
    width = 4 * head_cols
    sub = embed_weight.shape[1]
    patch = embed_weight.shape[0]
    classes = head_weight.shape[0]
    boxes = box_bounds.shape[2]
    own_heads = position_bias.shape[0]
    heads = own_heads * 4
    hidden_cols = up_weight.shape[1] - 3 * head_cols
    up_bits = list(range(1, dp_bits()))
    down_bits = up_bits[::-1]

    ints = jnp.concatenate(
        [clip_len.reshape(-1), box_count.reshape(-1), box_bounds.reshape(-1), box_labels.reshape(-1)]
    )
    total_ints = ints.shape[0]
    ints = jnp.pad(ints, (0, -total_ints % 1024)).reshape(-1, 128)
    ints = regroup(ints).reshape(-1)
    patches_t = regroup(patches.transpose(0, 2, 1))
    memory_t = regroup(memory.transpose(0, 1, 3, 2))
    lengths_all = ints[:5]
    counts = ints[5:8]
    bounds = ints[8 : 8 + MICRO * boxes * 2].reshape(MICRO, boxes, 2)
    labels = ints[8 + MICRO * boxes * 2 : total_ints].reshape(MICRO * boxes, classes)

    vec_hi = lax.reduce_precision(vector_weight, 8, 7)
    vec_mid = lax.reduce_precision(vector_weight - vec_hi, 8, 7)
    vec_lo = vector_weight - vec_hi - vec_mid
    small = jnp.concatenate(
        [embed_weight, head_weight, vec_hi, vec_mid, vec_lo], axis=0
    ).astype(bf16).T
    small = jnp.concatenate(gather_mp(small), axis=0)
    place = jnp.arange(4 * sub)
    small = product(
        one_hot_rows(((place // sub) ^ mp_index) * sub + place % sub, 4 * sub), small
    ).astype(bf16)
    small = jnp.concatenate(gather_dp(small, up_bits))
    embed_t = small[:, :patch]
    head_t = small[:, patch : patch + classes]
    vec3 = small[:, patch + classes :].astype(f32)
    vectors = (vec3[:, :7] + vec3[:, 7:14] + vec3[:, 14:]).T
    vectors = jnp.pad(vectors, ((0, 1), (0, 0)))

    taps_pos = jnp.concatenate(
        [
            conv_weight.reshape(12, head_cols),
            jnp.pad(position_bias.reshape(1, -1), ((0, 0), (0, head_cols - position_bias.size))),
        ]
    )
    taps_pos = gather_mp(taps_pos)
    conv_all = jnp.concatenate([t[:12] for t in taps_pos], axis=1).reshape(2, 6, width)
    rel_bias = jnp.concatenate(
        [t[12, : position_bias.size].reshape(position_bias.shape) for t in taps_pos], axis=0
    )

    up_low = up_weight.astype(bf16)
    down_low = down_weight.astype(bf16)
    pieces = gather_mp(
        jnp.concatenate([up_low[:, : 3 * head_cols], down_low[:, :head_cols]], axis=1)
    )

    def columns(first, last):
        return jnp.concatenate(
            [p[:, j * head_cols : (j + 1) * head_cols] for j in range(first, last) for p in pieces],
            axis=1,
        )

    w_qk = gather_dp(columns(0, 2), up_bits)
    w_vo = gather_dp(columns(2, 4), down_bits)
    w_back = gather_dp(jnp.concatenate(gather_mp(down_low[:, head_cols:]), axis=1), up_bits)
    w_hidden = gather_dp(jnp.concatenate(gather_mp(up_low[:, 3 * head_cols :]), axis=1), down_bits)

    place = jnp.arange(rows)
    token = 8 * (place % eighth) + 4 * ((place // eighth) % 2) + place // (2 * eighth)
    token_order = one_hot_rows(token, rows)
    mem_rows = memory.shape[2]
    half_mem = mem_rows // 2
    mem_place = jnp.arange(mem_rows)
    mem_order = one_hot_rows(2 * (mem_place % half_mem) + mem_place // half_mem, mem_rows)
    mem_two = swap_dp(memory_t, 2)
    mem_parts = (memory_t, swap_dp(memory_t, 1), mem_two, swap_dp(mem_two, 1))
    mem_full = memory_in(
        jnp.stack(
            [
                (((c ^ mp_index) // 2) ^ core) + 2 * (((c ^ mp_index) % 2) ^ across)
                for c in range(4)
            ]
        ),
        mem_order,
        mem_parts,
    )

    patches_in, embedded, normed, query, raw_keys, raw_values, pools = embed(
        patches_t, token_order, embed_t, vectors, conv_all, w_qk, w_vo
    )
    stored = [[(mem_full, 0)], [(mem_full, 1)]]
    for m in range(MICRO):
        one = swap_dp(pools[m : m + 1], 1)
        two = swap_dp(pools[m : m + 1], 2)
        three = swap_dp(two, 1)
        stored.append([(pools, m), (one, 0), (two, 0), (three, 0)])

    part_quarter = [2 * (core ^ (s % 2)) + (across ^ (s // 2)) for s in range(4)]
    pool_place = jnp.arange(pooled)
    pool_token = 2 * (pool_place % half_pool) + pool_place // half_pool
    now_index = jnp.concatenate([pq * pooled + pool_token for pq in part_quarter])
    pool_index = jnp.concatenate([pq * half_pool + jnp.arange(half_pool) for pq in part_quarter])
    mem_index = jnp.arange(half_mem)

    def key_bias(m):
        sides = [
            (now_index, lengths_all[2 + m] // 4),
            (mem_index if m == 0 else pool_index, lengths_all[1 + m] // 8),
            (mem_index if m < 2 else pool_index, lengths_all[m] // 8),
        ]
        return jnp.concatenate(
            [
                jnp.where((index < limit)[None, :], rel_bias[:, g : g + 1], -1e30)
                for g, (index, limit) in enumerate(sides)
            ],
            axis=1,
        ).reshape(heads // QUAD, QUAD, -1)

    attended, saved = None, []
    for m in range(MICRO):
        attended, probs, keys, values = attend(
            m, query, conv_all, key_bias(m), stored[m + 2], stored[m + 1], stored[m], attended
        )
        saved.append((keys, values, probs))

    position = quarter * rows + token
    within = position % FRAME
    live = position[None, :] < lengths_all[2:, None]
    inside = (
        (within[None, None, :] >= bounds[:, :, 0:1])
        & (within[None, None, :] < bounds[:, :, 1:2])
        & live[:, None, :]
    )
    denominator = ((bounds[:, :, 1] - bounds[:, :, 0]) * (lengths_all[2:, None] // FRAME)).astype(
        f32
    )
    select = inside.astype(f32) / denominator[:, :, None]
    first_res, normed_mlp, active, slope, second_res, feature = mlp(
        attended, embedded, vectors, select, w_vo, w_back, w_hidden
    )
    feature = group_sum_features(feature.reshape(MICRO * boxes, width)).astype(bf16)
    logits = product(feature, head_t)
    target = labels.astype(f32)
    keep = (jnp.arange(boxes)[None, :] < counts[:, None]).astype(f32).reshape(-1, 1)
    lead = (quarter == 0).astype(f32)
    loss_part = jnp.sum((jax.nn.softplus(logits) - target * logits) * keep) * lead
    grad_logits = ((jax.nn.sigmoid(logits) - target) * keep).astype(bf16)

    grad_head = contract_rows(feature, grad_logits) * lead
    grad_feature = contract_last(grad_logits, head_t).reshape(MICRO, boxes, width)
    grad_branch, grad_hidden, grad_attn, grad_first, grad_attended, sums = mlp_back(
        grad_feature, select, second_res, first_res, slope, vectors, w_vo, w_back, w_hidden
    )
    half = width // 2

    def weight_grad(left, right):
        return tuple(
            contract_rows(left[:, at : at + half], right).astype(bf16) for at in (0, half)
        )

    back_grad = scatter_dp(*weight_grad(grad_branch, active), down_bits)
    hidden_grad = scatter_dp(*weight_grad(normed_mlp, grad_hidden), up_bits)
    out_grad = weight_grad(grad_attn, attended)

    dq, pool_grads, bias_grad, mem_taps = None, [], 0.0, 0.0
    for m in range(MICRO):
        keys, values, probs = saved[m]
        dq, kept, sent, taps_part, bias_part = attend_back(
            m, query, keys, values, probs, grad_attended, stored[m + 1], stored[m], dq
        )
        got = swap_dp(sent, 1)
        away = (kept[:, 1].astype(f32) + got[:, 1].astype(f32)).astype(bf16)
        mine = kept[:, 0].astype(f32) + got[:, 0].astype(f32)
        pool_grads.append(mine + swap_dp(away, 2).astype(f32))
        bias_grad = bias_grad + bias_part
        mem_taps = mem_taps + taps_part
    projected_grad, embedded_grad, embed_sums, taps_grad = embed_back(
        dq,
        jnp.stack(pool_grads),
        raw_keys,
        raw_values,
        conv_all,
        embedded,
        grad_first,
        vectors,
        w_qk,
        w_vo,
    )
    qk_grad = scatter_dp(*weight_grad(normed, projected_grad[:, : 2 * width]), up_bits)
    v_grad = weight_grad(normed, projected_grad[:, 2 * width :])
    vo_grad = scatter_dp(
        *(jnp.concatenate([a, b], axis=1) for a, b in zip(v_grad, out_grad)), down_bits
    )
    grad_embed = contract_rows(embedded_grad, patches_in)
    grad_vectors = jnp.concatenate([embed_sums[:3], sums[:4]])

    small_grad = jnp.concatenate([grad_embed, grad_head, grad_vectors.T], axis=1)
    small_grad = scatter_dp(small_grad[:half], small_grad[half:], up_bits)
    small_grad = scatter_mp(
        [
            lax.dynamic_slice_in_dim(small_grad, (mp_index ^ s) * sub, sub, axis=0)
            for s in range(4)
        ]
    ).T
    embed_grad = small_grad[:patch]
    head_grad = small_grad[patch : patch + classes]
    vector_grad = small_grad[patch + classes :]

    def pieces_of(array, count):
        return [array[:, s * count : (s + 1) * count] for s in range(4)]

    back_mine = scatter_mp(pieces_of(back_grad, hidden_cols))
    hidden_mine = scatter_mp(pieces_of(hidden_grad, hidden_cols))
    attn_mine = scatter_mp(
        [
            jnp.concatenate(
                [
                    part[:, (4 * i + s) * head_cols : (4 * i + s + 1) * head_cols]
                    for part in (qk_grad, vo_grad)
                    for i in range(2)
                ],
                axis=1,
            )
            for s in range(4)
        ]
    )
    down_grad = jnp.concatenate([attn_mine[:, 3 * head_cols :], back_mine], axis=1)
    up_grad = jnp.concatenate([attn_mine[:, : 3 * head_cols], hidden_mine], axis=1)

    count_local = jnp.sum(box_count).astype(f32) * (mp_index == 0).astype(f32)
    taps_rows = jnp.stack(
        [
            jnp.concatenate([taps_grad[4 * ch : 4 * ch + 4], mem_taps[ch]], axis=0)
            for ch in range(2)
        ]
    ).reshape(12, 4, head_cols)
    scalars = jnp.stack([loss_part, count_local])
    last = jnp.concatenate(
        [
            bias_grad.reshape(heads, 128)[:, :3].reshape(4, -1),
            jnp.broadcast_to(scalars[None], (4, 2)),
        ],
        axis=1,
    )
    last = jnp.pad(last, ((0, 0), (0, head_cols - last.shape[1])))
    flat = jnp.concatenate([taps_rows, last[None]]).transpose(1, 0, 2)
    flat = sum_dp(flat)
    flat = scatter_mp([flat[s] for s in range(4)])
    conv_grad = flat[:12].reshape(2, 6, head_cols)
    position_grad = flat[12, : own_heads * 3].reshape(own_heads, 3)
    loss_global = flat[12, own_heads * 3]
    box_total = flat[12, own_heads * 3 + 1]

    reduced = (up_grad, down_grad, embed_grad, head_grad, vector_grad, conv_grad, position_grad)
    squares = sum((jnp.sum(gradient * gradient) for gradient in reduced[:5]))
    squares = squares + (
        jnp.sum(conv_grad * conv_grad) + jnp.sum(position_grad * position_grad)
    ) / dp_count
    square_total = sum_all(jnp.full((8, 128), squares, f32))[0, 0]
    grad_norm = jnp.sqrt(square_total) / box_total
    scaling = jnp.minimum(1.0, THRESHOLD / grad_norm) / box_total
    masters = (
        up_weight,
        down_weight,
        embed_weight,
        head_weight,
        vector_weight,
        conv_weight,
        position_bias,
    )
    moments = (
        up_moment,
        down_moment,
        embed_moment,
        head_moment,
        vector_moment,
        conv_moment,
        position_moment,
    )
    averages = (
        up_average,
        down_average,
        embed_average,
        head_average,
        vector_average,
        conv_average,
        position_average,
    )
    rates = (LEARNING,) * 4 + (VECTOR_LEARNING,) * 3
    results = [
        apply_update(weight, gradient * scaling, moment, average, rate)
        for weight, gradient, moment, average, rate in zip(
            masters, reduced, moments, averages, rates
        )
    ]

    target_row = jnp.arange(4 * pooled)
    target_quarter, target_rest = target_row // pooled, target_row % pooled
    source_row = (
        (((target_quarter // 2) ^ core) + 2 * ((target_quarter % 2) ^ across)) * pooled
        + (target_rest % 2) * half_pool
        + target_rest // 2
    )
    new_memory = memory_out(
        (quarter ^ mp_index)[None],
        one_hot_rows(source_row, 4 * pooled).T,
        stored[3] + stored[4],
    )
    new_memory = regroup(new_memory).transpose(0, 1, 3, 2)
    return (
        (loss_global, box_total, grad_norm, new_memory)
        + tuple(r[0] for r in results)
        + tuple(r[1] for r in results)
        + tuple(r[2] for r in results)
        + (results[0][0].astype(bf16), results[1][0].astype(bf16))
    )


def solution(mesh):
    both = ("dp", "mp")
    weight_specs = (
        P("dp", "mp"),
        P("dp", "mp"),
        P(None, both),
        P(None, both),
        P(None, both),
        P(None, None, "mp"),
        P("mp", None),
    )
    memory_spec = P(None, None, "dp", "mp")
    return jax.shard_map(
        shards,
        mesh=mesh,
        in_specs=(
            P(None, both, None),
            P("dp", None),
            P("dp", None),
            P("dp", None, None, None),
            P("dp", None, None, None),
            memory_spec,
        )
        + weight_specs * 3,
        out_specs=(P(), P(), P(), memory_spec)
        + weight_specs * 3
        + (P("dp", "mp"), P("dp", "mp")),
        check_vma=False,
    )
```

time: 864 us -> 704 us (0.81)
  local copies, waits for them, and re-layouts: 210 us -> 56.9 us
  matrix products: 149 us -> 42.1 us
  Pallas kernels: 60.7 us -> 162 us
  waiting for transfers between devices: 157 us -> 229 us
  other arithmetic: 122 us -> 58.7 us
    pallas_call x6 -> x12, Pallas kernels: 60.7 us -> 162 us  [call(): pl.pallas_call(body, grid=grid, in_specs=in_specs, out_specs=out_specs, o...]
    ppermute x56, waiting for transfers between devices: 117 us -> 188 us  [swap_dp(): return lax.ppermute(inputs, 'dp', [(i, i ^ mask) for i in range(size)])]
    dot_general x5 -> x2, matrix products: 71.2 us -> 1.96 us  [product(): return jnp.dot(first_operand, second_operand, preferred_element_type=f32)]
    unnamed x558 -> x322, local copies, waits for them, and re-layouts: 88.3 us -> 38.3 us
    another operation x55 -> x3, local copies, waits for them, and re-layouts: 46 us -> 0.29 us  [the longest x24 15.2 us: shards(): jnp.stack([jnp.sum(part * stored[which][ch][0].astype(f32), axis=0), jnp....]
    dot_general x6 -> x1, matrix products: 35.3 us -> 1.04 us  [contract_last(): lax.dot_general(first_operand, second_operand, (((1,), (1,)), ((), ())),...]
    squeeze x18 -> x1, local copies, waits for them, and re-layouts: 16.3 us -> 0.01 us  [shards(): mem_taps[ch]]
    reduce_sum x17 -> x0, other arithmetic: 16.2 us -> none  [the longest x5 6.32 us: shards(): jnp.sum(part * stored[which][ch][0].astype(f32), axis=0)]
  transfers between devices with their start and end apart: 85 -> 92, of which waited for: 29 -> 36; matrix products, arithmetic and copies ran while one was open for 35% -> 10% of each run, Pallas kernels for 3% -> 7%
where the time goes in v2:
time: 704 us; the launch traced here: 696 us
  waiting for transfers between devices  229 us (33%)
  Pallas kernels  162 us (23%)
  starting transfers between devices  121 us (17%)
  other arithmetic  58.7 us (8%)
  local copies, waits for them, and re-layouts  56.9 us (8%)
  matrix products  42.1 us (6%)
  between operations  26.2 us (4%)
    ppermute x56, waiting for transfers between devices, swap_dp(): return lax.ppermute(inputs, 'dp', [(i, i ^ mask) for i in range(size)])  188 us
    pallas_call x12, Pallas kernels, call(): pl.pallas_call(body, grid=grid, in_specs=in_specs, out_specs=out_specs, o...  162 us
    ppermute x32, starting transfers between devices, swap_mp(): return lax.ppermute(inputs, 'mp', [(i, i ^ mask) for i in range(size)])  58.5 us
    ppermute x56, starting transfers between devices, swap_dp(): return lax.ppermute(inputs, 'dp', [(i, i ^ mask) for i in range(size)])  44.9 us
    ppermute x32, waiting for transfers between devices, swap_mp(): return lax.ppermute(inputs, 'mp', [(i, i ^ mask) for i in range(size)])  40.8 us
    dot_general x12, matrix products, contract_rows(): lax.dot_general(first_operand, second_operand, (((0,), (0,)), ((), ())),...  39.1 us
    unnamed x322, local copies, waits for them, and re-layouts  38.3 us
    ppermute x4, starting transfers between devices, regroup(): return lax.ppermute(inputs, ('dp', 'mp'), pairs)  17.5 us
  transfers between devices with their start and end apart: 92, of which 36 were waited for; matrix products, arithmetic and copies ran while one was open for 10% of the time, Pallas kernels for 7%

profile of v2, /device:TPU:0, one launch (start us, length us, event | category | flops | bytes accessed | tf_op | source)
XLA Modules:
  0.0 696.2 jit_solution(16012021369673171252)
XLA Ops:
  3.3 5.1 collective-permute-start.3
  10.6 3.8 collective-permute-start.9
  22.8 2.6 collective-permute-start.8
  42.5 2.4 collective-permute-start.7
  50.2 2.2 collective-permute-start.33
  54.6 3.4 collective-permute-done.4
  59.9 2.7 collective-permute-start.12
  62.5 8.5 %collective-permute-start.41 = (bf16[96,768]{1,0:T(8,128)(2,1)S(1)}, bf16[96,768]{1,0:T(8,128)(2,1)S(1)}, u32[]{:S(2)}, u32[]{:S(2)}) collective-permute-start(bf16[96,768]{1,0:T(8,128)(2,1)S(1)} %slice.770), channel_id=1, source_target_pairs={{0,3},{1,2},{2,1},{3,0},{4,7},{5,6},{6,5},{7,4},{8,11},{9,10},{10,... | collective-permute-start | bytes 442376 | tf_op jit(solution)/shard_map/ppermute | solution.py:56
  72.7 9.5 %collective-permute-start = (bf16[3,441,384]{2,1,0:T(8,128)(2,1)}, bf16[3,441,384]{2,1,0:T(8,128)(2,1)}, u32[]{:S(2)}, u32[]{:S(2)}) collective-permute-start(bf16[3,441,384]{2,1,0:T(8,128)(2,1)} %bitcast.231), channel_id=1, source_target_pairs={{0,0},{1,8},{2,4},{3,12},{4,2},{5,10},{6,6},{7,14},{8,1},{9,9},{10... | collective-permute-start | bytes 3048200 | tf_op jit(solution)/shard_map/ppermute | solution.py:70
  82.3 6.0 collective-permute-start.29
  90.3 12.0 %collective-permute-start.13 = (bf16[96,1536]{1,0:T(8,128)(2,1)S(1)}, bf16[96,1536]{1,0:T(8,128)(2,1)S(1)}, u32[]{:S(2)}, u32[]{:S(2)}) collective-permute-start(bf16[96,1536]{1,0:T(8,128)(2,1)S(1)} %concatenate.175), channel_id=1, source_target_pairs={{0,8},{4,12},{8,0},{12,4},{16,24},{20,28},{24,16},{28,20},{1,9},{5... | collective-permute-start | bytes 884744 | tf_op jit(solution)/shard_map/ppermute | solution.py:51
  104.4 11.2 %collective-permute-done.13 = bf16[96,1536]{1,0:T(8,128)(2,1)S(1)} collective-permute-done((bf16[96,1536]{1,0:T(8,128)(2,1)S(1)}, bf16[96,1536]{1,0:T(8,128)(2,1)S(1)}, u32[]{:S(2)}, u32[]{:S(2)}) %collective-permute-start.13) | collective-permute-done | bytes 294944 | tf_op jit(solution)/shard_map/ppermute | solution.py:51
  118.9 25.5 %collective-permute-done.36 = bf16[96,3072]{1,0:T(8,128)(2,1)S(1)} collective-permute-done((bf16[96,3072]{1,0:T(8,128)(2,1)}, bf16[96,3072]{1,0:T(8,128)(2,1)S(1)}, u32[]{:S(2)}, u32[]{:S(2)}) %collective-permute-start.36) | collective-permute-done | bytes 589856 | tf_op jit(solution)/shard_map/ppermute | solution.py:51
  147.0 2.4 collective-permute-start.17
  153.0 7.9 %collective-permute-done.14 = bf16[192,1536]{1,0:T(8,128)(2,1)} collective-permute-done((bf16[192,1536]{1,0:T(8,128)(2,1)}, bf16[192,1536]{1,0:T(8,128)(2,1)}, u32[]{:S(2)}, u32[]{:S(2)}) %collective-permute-start.14) | collective-permute-done | bytes 589856 | tf_op jit(solution)/shard_map/ppermute | solution.py:51
  160.9 2.4 collective-permute-start.43
  166.0 18.3 %collective-permute-done.37 = bf16[192,3072]{1,0:T(8,128)(2,1)} collective-permute-done((bf16[192,3072]{1,0:T(8,128)(2,1)}, bf16[192,3072]{1,0:T(8,128)(2,1)}, u32[]{:S(2)}, u32[]{:S(2)}) %collective-permute-start.37) | collective-permute-done | bytes 1179680 | tf_op jit(solution)/shard_map/ppermute | solution.py:51
  184.3 4.6 pad_maximum_fusion.wb0
  189.6 10.3 %collective-permute-done.43 = bf16[192,3072]{1,0:T(8,128)(2,1)S(1)} collective-permute-done((bf16[192,3072]{1,0:T(8,128)(2,1)}, bf16[192,3072]{1,0:T(8,128)(2,1)S(1)}, u32[]{:S(2)}, u32[]{:S(2)}) %collective-permute-start.43) | collective-permute-done | bytes 1179680 | tf_op jit(solution)/shard_map/ppermute | solution.py:51
  200.0 3.5 pad_maximum_fusion.1.wh0
  206.4 11.9 %shard_map.466 = (bf16[1152,441]{1,0:T(8,128)(2,1)S(1)}, f32[1152,768]{1,0:T(8,128)}, bf16[1152,768]{1,0:T(8,128)(2,1)}, bf16[1152,768]{1,0:T(8,128)(2,1)}, bf16...) custom-call(bf16[3,441,384]{2,1,0:T(8,128)(2,1)} %collective-permute-done.patch_ref, ...), custom_call_target="tpu_custom_call" | custom-call | flops 4857200640 | bytes 6768384 | tf_op jit(solution)/shard_map/pallas_call | solution.py:143
  221.3 7.2 %collective-permute-done.27.refs_2_.refs_6_.refs_10_ = bf16[1,2,96,768]{3,2,1,0:T(8,128)(2,1)S(1)} collective-permute-done((bf16[1,2,96,768]{3,2,1,0:T(8,128)(2,1)S(1)}, bf16[1,2,96,768]{3,2,1,0:T(8,128)(2,1)S(1)}, u32[]{:S(2)}, u32[]{:S(2)}) %collective-permute-start.27) | collective-permute-done | bytes 294944 | tf_op jit(solution)/shard_map/ppermute | solution.py:51
  228.7 3.7 shard_map.467.refs_4_.refs_5_.refs_8_.refs_0_.refs_1_
  236.0 10.0 %shard_map.468 = (bf16[1152,768]{1,0:T(8,128)(2,1)S(1)}, bf16[12,384,768]{2,1,0:T(8,128)(2,1)}, bf16[768,768]{1,0:T(8,128)(2,1)S(1)}, bf16[768,768]{1,0:T(8,128)(2,1)S(1)}) custom-call(bf16[1152,768]{1,0:T(8,128)(2,1)} %get-tuple-element.77.q_ref, f32[2,6,768]{2,1,0:T(8,128)S(1)} %copy-done.34, f32[3,4,768]{2,1,0:T(4,128)S(1)} %pad_maximum_fusion.28.bias_ref, ...), custom_call_target="tpu_custom_call" | custom-call | flops 3623878656 | bytes 8331264 | tf_op jit(solution)/shard_map/pallas_call | solution.py:143
  248.7 10.0 %shard_map.469 = (bf16[1152,768]{1,0:T(8,128)(2,1)}, bf16[12,384,768]{2,1,0:T(8,128)(2,1)}, bf16[768,768]{1,0:T(8,128)(2,1)S(1)}, bf16[768,768]{1,0:T(8,128)(2,1)S(1)}) custom-call(bf16[1152,768]{1,0:T(8,128)(2,1)} %get-tuple-element.77.q_ref, f32[2,6,768]{2,1,0:T(8,128)S(1)} %copy-done.34, ...), custom_call_target="tpu_custom_call", output_to_operand_aliasing={{0}: (12, {})} | custom-call | flops 3623878656 | bytes 9510912 | tf_op jit(solution)/shard_map/pallas_call | solution.py:143
  261.0 9.7 %shard_map.470 = (bf16[1152,768]{1,0:T(8,128)(2,1)}, bf16[12,384,768]{2,1,0:T(8,128)(2,1)}, bf16[768,768]{1,0:T(8,128)(2,1)S(1)}, bf16[768,768]{1,0:T(8,128)(2,1)S(1)}) custom-call(bf16[1152,768]{1,0:T(8,128)(2,1)} %get-tuple-element.77.q_ref, f32[2,6,768]{2,1,0:T(8,128)S(1)} %copy-done.34, ...), custom_call_target="tpu_custom_call", output_to_operand_aliasing={{0}: (15, {})} | custom-call | flops 3623878656 | bytes 8921088 | tf_op jit(solution)/shard_map/pallas_call | solution.py:143
  274.2 34.2 %shard_map.471 = (f32[1152,768]{1,0:T(8,128)}, bf16[1152,768]{1,0:T(8,128)(2,1)S(1)}, bf16[1152,3072]{1,0:T(8,128)(2,1)}, bf16[1152,3072]{1,0:T(8,128)(2,1)}, f3...) custom-call(bf16[1152,768]{1,0:T(8,128)(2,1)S(1)} %copy-done.1, f32[1152,768]{1,0:T(8,128)} %get-tuple-element.85.embedded_ref, ...), custom_call_target="tpu_custom_call" | custom-call | flops 12230590464 | bytes 17166336 | tf_op jit(solution)/shard_map/pallas_call | solution.py:143
  322.3 29.5 %shard_map.472 = (bf16[1152,768]{1,0:T(8,128)(2,1)S(1)}, bf16[1152,3072]{1,0:T(8,128)(2,1)}, bf16[1152,768]{1,0:T(8,128)(2,1)S(1)}, f32[1152,768]{1,0:T(8,128)},...) custom-call(f32[3,8,768]{2,1,0:T(8,128)S(1)} %convolution_bitcast_fusion.pull_ref, f32[3,8,384]{2,1,0:T(8,128)S(1)} %copy-done.40, ...), custom_call_target="tpu_custom_call" | custom-call | flops 12230590464 | bytes 26087424 | tf_op jit(solution)/shard_map/pallas_call | solution.py:143
  351.8 7.8 %convolution_convert_fusion.2 = bf16[384,3072]{1,0:T(8,128)(2,1)} fusion(bf16[1152,3072]{1,0:T(8,128)(2,1)} %get-tuple-element.120, bf16[1152,768]{1,0:T(8,128)(2,1)S(1)} %copy-done.48), kind=kOutput, calls=%fused_computation.2 | convolution fusion | flops 2719088640 | bytes 10321920 | tf_op jit(solution)/shard_map/dot_general | solution.py:38
  359.6 4.6 convolution_convert_fusion.3
  367.8 4.9 convolution_convert_fusion
  372.7 4.6 convolution_convert_fusion.1
  377.3 12.9 %shard_map.473 = (bf16[1152,768]{1,0:T(8,128)(2,1)S(1)}, bf16[2,2,96,768]{3,2,1,0:T(8,128)(2,1)S(1)}, bf16[2,2,96,768]{3,2,1,0:T(8,128)(2,1)S(1)}, f32[2,2,768]{2,1,0:T(2,128)S(1)}, f32[3,4,128]{2,1,0:T(4,128)S(1)}) custom-call(bf16[1152,768]{1,0:T(8,128)(2,1)} %get-tuple-element.77.q_ref, bf16[768,768]{1,0:T(8,128)(2,1)S(1)} %copy-done.60, ...), custom_call_target="tpu_custom_call" | custom-call | flops 7247757312 | bytes 17694720 | tf_op jit(solution)/shard_map/pallas_call | solution.py:143
  393.3 13.4 %shard_map.474 = (bf16[1152,768]{1,0:T(8,128)(2,1)}, bf16[2,2,96,768]{3,2,1,0:T(8,128)(2,1)S(1)}, bf16[2,2,96,768]{3,2,1,0:T(8,128)(2,1)S(1)}, f32[2,2,768]{2,1,0:T(2,128)S(1)}, f32[3,4,128]{2,1,0:T(4,128)S(1)}) custom-call(bf16[1152,768]{1,0:T(8,128)(2,1)} %get-tuple-element.77.q_ref, ...), custom_call_target="tpu_custom_call", output_to_operand_aliasing={{0}: (10, {})} | custom-call | flops 7247757312 | bytes 18874368 | tf_op jit(solution)/shard_map/pallas_call | solution.py:143
  408.3 13.4 %shard_map.475 = (bf16[1152,768]{1,0:T(8,128)(2,1)}, bf16[2,2,96,768]{3,2,1,0:T(8,128)(2,1)S(1)}, bf16[2,2,96,768]{3,2,1,0:T(8,128)(2,1)S(1)}, f32[2,2,768]{2,1,0:T(2,128)S(1)}, f32[3,4,128]{2,1,0:T(4,128)S(1)}) custom-call(bf16[1152,768]{1,0:T(8,128)(2,1)} %get-tuple-element.77.q_ref, ...), custom_call_target="tpu_custom_call", output_to_operand_aliasing={{0}: (13, {})} | custom-call | flops 7247757312 | bytes 18284544 | tf_op jit(solution)/shard_map/pallas_call | solution.py:143
  431.1 6.5 collective-permute-done.52
  437.7 6.2 collective-permute-done.50
  444.1 5.8 collective-permute-done.48
  452.2 11.8 %shard_map.476 = (bf16[1152,2304]{1,0:T(8,128)(2,1)}, bf16[1152,768]{1,0:T(8,128)(2,1)}, f32[8,768]{1,0:T(8,128)S(1)}, f32[8,768]{1,0:T(8,128)S(1)}) custom-call(bf16[1152,768]{1,0:T(8,128)(2,1)} %get-tuple-element.99.dq_ref, f32[3,2,96,768]{3,2,1,0:T(8,128)} %pad_maximum_fusion.2.pool_ref, bf16[1152,768]{1,0:T(8,128)(2,1)} %get-tuple-element.106.key_ref, ...), custom_call_target="tpu_custom_call" | custom-call | flops 4076863488 | bytes 18935808 | tf_op jit(solution)/shard_map/pallas_call | solution.py:143
  464.0 3.4 fusion.17
  469.3 2.8 fusion.7
  472.1 2.8 fusion.4
  475.6 2.6 fusion.141
  479.8 2.8 collective-permute-done.54
  484.4 2.5 collective-permute-done.55
  488.1 3.3 collective-permute-start.56
  502.7 9.5 %collective-permute-done.81 = f32[192,528]{1,0:T(8,128)} collective-permute-done((f32[192,528]{1,0:T(8,128)}, f32[192,528]{1,0:T(8,128)}, u32[]{:S(2)}, u32[]{:S(2)}) %collective-permute-start.81) | collective-permute-done | bytes 405536 | tf_op jit(solution)/shard_map/ppermute | solution.py:51
  516.2 6.4 collective-permute-done.82
  530.0 5.2 collective-permute-done.85
  535.8 14.2 %collective-permute-done.84 = f32[24,528]{0,1:T(8,128)S(1)} collective-permute-done((f32[24,528]{0,1:T(8,128)S(1)}, f32[24,528]{0,1:T(8,128)S(1)}, u32[]{:S(2)}, u32[]{:S(2)}) %collective-permute-start.84) | collective-permute-done | bytes 50720 | tf_op jit(solution)/shard_map/ppermute | solution.py:56
  556.0 2.5 add_convert_fusion.1
  559.6 6.7 collective-permute-done.60
  567.0 29.6 %collective-permute-done.64 = bf16[96,1536]{1,0:T(8,128)(2,1)S(1)} collective-permute-done((bf16[96,1536]{1,0:T(8,128)(2,1)S(1)}, bf16[96,1536]{1,0:T(8,128)(2,1)S(1)}, u32[]{:S(2)}, u32[]{:S(2)}) %collective-permute-start.64) | collective-permute-done | bytes 294944 | tf_op jit(solution)/shard_map/ppermute | solution.py:51
  598.9 3.3 collective-permute-start.65
  607.3 2.5 collective-permute-done.66
  612.2 13.8 %collective-permute-done.70 = bf16[96,3072]{1,0:T(8,128)(2,1)S(1)} collective-permute-done((bf16[96,3072]{1,0:T(8,128)(2,1)S(1)}, bf16[96,3072]{1,0:T(8,128)(2,1)S(1)}, u32[]{:S(2)}, u32[]{:S(2)}) %collective-permute-start.70) | collective-permute-done | bytes 589856 | tf_op jit(solution)/shard_map/ppermute | solution.py:51
  627.2 3.4 collective-permute-start.71
  630.7 5.1 collective-permute-done.76
  636.0 2.6 collective-permute-start.79
  641.4 3.4 collective-permute-done.79
  644.8 8.9 %collective-permute-done.78 = bf16[96,768]{1,0:T(8,128)(2,1)S(1)} collective-permute-done((bf16[96,768]{1,0:T(8,128)(2,1)S(1)}, bf16[96,768]{1,0:T(8,128)(2,1)S(1)}, u32[]{:S(2)}, u32[]{:S(2)}) %collective-permute-start.78) | collective-permute-done | bytes 147488 | tf_op jit(solution)/shard_map/ppermute | solution.py:56
  660.1 3.3 collective-permute-done.87
  663.9 3.1 collective-permute-done.88
  672.2 2.8 collective-permute-start.90
  (679 shorter events, 171.3 us)
Async XLA Ops:
  3.3 46.9 %collective-permute-start.3 = (bf16[24,542]{1,0:T(8,128)(2,1)S(1)}, bf16[24,542]{1,0:T(8,128)(2,1)S(1)}, u32[]{:S(2)}, u32[]{:S(2)}) collective-permute-start(bf16[24,542]{1,0:T(8,128)(2,1)S(1)} %bitcast.215), channel_id=1, source_target_pairs={{0,3},{1,2},{2,1},{3,0},{4,7},{5,6},{6,5},{7,4},{8,11},{9,10},{10,... | collective-permute-start | bytes 78056 | tf_op jit(solution)/shard_map/ppermute | solution.py:56
  8.4 44.0 %collective-permute-start.2 = (bf16[24,542]{1,0:T(8,128)(2,1)S(1)}, bf16[24,542]{1,0:T(8,128)(2,1)S(1)}, u32[]{:S(2)}, u32[]{:S(2)}) collective-permute-start(bf16[24,542]{1,0:T(8,128)(2,1)S(1)} %bitcast.216), channel_id=1, source_target_pairs={{0,2},{1,3},{2,0},{3,1},{4,6},{5,7},{6,4},{7,5},{8,10},{9,11},{10,... | collective-permute-start | bytes 78056 | tf_op jit(solution)/shard_map/ppermute | solution.py:56
  8.4 44.1 %collective-permute-start.1 = (bf16[24,542]{1,0:T(8,128)(2,1)S(1)}, bf16[24,542]{1,0:T(8,128)(2,1)S(1)}, u32[]{:S(2)}, u32[]{:S(2)}) collective-permute-start(bf16[24,542]{1,0:T(8,128)(2,1)S(1)} %bitcast.217), channel_id=1, source_target_pairs={{0,1},{1,0},{2,3},{3,2},{4,5},{5,4},{6,7},{7,6},{8,9},{9,8},{10,11... | collective-permute-start | bytes 78056 | tf_op jit(solution)/shard_map/ppermute | solution.py:56
  10.6 31.9 %collective-permute-start.9 = (f32[13,192]{1,0:T(8,128)S(1)}, f32[13,192]{1,0:T(8,128)S(1)}, u32[]{:S(2)}, u32[]{:S(2)}) collective-permute-start(f32[13,192]{1,0:T(8,128)S(1)} %select_maximum_fusion), channel_id=1, source_target_pairs={{0,3},{1,2},{2,1},{3,0},{4,7},{5,6},{6,5},{7,4},{8,11},{9,10},{10,... | collective-permute-start | bytes 29960 | tf_op jit(solution)/shard_map/ppermute | solution.py:56
  22.8 22.1 %collective-permute-start.8 = (f32[13,192]{1,0:T(8,128)S(1)}, f32[13,192]{1,0:T(8,128)S(1)}, u32[]{:S(2)}, u32[]{:S(2)}) collective-permute-start(f32[13,192]{1,0:T(8,128)S(1)} %select_maximum_fusion), channel_id=1, source_target_pairs={{0,2},{1,3},{2,0},{3,1},{4,6},{5,7},{6,4},{7,5},{8,10},{9,11},{10,... | collective-permute-start | bytes 29960 | tf_op jit(solution)/shard_map/ppermute | solution.py:56
  44.9 14.9 %collective-permute-start.35 = (bf16[96,768]{1,0:T(8,128)(2,1)S(1)}, bf16[96,768]{1,0:T(8,128)(2,1)S(1)}, u32[]{:S(2)}, u32[]{:S(2)}) collective-permute-start(bf16[96,768]{1,0:T(8,128)(2,1)S(1)} %slice.769), channel_id=1, source_target_pairs={{0,3},{1,2},{2,1},{3,0},{4,7},{5,6},{6,5},{7,4},{8,11},{9,10},{10,... | collective-permute-start | bytes 442376 | tf_op jit(solution)/shard_map/ppermute | solution.py:56
  48.0 14.5 %collective-permute-start.34 = (bf16[96,768]{1,0:T(8,128)(2,1)S(1)}, bf16[96,768]{1,0:T(8,128)(2,1)S(1)}, u32[]{:S(2)}, u32[]{:S(2)}) collective-permute-start(bf16[96,768]{1,0:T(8,128)(2,1)S(1)} %slice.769), channel_id=1, source_target_pairs={{0,2},{1,3},{2,0},{3,1},{4,6},{5,7},{6,4},{7,5},{8,10},{9,11},{10,... | collective-permute-start | bytes 442376 | tf_op jit(solution)/shard_map/ppermute | solution.py:56
  50.2 20.8 %collective-permute-start.33 = (bf16[96,768]{1,0:T(8,128)(2,1)S(1)}, bf16[96,768]{1,0:T(8,128)(2,1)S(1)}, u32[]{:S(2)}, u32[]{:S(2)}) collective-permute-start(bf16[96,768]{1,0:T(8,128)(2,1)S(1)} %slice.769), channel_id=1, source_target_pairs={{0,1},{1,0},{2,3},{3,2},{4,5},{5,4},{6,7},{7,6},{8,9},{9,8},{10,11... | collective-permute-start | bytes 442376 | tf_op jit(solution)/shard_map/ppermute | solution.py:56
  52.5 19.5 %collective-permute-start.10 = (bf16[96,768]{1,0:T(8,128)(2,1)S(1)}, bf16[96,768]{1,0:T(8,128)(2,1)S(1)}, u32[]{:S(2)}, u32[]{:S(2)}) collective-permute-start(bf16[96,768]{1,0:T(8,128)(2,1)S(1)} %pad_maximum_fusion.19), channel_id=1, source_target_pairs={{0,1},{1,0},{2,3},{3,2},{4,5},{5,4},{6,7},{7,6},{8,9},{9,8},{10,11... | collective-permute-start | bytes 442376 | tf_op jit(solution)/shard_map/ppermute | solution.py:56
  58.0 14.7 %collective-permute-start.11 = (bf16[96,768]{1,0:T(8,128)(2,1)S(1)}, bf16[96,768]{1,0:T(8,128)(2,1)S(1)}, u32[]{:S(2)}, u32[]{:S(2)}) collective-permute-start(bf16[96,768]{1,0:T(8,128)(2,1)S(1)} %pad_maximum_fusion.19), channel_id=1, source_target_pairs={{0,2},{1,3},{2,0},{3,1},{4,6},{5,7},{6,4},{7,5},{8,10},{9,11},{10,... | collective-permute-start | bytes 442376 | tf_op jit(solution)/shard_map/ppermute | solution.py:56
  59.9 22.4 %collective-permute-start.12 = (bf16[96,768]{1,0:T(8,128)(2,1)S(1)}, bf16[96,768]{1,0:T(8,128)(2,1)S(1)}, u32[]{:S(2)}, u32[]{:S(2)}) collective-permute-start(bf16[96,768]{1,0:T(8,128)(2,1)S(1)} %pad_maximum_fusion.19), channel_id=1, source_target_pairs={{0,3},{1,2},{2,1},{3,0},{4,7},{5,6},{6,5},{7,4},{8,11},{9,10},{10,... | collective-permute-start | bytes 442376 | tf_op jit(solution)/shard_map/ppermute | solution.py:56
  62.5 26.2 %collective-permute-start.41 = (bf16[96,768]{1,0:T(8,128)(2,1)S(1)}, bf16[96,768]{1,0:T(8,128)(2,1)S(1)}, u32[]{:S(2)}, u32[]{:S(2)}) collective-permute-start(bf16[96,768]{1,0:T(8,128)(2,1)S(1)} %slice.770), channel_id=1, source_target_pairs={{0,3},{1,2},{2,1},{3,0},{4,7},{5,6},{6,5},{7,4},{8,11},{9,10},{10,... | collective-permute-start | bytes 442376 | tf_op jit(solution)/shard_map/ppermute | solution.py:56
  71.1 19.3 %collective-permute-start.40 = (bf16[96,768]{1,0:T(8,128)(2,1)S(1)}, bf16[96,768]{1,0:T(8,128)(2,1)S(1)}, u32[]{:S(2)}, u32[]{:S(2)}) collective-permute-start(bf16[96,768]{1,0:T(8,128)(2,1)S(1)} %slice.770), channel_id=1, source_target_pairs={{0,2},{1,3},{2,0},{3,1},{4,6},{5,7},{6,4},{7,5},{8,10},{9,11},{10,... | collective-permute-start | bytes 442376 | tf_op jit(solution)/shard_map/ppermute | solution.py:56
  72.0 30.4 %collective-permute-start.39 = (bf16[96,768]{1,0:T(8,128)(2,1)S(1)}, bf16[96,768]{1,0:T(8,128)(2,1)S(1)}, u32[]{:S(2)}, u32[]{:S(2)}) collective-permute-start(bf16[96,768]{1,0:T(8,128)(2,1)S(1)} %slice.770), channel_id=1, source_target_pairs={{0,1},{1,0},{2,3},{3,2},{4,5},{5,4},{6,7},{7,6},{8,9},{9,8},{10,11... | collective-permute-start | bytes 442376 | tf_op jit(solution)/shard_map/ppermute | solution.py:56
  72.7 130.9 %collective-permute-start = (bf16[3,441,384]{2,1,0:T(8,128)(2,1)}, bf16[3,441,384]{2,1,0:T(8,128)(2,1)}, u32[]{:S(2)}, u32[]{:S(2)}) collective-permute-start(bf16[3,441,384]{2,1,0:T(8,128)(2,1)} %bitcast.231), channel_id=1, source_target_pairs={{0,0},{1,8},{2,4},{3,12},{4,2},{5,10},{6,6},{7,14},{8,1},{9,9},{10... | collective-permute-start | bytes 3048200 | tf_op jit(solution)/shard_map/ppermute | solution.py:70
  82.3 64.7 %collective-permute-start.29 = (bf16[2,2,192,384]{3,2,1,0:T(8,128)(2,1)}, bf16[2,2,192,384]{3,2,1,0:T(8,128)(2,1)}, u32[]{:S(2)}, u32[]{:S(2)}) collective-permute-start(bf16[2,2,192,384]{3,2,1,0:T(8,128)(2,1)} %bitcast.232), channel_id=1, source_target_pairs={{0,0},{1,8},{2,4},{3,12},{4,2},{5,10},{6,6},{7,14},{8,1},{9,9},{10... | collective-permute-start | bytes 1769480 | tf_op jit(solution)/shard_map/ppermute | solution.py:70
  88.7 15.2 %collective-permute-start.5 = (bf16[192,542]{0,1:T(8,128)(2,1)S(1)}, bf16[192,542]{0,1:T(8,128)(2,1)S(1)}, u32[]{:S(2)}, u32[]{:S(2)}) collective-permute-start(bf16[192,542]{0,1:T(8,128)(2,1)S(1)} %pad_maximum_fusion.18), channel_id=1, source_target_pairs={{0,16},{4,20},{8,24},{12,28},{16,0},{20,4},{24,8},{28,12},{1,17},{... | collective-permute-start | bytes 624392 | tf_op jit(solution)/shard_map/ppermute | solution.py:51
  90.3 25.2 %collective-permute-start.13 = (bf16[96,1536]{1,0:T(8,128)(2,1)S(1)}, bf16[96,1536]{1,0:T(8,128)(2,1)S(1)}, u32[]{:S(2)}, u32[]{:S(2)}) collective-permute-start(bf16[96,1536]{1,0:T(8,128)(2,1)S(1)} %concatenate.175), channel_id=1, source_target_pairs={{0,8},{4,12},{8,0},{12,4},{16,24},{20,28},{24,16},{28,20},{1,9},{5... | collective-permute-start | bytes 884744 | tf_op jit(solution)/shard_map/ppermute | solution.py:51
  102.4 15.6 %collective-permute-start.16 = (bf16[96,1536]{1,0:T(8,128)(2,1)S(1)}, bf16[96,1536]{1,0:T(8,128)(2,1)S(1)}, u32[]{:S(2)}, u32[]{:S(2)}) collective-permute-start(bf16[96,1536]{1,0:T(8,128)(2,1)S(1)} %concatenate.178), channel_id=1, source_target_pairs={{0,16},{4,20},{8,24},{12,28},{16,0},{20,4},{24,8},{28,12},{1,17},{... | collective-permute-start | bytes 884744 | tf_op jit(solution)/shard_map/ppermute | solution.py:51
  104.0 40.4 %collective-permute-start.36 = (bf16[96,3072]{1,0:T(8,128)(2,1)}, bf16[96,3072]{1,0:T(8,128)(2,1)S(1)}, u32[]{:S(2)}, u32[]{:S(2)}) collective-permute-start(bf16[96,3072]{1,0:T(8,128)(2,1)} %pad_maximum_fusion.13), channel_id=1, source_target_pairs={{0,8},{4,12},{8,0},{12,4},{16,24},{20,28},{24,16},{28,20},{1,9},{5... | collective-permute-start | bytes 1769480 | tf_op jit(solution)/shard_map/ppermute | solution.py:51
  115.6 33.9 %collective-permute-start.42 = (bf16[96,3072]{1,0:T(8,128)(2,1)S(1)}, bf16[96,3072]{1,0:T(8,128)(2,1)S(1)}, u32[]{:S(2)}, u32[]{:S(2)}) collective-permute-start(bf16[96,3072]{1,0:T(8,128)(2,1)S(1)} %pad_maximum_fusion.14), channel_id=1, source_target_pairs={{0,16},{4,20},{8,24},{12,28},{16,0},{20,4},{24,8},{28,12},{1,17},{... | collective-permute-start | bytes 1769480 | tf_op jit(solution)/shard_map/ppermute | solution.py:51
  118.0 32.7 %collective-permute-start.6 = (bf16[384,542]{0,1:T(8,128)(2,1)S(1)}, bf16[384,542]{0,1:T(8,128)(2,1)S(1)}, u32[]{:S(2)}, u32[]{:S(2)}) collective-permute-start(bf16[384,542]{0,1:T(8,128)(2,1)S(1)} %pad_maximum_fusion.16), channel_id=1, source_target_pairs={{0,4},{4,0},{8,12},{12,8},{16,20},{20,16},{24,28},{28,24},{1,5},{5... | collective-permute-start | bytes 1248776 | tf_op jit(solution)/shard_map/ppermute | solution.py:51
  144.4 16.6 %collective-permute-start.14 = (bf16[192,1536]{1,0:T(8,128)(2,1)}, bf16[192,1536]{1,0:T(8,128)(2,1)}, u32[]{:S(2)}, u32[]{:S(2)}) collective-permute-start(bf16[192,1536]{1,0:T(8,128)(2,1)} %pad_maximum_fusion.11), channel_id=1, source_target_pairs={{0,16},{4,20},{8,24},{12,28},{16,0},{20,4},{24,8},{28,12},{1,17},{... | collective-permute-start | bytes 1769480 | tf_op jit(solution)/shard_map/ppermute | solution.py:51
  147.0 17.6 %collective-permute-start.17 = (bf16[192,1536]{1,0:T(8,128)(2,1)}, bf16[192,1536]{1,0:T(8,128)(2,1)}, u32[]{:S(2)}, u32[]{:S(2)}) collective-permute-start(bf16[192,1536]{1,0:T(8,128)(2,1)} %pad_maximum_fusion.12), channel_id=1, source_target_pairs={{0,8},{4,12},{8,0},{12,4},{16,24},{20,28},{24,16},{28,20},{1,9},{5... | collective-permute-start | bytes 1769480 | tf_op jit(solution)/shard_map/ppermute | solution.py:51
  149.5 39.5 %collective-permute-start.31 = (bf16[2,2,192,384]{3,2,1,0:T(8,128)(2,1)}, bf16[2,2,192,384]{3,2,1,0:T(8,128)(2,1)}, u32[]{:S(2)}, u32[]{:S(2)}) collective-permute-start(bf16[2,2,192,384]{3,2,1,0:T(8,128)(2,1)} %collective-permute-done.29.one_ref), channel_id=1, source_target_pairs={{0,8},{4,12},{8,0},{12,4},{16,24},{20,28},{24,16},{28,20},{1,9},{5... | collective-permute-start | bytes 1769480 | tf_op jit(solution)/shard_map/ppermute | solution.py:51
  150.7 33.5 %collective-permute-start.37 = (bf16[192,3072]{1,0:T(8,128)(2,1)}, bf16[192,3072]{1,0:T(8,128)(2,1)}, u32[]{:S(2)}, u32[]{:S(2)}) collective-permute-start(bf16[192,3072]{1,0:T(8,128)(2,1)} %pad_maximum_fusion.6), channel_id=1, source_target_pairs={{0,16},{4,20},{8,24},{12,28},{16,0},{20,4},{24,8},{28,12},{1,17},{... | collective-permute-start | bytes 3538952 | tf_op jit(solution)/shard_map/ppermute | solution.py:51
  160.9 38.9 %collective-permute-start.43 = (bf16[192,3072]{1,0:T(8,128)(2,1)}, bf16[192,3072]{1,0:T(8,128)(2,1)S(1)}, u32[]{:S(2)}, u32[]{:S(2)}) collective-permute-start(bf16[192,3072]{1,0:T(8,128)(2,1)} %pad_maximum_fusion.7), channel_id=1, source_target_pairs={{0,8},{4,12},{8,0},{12,4},{16,24},{20,28},{24,16},{28,20},{1,9},{5... | collective-permute-start | bytes 3538952 | tf_op jit(solution)/shard_map/ppermute | solution.py:51
  164.6 39.6 %collective-permute-start.15 = (bf16[384,1536]{1,0:T(8,128)(2,1)S(1)}, bf16[384,1536]{1,0:T(8,128)(2,1)S(1)}, u32[]{:S(2)}, u32[]{:S(2)}) collective-permute-start(bf16[384,1536]{1,0:T(8,128)(2,1)S(1)} %pad_maximum_fusion.4.qk0), channel_id=1, source_target_pairs={{0,4},{4,0},{8,12},{12,8},{16,20},{20,16},{24,28},{28,24},{1,5},{5... | collective-permute-start | bytes 3538952 | tf_op jit(solution)/shard_map/ppermute | solution.py:51
  184.3 20.0 %collective-permute-start.18 = (bf16[384,1536]{1,0:T(8,128)(2,1)S(1)}, bf16[384,1536]{1,0:T(8,128)(2,1)S(1)}, u32[]{:S(2)}, u32[]{:S(2)}) collective-permute-start(bf16[384,1536]{1,0:T(8,128)(2,1)S(1)} %pad_maximum_fusion.5.vo0), channel_id=1, source_target_pairs={{0,4},{4,0},{8,12},{12,8},{16,20},{20,16},{24,28},{28,24},{1,5},{5... | collective-permute-start | bytes 3538952 | tf_op jit(solution)/shard_map/ppermute | solution.py:51
  189.0 31.6 %collective-permute-start.30 = (bf16[2,2,192,384]{3,2,1,0:T(8,128)(2,1)}, bf16[2,2,192,384]{3,2,1,0:T(8,128)(2,1)S(1)}, u32[]{:S(2)}, u32[]{:S(2)}) collective-permute-start(bf16[2,2,192,384]{3,2,1,0:T(8,128)(2,1)} %collective-permute-done.29.one_ref), channel_id=1, source_target_pairs={{0,4},{4,0},{8,12},{12,8},{16,20},{20,16},{24,28},{28,24},{1,5},{5... | collective-permute-start | bytes 1769480 | tf_op jit(solution)/shard_map/ppermute | solution.py:51
  199.9 20.8 %collective-permute-start.32 = (bf16[2,2,192,384]{3,2,1,0:T(8,128)(2,1)}, bf16[2,2,192,384]{3,2,1,0:T(8,128)(2,1)S(1)}, u32[]{:S(2)}, u32[]{:S(2)}) collective-permute-start(bf16[2,2,192,384]{3,2,1,0:T(8,128)(2,1)} %collective-permute-done.31.three_ref), channel_id=1, source_target_pairs={{0,4},{4,0},{8,12},{12,8},{16,20},{20,16},{24,28},{28,24},{1,5},{5... | collective-permute-start | bytes 1769480 | tf_op jit(solution)/shard_map/ppermute | solution.py:51
  203.6 69.1 %collective-permute-start.38 = (bf16[384,3072]{1,0:T(8,128)(2,1)S(1)}, bf16[384,3072]{1,0:T(8,128)(2,1)}, u32[]{:S(2)}, u32[]{:S(2)}) collective-permute-start(bf16[384,3072]{1,0:T(8,128)(2,1)S(1)} %pad_maximum_fusion.wb0), channel_id=1, source_target_pairs={{0,4},{4,0},{8,12},{12,8},{16,20},{20,16},{24,28},{28,24},{1,5},{5... | collective-permute-start | bytes 7077896 | tf_op jit(solution)/shard_map/ppermute | solution.py:51
  204.2 68.6 %collective-permute-start.44 = (bf16[384,3072]{1,0:T(8,128)(2,1)S(1)}, bf16[384,3072]{1,0:T(8,128)(2,1)}, u32[]{:S(2)}, u32[]{:S(2)}) collective-permute-start(bf16[384,3072]{1,0:T(8,128)(2,1)S(1)} %pad_maximum_fusion.1.wh0), channel_id=1, source_target_pairs={{0,4},{4,0},{8,12},{12,8},{16,20},{20,16},{24,28},{28,24},{1,5},{5... | collective-permute-start | bytes 7077896 | tf_op jit(solution)/shard_map/ppermute | solution.py:51
  220.6 13.7 %collective-permute-start.26 = (bf16[1,2,96,768]{3,2,1,0:T(8,128)(2,1)S(1)}, bf16[1,2,96,768]{3,2,1,0:T(8,128)(2,1)S(1)}, u32[]{:S(2)}, u32[]{:S(2)}) collective-permute-start(bf16[1,2,96,768]{3,2,1,0:T(8,128)(2,1)S(1)} %get-tuple-element.273), channel_id=1, source_target_pairs={{0,4},{4,0},{8,12},{12,8},{16,20},{20,16},{24,28},{28,24},{1,5},{5... | collective-permute-start | bytes 884744 | tf_op jit(solution)/shard_map/ppermute | solution.py:51
  220.6 13.2 %collective-permute-start.24 = (bf16[1,2,96,768]{3,2,1,0:T(8,128)(2,1)S(1)}, bf16[1,2,96,768]{3,2,1,0:T(8,128)(2,1)S(1)}, u32[]{:S(2)}, u32[]{:S(2)}) collective-permute-start(bf16[1,2,96,768]{3,2,1,0:T(8,128)(2,1)S(1)} %get-tuple-element.274), channel_id=1, source_target_pairs={{0,8},{4,12},{8,0},{12,4},{16,24},{20,28},{24,16},{28,20},{1,9},{5... | collective-permute-start | bytes 884744 | tf_op jit(solution)/shard_map/ppermute | solution.py:51
  233.8 14.8 %collective-permute-start.23 = (bf16[1,2,96,768]{3,2,1,0:T(8,128)(2,1)S(1)}, bf16[1,2,96,768]{3,2,1,0:T(8,128)(2,1)S(1)}, u32[]{:S(2)}, u32[]{:S(2)}) collective-permute-start(bf16[1,2,96,768]{3,2,1,0:T(8,128)(2,1)S(1)} %get-tuple-element.274), channel_id=1, source_target_pairs={{0,4},{4,0},{8,12},{12,8},{16,20},{20,16},{24,28},{28,24},{1,5},{5... | collective-permute-start | bytes 884744 | tf_op jit(solution)/shard_map/ppermute | solution.py:51
  234.3 14.0 %collective-permute-start.21 = (bf16[1,2,96,768]{3,2,1,0:T(8,128)(2,1)S(1)}, bf16[1,2,96,768]{3,2,1,0:T(8,128)(2,1)S(1)}, u32[]{:S(2)}, u32[]{:S(2)}) collective-permute-start(bf16[1,2,96,768]{3,2,1,0:T(8,128)(2,1)S(1)} %get-tuple-element.275), channel_id=1, source_target_pairs={{0,8},{4,12},{8,0},{12,4},{16,24},{20,28},{24,16},{28,20},{1,9},{5... | collective-permute-start | bytes 884744 | tf_op jit(solution)/shard_map/ppermute | solution.py:51
  236.0 12.7 %collective-permute-start.25 = (bf16[1,2,96,768]{3,2,1,0:T(8,128)(2,1)S(1)}, bf16[1,2,96,768]{3,2,1,0:T(8,128)(2,1)S(1)}, u32[]{:S(2)}, u32[]{:S(2)}) collective-permute-start(bf16[1,2,96,768]{3,2,1,0:T(8,128)(2,1)S(1)} %collective-permute-done.24.refs_2_.refs_6_), channel_id=1, source_target_pairs={{0,4},{4,0},{8,12},{12,8},{16,20},{20,16},{24,28},{28,24},{1,5},{5... | collective-permute-start | bytes 884744 | tf_op jit(solution)/shard_map/ppermute | solution.py:51
  248.2 12.7 %collective-permute-start.20 = (bf16[1,2,96,768]{3,2,1,0:T(8,128)(2,1)S(1)}, bf16[1,2,96,768]{3,2,1,0:T(8,128)(2,1)S(1)}, u32[]{:S(2)}, u32[]{:S(2)}) collective-permute-start(bf16[1,2,96,768]{3,2,1,0:T(8,128)(2,1)S(1)} %get-tuple-element.275), channel_id=1, source_target_pairs={{0,4},{4,0},{8,12},{12,8},{16,20},{20,16},{24,28},{28,24},{1,5},{5... | collective-permute-start | bytes 884744 | tf_op jit(solution)/shard_map/ppermute | solution.py:51
  248.6 12.3 %collective-permute-start.22 = (bf16[1,2,96,768]{3,2,1,0:T(8,128)(2,1)S(1)}, bf16[1,2,96,768]{3,2,1,0:T(8,128)(2,1)S(1)}, u32[]{:S(2)}, u32[]{:S(2)}) collective-permute-start(bf16[1,2,96,768]{3,2,1,0:T(8,128)(2,1)S(1)} %collective-permute-done.21.refs_2_.refs_6_), channel_id=1, source_target_pairs={{0,4},{4,0},{8,12},{12,8},{16,20},{20,16},{24,28},{28,24},{1,5},{5... | collective-permute-start | bytes 884744 | tf_op jit(solution)/shard_map/ppermute | solution.py:51
  428.9 15.1 %collective-permute-start.50 = (bf16[2,96,768]{2,1,0:T(8,128)(2,1)S(1)}, bf16[2,96,768]{2,1,0:T(8,128)(2,1)S(1)}, u32[]{:S(2)}, u32[]{:S(2)}) collective-permute-start(bf16[2,96,768]{2,1,0:T(8,128)(2,1)S(1)} %fusion.49), channel_id=1, source_target_pairs={{0,8},{4,12},{8,0},{12,4},{16,24},{20,28},{24,16},{28,20},{1,9},{5... | collective-permute-start | bytes 884744 | tf_op jit(solution)/shard_map/ppermute | solution.py:51
  430.1 19.8 %collective-permute-start.48 = (bf16[2,96,768]{2,1,0:T(8,128)(2,1)S(1)}, bf16[2,96,768]{2,1,0:T(8,128)(2,1)S(1)}, u32[]{:S(2)}, u32[]{:S(2)}) collective-permute-start(bf16[2,96,768]{2,1,0:T(8,128)(2,1)S(1)} %fusion.48), channel_id=1, source_target_pairs={{0,8},{4,12},{8,0},{12,4},{16,24},{20,28},{24,16},{28,20},{1,9},{5... | collective-permute-start | bytes 884744 | tf_op jit(solution)/shard_map/ppermute | solution.py:51
  475.1 26.2 %collective-permute-start.59 = (bf16[384,1536]{1,0:T(8,128)(2,1)}, bf16[384,1536]{1,0:T(8,128)(2,1)}, u32[]{:S(2)}, u32[]{:S(2)}) collective-permute-start(bf16[384,1536]{1,0:T(8,128)(2,1)} %fusion.7), channel_id=1, source_target_pairs={{0,4},{4,0},{8,12},{12,8},{16,20},{20,16},{24,28},{28,24},{1,5},{5... | collective-permute-start | bytes 3538952 | tf_op jit(solution)/shard_map/ppermute | solution.py:51
  479.8 15.8 %collective-permute-start.80 = (f32[384,528]{0,1:T(8,128)}, f32[384,528]{0,1:T(8,128)}, u32[]{:S(2)}, u32[]{:S(2)}) collective-permute-start(f32[384,528]{0,1:T(8,128)} %get-tuple-element.267), channel_id=1, source_target_pairs={{0,4},{4,0},{8,12},{12,8},{16,20},{20,16},{24,28},{28,24},{1,5},{5... | collective-permute-start | bytes 2433032 | tf_op jit(solution)/shard_map/ppermute | solution.py:51
  492.5 59.9 %collective-permute-start.68 = (bf16[384,3072]{1,0:T(8,128)(2,1)}, bf16[384,3072]{1,0:T(8,128)(2,1)}, u32[]{:S(2)}, u32[]{:S(2)}) collective-permute-start(bf16[384,3072]{1,0:T(8,128)(2,1)} %convolution_convert_fusion.2), channel_id=1, source_target_pairs={{0,4},{4,0},{8,12},{12,8},{16,20},{20,16},{24,28},{28,24},{1,5},{5... | collective-permute-start | bytes 7077896 | tf_op jit(solution)/shard_map/ppermute | solution.py:51
  492.5 63.5 %collective-permute-start.74 = (bf16[384,3072]{1,0:T(8,128)(2,1)}, bf16[384,3072]{1,0:T(8,128)(2,1)}, u32[]{:S(2)}, u32[]{:S(2)}) collective-permute-start(bf16[384,3072]{1,0:T(8,128)(2,1)} %convolution_convert_fusion), channel_id=1, source_target_pairs={{0,4},{4,0},{8,12},{12,8},{16,20},{20,16},{24,28},{28,24},{1,5},{5... | collective-permute-start | bytes 7077896 | tf_op jit(solution)/shard_map/ppermute | solution.py:51
  493.1 34.4 %collective-permute-start.62 = (bf16[384,1536]{1,0:T(8,128)(2,1)}, bf16[384,1536]{1,0:T(8,128)(2,1)}, u32[]{:S(2)}, u32[]{:S(2)}) collective-permute-start(bf16[384,1536]{1,0:T(8,128)(2,1)} %pad_maximum_fusion.9), channel_id=1, source_target_pairs={{0,4},{4,0},{8,12},{12,8},{16,20},{20,16},{24,28},{28,24},{1,5},{5... | collective-permute-start | bytes 3538952 | tf_op jit(solution)/shard_map/ppermute | solution.py:51
  498.3 13.9 %collective-permute-start.81 = (f32[192,528]{1,0:T(8,128)}, f32[192,528]{1,0:T(8,128)}, u32[]{:S(2)}, u32[]{:S(2)}) collective-permute-start(f32[192,528]{1,0:T(8,128)} %bitcast.73), channel_id=1, source_target_pairs={{0,8},{4,12},{8,0},{12,4},{16,24},{20,28},{24,16},{28,20},{1,9},{5... | collective-permute-start | bytes 1216520 | tf_op jit(solution)/shard_map/ppermute | solution.py:51
  525.8 24.3 %collective-permute-start.84 = (f32[24,528]{0,1:T(8,128)S(1)}, f32[24,528]{0,1:T(8,128)S(1)}, u32[]{:S(2)}, u32[]{:S(2)}) collective-permute-start(f32[24,528]{0,1:T(8,128)S(1)} %get-tuple-element.304), channel_id=1, source_target_pairs={{0,2},{1,3},{2,0},{3,1},{4,6},{5,7},{6,4},{7,5},{8,10},{9,11},{10,... | collective-permute-start | bytes 152072 | tf_op jit(solution)/shard_map/ppermute | solution.py:56
  527.5 22.9 %collective-permute-start.83 = (f32[24,528]{0,1:T(8,128)S(1)}, f32[24,528]{0,1:T(8,128)S(1)}, u32[]{:S(2)}, u32[]{:S(2)}) collective-permute-start(f32[24,528]{0,1:T(8,128)S(1)} %get-tuple-element.302), channel_id=1, source_target_pairs={{0,1},{1,0},{2,3},{3,2},{4,5},{5,4},{6,7},{7,6},{8,9},{9,8},{10,11... | collective-permute-start | bytes 152072 | tf_op jit(solution)/shard_map/ppermute | solution.py:56
  535.3 23.8 %collective-permute-start.63 = (bf16[192,1536]{1,0:T(8,128)(2,1)S(1)}, bf16[192,1536]{1,0:T(8,128)(2,1)S(1)}, u32[]{:S(2)}, u32[]{:S(2)}) collective-permute-start(bf16[192,1536]{1,0:T(8,128)(2,1)S(1)} %get-tuple-element.265), channel_id=1, source_target_pairs={{0,16},{4,20},{8,24},{12,28},{16,0},{20,4},{24,8},{28,12},{1,17},{... | collective-permute-start | bytes 1769480 | tf_op jit(solution)/shard_map/ppermute | solution.py:51
  550.0 16.2 %collective-permute-start.60 = (bf16[192,1536]{1,0:T(8,128)(2,1)S(1)}, bf16[192,1536]{1,0:T(8,128)(2,1)S(1)}, u32[]{:S(2)}, u32[]{:S(2)}) collective-permute-start(bf16[192,1536]{1,0:T(8,128)(2,1)S(1)} %bitcast.209), channel_id=1, source_target_pairs={{0,8},{4,12},{8,0},{12,4},{16,24},{20,28},{24,16},{28,20},{1,9},{5... | collective-permute-start | bytes 1769480 | tf_op jit(solution)/shard_map/ppermute | solution.py:51
  554.2 55.9 %collective-permute-start.69 = (bf16[192,3072]{1,0:T(8,128)(2,1)S(1)}, bf16[192,3072]{1,0:T(8,128)(2,1)S(1)}, u32[]{:S(2)}, u32[]{:S(2)}) collective-permute-start(bf16[192,3072]{1,0:T(8,128)(2,1)S(1)} %bitcast.204), channel_id=1, source_target_pairs={{0,8},{4,12},{8,0},{12,4},{16,24},{20,28},{24,16},{28,20},{1,9},{5... | collective-permute-start | bytes 3538952 | tf_op jit(solution)/shard_map/ppermute | solution.py:51
  558.5 52.4 %collective-permute-start.75 = (bf16[192,3072]{1,0:T(8,128)(2,1)S(1)}, bf16[192,3072]{1,0:T(8,128)(2,1)S(1)}, u32[]{:S(2)}, u32[]{:S(2)}) collective-permute-start(bf16[192,3072]{1,0:T(8,128)(2,1)S(1)} %get-tuple-element.263), channel_id=1, source_target_pairs={{0,16},{4,20},{8,24},{12,28},{16,0},{20,4},{24,8},{28,12},{1,17},{... | collective-permute-start | bytes 3538952 | tf_op jit(solution)/shard_map/ppermute | solution.py:51
  559.2 37.3 %collective-permute-start.64 = (bf16[96,1536]{1,0:T(8,128)(2,1)S(1)}, bf16[96,1536]{1,0:T(8,128)(2,1)S(1)}, u32[]{:S(2)}, u32[]{:S(2)}) collective-permute-start(bf16[96,1536]{1,0:T(8,128)(2,1)S(1)} %fusion.54), channel_id=1, source_target_pairs={{0,8},{4,12},{8,0},{12,4},{16,24},{20,28},{24,16},{28,20},{1,9},{5... | collective-permute-start | bytes 884744 | tf_op jit(solution)/shard_map/ppermute | solution.py:51
  566.4 30.4 %collective-permute-start.61 = (bf16[96,1536]{1,0:T(8,128)(2,1)S(1)}, bf16[96,1536]{1,0:T(8,128)(2,1)S(1)}, u32[]{:S(2)}, u32[]{:S(2)}) collective-permute-start(bf16[96,1536]{1,0:T(8,128)(2,1)S(1)} %fusion.52), channel_id=1, source_target_pairs={{0,16},{4,20},{8,24},{12,28},{16,0},{20,4},{24,8},{28,12},{1,17},{... | collective-permute-start | bytes 884744 | tf_op jit(solution)/shard_map/ppermute | solution.py:51
  605.8 64.0 %collective-permute-start.91 = (bf16[2,2,192,384]{3,2,1,0:T(8,128)(2,1)S(1)}, bf16[2,2,192,384]{3,2,1,0:T(8,128)(2,1)}, u32[]{:S(2)}, u32[]{:S(2)}) collective-permute-start(bf16[2,2,192,384]{3,2,1,0:T(8,128)(2,1)S(1)} %copy-done.16), channel_id=1, source_target_pairs={{0,0},{1,8},{2,4},{3,12},{4,2},{5,10},{6,6},{7,14},{8,1},{9,9},{10... | collective-permute-start | bytes 1769480 | tf_op jit(solution)/shard_map/ppermute | solution.py:70
  610.3 15.6 %collective-permute-start.70 = (bf16[96,3072]{1,0:T(8,128)(2,1)S(1)}, bf16[96,3072]{1,0:T(8,128)(2,1)S(1)}, u32[]{:S(2)}, u32[]{:S(2)}) collective-permute-start(bf16[96,3072]{1,0:T(8,128)(2,1)S(1)} %fusion.37), channel_id=1, source_target_pairs={{0,16},{4,20},{8,24},{12,28},{16,0},{20,4},{24,8},{28,12},{1,17},{... | collective-permute-start | bytes 1769480 | tf_op jit(solution)/shard_map/ppermute | solution.py:51
  611.0 24.7 %collective-permute-start.76 = (bf16[96,3072]{1,0:T(8,128)(2,1)S(1)}, bf16[96,3072]{1,0:T(8,128)(2,1)S(1)}, u32[]{:S(2)}, u32[]{:S(2)}) collective-permute-start(bf16[96,3072]{1,0:T(8,128)(2,1)S(1)} %fusion.39), channel_id=1, source_target_pairs={{0,8},{4,12},{8,0},{12,4},{16,24},{20,28},{24,16},{28,20},{1,9},{5... | collective-permute-start | bytes 1769480 | tf_op jit(solution)/shard_map/ppermute | solution.py:51
  626.2 12.4 %collective-permute-start.73 = (bf16[96,768]{1,0:T(8,128)(2,1)S(1)}, bf16[96,768]{1,0:T(8,128)(2,1)S(1)}, u32[]{:S(2)}, u32[]{:S(2)}) collective-permute-start(bf16[96,768]{1,0:T(8,128)(2,1)S(1)} %get-tuple-element.280), channel_id=1, source_target_pairs={{0,3},{1,2},{2,1},{3,0},{4,7},{5,6},{6,5},{7,4},{8,11},{9,10},{10,... | collective-permute-start | bytes 442376 | tf_op jit(solution)/shard_map/ppermute | solution.py:56
  627.2 14.0 %collective-permute-start.72 = (bf16[96,768]{1,0:T(8,128)(2,1)S(1)}, bf16[96,768]{1,0:T(8,128)(2,1)S(1)}, u32[]{:S(2)}, u32[]{:S(2)}) collective-permute-start(bf16[96,768]{1,0:T(8,128)(2,1)S(1)} %get-tuple-element.281), channel_id=1, source_target_pairs={{0,2},{1,3},{2,0},{3,1},{4,6},{5,7},{6,4},{7,5},{8,10},{9,11},{10,... | collective-permute-start | bytes 442376 | tf_op jit(solution)/shard_map/ppermute | solution.py:56
  627.2 14.1 %collective-permute-start.71 = (bf16[96,768]{1,0:T(8,128)(2,1)S(1)}, bf16[96,768]{1,0:T(8,128)(2,1)S(1)}, u32[]{:S(2)}, u32[]{:S(2)}) collective-permute-start(bf16[96,768]{1,0:T(8,128)(2,1)S(1)} %get-tuple-element.279), channel_id=1, source_target_pairs={{0,1},{1,0},{2,3},{3,2},{4,5},{5,4},{6,7},{7,6},{8,9},{9,8},{10,11... | collective-permute-start | bytes 442376 | tf_op jit(solution)/shard_map/ppermute | solution.py:56
  638.6 15.1 %collective-permute-start.78 = (bf16[96,768]{1,0:T(8,128)(2,1)S(1)}, bf16[96,768]{1,0:T(8,128)(2,1)S(1)}, u32[]{:S(2)}, u32[]{:S(2)}) collective-permute-start(bf16[96,768]{1,0:T(8,128)(2,1)S(1)} %get-tuple-element.278), channel_id=1, source_target_pairs={{0,2},{1,3},{2,0},{3,1},{4,6},{5,7},{6,4},{7,5},{8,10},{9,11},{10,... | collective-permute-start | bytes 442376 | tf_op jit(solution)/shard_map/ppermute | solution.py:56
  641.3 12.4 %collective-permute-start.77 = (bf16[96,768]{1,0:T(8,128)(2,1)S(1)}, bf16[96,768]{1,0:T(8,128)(2,1)S(1)}, u32[]{:S(2)}, u32[]{:S(2)}) collective-permute-start(bf16[96,768]{1,0:T(8,128)(2,1)S(1)} %get-tuple-element.276), channel_id=1, source_target_pairs={{0,1},{1,0},{2,3},{3,2},{4,5},{5,4},{6,7},{7,6},{8,9},{9,8},{10,11... | collective-permute-start | bytes 442376 | tf_op jit(solution)/shard_map/ppermute | solution.py:56
  (176 other events, 2517.6 us)

commit v3 on v2

--- a/solution.py
+++ b/solution.py
@@ -21,7 +21,7 @@
 f32 = jnp.float32
 
 
-NEAR = 48 * 1024 * 1024
+NEAR = 60 * 1024 * 1024
 
 
 def product(first_operand, second_operand):
@@ -38,12 +38,6 @@
     return lax.dot_general(
         first_operand, second_operand, (((0,), (0,)), ((), ())), preferred_element_type=f32
     )
-
-
-def apply_update(weight, gradient, moment, average, rate):
-    moment = MOMENTUM * moment + gradient
-    updated = weight - rate * (gradient + MOMENTUM * moment)
-    return (updated, moment, AVERAGING * average + (1.0 - AVERAGING) * updated)
 
 
 def swap_dp(inputs, mask):
@@ -65,51 +59,64 @@
     pairs = []
     for d in range(count):
         for z in range(4):
-            hi, x, k = d // 4, (d // 2) % 2, d % 2
-            pairs.append((d * 4 + z, (hi * 4 + (z % 2) * 2 + z // 2) * 4 + 2 * k + x))
+            moved = (d % 2) ^ (z // 2)
+            pairs.append((d * 4 + z, (d ^ moved) * 4 + (z ^ (2 * moved))))
     return lax.ppermute(inputs, ("dp", "mp"), pairs)
+
+
+def pick(pieces):
+    odd = lax.axis_index("mp") % 2 == 1
+    return [jnp.where(odd, pieces[c ^ 1], pieces[c]) for c in range(4)]
 
 
 def gather_mp(inputs):
     return [inputs] + [swap_mp(inputs, s) for s in (1, 2, 3)]
 
 
+def trade_mp(pieces):
+    return (pieces[0],) + tuple(swap_mp(pieces[s], s) for s in (1, 2, 3))
+
+
 def scatter_mp(pieces):
+    return sum(p.astype(f32) for p in trade_mp(pieces))
+
+
+def spread_dp(inputs):
+    return [inputs] + [swap_dp(inputs, b) for b in range(2, lax.axis_size("dp"), 2)]
+
+
+def spread_core(pieces):
+    pieces = pieces + [swap_dp(p, 1) for p in pieces]
+    if pieces[0].shape[0] % 16:
+        pieces = [jnp.concatenate(pieces)]
+    return tuple(pieces)
+
+
+def halve_dp(near, far):
+    got = [swap_dp(f, 1) for f in far]
+    count = lax.axis_size("dp") // 2
+    rows = near[0].shape[0] // count
+    return [
+        jnp.concatenate(
+            [
+                n[i * rows : (i + 1) * rows].astype(f32) + g[i * rows : (i + 1) * rows].astype(f32)
+                for n, g in zip(near, got)
+            ],
+            axis=1,
+        ).astype(bf16)
+        for i in range(count)
+    ]
+
+
+def collect_dp(pieces):
     total = pieces[0].astype(f32)
-    for s in (1, 2, 3):
-        total = total + swap_mp(pieces[s], s).astype(f32)
+    for i, piece in enumerate(pieces[1:]):
+        total = total + swap_dp(piece, 2 * i + 2).astype(f32)
     return total
 
 
-def gather_dp(inputs, order):
-    pieces = {0: inputs}
-    rows = inputs.shape[0]
-    for bit in order:
-        keys = sorted(pieces)
-        sent = jnp.concatenate([pieces[k] for k in keys]) if len(keys) > 1 else inputs
-        got = swap_dp(sent, 1 << bit)
-        for i, k in enumerate(keys):
-            pieces[k ^ (1 << bit)] = got[i * rows : (i + 1) * rows]
-    near = jnp.concatenate([pieces[k] for k in sorted(pieces)])
-    return near, swap_dp(near, 1)
-
-
-def scatter_dp(near, far, order):
-    got = swap_dp(far, 1)
-    left = list(range(1, dp_bits()))
-    rows = near.shape[0] >> len(left)
-    columns = near.shape[1]
-    kind = far.dtype
-    for bit in order:
-        at = left.index(bit)
-        shape = (-1, 2, rows << at, columns)
-        mine, other = near.reshape(shape), got.reshape(shape)
-        away = (mine[:, 1].astype(f32) + other[:, 1].astype(f32)).astype(kind)
-        near = (mine[:, 0].astype(f32) + other[:, 0].astype(f32)).astype(kind)
-        near = near.reshape(-1, columns)
-        got = swap_dp(away.reshape(-1, columns), 1 << bit)
-        left.remove(bit)
-    return (near.astype(f32) + got.astype(f32)).astype(kind)
+def after(value, *events):
+    return lax.optimization_barrier((value,) + events)[0]
 
 
 def sum_dp(inputs):
@@ -118,50 +125,55 @@
     return inputs
 
 
-def sum_all(inputs):
-    inputs = sum_dp(inputs)
-    for mask in (1, 2):
-        inputs = inputs + swap_mp(inputs, mask)
-    return inputs
-
-
 def group_sum_features(inputs):
     count = lax.axis_size("dp")
     width = inputs.shape[1] // count
     order = [b for b in range(count) if b % 2 == 0] + [b for b in range(count) if b % 2]
-    for mask in (1, 2):
-        got = swap_dp(inputs, mask)
-        at = [order.index(b ^ mask) for b in order]
-        inputs = inputs + jnp.concatenate(
-            [got[:, p * width : (p + 1) * width] for p in at], axis=1
-        )
-    return inputs
-
-
-def call(body, grid, in_specs, out_specs, out_shape, operands, flops, scratch=(), alias=None):
+    at = [order.index(b ^ 1) for b in order]
+    got = swap_dp(inputs, 1)
+    inputs = inputs + jnp.concatenate([got[:, p * width : (p + 1) * width] for p in at], axis=1)
+    return inputs + swap_mp(inputs, 1)
+
+
+def call(
+    body, grid, in_specs, out_specs, out_shape, operands, flops, scratch=(), alias=None, events=()
+):
     moved = sum(o.size * o.dtype.itemsize for o in operands)
+    known, late = len(operands), len(operands) + len(events)
+
+    def run(*refs):
+        body(*refs[:known], *refs[late:])
+
     return pl.pallas_call(
-        body,
+        run,
         grid=grid,
-        in_specs=in_specs,
+        in_specs=list(in_specs) + [pl.BlockSpec(memory_space=pl.ANY)] * len(events),
         out_specs=out_specs,
         out_shape=out_shape,
         scratch_shapes=list(scratch),
         input_output_aliases=alias or {},
         compiler_params=pltpu.CompilerParams(vmem_limit_bytes=NEAR),
-        cost_estimate=pl.CostEstimate(flops=flops, bytes_accessed=moved, transcendentals=0),
-    )(*operands)
+        cost_estimate=pl.CostEstimate(flops=1000, bytes_accessed=1000, transcendentals=0),
+    )(*operands, *events)
 
 
 def whole(array):
     return pl.BlockSpec(array.shape, lambda *i, n=array.ndim: (0,) * n)
 
 
-def fetch(pairs, sems):
-    copies = [
-        pltpu.make_async_copy(source, target, sems.at[i])
-        for i, (source, target) in enumerate(pairs)
-    ]
+def fetch(pieces, targets, sems):
+    copies, at = [], 0
+    for piece in pieces:
+        rows = piece.shape[0]
+        for column, target in targets:
+            copies.append(
+                pltpu.make_async_copy(
+                    piece.at[:, column : column + target.shape[1]],
+                    target.at[at : at + rows],
+                    sems.at[len(copies)],
+                )
+            )
+        at += rows
     for copy in copies:
         copy.start()
     for copy in copies:
@@ -239,29 +251,25 @@
     )
 
 
-def embed_kernel(
-    patch_ref, order_ref, embed_ref, vec_ref, taps_ref, qk0, qk1, vo0, vo1,
-    sorted_ref, embedded_ref, normed_ref, query_ref, key_ref, value_ref, pool_ref,
-    qk_s, v_s, sems,
-):
+def embed_kernel(count, patch_ref, order_ref, taps_ref, *refs):
+    pieces = refs[:count]
+    (
+        sorted_ref, embedded_ref, normed_ref, query_ref, key_ref, value_ref, pool_ref,
+        vec_ref, head_ref, qk_s, v_s, small_s, sems,
+    ) = refs[count:]
     width = embedded_ref.shape[1]
-    half = width // 2
+    edge = small_s.shape[1] - 128
 
     @pl.when(pl.program_id(0) == 0)
     def _():
-        fetch(
-            [
-                (qk0, qk_s.at[:half]),
-                (qk1, qk_s.at[half:]),
-                (vo0.at[:, :width], v_s.at[:half]),
-                (vo1.at[:, :width], v_s.at[half:]),
-            ],
-            sems,
-        )
+        fetch(pieces, ((0, qk_s), (2 * width, v_s), (3 * width, small_s)), sems)
+        turned = small_s[:, edge:].astype(f32).T
+        vec_ref[...] = turned[0:8] + turned[8:16] + turned[16:24]
+        head_ref[...] = turned[24 : 24 + head_ref.shape[0]].astype(bf16)
 
     patch = contract_last(order_ref[...], patch_ref[0]).astype(bf16)
     sorted_ref[...] = patch
-    embedded = contract_last(patch, embed_ref[...]) + vec_ref[0:1]
+    embedded = contract_last(patch, small_s[:, : patch.shape[1]]) + vec_ref[0:1]
     embedded_ref[...] = embedded
     unit, _ = standard(embedded)
     normed = (unit * vec_ref[1:2] + vec_ref[2:3]).astype(bf16)
@@ -277,36 +285,45 @@
         pool_ref[0, ch] = pooled.astype(bf16)
 
 
-def embed(patches_t, order, embed_t, vec, taps, qk, vo):
+def embed(patches_t, order, taps, weights, classes, events=()):
     _, patch, rows = patches_t.shape
-    width = vec.shape[1]
+    width = taps.shape[2]
     total = MICRO * rows
+    edge = weights[0].shape[1] - 3 * width
 
     def tile(columns):
         return pl.BlockSpec((rows, columns), lambda i: (i, 0))
 
-    anywhere = pl.BlockSpec(memory_space=pl.ANY)
     return call(
-        embed_kernel,
+        functools.partial(embed_kernel, len(weights)),
         (MICRO,),
-        [pl.BlockSpec((1, patch, rows), lambda i: (i, 0, 0))]
-        + [whole(a) for a in (order, embed_t, vec, taps)]
-        + [anywhere] * 4,
+        [pl.BlockSpec((1, patch, rows), lambda i: (i, 0, 0)), whole(order), whole(taps)]
+        + [pl.BlockSpec(memory_space=pl.ANY)] * len(weights),
         [tile(patch), tile(width), tile(width), tile(width), tile(width), tile(width)]
-        + [pl.BlockSpec((1, 2, rows // 4, width), lambda i: (i, 0, 0, 0))],
+        + [
+            pl.BlockSpec((1, 2, rows // 4, width), lambda i: (i, 0, 0, 0)),
+            pl.BlockSpec((8, width), lambda i: (0, 0)),
+            pl.BlockSpec((classes, width), lambda i: (0, 0)),
+        ],
         [
             jax.ShapeDtypeStruct((total, patch), bf16),
             jax.ShapeDtypeStruct((total, width), f32),
         ]
         + [jax.ShapeDtypeStruct((total, width), bf16)] * 4
-        + [jax.ShapeDtypeStruct((MICRO, 2, rows // 4, width), bf16)],
-        (patches_t, order, embed_t, vec, taps) + qk + vo,
+        + [
+            jax.ShapeDtypeStruct((MICRO, 2, rows // 4, width), bf16),
+            jax.ShapeDtypeStruct((8, width), f32),
+            jax.ShapeDtypeStruct((classes, width), bf16),
+        ],
+        (patches_t, order, taps) + weights,
         2 * total * width * (patch + 3 * width),
         scratch=[
             pltpu.VMEM((width, 2 * width), bf16),
             pltpu.VMEM((width, width), bf16),
-            pltpu.SemaphoreType.DMA((4,)),
-        ],
+            pltpu.VMEM((width, edge), bf16),
+            pltpu.SemaphoreType.DMA((3 * len(weights),)),
+        ],
+        events=events,
     )
 
 
@@ -354,7 +371,7 @@
     ]
 
 
-def attend(micro, query, taps, bias, now, newer, older, before):
+def attend(micro, query, taps, bias, now, newer, older, before, events=()):
     rows = query.shape[0] // MICRO
     width = query.shape[1]
     count = bias.shape[2]
@@ -391,6 +408,7 @@
         operands,
         4 * rows * count * width * 4,
         alias=alias,
+        events=events,
     )
 
 
@@ -450,7 +468,7 @@
         taps_ref[ch, 1:2] = second
 
 
-def attend_back(micro, query, keys, values, probs, grad, newer, older, before):
+def attend_back(micro, query, keys, values, probs, grad, newer, older, before, events=()):
     heads, rows, count = probs.shape
     width = query.shape[1]
     quads = heads // QUAD
@@ -491,6 +509,7 @@
         operands,
         8 * rows * count * width * 4,
         alias=alias,
+        events=events,
     )
 
 
@@ -514,27 +533,26 @@
     return inputs * share, share + inputs * bell * 0.3989422804014327
 
 
-def mlp_kernel(
-    attended_ref, embedded_ref, vec_ref, select_ref, vo0, vo1, wb0, wb1, wh0, wh1,
-    first_ref, normed_ref, active_ref, slope_ref, second_ref, feature_ref,
-    wo_s, wb_s, wh_s, sems,
-):
+def mlp_weights(width, units, count):
+    return [
+        pltpu.VMEM((width, width), bf16),
+        pltpu.VMEM((width, units), bf16),
+        pltpu.VMEM((width, units), bf16),
+        pltpu.SemaphoreType.DMA((3 * count,)),
+    ]
+
+
+def mlp_kernel(count, attended_ref, embedded_ref, vec_ref, select_ref, *refs):
+    (
+        first_ref, normed_ref, active_ref, slope_ref, second_ref, feature_ref,
+        wo_s, wb_s, wh_s, sems,
+    ) = refs[count:]
     width = embedded_ref.shape[1]
-    half = width // 2
 
     @pl.when(pl.program_id(0) == 0)
     def _():
-        fetch(
-            [
-                (vo0.at[:, width:], wo_s.at[:half]),
-                (vo1.at[:, width:], wo_s.at[half:]),
-                (wh0, wh_s.at[:half]),
-                (wh1, wh_s.at[half:]),
-                (wb0, wb_s.at[:half]),
-                (wb1, wb_s.at[half:]),
-            ],
-            sems,
-        )
+        units = wb_s.shape[1]
+        fetch(refs[:count], ((0, wb_s), (units, wh_s), (2 * units, wo_s)), sems)
 
     first = embedded_ref[...] + contract_last(attended_ref[...], wo_s[...])
     first_ref[...] = first
@@ -558,17 +576,17 @@
     )
 
 
-def mlp(attended, embedded, vec, select, vo, wb, wh):
+def mlp(attended, embedded, vec, select, weights, events=()):
     total, width = embedded.shape
     rows = total // MICRO
-    units = wb[0].shape[1]
+    units = (weights[0].shape[1] - width) // 2
     boxes = select.shape[1]
 
     def tile(columns):
         return pl.BlockSpec((rows, columns), lambda i: (i, 0))
 
     return call(
-        mlp_kernel,
+        functools.partial(mlp_kernel, len(weights)),
         (MICRO,),
         [
             tile(width),
@@ -576,7 +594,7 @@
             whole(vec),
             pl.BlockSpec((1, boxes, rows), lambda i: (i, 0, 0)),
         ]
-        + [pl.BlockSpec(memory_space=pl.ANY)] * 6,
+        + [pl.BlockSpec(memory_space=pl.ANY)] * len(weights),
         [tile(width), tile(width), tile(units), tile(units), tile(width)]
         + [pl.BlockSpec((1, boxes, width), lambda i: (i, 0, 0))],
         [
@@ -587,39 +605,27 @@
             jax.ShapeDtypeStruct((total, width), f32),
             jax.ShapeDtypeStruct((MICRO, boxes, width), f32),
         ],
-        (attended, embedded, vec, select) + vo + wb + wh,
+        (attended, embedded, vec, select) + weights,
         2 * total * width * (width + 2 * units),
-        scratch=[
-            pltpu.VMEM((width, width), bf16),
-            pltpu.VMEM((width, units), bf16),
-            pltpu.VMEM((width, units), bf16),
-            pltpu.SemaphoreType.DMA((6,)),
-        ],
+        scratch=mlp_weights(width, units, len(weights)),
+        events=events,
     )
 
 
 def mlp_back_kernel(
-    pull_ref, select_ref, second_ref, first_ref, slope_ref, vec_ref, vo0, vo1, wb0, wb1, wh0, wh1,
-    branch_ref, hidden_ref, attn_ref, first_grad_ref, attended_ref, sums_ref,
-    wo_s, wb_s, wh_s, sems,
+    count, pull_ref, select_ref, second_ref, first_ref, slope_ref, vec_ref, *refs
 ):
+    (
+        branch_ref, hidden_ref, attn_ref, first_grad_ref, attended_ref, sums_ref,
+        wo_s, wb_s, wh_s, sems,
+    ) = refs[count:]
     width = second_ref.shape[1]
-    half = width // 2
 
     @pl.when(pl.program_id(0) == 0)
     def _():
         sums_ref[...] = jnp.zeros_like(sums_ref)
-        fetch(
-            [
-                (vo0.at[:, width:], wo_s.at[:half]),
-                (vo1.at[:, width:], wo_s.at[half:]),
-                (wh0, wh_s.at[:half]),
-                (wh1, wh_s.at[half:]),
-                (wb0, wb_s.at[:half]),
-                (wb1, wb_s.at[half:]),
-            ],
-            sems,
-        )
+        units = wb_s.shape[1]
+        fetch(refs[:count], ((0, wb_s), (units, wh_s), (2 * units, wo_s)), sems)
 
     pull = lax.dot_general(
         select_ref[0],
@@ -651,17 +657,17 @@
     attended_ref[...] = product(attn, wo_s[...]).astype(bf16)
 
 
-def mlp_back(pull, select, second, first, slope, vec, vo, wb, wh):
+def mlp_back(pull, select, second, first, slope, vec, weights, events=()):
     total, width = second.shape
     rows = total // MICRO
-    units = wb[0].shape[1]
+    units = (weights[0].shape[1] - width) // 2
     boxes = select.shape[1]
 
     def tile(columns):
         return pl.BlockSpec((rows, columns), lambda i: (i, 0))
 
     return call(
-        mlp_back_kernel,
+        functools.partial(mlp_back_kernel, len(weights)),
         (MICRO,),
         [
             pl.BlockSpec((1, boxes, width), lambda i: (i, 0, 0)),
@@ -671,7 +677,7 @@
             tile(units),
             whole(vec),
         ]
-        + [pl.BlockSpec(memory_space=pl.ANY)] * 6,
+        + [pl.BlockSpec(memory_space=pl.ANY)] * len(weights),
         [tile(width), tile(units), tile(width), tile(width), tile(width)]
         + [pl.BlockSpec((8, width), lambda i: (0, 0))],
         [
@@ -682,39 +688,24 @@
             jax.ShapeDtypeStruct((total, width), bf16),
             jax.ShapeDtypeStruct((8, width), f32),
         ],
-        (pull, select, second, first, slope, vec) + vo + wb + wh,
+        (pull, select, second, first, slope, vec) + weights,
         2 * total * width * (width + 2 * units),
-        scratch=[
-            pltpu.VMEM((width, width), bf16),
-            pltpu.VMEM((width, units), bf16),
-            pltpu.VMEM((width, units), bf16),
-            pltpu.SemaphoreType.DMA((6,)),
-        ],
+        scratch=mlp_weights(width, units, len(weights)),
+        events=events,
     )
 
 
 def embed_back_kernel(
-    dq_ref, pool_ref, key_ref, value_ref, taps_ref, embedded_ref, first_ref, vec_ref,
-    qk0, qk1, vo0, vo1,
-    projected_ref, grad_ref, sums_ref, taps_out,
-    qk_s, v_s, sems,
+    count, dq_ref, pool_ref, key_ref, value_ref, taps_ref, embedded_ref, first_ref, vec_ref, *refs
 ):
+    projected_ref, grad_ref, sums_ref, taps_out, qk_s, v_s, sems = refs[count:]
     width = embedded_ref.shape[1]
-    half = width // 2
 
     @pl.when(pl.program_id(0) == 0)
     def _():
         sums_ref[...] = jnp.zeros_like(sums_ref)
         taps_out[...] = jnp.zeros_like(taps_out)
-        fetch(
-            [
-                (qk0, qk_s.at[:half]),
-                (qk1, qk_s.at[half:]),
-                (vo0.at[:, :width], v_s.at[:half]),
-                (vo1.at[:, :width], v_s.at[half:]),
-            ],
-            sems,
-        )
+        fetch(refs[:count], ((0, qk_s), (2 * width, v_s)), sems)
 
     projected_ref[:, :width] = dq_ref[...]
     rows = pool_ref.shape[2]
@@ -737,7 +728,7 @@
     sums_ref[0:1] += jnp.sum(grad.astype(f32), axis=0, keepdims=True)
 
 
-def embed_back(dq, pool, keys, values, taps, embedded, first_grad, vec, qk, vo):
+def embed_back(dq, pool, keys, values, taps, embedded, first_grad, vec, weights, events=()):
     total, width = embedded.shape
     rows = total // MICRO
 
@@ -745,7 +736,7 @@
         return pl.BlockSpec((rows, columns), lambda i: (i, 0))
 
     return call(
-        embed_back_kernel,
+        functools.partial(embed_back_kernel, len(weights)),
         (MICRO,),
         [
             tile(width),
@@ -757,7 +748,7 @@
             tile(width),
             whole(vec),
         ]
-        + [pl.BlockSpec(memory_space=pl.ANY)] * 4,
+        + [pl.BlockSpec(memory_space=pl.ANY)] * len(weights),
         [
             tile(3 * width),
             tile(width),
@@ -770,13 +761,89 @@
             jax.ShapeDtypeStruct((8, width), f32),
             jax.ShapeDtypeStruct((8, width), f32),
         ],
-        (dq, pool, keys, values, taps, embedded, first_grad, vec) + qk + vo,
+        (dq, pool, keys, values, taps, embedded, first_grad, vec) + weights,
         2 * total * width * 3 * width,
         scratch=[
             pltpu.VMEM((width, 2 * width), bf16),
             pltpu.VMEM((width, width), bf16),
-            pltpu.SemaphoreType.DMA((4,)),
-        ],
+            pltpu.SemaphoreType.DMA((2 * len(weights),)),
+        ],
+        events=events,
+    )
+
+
+def squares_kernel(count, *refs):
+    grads = refs[:count]
+    names = refs[count:]
+    rest_ref, share_ref, place_ref = names[:3]
+    attn_out, small_out, total_out = names[3:]
+    attn = grads[0][...].astype(f32)
+    small = grads[count // 2][...].astype(f32)
+    for i in range(1, count // 2):
+        attn = attn + grads[i][...].astype(f32)
+        small = small + grads[count // 2 + i][...].astype(f32)
+    attn_out[...] = attn
+    small_out[...] = small
+    share = share_ref[...] * place_ref[...]
+    total = (
+        jnp.sum(attn * attn)
+        + jnp.sum(small * small)
+        + jnp.sum(rest_ref[...] * rest_ref[...])
+        + jnp.sum(share * share_ref[...])
+    )
+    total_out[...] = jnp.zeros_like(total_out) + total
+
+
+def squares_of(attn, small, rest, share, place):
+    operands = attn + small + (rest, share, place)
+    return call(
+        functools.partial(squares_kernel, len(attn) + len(small)),
+        (1,),
+        [whole(o) for o in operands],
+        [whole(attn[0]), whole(small[0]), pl.BlockSpec((8, 128), lambda i: (0, 0))],
+        [
+            jax.ShapeDtypeStruct(attn[0].shape, f32),
+            jax.ShapeDtypeStruct(small[0].shape, f32),
+            jax.ShapeDtypeStruct((8, 128), f32),
+        ],
+        operands,
+        0,
+    )
+
+
+def update_kernel(rates, one_ref, two_ref, boxes_ref, *refs):
+    count = len(rates)
+    grads, weights, moments, averages = (refs[i * count : (i + 1) * count] for i in range(4))
+    outs = refs[4 * count :]
+    boxes = boxes_ref[0:1, 0:1]
+    norm = jnp.sqrt(one_ref[0:1, 0:1] + two_ref[0:1, 0:1]) / boxes
+    outs[0][...] = norm
+    scaling = jnp.minimum(1.0, THRESHOLD / norm) / boxes
+    for i, rate in enumerate(rates):
+        factor = scaling if weights[i].ndim == 2 else scaling[None]
+        grad = grads[i][...] * factor
+        moment = MOMENTUM * moments[i][...] + grad
+        updated = weights[i][...] - rate * (grad + MOMENTUM * moment)
+        outs[1 + i][...] = updated
+        outs[1 + count + i][...] = moment
+        outs[1 + 2 * count + i][...] = AVERAGING * averages[i][...] + (1.0 - AVERAGING) * updated
+        if i < 2:
+            outs[1 + 3 * count + i][...] = updated.astype(bf16)
+
+
+def update(one, two, boxes, grads, weights, moments, averages, rates):
+    operands = (one, two, boxes) + grads + weights + moments + averages
+    kept = [jax.ShapeDtypeStruct(w.shape, f32) for w in weights]
+    shapes = [jax.ShapeDtypeStruct((1, 1), f32)] + kept * 3
+    shapes = shapes + [jax.ShapeDtypeStruct(w.shape, bf16) for w in weights[:2]]
+    return call(
+        functools.partial(update_kernel, rates),
+        (1,),
+        [whole(o) for o in operands],
+        [pl.BlockSpec(o.shape, lambda i, n=len(o.shape): (0,) * n) for o in shapes],
+        shapes,
+        operands,
+        0,
     )
 
 
@@ -816,7 +883,8 @@
     dp_index = lax.axis_index("dp")
     mp_index = lax.axis_index("mp")
     dp_count = lax.axis_size("dp")
-    across, core = (dp_index // 2) % 2, dp_index % 2
+    across, core = mp_index % 2, dp_index % 2
+    upper = mp_index - across
     quarter = 2 * core + across
     rows = patches.shape[1]
     eighth = rows // 8
@@ -831,8 +899,6 @@
     own_heads = position_bias.shape[0]
     heads = own_heads * 4
     hidden_cols = up_weight.shape[1] - 3 * head_cols
-    up_bits = list(range(1, dp_bits()))
-    down_bits = up_bits[::-1]
 
     ints = jnp.concatenate(
         [clip_len.reshape(-1), box_count.reshape(-1), box_bounds.reshape(-1), box_labels.reshape(-1)]
@@ -840,59 +906,64 @@
     total_ints = ints.shape[0]
     ints = jnp.pad(ints, (0, -total_ints % 1024)).reshape(-1, 128)
     ints = regroup(ints).reshape(-1)
-    patches_t = regroup(patches.transpose(0, 2, 1))
-    memory_t = regroup(memory.transpose(0, 1, 3, 2))
     lengths_all = ints[:5]
     counts = ints[5:8]
     bounds = ints[8 : 8 + MICRO * boxes * 2].reshape(MICRO, boxes, 2)
     labels = ints[8 + MICRO * boxes * 2 : total_ints].reshape(MICRO * boxes, classes)
 
-    vec_hi = lax.reduce_precision(vector_weight, 8, 7)
-    vec_mid = lax.reduce_precision(vector_weight - vec_hi, 8, 7)
-    vec_lo = vector_weight - vec_hi - vec_mid
-    small = jnp.concatenate(
-        [embed_weight, head_weight, vec_hi, vec_mid, vec_lo], axis=0
-    ).astype(bf16).T
-    small = jnp.concatenate(gather_mp(small), axis=0)
-    place = jnp.arange(4 * sub)
-    small = product(
-        one_hot_rows(((place // sub) ^ mp_index) * sub + place % sub, 4 * sub), small
-    ).astype(bf16)
-    small = jnp.concatenate(gather_dp(small, up_bits))
-    embed_t = small[:, :patch]
-    head_t = small[:, patch : patch + classes]
-    vec3 = small[:, patch + classes :].astype(f32)
-    vectors = (vec3[:, :7] + vec3[:, 7:14] + vec3[:, 14:]).T
-    vectors = jnp.pad(vectors, ((0, 1), (0, 0)))
-
+    def in_three(array):
+        high = lax.reduce_precision(array, 8, 7)
+        middle = lax.reduce_precision(array - high, 8, 7)
+        return [high, middle, array - high - middle]
+
+    edge = patch + (-patch % 128)
+    columns_in = [jnp.pad(embed_weight, ((0, edge - patch), (0, 0)))]
+    columns_in += [jnp.pad(v, ((0, 1), (0, 0))) for v in in_three(vector_weight)]
+    columns_in += [jnp.pad(head_weight, ((0, 128 - 24 - classes), (0, 0)))]
     taps_pos = jnp.concatenate(
         [
             conv_weight.reshape(12, head_cols),
             jnp.pad(position_bias.reshape(1, -1), ((0, 0), (0, head_cols - position_bias.size))),
         ]
     )
-    taps_pos = gather_mp(taps_pos)
-    conv_all = jnp.concatenate([t[:12] for t in taps_pos], axis=1).reshape(2, 6, width)
-    rel_bias = jnp.concatenate(
-        [t[12, : position_bias.size].reshape(position_bias.shape) for t in taps_pos], axis=0
-    )
-
+    taps_pos = jnp.concatenate(in_three(taps_pos)).reshape(sub, -1)
+    small = jnp.concatenate([jnp.concatenate(columns_in).T, taps_pos], axis=1).astype(bf16)
     up_low = up_weight.astype(bf16)
     down_low = down_weight.astype(bf16)
+    pieces = gather_mp(up_low[:, : 3 * head_cols])
+    small = gather_mp(small)
+    place = jnp.arange(4 * sub)
+    small_mine = product(
+        one_hot_rows(((place // sub) ^ mp_index) * sub + place % sub, 4 * sub),
+        jnp.concatenate([p[:, : edge + 128] for p in small]),
+    ).astype(bf16)
+    taps_pos = jnp.stack(pick([p[:, edge + 128 :] for p in small])).reshape(4, 3, 13, head_cols)
+    taps_pos = jnp.sum(taps_pos.astype(f32), axis=1)
+    conv_all = taps_pos[:, :12].transpose(1, 0, 2).reshape(2, 6, width)
+    rel_bias = taps_pos[:, 12, : position_bias.size].reshape(heads, 3)
+    weights = jnp.concatenate(
+        [p[:, j * head_cols : (j + 1) * head_cols] for j in range(3) for p in pick(pieces)]
+        + [small_mine],
+        axis=1,
+    )
+    weights = spread_core(spread_dp(weights))
+    q_pieces = pieces
     pieces = gather_mp(
-        jnp.concatenate([up_low[:, : 3 * head_cols], down_low[:, :head_cols]], axis=1)
-    )
-
-    def columns(first, last):
-        return jnp.concatenate(
-            [p[:, j * head_cols : (j + 1) * head_cols] for j in range(first, last) for p in pieces],
+        after(
+            jnp.concatenate([down_low, up_low[:, 3 * head_cols :]], axis=1), *pieces, *small
+        )
+    )
+    patches_t = regroup(after(patches.transpose(0, 2, 1), *q_pieces, *small))
+    pieces = [after(p, *weights, patches_t) for p in pieces]
+    edges = (head_cols, head_cols + hidden_cols, head_cols + 2 * hidden_cols)
+    rest = spread_dp(
+        jnp.concatenate(
+            [p[:, edges[0] : edges[1]] for p in pieces]
+            + [p[:, edges[1] :] for p in pieces]
+            + pick([p[:, : edges[0]] for p in pieces]),
             axis=1,
         )
-
-    w_qk = gather_dp(columns(0, 2), up_bits)
-    w_vo = gather_dp(columns(2, 4), down_bits)
-    w_back = gather_dp(jnp.concatenate(gather_mp(down_low[:, head_cols:]), axis=1), up_bits)
-    w_hidden = gather_dp(jnp.concatenate(gather_mp(up_low[:, 3 * head_cols :]), axis=1), down_bits)
+    )
 
     place = jnp.arange(rows)
     token = 8 * (place % eighth) + 4 * ((place // eighth) % 2) + place // (2 * eighth)
@@ -901,12 +972,30 @@
     half_mem = mem_rows // 2
     mem_place = jnp.arange(mem_rows)
     mem_order = one_hot_rows(2 * (mem_place % half_mem) + mem_place // half_mem, mem_rows)
-    mem_two = swap_dp(memory_t, 2)
+    (
+        patches_in,
+        embedded,
+        normed,
+        query,
+        raw_keys,
+        raw_values,
+        pools,
+        vectors,
+        head_low,
+    ) = embed(patches_t, token_order, conv_all, weights, classes)
+    stored = []
+    for m in range(MICRO):
+        one = swap_dp(pools[m : m + 1], 1)
+        two = swap_mp(pools[m : m + 1], 1)
+        three = swap_dp(two, 1)
+        stored.append([(pools, m), (one, 0), (two, 0), (three, 0)])
+    memory_t = regroup(after(memory.transpose(0, 1, 3, 2), patches_t))
+    mem_two = swap_mp(memory_t, 1)
     mem_parts = (memory_t, swap_dp(memory_t, 1), mem_two, swap_dp(mem_two, 1))
     mem_full = memory_in(
         jnp.stack(
             [
-                (((c ^ mp_index) // 2) ^ core) + 2 * (((c ^ mp_index) % 2) ^ across)
+                (((c ^ upper) // 2) ^ core) + 2 * (((c ^ upper) % 2) ^ across)
                 for c in range(4)
             ]
         ),
@@ -914,15 +1003,7 @@
         mem_parts,
     )
 
-    patches_in, embedded, normed, query, raw_keys, raw_values, pools = embed(
-        patches_t, token_order, embed_t, vectors, conv_all, w_qk, w_vo
-    )
-    stored = [[(mem_full, 0)], [(mem_full, 1)]]
-    for m in range(MICRO):
-        one = swap_dp(pools[m : m + 1], 1)
-        two = swap_dp(pools[m : m + 1], 2)
-        three = swap_dp(two, 1)
-        stored.append([(pools, m), (one, 0), (two, 0), (three, 0)])
+    stored = [[(mem_full, 0)], [(mem_full, 1)]] + stored
 
     part_quarter = [2 * (core ^ (s % 2)) + (across ^ (s // 2)) for s in range(4)]
     pool_place = jnp.arange(pooled)
@@ -945,12 +1026,13 @@
             axis=1,
         ).reshape(heads // QUAD, QUAD, -1)
 
-    attended, saved = None, []
-    for m in range(MICRO):
+    attended, saved = None, {}
+    for m in (2, 1, 0):
         attended, probs, keys, values = attend(
             m, query, conv_all, key_bias(m), stored[m + 2], stored[m + 1], stored[m], attended
         )
-        saved.append((keys, values, probs))
+        saved[m] = (keys, values, probs)
+    rest = spread_core([after(p, attended) for p in rest])
 
     position = quarter * rows + token
     within = position % FRAME
@@ -964,11 +1046,25 @@
         f32
     )
     select = inside.astype(f32) / denominator[:, :, None]
+    target_row = jnp.arange(4 * pooled)
+    target_quarter, target_rest = target_row // pooled, target_row % pooled
+    source_row = (
+        (((target_quarter // 2) ^ core) + 2 * ((target_quarter % 2) ^ across)) * pooled
+        + (target_rest % 2) * half_pool
+        + target_rest // 2
+    )
+    new_memory = memory_out(
+        (quarter ^ upper)[None],
+        one_hot_rows(source_row, 4 * pooled).T,
+        stored[3] + stored[4],
+    )
     first_res, normed_mlp, active, slope, second_res, feature = mlp(
-        attended, embedded, vectors, select, w_vo, w_back, w_hidden
-    )
-    feature = group_sum_features(feature.reshape(MICRO * boxes, width)).astype(bf16)
-    logits = product(feature, head_t)
+        attended, embedded, vectors, select, rest, events=(new_memory,)
+    )
+    new_memory = regroup(new_memory)
+    feature = after(feature.reshape(MICRO * boxes, width), new_memory)
+    feature = group_sum_features(feature).astype(bf16)
+    logits = contract_last(feature, head_low)
     target = labels.astype(f32)
     keep = (jnp.arange(boxes)[None, :] < counts[:, None]).astype(f32).reshape(-1, 1)
     lead = (quarter == 0).astype(f32)
@@ -976,33 +1072,34 @@
     grad_logits = ((jax.nn.sigmoid(logits) - target) * keep).astype(bf16)
 
     grad_head = contract_rows(feature, grad_logits) * lead
-    grad_feature = contract_last(grad_logits, head_t).reshape(MICRO, boxes, width)
+    grad_feature = product(grad_logits, head_low).reshape(MICRO, boxes, width)
     grad_branch, grad_hidden, grad_attn, grad_first, grad_attended, sums = mlp_back(
-        grad_feature, select, second_res, first_res, slope, vectors, w_vo, w_back, w_hidden
+        grad_feature, select, second_res, first_res, slope, vectors, rest
     )
     half = width // 2
 
-    def weight_grad(left, right):
-        return tuple(
-            contract_rows(left[:, at : at + half], right).astype(bf16) for at in (0, half)
-        )
-
-    back_grad = scatter_dp(*weight_grad(grad_branch, active), down_bits)
-    hidden_grad = scatter_dp(*weight_grad(normed_mlp, grad_hidden), up_bits)
-    out_grad = weight_grad(grad_attn, attended)
+    def weight_grad(left, right, at):
+        return contract_rows(left[:, at : at + half], right).astype(bf16)
+
+    sides = ((grad_branch, active), (normed_mlp, grad_hidden), (grad_attn, attended))
+    rest_far = [weight_grad(*side, half) for side in sides]
+    rest_near = [weight_grad(*side, 0) for side in sides]
+    rest_pieces = halve_dp(rest_near, rest_far)
 
     dq, pool_grads, bias_grad, mem_taps = None, [], 0.0, 0.0
+    events = tuple(rest_pieces)
     for m in range(MICRO):
         keys, values, probs = saved[m]
         dq, kept, sent, taps_part, bias_part = attend_back(
-            m, query, keys, values, probs, grad_attended, stored[m + 1], stored[m], dq
+            m, query, keys, values, probs, grad_attended, stored[m + 1], stored[m], dq, events
         )
         got = swap_dp(sent, 1)
         away = (kept[:, 1].astype(f32) + got[:, 1].astype(f32)).astype(bf16)
         mine = kept[:, 0].astype(f32) + got[:, 0].astype(f32)
-        pool_grads.append(mine + swap_dp(away, 2).astype(f32))
+        pool_grads.append(mine + swap_mp(away, 1).astype(f32))
         bias_grad = bias_grad + bias_part
         mem_taps = mem_taps + taps_part
+        events = (away,)
     projected_grad, embedded_grad, embed_sums, taps_grad = embed_back(
         dq,
         jnp.stack(pool_grads),
@@ -1012,56 +1109,78 @@
         embedded,
         grad_first,
         vectors,
-        w_qk,
-        w_vo,
-    )
-    qk_grad = scatter_dp(*weight_grad(normed, projected_grad[:, : 2 * width]), up_bits)
-    v_grad = weight_grad(normed, projected_grad[:, 2 * width :])
-    vo_grad = scatter_dp(
-        *(jnp.concatenate([a, b], axis=1) for a, b in zip(v_grad, out_grad)), down_bits
-    )
-    grad_embed = contract_rows(embedded_grad, patches_in)
+        weights,
+    )
+    rest_total = collect_dp(rest_pieces)
     grad_vectors = jnp.concatenate([embed_sums[:3], sums[:4]])
 
-    small_grad = jnp.concatenate([grad_embed, grad_head, grad_vectors.T], axis=1)
-    small_grad = scatter_dp(small_grad[:half], small_grad[half:], up_bits)
-    small_grad = scatter_mp(
-        [
-            lax.dynamic_slice_in_dim(small_grad, (mp_index ^ s) * sub, sub, axis=0)
+    def small_grad(at):
+        return jnp.concatenate(
+            [
+                contract_rows(embedded_grad[:, at : at + half], patches_in),
+                grad_head[at : at + half],
+                grad_vectors[:, at : at + half].T,
+            ],
+            axis=1,
+        ).astype(bf16)
+
+    attn_far = [small_grad(half), weight_grad(normed, projected_grad, half)]
+    attn_near = [small_grad(0), weight_grad(normed, projected_grad, 0)]
+    rest_total = after(rest_total, *attn_far)
+    units = 4 * hidden_cols
+    rest_pieces = []
+    out_blocks = pick(
+        [
+            rest_total[:, 2 * units + c * head_cols : 2 * units + (c + 1) * head_cols]
+            for c in range(4)
+        ]
+    )
+    for s in range(4):
+        piece = jnp.concatenate(
+            [
+                out_blocks[s],
+                rest_total[:, s * hidden_cols : (s + 1) * hidden_cols],
+                rest_total[:, units + s * hidden_cols : units + (s + 1) * hidden_cols],
+            ],
+            axis=1,
+        )
+        rest_pieces.append(piece if s == 0 else piece.astype(bf16))
+    rest_mine = scatter_mp(rest_pieces)
+    attn_total = collect_dp(halve_dp(attn_near, attn_far))
+    small_size = patch + classes + 7
+    small_total = attn_total[:, :small_size].astype(bf16)
+    small_parts = trade_mp(
+        [
+            lax.dynamic_slice_in_dim(small_total, (mp_index ^ s) * sub, sub, axis=0)
             for s in range(4)
         ]
-    ).T
-    embed_grad = small_grad[:patch]
-    head_grad = small_grad[patch : patch + classes]
-    vector_grad = small_grad[patch + classes :]
-
-    def pieces_of(array, count):
-        return [array[:, s * count : (s + 1) * count] for s in range(4)]
-
-    back_mine = scatter_mp(pieces_of(back_grad, hidden_cols))
-    hidden_mine = scatter_mp(pieces_of(hidden_grad, hidden_cols))
-    attn_mine = scatter_mp(
-        [
-            jnp.concatenate(
-                [
-                    part[:, (4 * i + s) * head_cols : (4 * i + s + 1) * head_cols]
-                    for part in (qk_grad, vo_grad)
-                    for i in range(2)
-                ],
-                axis=1,
-            )
-            for s in range(4)
-        ]
-    )
-    down_grad = jnp.concatenate([attn_mine[:, 3 * head_cols :], back_mine], axis=1)
-    up_grad = jnp.concatenate([attn_mine[:, : 3 * head_cols], hidden_mine], axis=1)
+    )
+    attn_parts = trade_mp(
+        pick(
+            [
+                jnp.concatenate(
+                    [
+                        attn_total[
+                            :,
+                            small_size + (4 * j + c) * head_cols : small_size
+                            + (4 * j + c + 1) * head_cols,
+                        ]
+                        for j in range(3)
+                    ],
+                    axis=1,
+                ).astype(bf16)
+                for c in range(4)
+            ]
+        )
+    )
 
     count_local = jnp.sum(box_count).astype(f32) * (mp_index == 0).astype(f32)
     taps_rows = jnp.stack(
         [
             jnp.concatenate([taps_grad[4 * ch : 4 * ch + 4], mem_taps[ch]], axis=0)
             for ch in range(2)
-        ]
+        ],
+        axis=1,
     ).reshape(12, 4, head_cols)
     scalars = jnp.stack([loss_part, count_local])
     last = jnp.concatenate(
@@ -1074,20 +1193,31 @@
     last = jnp.pad(last, ((0, 0), (0, head_cols - last.shape[1])))
     flat = jnp.concatenate([taps_rows, last[None]]).transpose(1, 0, 2)
     flat = sum_dp(flat)
-    flat = scatter_mp([flat[s] for s in range(4)])
-    conv_grad = flat[:12].reshape(2, 6, head_cols)
-    position_grad = flat[12, : own_heads * 3].reshape(own_heads, 3)
+    flat = scatter_mp(pick([flat[c] for c in range(4)]))
     loss_global = flat[12, own_heads * 3]
     box_total = flat[12, own_heads * 3 + 1]
-
-    reduced = (up_grad, down_grad, embed_grad, head_grad, vector_grad, conv_grad, position_grad)
-    squares = sum((jnp.sum(gradient * gradient) for gradient in reduced[:5]))
-    squares = squares + (
-        jnp.sum(conv_grad * conv_grad) + jnp.sum(position_grad * position_grad)
-    ) / dp_count
-    square_total = sum_all(jnp.full((8, 128), squares, f32))[0, 0]
-    grad_norm = jnp.sqrt(square_total) / box_total
-    scaling = jnp.minimum(1.0, THRESHOLD / grad_norm) / box_total
+    spot_row = jnp.arange(13)[:, None]
+    spot_column = jnp.arange(head_cols)[None, :]
+    counted = ((spot_row < 12) | (spot_column < own_heads * 3)).astype(f32) / dp_count
+    attn_mine, small_mine, squares = squares_of(attn_parts, small_parts, rest_mine, flat, counted)
+    for bit in range(dp_bits()):
+        squares = squares + swap_dp(squares, 1 << bit)
+    squares = squares + swap_mp(squares, 1)
+    squares_two = swap_mp(squares, 2)
+
+    def turned(arrays):
+        up, down, embed_part, head, vector, conv, position = arrays
+        return (up, down, embed_part.T, head.T, vector, conv.transpose(1, 0, 2), position)
+
+    grads = (
+        jnp.concatenate([attn_mine, rest_mine[:, head_cols + hidden_cols :]], axis=1),
+        rest_mine[:, : head_cols + hidden_cols],
+        small_mine[:, :patch],
+        small_mine[:, patch : patch + classes],
+        small_mine[:, patch + classes :].T,
+        flat[:12].reshape(6, 2, head_cols),
+        flat[12, : own_heads * 3].reshape(own_heads, 3),
+    )
     masters = (
         up_weight,
         down_weight,
@@ -1116,32 +1246,23 @@
         position_average,
     )
     rates = (LEARNING,) * 4 + (VECTOR_LEARNING,) * 3
-    results = [
-        apply_update(weight, gradient * scaling, moment, average, rate)
-        for weight, gradient, moment, average, rate in zip(
-            masters, reduced, moments, averages, rates
-        )
-    ]
-
-    target_row = jnp.arange(4 * pooled)
-    target_quarter, target_rest = target_row // pooled, target_row % pooled
-    source_row = (
-        (((target_quarter // 2) ^ core) + 2 * ((target_quarter % 2) ^ across)) * pooled
-        + (target_rest % 2) * half_pool
-        + target_rest // 2
-    )
-    new_memory = memory_out(
-        (quarter ^ mp_index)[None],
-        one_hot_rows(source_row, 4 * pooled).T,
-        stored[3] + stored[4],
-    )
-    new_memory = regroup(new_memory).transpose(0, 1, 3, 2)
+    made = update(
+        squares,
+        squares_two,
+        box_total.reshape(1, 1),
+        grads,
+        turned(masters),
+        turned(moments),
+        turned(averages),
+        rates,
+    )
+    grad_norm = made[0].reshape(())
+    results = []
+    for i in range(3):
+        results.extend(turned(made[1 + 7 * i : 8 + 7 * i]))
+
     return (
-        (loss_global, box_total, grad_norm, new_memory)
-        + tuple(r[0] for r in results)
-        + tuple(r[1] for r in results)
-        + tuple(r[2] for r in results)
-        + (results[0][0].astype(bf16), results[1][0].astype(bf16))
+        (loss_global, box_total, grad_norm, new_memory.transpose(0, 1, 3, 2)) + tuple(results) + tuple(made[22:24])
     )
 
 

time: 704 us -> 541 us (0.77)
  waiting for transfers between devices: 229 us -> 106 us
  starting transfers between devices: 121 us -> 88.3 us
  Pallas kernels: 162 us -> 180 us
  local copies, waits for them, and re-layouts: 56.9 us -> 43.1 us
  between operations: 26.2 us -> 16.9 us
    ppermute x56 -> x43, waiting for transfers between devices: 188 us -> 58.2 us  [swap_dp(): return lax.ppermute(inputs, 'dp', [(i, i ^ mask) for i in range(size)])]
    unnamed x322 -> x174, local copies, waits for them, and re-layouts: 38.3 us -> 6.23 us
    ppermute x56 -> x43, starting transfers between devices: 44.9 us -> 22.5 us  [swap_dp(): return lax.ppermute(inputs, 'dp', [(i, i ^ mask) for i in range(size)])]
    pallas_call x12 -> x14, Pallas kernels: 162 us -> 180 us  [call(): pl.pallas_call(run, grid=grid, in_specs=list(in_specs) + [pl.BlockSpec(me...]
    convert_element_type x18 -> x1, other arithmetic: 15.7 us -> 0.01 us  [shards(): feature = group_sum_features(feature).astype(bf16)]
    ppermute x32 -> x31, starting transfers between devices: 58.5 us -> 47.8 us  [swap_mp(): return lax.ppermute(inputs, 'mp', [(i, i ^ mask) for i in range(size)])]
    another operation x4 -> x14, other arithmetic: 2.33 us -> 11.8 us
    ppermute x32 -> x31, waiting for transfers between devices: 40.8 us -> 47.5 us  [swap_mp(): return lax.ppermute(inputs, 'mp', [(i, i ^ mask) for i in range(size)])]
  transfers between devices with their start and end apart: 92 -> 78, of which waited for: 36 -> 24; matrix products, arithmetic and copies ran while one was open for 10% -> 22% of each run, Pallas kernels for 7% -> 22%
where the time goes in v3:
time: 541 us; the launch traced here: 534 us
  Pallas kernels  180 us (33%)
  waiting for transfers between devices  106 us (20%)
  starting transfers between devices  88.3 us (16%)
  other arithmetic  60.2 us (11%)
  local copies, waits for them, and re-layouts  43.1 us (8%)
  matrix products  39.9 us (7%)
  between operations  16.9 us (3%)
    pallas_call x14, Pallas kernels, call(): pl.pallas_call(run, grid=grid, in_specs=list(in_specs) + [pl.BlockSpec(me...  180 us
    ppermute x43, waiting for transfers between devices, swap_dp(): return lax.ppermute(inputs, 'dp', [(i, i ^ mask) for i in range(size)])  58.2 us
    ppermute x31, starting transfers between devices, swap_mp(): return lax.ppermute(inputs, 'mp', [(i, i ^ mask) for i in range(size)])  47.8 us
    ppermute x31, waiting for transfers between devices, swap_mp(): return lax.ppermute(inputs, 'mp', [(i, i ^ mask) for i in range(size)])  47.5 us
    dot_general x11, matrix products, contract_rows(): lax.dot_general(first_operand, second_operand, (((0,), (0,)), ((), ())),...  38.1 us
    ppermute x43, starting transfers between devices, swap_dp(): return lax.ppermute(inputs, 'dp', [(i, i ^ mask) for i in range(size)])  22.5 us
    ppermute x4, starting transfers between devices, regroup(): return lax.ppermute(inputs, ('dp', 'mp'), pairs)  18 us
    another operation x13, other arithmetic  11.2 us
  transfers between devices with their start and end apart: 78, of which 24 were waited for; matrix products, arithmetic and copies ran while one was open for 22% of the time, Pallas kernels for 22%

profile of v3, /device:TPU:0, one launch (start us, length us, event | category | flops | bytes accessed | tf_op | source)
XLA Modules:
  0.0 533.9 jit_solution(16550960024072154683)
XLA Ops:
  1.9 3.1 collective-permute-start
  5.0 2.6 collective-permute-start.1
  12.4 3.9 collective-permute-start.5
  20.3 2.0 collective-permute-start.2
  24.1 2.9 collective-permute-done.2
  31.1 9.4 %collective-permute-start.6 = (bf16[3,441,384]{2,1,0:T(8,128)(2,1)}, bf16[3,441,384]{2,1,0:T(8,128)(2,1)}, u32[]{:S(2)}, u32[]{:S(2)}) collective-permute-start(bf16[3,441,384]{2,1,0:T(8,128)(2,1)} %bitcast), channel_id=1, source_target_pairs={{0,0},{1,1},{2,4},{3,5},{4,2},{5,3},{6,6},{7,7},{8,8},{9,9},{10,12... | collective-permute-start | bytes 3048200 | tf_op jit(solution)/shard_map/ppermute | solution.py:64
  51.6 1.6 collective-permute-done.8.refs_5_.refs_10_
  55.8 2.3 collective-permute-start.28
  60.4 6.2 %collective-permute-start.24 = (bf16[2,2,192,384]{3,2,1,0:T(8,128)(2,1)}, bf16[2,2,192,384]{3,2,1,0:T(8,128)(2,1)}, u32[]{:S(2)}, u32[]{:S(2)}) collective-permute-start(bf16[2,2,192,384]{3,2,1,0:T(8,128)(2,1)} %bitcast.149), channel_id=1, source_target_pairs={{0,0},{1,1},{2,4},{3,5},{4,2},{5,3},{6,6},{7,7},{8,8},{9,9},{10,12... | collective-permute-start | bytes 1769480 | tf_op jit(solution)/shard_map/ppermute | solution.py:64
  66.6 12.7 %shard_map.466 = (bf16[1152,441]{1,0:T(8,128)(2,1)}, f32[1152,768]{1,0:T(8,128)}, bf16[1152,768]{1,0:T(8,128)(2,1)}, bf16[1152,768]{1,0:T(8,128)(2,1)}, bf16[115...) custom-call(bf16[3,441,384]{2,1,0:T(8,128)(2,1)} %collective-permute, ...), custom_call_target="tpu_custom_call" | custom-call | flops 1000 | bytes 1000 | tf_op jit(solution)/shard_map/pallas_call | solution.py:147
  79.4 2.0 fusion.78
  81.4 2.8 collective-permute-start.16
  90.3 6.6 %collective-permute-done.29 = bf16[96,1728]{1,0:T(8,128)(2,1)} collective-permute-done((bf16[96,1728]{1,0:T(8,128)(2,1)}, bf16[96,1728]{1,0:T(8,128)(2,1)}, u32[]{:S(2)}, u32[]{:S(2)}) %collective-permute-start.29) | collective-permute-done | bytes 331808 | tf_op jit(solution)/shard_map/ppermute | solution.py:50
  96.9 2.0 fusion.82
  98.9 6.9 %collective-permute-done.16.refs_5_.refs_8_ = bf16[1,2,96,768]{3,2,1,0:T(8,128)(2,1)S(1)} collective-permute-done((bf16[1,2,96,768]{3,2,1,0:T(8,128)(2,1)S(1)}, bf16[1,2,96,768]{3,2,1,0:T(8,128)(2,1)S(1)}, u32[]{:S(2)}, u32[]{:S(2)}) %collective-permute-start.16) | collective-permute-done | bytes 294944 | tf_op jit(solution)/shard_map/ppermute | solution.py:50
  105.9 2.3 fusion.80
  108.2 3.9 collective-permute-done.19.refs_9_.refs_5_.refs_4_.refs_7_
  113.7 2.2 concatenate.175.refs_4_.refs_6_
  118.4 1.6 collective-permute-start.32
  122.5 8.4 %collective-permute-done.26.refs_4_ = bf16[2,2,192,384]{3,2,1,0:T(8,128)(2,1)} collective-permute-done((bf16[2,2,192,384]{3,2,1,0:T(8,128)(2,1)}, bf16[2,2,192,384]{3,2,1,0:T(8,128)(2,1)}, u32[]{:S(2)}, u32[]{:S(2)}) %collective-permute-start.26) | collective-permute-done | bytes 589856 | tf_op jit(solution)/shard_map/ppermute | solution.py:50
  134.7 10.2 %shard_map.467 = (bf16[1152,768]{1,0:T(8,128)(2,1)}, bf16[12,384,768]{2,1,0:T(8,128)(2,1)}, bf16[768,768]{1,0:T(8,128)(2,1)}, bf16[768,768]{1,0:T(8,128)(2,1)}) custom-call(bf16[1152,768]{1,0:T(8,128)(2,1)} %get-tuple-element.120.refs_0_, f32[2,6,768]{2,1,0:T(8,128)} %reshape.695.refs_2_.refs_1_.refs_4_, f32[3,4,768]{2,1,0:T(4,128)} %pad_maximum_fusion.18.refs_2_, ...), custom_call_target="tpu_custom_call" | custom-call | flops 1000 | bytes 1000 | tf_op jit(solution)/shard_map/pallas_call | solution.py:147
  145.7 5.1 shard_map.468.refs_11_.refs_7_.refs_8_.refs_5_.refs_6_.refs_9_
  150.9 10.2 %shard_map.469 = (bf16[1152,768]{1,0:T(8,128)(2,1)}, bf16[12,384,768]{2,1,0:T(8,128)(2,1)}, bf16[768,768]{1,0:T(8,128)(2,1)}, bf16[768,768]{1,0:T(8,128)(2,1)}) custom-call(bf16[1152,768]{1,0:T(8,128)(2,1)} %get-tuple-element.120.refs_0_, f32[2,6,768]{2,1,0:T(8,128)} %reshape.695.refs_2_.refs_1_.refs_4_, ...), custom_call_target="tpu_custom_call", output_to_operand_aliasing={{0}: (12, {})} | custom-call | flops 1000 | bytes 1000 | tf_op jit(solution)/shard_map/pallas_call | solution.py:147
  161.1 10.5 %shard_map.470 = (bf16[1152,768]{1,0:T(8,128)(2,1)}, bf16[12,384,768]{2,1,0:T(8,128)(2,1)}, bf16[768,768]{1,0:T(8,128)(2,1)}, bf16[768,768]{1,0:T(8,128)(2,1)}) custom-call(bf16[1152,768]{1,0:T(8,128)(2,1)} %get-tuple-element.120.refs_0_, f32[2,6,768]{2,1,0:T(8,128)} %reshape.695.refs_2_.refs_1_.refs_4_, ...), custom_call_target="tpu_custom_call", output_to_operand_aliasing={{0}: (9, {})} | custom-call | flops 1000 | bytes 1000 | tf_op jit(solution)/shard_map/pallas_call | solution.py:147
  171.6 6.2 %collective-permute-done.32.refs_6_.refs_8_ = bf16[96,6912]{1,0:T(8,128)(2,1)} collective-permute-done((bf16[96,6912]{1,0:T(8,128)(2,1)S(1)}, bf16[96,6912]{1,0:T(8,128)(2,1)}, u32[]{:S(2)}, u32[]{:S(2)}) %collective-permute-start.32) | collective-permute-done | bytes 1327136 | tf_op jit(solution)/shard_map/ppermute | solution.py:45
  179.8 4.3 shard_map.471.refs_12_
  184.1 1.7 collective-permute-start.38
  187.0 35.1 %shard_map.472 = (f32[1152,768]{1,0:T(8,128)}, bf16[1152,768]{1,0:T(8,128)(2,1)}, bf16[1152,3072]{1,0:T(8,128)(2,1)}, bf16[1152,3072]{1,0:T(8,128)(2,1)}, f32[1152,768]{1,0:T(8,128)}, /*index=5*/f32[3,8,768]{2,1,0:T(8,128)}) custom-call(bf16[1152,768]{1,0:T(8,128)(2,1)} %get-tuple-element.128.refs_0_, f32[1152,768]{1,0:T(8,128)} %get-tuple-element.129.refs_1_.refs_5_, ...), custom_call_target="tpu_custom_call" | custom-call | flops 1000 | bytes 1000 | tf_op jit(solution)/shard_map/pallas_call | solution.py:147
  225.9 3.2 collective-permute-done.40
  230.6 29.6 %shard_map.473 = (bf16[1152,768]{1,0:T(8,128)(2,1)}, bf16[1152,3072]{1,0:T(8,128)(2,1)}, bf16[1152,768]{1,0:T(8,128)(2,1)}, f32[1152,768]{1,0:T(8,128)}, bf16[1152,768]{1,0:T(8,128)(2,1)}, /*index=5*/f32[8,768]{1,0:T(8,128)}) custom-call(f32[3,8,768]{2,1,0:T(8,128)} %convolution_bitcast_fusion.refs_0_, f32[3,8,384]{2,1,0:T(8,128)} %convert_divide_fusion.refs_3_.refs_1_, ...), custom_call_target="tpu_custom_call" | custom-call | flops 1000 | bytes 1000 | tf_op jit(solution)/shard_map/pallas_call | solution.py:147
  260.3 2.3 convolution_convert_fusion.6
  262.7 6.4 %convolution_convert_fusion = bf16[384,3072]{1,0:T(8,128)(2,1)S(1)} fusion(bf16[1152,3072]{1,0:T(8,128)(2,1)} %get-tuple-element.156, bf16[1152,768]{1,0:T(8,128)(2,1)S(1)} %copy-done.76), kind=kOutput, calls=%fused_computation | convolution fusion | flops 2719088640 | bytes 10321920 | tf_op jit(solution)/shard_map/dot_general | solution.py:38
  269.7 3.5 convolution_convert_fusion.2
  274.3 3.7 convolution_convert_fusion.1
  278.0 3.5 convolution_convert_fusion.3
  288.3 13.8 %shard_map.474 = (bf16[1152,768]{1,0:T(8,128)(2,1)}, bf16[2,2,96,768]{3,2,1,0:T(8,128)(2,1)}, bf16[2,2,96,768]{3,2,1,0:T(8,128)(2,1)}, f32[2,2,768]{2,1,0:T(2,128)}, f32[3,4,128]{2,1,0:T(4,128)}) custom-call(bf16[1152,768]{1,0:T(8,128)(2,1)} %get-tuple-element.120.refs_0_, bf16[768,768]{1,0:T(8,128)(2,1)} %get-tuple-element.150.refs_1_, ...), custom_call_target="tpu_custom_call" | custom-call | flops 1000 | bytes 1000 | tf_op jit(solution)/shard_map/pallas_call | solution.py:147
  310.3 14.3 %shard_map.475 = (bf16[1152,768]{1,0:T(8,128)(2,1)}, bf16[2,2,96,768]{3,2,1,0:T(8,128)(2,1)}, bf16[2,2,96,768]{3,2,1,0:T(8,128)(2,1)}, f32[2,2,768]{2,1,0:T(2,128)}, f32[3,4,128]{2,1,0:T(4,128)}) custom-call(bf16[1152,768]{1,0:T(8,128)(2,1)} %get-tuple-element.120.refs_0_, ...), custom_call_target="tpu_custom_call", output_to_operand_aliasing={{0}: (10, {})} | custom-call | flops 1000 | bytes 1000 | tf_op jit(solution)/shard_map/pallas_call | solution.py:147
  326.6 1.8 collective-permute-start.69
  330.1 2.0 fusion.13
  334.1 13.7 %shard_map.476 = (bf16[1152,768]{1,0:T(8,128)(2,1)}, bf16[2,2,96,768]{3,2,1,0:T(8,128)(2,1)}, bf16[2,2,96,768]{3,2,1,0:T(8,128)(2,1)}, f32[2,2,768]{2,1,0:T(2,128)}, f32[3,4,128]{2,1,0:T(4,128)}) custom-call(bf16[1152,768]{1,0:T(8,128)(2,1)} %get-tuple-element.120.refs_0_, ...), custom_call_target="tpu_custom_call", output_to_operand_aliasing={{0}: (13, {})} | custom-call | flops 1000 | bytes 1000 | tf_op jit(solution)/shard_map/pallas_call | solution.py:147
  353.9 5.9 %collective-permute-done.69 = bf16[96,6912]{1,0:T(8,128)(2,1)} collective-permute-done((bf16[96,6912]{1,0:T(8,128)(2,1)}, bf16[96,6912]{1,0:T(8,128)(2,1)}, u32[]{:S(2)}, u32[]{:S(2)}) %collective-permute-start.69) | collective-permute-done | bytes 1327136 | tf_op jit(solution)/shard_map/ppermute | solution.py:45
  359.8 28.0 %collective-permute-done.68 = bf16[96,6912]{1,0:T(8,128)(2,1)} collective-permute-done((bf16[96,6912]{1,0:T(8,128)(2,1)S(1)}, bf16[96,6912]{1,0:T(8,128)(2,1)}, u32[]{:S(2)}, u32[]{:S(2)}) %collective-permute-start.68) | collective-permute-done | bytes 1327136 | tf_op jit(solution)/shard_map/ppermute | solution.py:45
  387.8 2.9 convert_add_fusion
  393.4 13.1 %shard_map.477 = (bf16[1152,2304]{1,0:T(8,128)(2,1)}, bf16[1152,768]{1,0:T(8,128)(2,1)}, f32[8,768]{1,0:T(8,128)}, f32[8,768]{1,0:T(8,128)}) custom-call(bf16[1152,768]{1,0:T(8,128)(2,1)} %get-tuple-element.164.refs_0_, f32[3,2,96,768]{3,2,1,0:T(8,128)} %pad_maximum_fusion.refs_1_, bf16[1152,768]{1,0:T(8,128)(2,1)} %get-tuple-element.167.refs_2_, ...), custom_call_target="tpu_custom_call" | custom-call | flops 1000 | bytes 1000 | tf_op jit(solution)/shard_map/pallas_call | solution.py:147
  406.5 3.2 convolution_convert_fusion.8
  411.6 6.5 %convolution_convert_fusion.4 = bf16[384,2304]{1,0:T(8,128)(2,1)} fusion(bf16[1152,2304]{1,0:T(8,128)(2,1)} %get-tuple-element.182, bf16[1152,768]{1,0:T(8,128)(2,1)} %get-tuple-element.181), kind=kOutput, calls=%fused_computation.4 | convolution fusion | flops 2039316480 | bytes 7962624 | tf_op jit(solution)/shard_map/dot_general | solution.py:38
  423.1 6.3 %convolution_convert_fusion.5 = bf16[384,2304]{1,0:T(8,128)(2,1)} fusion(bf16[1152,2304]{1,0:T(8,128)(2,1)} %get-tuple-element.182, bf16[1152,768]{1,0:T(8,128)(2,1)S(1)} %copy-done.75), kind=kOutput, calls=%fused_computation.5 | convolution fusion | flops 2039316480 | bytes 7962624 | tf_op jit(solution)/shard_map/dot_general | solution.py:38
  438.4 2.3 collective-permute-done.52
  441.3 3.4 collective-permute-start.55
  444.7 1.8 add_convert_fusion.23
  446.6 2.6 add_convert_fusion.12
  462.4 3.4 collective-permute-start.72
  468.2 7.6 %collective-permute-done.59 = bf16[96,2832]{1,0:T(8,128)(2,1)} collective-permute-done((bf16[96,2832]{1,0:T(8,128)(2,1)}, bf16[96,2832]{1,0:T(8,128)(2,1)}, u32[]{:S(2)}, u32[]{:S(2)}) %collective-permute-start.59) | collective-permute-done | bytes 543776 | tf_op jit(solution)/shard_map/ppermute | solution.py:45
  475.9 1.8 add_convert_fusion.8
  479.3 2.0 collective-permute-start.64
  481.5 7.6 %collective-permute-start.62 = (bf16[96,576]{1,0:T(8,128)(2,1)S(1)}, bf16[96,576]{1,0:T(8,128)(2,1)S(1)}, u32[]{:S(2)}, u32[]{:S(2)}) collective-permute-start(bf16[96,576]{1,0:T(8,128)(2,1)S(1)} %get-tuple-element.279), channel_id=1, source_target_pairs={{0,2},{1,3},{2,0},{3,1},{4,6},{5,7},{6,4},{7,5},{8,10},{9,11},{10,... | collective-permute-start | bytes 331784 | tf_op jit(solution)/shard_map/ppermute | solution.py:50
  489.1 6.3 %collective-permute-done.71 = bf16[96,1728]{1,0:T(8,128)(2,1)S(1)} collective-permute-done((bf16[96,1728]{1,0:T(8,128)(2,1)S(1)}, bf16[96,1728]{1,0:T(8,128)(2,1)S(1)}, u32[]{:S(2)}, u32[]{:S(2)}) %collective-permute-start.71) | collective-permute-done | bytes 331808 | tf_op jit(solution)/shard_map/ppermute | solution.py:50
  495.4 5.0 collective-permute-start.63
  501.5 3.7 collective-permute-done.65.refs_6_
  506.9 2.4 shard_map.478
  513.0 2.0 collective-permute-done.74
  519.1 1.9 pad_maximum_fusion.8.refs_3_
  525.6 1.6 collective-permute-done.77.refs_1_
  527.8 5.0 shard_map.479
  (482 shorter events, 124.3 us)
Async XLA Ops:
  1.9 22.0 %collective-permute-start = (bf16[96,576]{1,0:T(8,128)(2,1)S(1)}, bf16[96,576]{1,0:T(8,128)(2,1)S(1)}, u32[]{:S(2)}, u32[]{:S(2)}) collective-permute-start(bf16[96,576]{1,0:T(8,128)(2,1)S(1)} %slice.712), channel_id=1, source_target_pairs={{0,1},{1,0},{2,3},{3,2},{4,5},{5,4},{6,7},{7,6},{8,9},{9,8},{10,11... | collective-permute-start | bytes 331784 | tf_op jit(solution)/shard_map/ppermute | solution.py:50
  5.0 19.1 %collective-permute-start.1 = (bf16[96,576]{1,0:T(8,128)(2,1)S(1)}, bf16[96,576]{1,0:T(8,128)(2,1)S(1)}, u32[]{:S(2)}, u32[]{:S(2)}) collective-permute-start(bf16[96,576]{1,0:T(8,128)(2,1)S(1)} %slice.712), channel_id=1, source_target_pairs={{0,2},{1,3},{2,0},{3,1},{4,6},{5,7},{6,4},{7,5},{8,10},{9,11},{10,... | collective-permute-start | bytes 331784 | tf_op jit(solution)/shard_map/ppermute | solution.py:50
  11.9 11.1 %collective-permute-start.3 = (bf16[24,952]{1,0:T(8,128)(2,1)S(1)}, bf16[24,952]{1,0:T(8,128)(2,1)S(1)}, u32[]{:S(2)}, u32[]{:S(2)}) collective-permute-start(bf16[24,952]{1,0:T(8,128)(2,1)S(1)} %pad_maximum_fusion.16), channel_id=1, source_target_pairs={{0,1},{1,0},{2,3},{3,2},{4,5},{5,4},{6,7},{7,6},{8,9},{9,8},{10,11... | collective-permute-start | bytes 137096 | tf_op jit(solution)/shard_map/ppermute | solution.py:50
  12.4 9.9 %collective-permute-start.4 = (bf16[24,952]{1,0:T(8,128)(2,1)S(1)}, bf16[24,952]{1,0:T(8,128)(2,1)S(1)}, u32[]{:S(2)}, u32[]{:S(2)}) collective-permute-start(bf16[24,952]{1,0:T(8,128)(2,1)S(1)} %pad_maximum_fusion.16), channel_id=1, source_target_pairs={{0,2},{1,3},{2,0},{3,1},{4,6},{5,7},{6,4},{7,5},{8,10},{9,11},{10,... | collective-permute-start | bytes 137096 | tf_op jit(solution)/shard_map/ppermute | solution.py:50
  12.4 7.9 %collective-permute-start.5 = (bf16[24,952]{1,0:T(8,128)(2,1)S(1)}, bf16[24,952]{1,0:T(8,128)(2,1)S(1)}, u32[]{:S(2)}, u32[]{:S(2)}) collective-permute-start(bf16[24,952]{1,0:T(8,128)(2,1)S(1)} %pad_maximum_fusion.16), channel_id=1, source_target_pairs={{0,3},{1,2},{2,1},{3,0},{4,7},{5,6},{6,5},{7,4},{8,11},{9,10},{10,... | collective-permute-start | bytes 137096 | tf_op jit(solution)/shard_map/ppermute | solution.py:50
  20.3 6.7 %collective-permute-start.2 = (bf16[96,576]{1,0:T(8,128)(2,1)S(1)}, bf16[96,576]{1,0:T(8,128)(2,1)S(1)}, u32[]{:S(2)}, u32[]{:S(2)}) collective-permute-start(bf16[96,576]{1,0:T(8,128)(2,1)S(1)} %slice.712), channel_id=1, source_target_pairs={{0,3},{1,2},{2,1},{3,0},{4,7},{5,6},{6,5},{7,4},{8,11},{9,10},{10,... | collective-permute-start | bytes 331784 | tf_op jit(solution)/shard_map/ppermute | solution.py:50
  22.3 19.7 %collective-permute-start.14 = (s32[16,128]{1,0:T(8,128)S(1)}, s32[16,128]{1,0:T(8,128)S(1)}, u32[]{:S(2)}, u32[]{:S(2)}) collective-permute-start(s32[16,128]{1,0:T(8,128)S(1)} %pad_bitcast_fusion), channel_id=1, source_target_pairs={{0,0},{1,1},{2,4},{3,5},{4,2},{5,3},{6,6},{7,7},{8,8},{9,9},{10,12... | collective-permute-start | bytes 24584 | tf_op jit(solution)/shard_map/ppermute | solution.py:64
  27.6 23.5 %collective-permute-start.7 = (bf16[96,2944]{1,0:T(8,128)(2,1)S(1)}, bf16[96,2944]{1,0:T(8,128)(2,1)S(1)}, u32[]{:S(2)}, u32[]{:S(2)}) collective-permute-start(bf16[96,2944]{1,0:T(8,128)(2,1)S(1)} %concatenate.167.refs_3_.refs_8_), channel_id=1, source_target_pairs={{0,8},{4,12},{8,0},{12,4},{16,24},{20,28},{24,16},{28,20},{1,9},{5... | collective-permute-start | bytes 1695752 | tf_op jit(solution)/shard_map/ppermute | solution.py:45
  29.1 24.0 %collective-permute-start.8 = (bf16[96,2944]{1,0:T(8,128)(2,1)S(1)}, bf16[96,2944]{1,0:T(8,128)(2,1)S(1)}, u32[]{:S(2)}, u32[]{:S(2)}) collective-permute-start(bf16[96,2944]{1,0:T(8,128)(2,1)S(1)} %concatenate.167.refs_3_.refs_8_), channel_id=1, source_target_pairs={{0,16},{4,20},{8,24},{12,28},{16,0},{20,4},{24,8},{28,12},{1,17},{... | collective-permute-start | bytes 1695752 | tf_op jit(solution)/shard_map/ppermute | solution.py:45
  30.7 22.5 %collective-permute-start.9 = (bf16[96,2944]{1,0:T(8,128)(2,1)S(1)}, bf16[96,2944]{1,0:T(8,128)(2,1)S(1)}, u32[]{:S(2)}, u32[]{:S(2)}) collective-permute-start(bf16[96,2944]{1,0:T(8,128)(2,1)S(1)} %concatenate.167.refs_3_.refs_8_), channel_id=1, source_target_pairs={{0,24},{4,28},{8,16},{12,20},{16,8},{20,12},{24,0},{28,4},{1,25},{... | collective-permute-start | bytes 1695752 | tf_op jit(solution)/shard_map/ppermute | solution.py:45
  31.1 26.9 %collective-permute-start.6 = (bf16[3,441,384]{2,1,0:T(8,128)(2,1)}, bf16[3,441,384]{2,1,0:T(8,128)(2,1)}, u32[]{:S(2)}, u32[]{:S(2)}) collective-permute-start(bf16[3,441,384]{2,1,0:T(8,128)(2,1)} %bitcast), channel_id=1, source_target_pairs={{0,0},{1,1},{2,4},{3,5},{4,2},{5,3},{6,6},{7,7},{8,8},{9,9},{10,12... | collective-permute-start | bytes 3048200 | tf_op jit(solution)/shard_map/ppermute | solution.py:64
  51.1 8.9 %collective-permute-start.11 = (bf16[96,2944]{1,0:T(8,128)(2,1)S(1)}, bf16[96,2944]{1,0:T(8,128)(2,1)S(1)}, u32[]{:S(2)}, u32[]{:S(2)}) collective-permute-start(bf16[96,2944]{1,0:T(8,128)(2,1)S(1)} %collective-permute-done.7.refs_4_.refs_9_), channel_id=1, source_target_pairs={{0,4},{4,0},{8,12},{12,8},{16,20},{20,16},{24,28},{28,24},{1,5},{5... | collective-permute-start | bytes 1695752 | tf_op jit(solution)/shard_map/ppermute | solution.py:45
  53.2 7.2 %collective-permute-start.12 = (bf16[96,2944]{1,0:T(8,128)(2,1)S(1)}, bf16[96,2944]{1,0:T(8,128)(2,1)}, u32[]{:S(2)}, u32[]{:S(2)}) collective-permute-start(bf16[96,2944]{1,0:T(8,128)(2,1)S(1)} %collective-permute-done.8.refs_5_.refs_10_), channel_id=1, source_target_pairs={{0,4},{4,0},{8,12},{12,8},{16,20},{20,16},{24,28},{28,24},{1,5},{5... | collective-permute-start | bytes 1695752 | tf_op jit(solution)/shard_map/ppermute | solution.py:45
  53.2 13.4 %collective-permute-start.13 = (bf16[96,2944]{1,0:T(8,128)(2,1)S(1)}, bf16[96,2944]{1,0:T(8,128)(2,1)}, u32[]{:S(2)}, u32[]{:S(2)}) collective-permute-start(bf16[96,2944]{1,0:T(8,128)(2,1)S(1)} %collective-permute-done.9.refs_6_.refs_11_), channel_id=1, source_target_pairs={{0,4},{4,0},{8,12},{12,8},{16,20},{20,16},{24,28},{28,24},{1,5},{5... | collective-permute-start | bytes 1695752 | tf_op jit(solution)/shard_map/ppermute | solution.py:45
  55.8 25.6 %collective-permute-start.28 = (bf16[96,1728]{1,0:T(8,128)(2,1)}, bf16[96,1728]{1,0:T(8,128)(2,1)}, u32[]{:S(2)}, u32[]{:S(2)}) collective-permute-start(bf16[96,1728]{1,0:T(8,128)(2,1)} %pad_maximum_fusion.11), channel_id=1, source_target_pairs={{0,1},{1,0},{2,3},{3,2},{4,5},{5,4},{6,7},{7,6},{8,9},{9,8},{10,11... | collective-permute-start | bytes 995336 | tf_op jit(solution)/shard_map/ppermute | solution.py:50
  58.1 26.1 %collective-permute-start.30 = (bf16[96,1728]{1,0:T(8,128)(2,1)}, bf16[96,1728]{1,0:T(8,128)(2,1)}, u32[]{:S(2)}, u32[]{:S(2)}) collective-permute-start(bf16[96,1728]{1,0:T(8,128)(2,1)} %pad_maximum_fusion.11), channel_id=1, source_target_pairs={{0,3},{1,2},{2,1},{3,0},{4,7},{5,6},{6,5},{7,4},{8,11},{9,10},{10,... | collective-permute-start | bytes 995336 | tf_op jit(solution)/shard_map/ppermute | solution.py:50
  60.0 36.9 %collective-permute-start.29 = (bf16[96,1728]{1,0:T(8,128)(2,1)}, bf16[96,1728]{1,0:T(8,128)(2,1)}, u32[]{:S(2)}, u32[]{:S(2)}) collective-permute-start(bf16[96,1728]{1,0:T(8,128)(2,1)} %pad_maximum_fusion.11), channel_id=1, source_target_pairs={{0,2},{1,3},{2,0},{3,1},{4,6},{5,7},{6,4},{7,5},{8,10},{9,11},{10,... | collective-permute-start | bytes 995336 | tf_op jit(solution)/shard_map/ppermute | solution.py:50
  60.4 51.7 %collective-permute-start.24 = (bf16[2,2,192,384]{3,2,1,0:T(8,128)(2,1)}, bf16[2,2,192,384]{3,2,1,0:T(8,128)(2,1)}, u32[]{:S(2)}, u32[]{:S(2)}) collective-permute-start(bf16[2,2,192,384]{3,2,1,0:T(8,128)(2,1)} %bitcast.149), channel_id=1, source_target_pairs={{0,0},{1,1},{2,4},{3,5},{4,2},{5,3},{6,6},{7,7},{8,8},{9,9},{10,12... | collective-permute-start | bytes 1769480 | tf_op jit(solution)/shard_map/ppermute | solution.py:64
  81.4 17.5 %collective-permute-start.15 = (bf16[1,2,96,768]{3,2,1,0:T(8,128)(2,1)S(1)}, bf16[1,2,96,768]{3,2,1,0:T(8,128)(2,1)S(1)}, u32[]{:S(2)}, u32[]{:S(2)}) collective-permute-start(bf16[1,2,96,768]{3,2,1,0:T(8,128)(2,1)S(1)} %get-tuple-element.251), channel_id=1, source_target_pairs={{0,4},{4,0},{8,12},{12,8},{16,20},{20,16},{24,28},{28,24},{1,5},{5... | collective-permute-start | bytes 884744 | tf_op jit(solution)/shard_map/ppermute | solution.py:45
  81.4 24.4 %collective-permute-start.16 = (bf16[1,2,96,768]{3,2,1,0:T(8,128)(2,1)S(1)}, bf16[1,2,96,768]{3,2,1,0:T(8,128)(2,1)S(1)}, u32[]{:S(2)}, u32[]{:S(2)}) collective-permute-start(bf16[1,2,96,768]{3,2,1,0:T(8,128)(2,1)S(1)} %get-tuple-element.251), channel_id=1, source_target_pairs={{0,1},{1,0},{2,3},{3,2},{4,5},{5,4},{6,7},{7,6},{8,9},{9,8},{10,11... | collective-permute-start | bytes 884744 | tf_op jit(solution)/shard_map/ppermute | solution.py:50
  84.2 21.6 %collective-permute-start.18 = (bf16[1,2,96,768]{3,2,1,0:T(8,128)(2,1)S(1)}, bf16[1,2,96,768]{3,2,1,0:T(8,128)(2,1)S(1)}, u32[]{:S(2)}, u32[]{:S(2)}) collective-permute-start(bf16[1,2,96,768]{3,2,1,0:T(8,128)(2,1)S(1)} %get-tuple-element.250), channel_id=1, source_target_pairs={{0,4},{4,0},{8,12},{12,8},{16,20},{20,16},{24,28},{28,24},{1,5},{5... | collective-permute-start | bytes 884744 | tf_op jit(solution)/shard_map/ppermute | solution.py:45
  96.8 15.2 %collective-permute-start.19 = (bf16[1,2,96,768]{3,2,1,0:T(8,128)(2,1)S(1)}, bf16[1,2,96,768]{3,2,1,0:T(8,128)(2,1)S(1)}, u32[]{:S(2)}, u32[]{:S(2)}) collective-permute-start(bf16[1,2,96,768]{3,2,1,0:T(8,128)(2,1)S(1)} %get-tuple-element.250), channel_id=1, source_target_pairs={{0,1},{1,0},{2,3},{3,2},{4,5},{5,4},{6,7},{7,6},{8,9},{9,8},{10,11... | collective-permute-start | bytes 884744 | tf_op jit(solution)/shard_map/ppermute | solution.py:50
  98.9 17.1 %collective-permute-start.21 = (bf16[1,2,96,768]{3,2,1,0:T(8,128)(2,1)}, bf16[1,2,96,768]{3,2,1,0:T(8,128)(2,1)S(1)}, u32[]{:S(2)}, u32[]{:S(2)}) collective-permute-start(bf16[1,2,96,768]{3,2,1,0:T(8,128)(2,1)} %get-tuple-element.249), channel_id=1, source_target_pairs={{0,4},{4,0},{8,12},{12,8},{16,20},{20,16},{24,28},{28,24},{1,5},{5... | collective-permute-start | bytes 884744 | tf_op jit(solution)/shard_map/ppermute | solution.py:45
  105.8 12.6 %collective-permute-start.22 = (bf16[1,2,96,768]{3,2,1,0:T(8,128)(2,1)}, bf16[1,2,96,768]{3,2,1,0:T(8,128)(2,1)S(1)}, u32[]{:S(2)}, u32[]{:S(2)}) collective-permute-start(bf16[1,2,96,768]{3,2,1,0:T(8,128)(2,1)} %get-tuple-element.249), channel_id=1, source_target_pairs={{0,1},{1,0},{2,3},{3,2},{4,5},{5,4},{6,7},{7,6},{8,9},{9,8},{10,11... | collective-permute-start | bytes 884744 | tf_op jit(solution)/shard_map/ppermute | solution.py:50
  105.8 14.2 %collective-permute-start.17 = (bf16[1,2,96,768]{3,2,1,0:T(8,128)(2,1)S(1)}, bf16[1,2,96,768]{3,2,1,0:T(8,128)(2,1)}, u32[]{:S(2)}, u32[]{:S(2)}) collective-permute-start(bf16[1,2,96,768]{3,2,1,0:T(8,128)(2,1)S(1)} %collective-permute-done.16.refs_5_.refs_8_), channel_id=1, source_target_pairs={{0,4},{4,0},{8,12},{12,8},{16,20},{20,16},{24,28},{28,24},{1,5},{5... | collective-permute-start | bytes 884744 | tf_op jit(solution)/shard_map/ppermute | solution.py:45
  112.1 8.6 %collective-permute-start.20 = (bf16[1,2,96,768]{3,2,1,0:T(8,128)(2,1)S(1)}, bf16[1,2,96,768]{3,2,1,0:T(8,128)(2,1)S(1)}, u32[]{:S(2)}, u32[]{:S(2)}) collective-permute-start(bf16[1,2,96,768]{3,2,1,0:T(8,128)(2,1)S(1)} %collective-permute-done.19.refs_9_.refs_5_.refs_4_.refs_7_), channel_id=1, source_target_pairs={{0,4},{4,0},{8,12},{12,8},{16,20},{20,16},{24,28},{28,24},{1,5},{5... | collective-permute-start | bytes 884744 | tf_op jit(solution)/shard_map/ppermute | solution.py:45
  112.1 18.9 %collective-permute-start.26 = (bf16[2,2,192,384]{3,2,1,0:T(8,128)(2,1)}, bf16[2,2,192,384]{3,2,1,0:T(8,128)(2,1)}, u32[]{:S(2)}, u32[]{:S(2)}) collective-permute-start(bf16[2,2,192,384]{3,2,1,0:T(8,128)(2,1)} %collective-permute-done.24.refs_2_), channel_id=1, source_target_pairs={{0,1},{1,0},{2,3},{3,2},{4,5},{5,4},{6,7},{7,6},{8,9},{9,8},{10,11... | collective-permute-start | bytes 1769480 | tf_op jit(solution)/shard_map/ppermute | solution.py:50
  116.0 55.6 %collective-permute-start.31 = (bf16[96,6912]{1,0:T(8,128)(2,1)S(1)}, bf16[96,6912]{1,0:T(8,128)(2,1)}, u32[]{:S(2)}, u32[]{:S(2)}) collective-permute-start(bf16[96,6912]{1,0:T(8,128)(2,1)S(1)} %concatenate.175.refs_4_.refs_6_), channel_id=1, source_target_pairs={{0,8},{4,12},{8,0},{12,4},{16,24},{20,28},{24,16},{28,20},{1,9},{5... | collective-permute-start | bytes 3981320 | tf_op jit(solution)/shard_map/ppermute | solution.py:45
  118.4 59.3 %collective-permute-start.32 = (bf16[96,6912]{1,0:T(8,128)(2,1)S(1)}, bf16[96,6912]{1,0:T(8,128)(2,1)}, u32[]{:S(2)}, u32[]{:S(2)}) collective-permute-start(bf16[96,6912]{1,0:T(8,128)(2,1)S(1)} %concatenate.175.refs_4_.refs_6_), channel_id=1, source_target_pairs={{0,16},{4,20},{8,24},{12,28},{16,0},{20,4},{24,8},{28,12},{1,17},{... | collective-permute-start | bytes 3981320 | tf_op jit(solution)/shard_map/ppermute | solution.py:45
  120.0 57.7 %collective-permute-start.33 = (bf16[96,6912]{1,0:T(8,128)(2,1)S(1)}, bf16[96,6912]{1,0:T(8,128)(2,1)}, u32[]{:S(2)}, u32[]{:S(2)}) collective-permute-start(bf16[96,6912]{1,0:T(8,128)(2,1)S(1)} %concatenate.175.refs_4_.refs_6_), channel_id=1, source_target_pairs={{0,24},{4,28},{8,16},{12,20},{16,8},{20,12},{24,0},{28,4},{1,25},{... | collective-permute-start | bytes 3981320 | tf_op jit(solution)/shard_map/ppermute | solution.py:45
  122.4 22.5 %collective-permute-start.25 = (bf16[2,2,192,384]{3,2,1,0:T(8,128)(2,1)}, bf16[2,2,192,384]{3,2,1,0:T(8,128)(2,1)S(1)}, u32[]{:S(2)}, u32[]{:S(2)}) collective-permute-start(bf16[2,2,192,384]{3,2,1,0:T(8,128)(2,1)} %collective-permute-done.24.refs_2_), channel_id=1, source_target_pairs={{0,4},{4,0},{8,12},{12,8},{16,20},{20,16},{24,28},{28,24},{1,5},{5... | collective-permute-start | bytes 1769480 | tf_op jit(solution)/shard_map/ppermute | solution.py:45
  131.0 14.0 %collective-permute-start.27 = (bf16[2,2,192,384]{3,2,1,0:T(8,128)(2,1)}, bf16[2,2,192,384]{3,2,1,0:T(8,128)(2,1)}, u32[]{:S(2)}, u32[]{:S(2)}) collective-permute-start(bf16[2,2,192,384]{3,2,1,0:T(8,128)(2,1)} %collective-permute-done.26.refs_4_), channel_id=1, source_target_pairs={{0,4},{4,0},{8,12},{12,8},{16,20},{20,16},{24,28},{28,24},{1,5},{5... | collective-permute-start | bytes 1769480 | tf_op jit(solution)/shard_map/ppermute | solution.py:45
  177.7 9.2 %collective-permute-start.34 = (bf16[96,6912]{1,0:T(8,128)(2,1)S(1)}, bf16[96,6912]{1,0:T(8,128)(2,1)}, u32[]{:S(2)}, u32[]{:S(2)}) collective-permute-start(bf16[96,6912]{1,0:T(8,128)(2,1)S(1)} %concatenate.175.refs_4_.refs_6_), channel_id=1, source_target_pairs={{0,4},{4,0},{8,12},{12,8},{16,20},{20,16},{24,28},{28,24},{1,5},{5... | collective-permute-start | bytes 3981320 | tf_op jit(solution)/shard_map/ppermute | solution.py:45
  177.7 9.2 %collective-permute-start.35 = (bf16[96,6912]{1,0:T(8,128)(2,1)}, bf16[96,6912]{1,0:T(8,128)(2,1)}, u32[]{:S(2)}, u32[]{:S(2)}) collective-permute-start(bf16[96,6912]{1,0:T(8,128)(2,1)} %collective-permute-done.31.refs_5_.refs_7_), channel_id=1, source_target_pairs={{0,4},{4,0},{8,12},{12,8},{16,20},{20,16},{24,28},{28,24},{1,5},{5... | collective-permute-start | bytes 3981320 | tf_op jit(solution)/shard_map/ppermute | solution.py:45
  178.2 8.7 %collective-permute-start.36 = (bf16[96,6912]{1,0:T(8,128)(2,1)}, bf16[96,6912]{1,0:T(8,128)(2,1)}, u32[]{:S(2)}, u32[]{:S(2)}) collective-permute-start(bf16[96,6912]{1,0:T(8,128)(2,1)} %collective-permute-done.32.refs_6_.refs_8_), channel_id=1, source_target_pairs={{0,4},{4,0},{8,12},{12,8},{16,20},{20,16},{24,28},{28,24},{1,5},{5... | collective-permute-start | bytes 3981320 | tf_op jit(solution)/shard_map/ppermute | solution.py:45
  178.3 8.7 %collective-permute-start.37 = (bf16[96,6912]{1,0:T(8,128)(2,1)}, bf16[96,6912]{1,0:T(8,128)(2,1)}, u32[]{:S(2)}, u32[]{:S(2)}) collective-permute-start(bf16[96,6912]{1,0:T(8,128)(2,1)} %collective-permute-done.33.refs_7_.refs_9_), channel_id=1, source_target_pairs={{0,4},{4,0},{8,12},{12,8},{16,20},{20,16},{24,28},{28,24},{1,5},{5... | collective-permute-start | bytes 3981320 | tf_op jit(solution)/shard_map/ppermute | solution.py:45
  184.1 38.0 %collective-permute-start.38 = (bf16[2,2,192,384]{3,2,1,0:T(8,128)(2,1)}, bf16[2,2,192,384]{3,2,1,0:T(8,128)(2,1)S(1)}, u32[]{:S(2)}, u32[]{:S(2)}) collective-permute-start(bf16[2,2,192,384]{3,2,1,0:T(8,128)(2,1)} %shard_map.471.refs_12_), channel_id=1, source_target_pairs={{0,0},{1,1},{2,4},{3,5},{4,2},{5,3},{6,6},{7,7},{8,8},{9,9},{10,12... | collective-permute-start | bytes 1769480 | tf_op jit(solution)/shard_map/ppermute | solution.py:64
  262.6 18.9 %collective-permute-start.43 = (bf16[384,768]{1,0:T(8,128)(2,1)S(1)}, bf16[384,768]{1,0:T(8,128)(2,1)S(1)}, u32[]{:S(2)}, u32[]{:S(2)}) collective-permute-start(bf16[384,768]{1,0:T(8,128)(2,1)S(1)} %convolution_convert_fusion.6), channel_id=1, source_target_pairs={{0,4},{4,0},{8,12},{12,8},{16,20},{20,16},{24,28},{28,24},{1,5},{5... | collective-permute-start | bytes 1769480 | tf_op jit(solution)/shard_map/ppermute | solution.py:45
  269.1 12.5 %collective-permute-start.42 = (bf16[384,3072]{1,0:T(8,128)(2,1)S(1)}, bf16[384,3072]{1,0:T(8,128)(2,1)S(1)}, u32[]{:S(2)}, u32[]{:S(2)}) collective-permute-start(bf16[384,3072]{1,0:T(8,128)(2,1)S(1)} %convolution_convert_fusion), channel_id=1, source_target_pairs={{0,4},{4,0},{8,12},{12,8},{16,20},{20,16},{24,28},{28,24},{1,5},{5... | collective-permute-start | bytes 7077896 | tf_op jit(solution)/shard_map/ppermute | solution.py:45
  273.1 9.3 %collective-permute-start.41 = (bf16[384,3072]{1,0:T(8,128)(2,1)S(1)}, bf16[384,3072]{1,0:T(8,128)(2,1)S(1)}, u32[]{:S(2)}, u32[]{:S(2)}) collective-permute-start(bf16[384,3072]{1,0:T(8,128)(2,1)S(1)} %convolution_convert_fusion.2), channel_id=1, source_target_pairs={{0,4},{4,0},{8,12},{12,8},{16,20},{20,16},{24,28},{28,24},{1,5},{5... | collective-permute-start | bytes 7077896 | tf_op jit(solution)/shard_map/ppermute | solution.py:45
  309.2 20.9 %collective-permute-start.46 = (bf16[2,96,768]{2,1,0:T(8,128)(2,1)S(1)}, bf16[2,96,768]{2,1,0:T(8,128)(2,1)}, u32[]{:S(2)}, u32[]{:S(2)}) collective-permute-start(bf16[2,96,768]{2,1,0:T(8,128)(2,1)S(1)} %fusion.17.refs_11_), channel_id=1, source_target_pairs={{0,1},{1,0},{2,3},{3,2},{4,5},{5,4},{6,7},{7,6},{8,9},{9,8},{10,11... | collective-permute-start | bytes 884744 | tf_op jit(solution)/shard_map/ppermute | solution.py:50
  325.8 6.3 %collective-permute-start.45 = (bf16[2,2,96,768]{3,2,0,1:T(8,128)(2,1)S(1)}, bf16[2,2,96,768]{3,2,0,1:T(8,128)(2,1)S(1)}, u32[]{:S(2)}, u32[]{:S(2)}) collective-permute-start(bf16[2,2,96,768]{3,2,0,1:T(8,128)(2,1)S(1)} %copy.131), channel_id=1, source_target_pairs={{0,4},{4,0},{8,12},{12,8},{16,20},{20,16},{24,28},{28,24},{1,5},{5... | collective-permute-start | bytes 1769480 | tf_op jit(solution)/shard_map/ppermute | solution.py:45
  326.6 33.2 %collective-permute-start.69 = (bf16[96,6912]{1,0:T(8,128)(2,1)}, bf16[96,6912]{1,0:T(8,128)(2,1)}, u32[]{:S(2)}, u32[]{:S(2)}) collective-permute-start(bf16[96,6912]{1,0:T(8,128)(2,1)} %pad_maximum_fusion.4.refs_10_), channel_id=1, source_target_pairs={{0,24},{4,28},{8,16},{12,20},{16,8},{20,12},{24,0},{28,4},{1,25},{... | collective-permute-start | bytes 3981320 | tf_op jit(solution)/shard_map/ppermute | solution.py:45
  328.5 59.3 %collective-permute-start.68 = (bf16[96,6912]{1,0:T(8,128)(2,1)S(1)}, bf16[96,6912]{1,0:T(8,128)(2,1)}, u32[]{:S(2)}, u32[]{:S(2)}) collective-permute-start(bf16[96,6912]{1,0:T(8,128)(2,1)S(1)} %copy-done.8), channel_id=1, source_target_pairs={{0,16},{4,20},{8,24},{12,28},{16,0},{20,4},{24,8},{28,12},{1,17},{... | collective-permute-start | bytes 3981320 | tf_op jit(solution)/shard_map/ppermute | solution.py:45
  328.9 58.9 %collective-permute-start.67 = (bf16[96,6912]{1,0:T(8,128)(2,1)S(1)}, bf16[96,6912]{1,0:T(8,128)(2,1)}, u32[]{:S(2)}, u32[]{:S(2)}) collective-permute-start(bf16[96,6912]{1,0:T(8,128)(2,1)S(1)} %copy-done.7), channel_id=1, source_target_pairs={{0,8},{4,12},{8,0},{12,4},{16,24},{20,28},{24,16},{28,20},{1,9},{5... | collective-permute-start | bytes 3981320 | tf_op jit(solution)/shard_map/ppermute | solution.py:45
  333.0 57.7 %collective-permute-start.47 = (bf16[2,96,768]{2,1,0:T(8,128)(2,1)}, bf16[2,96,768]{2,1,0:T(8,128)(2,1)}, u32[]{:S(2)}, u32[]{:S(2)}) collective-permute-start(bf16[2,96,768]{2,1,0:T(8,128)(2,1)} %fusion.18.refs_14_), channel_id=1, source_target_pairs={{0,1},{1,0},{2,3},{3,2},{4,5},{5,4},{6,7},{7,6},{8,9},{9,8},{10,11... | collective-permute-start | bytes 884744 | tf_op jit(solution)/shard_map/ppermute | solution.py:50
  352.8 39.0 %collective-permute-start.49 = (bf16[2,96,768]{2,1,0:T(8,128)(2,1)S(1)}, bf16[2,96,768]{2,1,0:T(8,128)(2,1)S(1)}, u32[]{:S(2)}, u32[]{:S(2)}) collective-permute-start(bf16[2,96,768]{2,1,0:T(8,128)(2,1)S(1)} %fusion.19), channel_id=1, source_target_pairs={{0,1},{1,0},{2,3},{3,2},{4,5},{5,4},{6,7},{7,6},{8,9},{9,8},{10,11... | collective-permute-start | bytes 884744 | tf_op jit(solution)/shard_map/ppermute | solution.py:50
  411.5 18.8 %collective-permute-start.50 = (f32[4,13,192]{2,1,0:T(8,128)S(1)}, f32[4,13,192]{2,1,0:T(8,128)S(1)}, u32[]{:S(2)}, u32[]{:S(2)}) collective-permute-start(f32[4,13,192]{2,1,0:T(8,128)S(1)} %maximum_bitcast_fusion), channel_id=1, source_target_pairs={{0,4},{4,0},{8,12},{12,8},{16,20},{20,16},{24,28},{28,24},{1,5},{5... | collective-permute-start | bytes 119816 | tf_op jit(solution)/shard_map/ppermute | solution.py:45
  418.1 28.4 %collective-permute-start.57 = (bf16[384,2304]{1,0:T(8,128)(2,1)}, bf16[384,2304]{1,0:T(8,128)(2,1)}, u32[]{:S(2)}, u32[]{:S(2)}) collective-permute-start(bf16[384,2304]{1,0:T(8,128)(2,1)} %convolution_convert_fusion.4), channel_id=1, source_target_pairs={{0,4},{4,0},{8,12},{12,8},{16,20},{20,16},{24,28},{28,24},{1,5},{5... | collective-permute-start | bytes 5308424 | tf_op jit(solution)/shard_map/ppermute | solution.py:45
  421.6 23.1 %collective-permute-start.56 = (bf16[384,528]{1,0:T(8,128)(2,1)}, bf16[384,528]{1,0:T(8,128)(2,1)}, u32[]{:S(2)}, u32[]{:S(2)}) collective-permute-start(bf16[384,528]{1,0:T(8,128)(2,1)} %pad_maximum_fusion.10), channel_id=1, source_target_pairs={{0,4},{4,0},{8,12},{12,8},{16,20},{20,16},{24,28},{28,24},{1,5},{5... | collective-permute-start | bytes 1216520 | tf_op jit(solution)/shard_map/ppermute | solution.py:45
  441.3 15.1 %collective-permute-start.55 = (f32[13,192]{1,0:T(8,128)S(1)}, f32[13,192]{1,0:T(8,128)S(1)}, u32[]{:S(2)}, u32[]{:S(2)}) collective-permute-start(f32[13,192]{1,0:T(8,128)S(1)} %get-tuple-element.310), channel_id=1, source_target_pairs={{0,3},{1,2},{2,1},{3,0},{4,7},{5,6},{6,5},{7,4},{8,11},{9,10},{10,... | collective-permute-start | bytes 29960 | tf_op jit(solution)/shard_map/ppermute | solution.py:50
  450.2 17.0 %collective-permute-start.60 = (bf16[96,2832]{1,0:T(8,128)(2,1)}, bf16[96,2832]{1,0:T(8,128)(2,1)}, u32[]{:S(2)}, u32[]{:S(2)}) collective-permute-start(bf16[96,2832]{1,0:T(8,128)(2,1)} %pad_maximum_fusion.7), channel_id=1, source_target_pairs={{0,24},{4,28},{8,16},{12,20},{16,8},{20,12},{24,0},{28,4},{1,25},{... | collective-permute-start | bytes 1631240 | tf_op jit(solution)/shard_map/ppermute | solution.py:45
  452.5 23.3 %collective-permute-start.59 = (bf16[96,2832]{1,0:T(8,128)(2,1)}, bf16[96,2832]{1,0:T(8,128)(2,1)}, u32[]{:S(2)}, u32[]{:S(2)}) collective-permute-start(bf16[96,2832]{1,0:T(8,128)(2,1)} %pad_maximum_fusion.6), channel_id=1, source_target_pairs={{0,16},{4,20},{8,24},{12,28},{16,0},{20,4},{24,8},{28,12},{1,17},{... | collective-permute-start | bytes 1631240 | tf_op jit(solution)/shard_map/ppermute | solution.py:45
  454.4 21.4 %collective-permute-start.58 = (bf16[96,2832]{1,0:T(8,128)(2,1)}, bf16[96,2832]{1,0:T(8,128)(2,1)}, u32[]{:S(2)}, u32[]{:S(2)}) collective-permute-start(bf16[96,2832]{1,0:T(8,128)(2,1)} %pad_maximum_fusion.5), channel_id=1, source_target_pairs={{0,8},{4,12},{8,0},{12,4},{16,24},{20,28},{24,16},{28,20},{1,9},{5... | collective-permute-start | bytes 1631240 | tf_op jit(solution)/shard_map/ppermute | solution.py:45
  456.5 5.9 %collective-permute-start.54 = (f32[13,192]{1,0:T(8,128)}, f32[13,192]{1,0:T(8,128)}, u32[]{:S(2)}, u32[]{:S(2)}) collective-permute-start(f32[13,192]{1,0:T(8,128)} %get-tuple-element.309), channel_id=1, source_target_pairs={{0,2},{1,3},{2,0},{3,1},{4,6},{5,7},{6,4},{7,5},{8,10},{9,11},{10,... | collective-permute-start | bytes 29960 | tf_op jit(solution)/shard_map/ppermute | solution.py:50
  456.5 9.3 %collective-permute-start.53 = (f32[13,192]{1,0:T(8,128)S(1)}, f32[13,192]{1,0:T(8,128)}, u32[]{:S(2)}, u32[]{:S(2)}) collective-permute-start(f32[13,192]{1,0:T(8,128)S(1)} %get-tuple-element.308), channel_id=1, source_target_pairs={{0,1},{1,0},{2,3},{3,2},{4,5},{5,4},{6,7},{7,6},{8,9},{9,8},{10,11... | collective-permute-start | bytes 29960 | tf_op jit(solution)/shard_map/ppermute | solution.py:50
  462.4 19.1 %collective-permute-start.72 = (bf16[96,1728]{1,0:T(8,128)(2,1)S(1)}, bf16[96,1728]{1,0:T(8,128)(2,1)S(1)}, u32[]{:S(2)}, u32[]{:S(2)}) collective-permute-start(bf16[96,1728]{1,0:T(8,128)(2,1)S(1)} %concatenate.199), channel_id=1, source_target_pairs={{0,3},{1,2},{2,1},{3,0},{4,7},{5,6},{6,5},{7,4},{8,11},{9,10},{10,... | collective-permute-start | bytes 995336 | tf_op jit(solution)/shard_map/ppermute | solution.py:50
  465.8 29.5 %collective-permute-start.71 = (bf16[96,1728]{1,0:T(8,128)(2,1)S(1)}, bf16[96,1728]{1,0:T(8,128)(2,1)S(1)}, u32[]{:S(2)}, u32[]{:S(2)}) collective-permute-start(bf16[96,1728]{1,0:T(8,128)(2,1)S(1)} %concatenate.198), channel_id=1, source_target_pairs={{0,2},{1,3},{2,0},{3,1},{4,6},{5,7},{6,4},{7,5},{8,10},{9,11},{10,... | collective-permute-start | bytes 995336 | tf_op jit(solution)/shard_map/ppermute | solution.py:50
  467.2 33.2 %collective-permute-start.70 = (bf16[96,1728]{1,0:T(8,128)(2,1)S(1)}, bf16[96,1728]{1,0:T(8,128)(2,1)S(1)}, u32[]{:S(2)}, u32[]{:S(2)}) collective-permute-start(bf16[96,1728]{1,0:T(8,128)(2,1)S(1)} %concatenate.197), channel_id=1, source_target_pairs={{0,1},{1,0},{2,3},{3,2},{4,5},{5,4},{6,7},{7,6},{8,9},{9,8},{10,11... | collective-permute-start | bytes 995336 | tf_op jit(solution)/shard_map/ppermute | solution.py:50
  478.7 27.4 %collective-permute-start.61 = (bf16[96,576]{1,0:T(8,128)(2,1)S(1)}, bf16[96,576]{1,0:T(8,128)(2,1)S(1)}, u32[]{:S(2)}, u32[]{:S(2)}) collective-permute-start(bf16[96,576]{1,0:T(8,128)(2,1)S(1)} %get-tuple-element.280), channel_id=1, source_target_pairs={{0,1},{1,0},{2,3},{3,2},{4,5},{5,4},{6,7},{7,6},{8,9},{9,8},{10,11... | collective-permute-start | bytes 331784 | tf_op jit(solution)/shard_map/ppermute | solution.py:50
  479.3 21.0 %collective-permute-start.64 = (bf16[24,528]{1,0:T(8,128)(2,1)S(1)}, bf16[24,528]{1,0:T(8,128)(2,1)S(1)}, u32[]{:S(2)}, u32[]{:S(2)}) collective-permute-start(bf16[24,528]{1,0:T(8,128)(2,1)S(1)} %get-tuple-element.288), channel_id=1, source_target_pairs={{0,1},{1,0},{2,3},{3,2},{4,5},{5,4},{6,7},{7,6},{8,9},{9,8},{10,11... | collective-permute-start | bytes 76040 | tf_op jit(solution)/shard_map/ppermute | solution.py:50
  481.5 24.7 %collective-permute-start.62 = (bf16[96,576]{1,0:T(8,128)(2,1)S(1)}, bf16[96,576]{1,0:T(8,128)(2,1)S(1)}, u32[]{:S(2)}, u32[]{:S(2)}) collective-permute-start(bf16[96,576]{1,0:T(8,128)(2,1)S(1)} %get-tuple-element.279), channel_id=1, source_target_pairs={{0,2},{1,3},{2,0},{3,1},{4,6},{5,7},{6,4},{7,5},{8,10},{9,11},{10,... | collective-permute-start | bytes 331784 | tf_op jit(solution)/shard_map/ppermute | solution.py:50
  495.4 10.8 %collective-permute-start.63 = (bf16[96,576]{1,0:T(8,128)(2,1)S(1)}, bf16[96,576]{1,0:T(8,128)(2,1)S(1)}, u32[]{:S(2)}, u32[]{:S(2)}) collective-permute-start(bf16[96,576]{1,0:T(8,128)(2,1)S(1)} %get-tuple-element.278), channel_id=1, source_target_pairs={{0,3},{1,2},{2,1},{3,0},{4,7},{5,6},{6,5},{7,4},{8,11},{9,10},{10,... | collective-permute-start | bytes 331784 | tf_op jit(solution)/shard_map/ppermute | solution.py:50
  500.4 5.8 %collective-permute-start.66 = (bf16[24,528]{1,0:T(8,128)(2,1)S(1)}, bf16[24,528]{1,0:T(8,128)(2,1)S(1)}, u32[]{:S(2)}, u32[]{:S(2)}) collective-permute-start(bf16[24,528]{1,0:T(8,128)(2,1)S(1)} %get-tuple-element.286), channel_id=1, source_target_pairs={{0,3},{1,2},{2,1},{3,0},{4,7},{5,6},{6,5},{7,4},{8,11},{9,10},{10,... | collective-permute-start | bytes 76040 | tf_op jit(solution)/shard_map/ppermute | solution.py:50
  (98 other events, 1038.6 us)

commit v4 on v3

--- a/solution.py
+++ b/solution.py
@@ -73,12 +73,15 @@
     return [inputs] + [swap_mp(inputs, s) for s in (1, 2, 3)]
 
 
-def trade_mp(pieces):
-    return (pieces[0],) + tuple(swap_mp(pieces[s], s) for s in (1, 2, 3))
-
-
-def scatter_mp(pieces):
-    return sum(p.astype(f32) for p in trade_mp(pieces))
+def halve_mp(pieces):
+    sent = jnp.concatenate([pieces[1], pieces[3]], axis=1).astype(bf16)
+    return pieces[0], (pieces[2], sent), swap_mp(sent, 1)
+
+
+def halve_more(near, far, got):
+    columns = near.shape[1]
+    far = far[0].astype(f32) + got[:, columns:].astype(f32)
+    return near.astype(f32) + got[:, :columns].astype(f32), swap_mp(far.astype(bf16), 2)
 
 
 def spread_dp(inputs):
@@ -86,7 +89,10 @@
 
 
 def spread_core(pieces):
-    pieces = pieces + [swap_dp(p, 1) for p in pieces]
+    return one_or_all(pieces + [swap_dp(p, 1) for p in pieces])
+
+
+def one_or_all(pieces):
     if pieces[0].shape[0] % 16:
         pieces = [jnp.concatenate(pieces)]
     return tuple(pieces)
@@ -108,21 +114,12 @@
     ]
 
 
-def collect_dp(pieces):
-    total = pieces[0].astype(f32)
-    for i, piece in enumerate(pieces[1:]):
-        total = total + swap_dp(piece, 2 * i + 2).astype(f32)
-    return total
+def trade_dp(pieces, first, last):
+    return [swap_dp(piece, 2 * first + 2 * i) for i, piece in enumerate(pieces[first:last])]
 
 
 def after(value, *events):
     return lax.optimization_barrier((value,) + events)[0]
-
-
-def sum_dp(inputs):
-    for bit in range(dp_bits()):
-        inputs = inputs + swap_dp(inputs, 1 << bit)
-    return inputs
 
 
 def group_sum_features(inputs):
@@ -138,7 +135,6 @@
 def call(
     body, grid, in_specs, out_specs, out_shape, operands, flops, scratch=(), alias=None, events=()
 ):
-    moved = sum(o.size * o.dtype.itemsize for o in operands)
     known, late = len(operands), len(operands) + len(events)
 
     def run(*refs):
@@ -158,10 +154,10 @@
 
 
 def whole(array):
-    return pl.BlockSpec(array.shape, lambda *i, n=array.ndim: (0,) * n)
-
-
-def fetch(pieces, targets, sems):
+    return pl.BlockSpec(array.shape, lambda *i, n=len(array.shape): (0,) * n)
+
+
+def transfers(pieces, targets, sems):
     copies, at = [], 0
     for piece in pieces:
         rows = piece.shape[0]
@@ -174,10 +170,23 @@
                 )
             )
         at += rows
+    return copies
+
+
+def begin(copies):
     for copy in copies:
         copy.start()
+
+
+def finish(copies):
     for copy in copies:
         copy.wait()
+
+
+def fetch(pieces, targets, sems):
+    copies = transfers(pieces, targets, sems)
+    begin(copies)
+    finish(copies)
 
 
 def standard(inputs):
@@ -206,7 +215,7 @@
     out_ref[0, 0] = contract_last(order_ref[...], jnp.concatenate(blocks)).astype(bf16)
 
 
-def memory_in(index, order, parts):
+def memory_in(index, order, parts, events=()):
     _, _, columns, rows = parts[0].shape
     return call(
         memory_in_kernel,
@@ -217,6 +226,7 @@
         jax.ShapeDtypeStruct((2, 2, rows, 4 * columns), bf16),
         (index, order) + tuple(parts),
         8 * rows * rows * 4 * columns,
+        events=events,
     )
 
 
@@ -248,6 +258,29 @@
         jax.ShapeDtypeStruct((2, 2, width // 4, 4 * rows), bf16),
         (index, order) + tuple(a for a, _ in parts),
         8 * (4 * rows) ** 2 * width,
+    )
+
+
+def join_kernel(main, odd_ref, *refs):
+    pieces, out_ref = refs[:-1], refs[-1]
+    odd = odd_ref[0] == 1
+    for c in range(4):
+        out_ref[:, c * main : (c + 1) * main] = pieces[c][:, :main]
+    tails = [p[:, main:].astype(f32) for p in pieces]
+    heads = [jnp.where(odd, tails[c ^ 1], tails[c]) for c in range(4)]
+    out_ref[:, 4 * main :] = jnp.concatenate(heads, axis=1).astype(bf16)
+
+
+def join(main, odd, pieces):
+    rows, columns = pieces[0].shape
+    return call(
+        functools.partial(join_kernel, main),
+        (1,),
+        [pl.BlockSpec(memory_space=pltpu.SMEM)] + [whole(p) for p in pieces],
+        pl.BlockSpec((rows, 4 * columns), lambda i: (0, 0)),
+        jax.ShapeDtypeStruct((rows, 4 * columns), bf16),
+        (odd,) + tuple(pieces),
+        0,
     )
 
 
@@ -454,7 +487,7 @@
         found = jnp.concatenate(parts).T * factor
         for s in range(4):
             target = send_ref if s % 2 else keep_ref
-            target[ch, s // 2] = found[s * part : (s + 1) * part].astype(bf16)
+            target[s // 2, ch] = found[s * part : (s + 1) * part].astype(bf16)
         at = half
         first = jnp.zeros((1, width), f32)
         second = jnp.zeros((1, width), f32)
@@ -536,38 +569,48 @@
 def mlp_weights(width, units, count):
     return [
         pltpu.VMEM((width, width), bf16),
-        pltpu.VMEM((width, units), bf16),
-        pltpu.VMEM((width, units), bf16),
-        pltpu.SemaphoreType.DMA((3 * count,)),
+        pltpu.VMEM((width, 2 * units), bf16),
+        pltpu.SemaphoreType.DMA((count,)),
+        pltpu.SemaphoreType.DMA((count,)),
     ]
 
 
 def mlp_kernel(count, attended_ref, embedded_ref, vec_ref, select_ref, *refs):
     (
         first_ref, normed_ref, active_ref, slope_ref, second_ref, feature_ref,
-        wo_s, wb_s, wh_s, sems,
+        out_s, both_s, out_sems, sems,
     ) = refs[count:]
-    width = embedded_ref.shape[1]
-
-    @pl.when(pl.program_id(0) == 0)
+    units = both_s.shape[1] // 2
+    out_copies = transfers(refs[:count], ((2 * units, out_s),), out_sems)
+    copies = transfers(refs[:count], ((0, both_s),), sems)
+    starting = pl.program_id(0) == 0
+
+    @pl.when(starting)
     def _():
-        units = wb_s.shape[1]
-        fetch(refs[:count], ((0, wb_s), (units, wh_s), (2 * units, wo_s)), sems)
-
-    first = embedded_ref[...] + contract_last(attended_ref[...], wo_s[...])
+        begin(out_copies)
+        begin(copies)
+        finish(out_copies)
+
+    first = embedded_ref[...] + contract_last(attended_ref[...], out_s[...])
     first_ref[...] = first
     unit, _ = standard(first)
     normed = (unit * vec_ref[3:4] + vec_ref[4:5]).astype(bf16)
     normed_ref[...] = normed
     total = first
-    chunk = 512
-    for at in range(0, wh_s.shape[1], chunk):
-        hidden = product(normed, wh_s[:, at : at + chunk])
+
+    @pl.when(starting)
+    def _():
+        finish(copies)
+
+    chunk = units // 4
+    for s in range(4):
+        at = s * chunk
+        hidden = product(normed, both_s[:, 2 * at + chunk : 2 * at + 2 * chunk])
         value, slope = gelu_pair(hidden)
         value = value.astype(bf16)
         active_ref[:, at : at + chunk] = value
         slope_ref[:, at : at + chunk] = slope.astype(bf16)
-        total = total + contract_last(value, wb_s[:, at : at + chunk])
+        total = total + contract_last(value, both_s[:, 2 * at : 2 * at + chunk])
     second_ref[...] = total
     unit, _ = standard(total)
     final = unit * vec_ref[5:6] + vec_ref[6:7]
@@ -617,15 +660,18 @@
 ):
     (
         branch_ref, hidden_ref, attn_ref, first_grad_ref, attended_ref, sums_ref,
-        wo_s, wb_s, wh_s, sems,
+        out_s, both_s, out_sems, sems,
     ) = refs[count:]
-    width = second_ref.shape[1]
-
-    @pl.when(pl.program_id(0) == 0)
+    units = both_s.shape[1] // 2
+    out_copies = transfers(refs[:count], ((2 * units, out_s),), out_sems)
+    copies = transfers(refs[:count], ((0, both_s),), sems)
+    starting = pl.program_id(0) == 0
+
+    @pl.when(starting)
     def _():
+        begin(copies)
+        begin(out_copies)
         sums_ref[...] = jnp.zeros_like(sums_ref)
-        units = wb_s.shape[1]
-        fetch(refs[:count], ((0, wb_s), (units, wh_s), (2 * units, wo_s)), sems)
 
     pull = lax.dot_general(
         select_ref[0],
@@ -640,13 +686,26 @@
     second_grad = standard_back(pull * vec_ref[5:6], unit, scale)
     branch = second_grad.astype(bf16)
     branch_ref[...] = branch
-    chunk = 512
+
+    @pl.when(starting)
+    def _():
+        finish(copies)
+
+    chunk = units // 4
     normed_grad = jnp.zeros(second_grad.shape, f32)
-    for at in range(0, wh_s.shape[1], chunk):
-        active_grad = product(branch, wb_s[:, at : at + chunk])
+    for s in range(4):
+        at = s * chunk
+        active_grad = product(branch, both_s[:, 2 * at : 2 * at + chunk])
         hidden_grad = (active_grad * slope_ref[:, at : at + chunk].astype(f32)).astype(bf16)
         hidden_ref[:, at : at + chunk] = hidden_grad
-        normed_grad = normed_grad + contract_last(hidden_grad, wh_s[:, at : at + chunk])
+        normed_grad = normed_grad + contract_last(
+            hidden_grad, both_s[:, 2 * at + chunk : 2 * at + 2 * chunk]
+        )
+
+    @pl.when(starting)
+    def _():
+        finish(out_copies)
+
     unit, scale = standard(first_ref[...])
     sums_ref[0:1] += jnp.sum(normed_grad * unit, axis=0, keepdims=True)
     sums_ref[1:2] += jnp.sum(normed_grad, axis=0, keepdims=True)
@@ -654,7 +713,7 @@
     first_grad_ref[...] = first_grad
     attn = first_grad.astype(bf16)
     attn_ref[...] = attn
-    attended_ref[...] = product(attn, wo_s[...]).astype(bf16)
+    attended_ref[...] = product(attn, out_s[...]).astype(bf16)
 
 
 def mlp_back(pull, select, second, first, slope, vec, weights, events=()):
@@ -696,150 +755,205 @@
 
 
 def embed_back_kernel(
-    count, dq_ref, pool_ref, key_ref, value_ref, taps_ref, embedded_ref, first_ref, vec_ref, *refs
+    count, dq_ref, key_ref, value_ref, taps_ref, embedded_ref, first_ref, normed_ref, patch_ref,
+    vec_ref, head_ref, more_ref, *refs
 ):
-    projected_ref, grad_ref, sums_ref, taps_out, qk_s, v_s, sems = refs[count:]
-    width = embedded_ref.shape[1]
-
-    @pl.when(pl.program_id(0) == 0)
+    pools = refs[: 3 * MICRO]
+    (
+        near_ref, far_ref, taps_out, qk_s, v_s, pool_s, sums_s, normed_s, projected_s, grad_s,
+        patch_s, sems,
+    ) = refs[3 * MICRO + count :]
+    rows, width = embedded_ref.shape
+    step = pl.program_id(0)
+
+    @pl.when(step == 0)
     def _():
-        sums_ref[...] = jnp.zeros_like(sums_ref)
+        sums_s[...] = jnp.zeros_like(sums_s)
+        sums_s[3:7] = more_ref[0:4]
+        sums_s[8 : 8 + head_ref.shape[0]] = head_ref[...]
         taps_out[...] = jnp.zeros_like(taps_out)
-        fetch(refs[:count], ((0, qk_s), (2 * width, v_s)), sems)
-
-    projected_ref[:, :width] = dq_ref[...]
-    rows = pool_ref.shape[2]
+        patch_s[...] = jnp.zeros_like(patch_s)
+        for m in range(MICRO):
+            kept, got, far = pools[3 * m : 3 * m + 3]
+            for ch in range(2):
+                pool_s[m, ch] = (
+                    kept[0, ch].astype(f32) + got[0, ch].astype(f32) + far[ch].astype(f32)
+                )
+        fetch(refs[3 * MICRO : 3 * MICRO + count], ((0, qk_s), (2 * width, v_s)), sems)
+
+    at = pl.multiple_of(step * rows, 128)
+    here = pl.ds(at, rows)
+    projected_s[here, :width] = dq_ref[...]
+    pooled = rows // 4
     for ch, raw_ref in ((0, key_ref), (1, value_ref)):
-        pool = pool_ref[0, ch]
+        pool = pool_s[step, ch]
         for t in range(4):
-            projected_ref[t * rows : (t + 1) * rows, (1 + ch) * width : (2 + ch) * width] = (
-                pool * taps_ref[ch, t : t + 1]
-            ).astype(bf16)
-            raw = raw_ref[t * rows : (t + 1) * rows].astype(f32)
+            projected_s[
+                pl.ds(at + t * pooled, pooled), (1 + ch) * width : (2 + ch) * width
+            ] = (pool * taps_ref[ch, t : t + 1]).astype(bf16)
+            raw = raw_ref[t * pooled : (t + 1) * pooled].astype(f32)
             taps_out[4 * ch + t : 4 * ch + t + 1] += jnp.sum(pool * raw, axis=0, keepdims=True)
-    normed_grad = contract_last(projected_ref[:, : 2 * width], qk_s[...])
-    normed_grad = normed_grad + contract_last(projected_ref[:, 2 * width :], v_s[...])
+    normed_grad = contract_last(projected_s[here, : 2 * width], qk_s[...])
+    normed_grad = normed_grad + contract_last(projected_s[here, 2 * width :], v_s[...])
     unit, scale = standard(embedded_ref[...])
-    sums_ref[1:2] += jnp.sum(normed_grad * unit, axis=0, keepdims=True)
-    sums_ref[2:3] += jnp.sum(normed_grad, axis=0, keepdims=True)
+    sums_s[1:2] += jnp.sum(normed_grad * unit, axis=0, keepdims=True)
+    sums_s[2:3] += jnp.sum(normed_grad, axis=0, keepdims=True)
     grad = standard_back(normed_grad * vec_ref[1:2], unit, scale) + first_ref[...]
     grad = grad.astype(bf16)
-    grad_ref[...] = grad
-    sums_ref[0:1] += jnp.sum(grad.astype(f32), axis=0, keepdims=True)
-
-
-def embed_back(dq, pool, keys, values, taps, embedded, first_grad, vec, weights, events=()):
+    sums_s[0:1] += jnp.sum(grad.astype(f32), axis=0, keepdims=True)
+    normed_s[:, here] = normed_ref[...].T
+    grad_s[:, here] = grad.T
+    patch_s[here, : patch_ref.shape[1]] = patch_ref[...]
+
+    @pl.when(step == MICRO - 1)
+    def _():
+        half = width // 2
+        edge = 3 * width + patch_s.shape[1]
+        for out_ref, top in ((far_ref, half), (near_ref, 0)):
+            part = slice(top, top + half)
+            for c in range(3):
+                out_ref[:, c * width : (c + 1) * width] = product(
+                    normed_s[part], projected_s[:, c * width : (c + 1) * width]
+                ).astype(bf16)
+            out_ref[:, 3 * width : edge] = product(grad_s[part], patch_s[...]).astype(bf16)
+            out_ref[:, edge:] = sums_s[:, part].T.astype(bf16)
+
+
+def embed_back(
+    dq, keys, values, taps, embedded, first_grad, normed, patches, vec, head, more, pools, weights,
+    events=(),
+):
     total, width = embedded.shape
     rows = total // MICRO
+    patch = patches.shape[1]
+    edge = patch + (-patch % 128)
+    columns = 3 * width + edge + 128
 
     def tile(columns):
         return pl.BlockSpec((rows, columns), lambda i: (i, 0))
 
+    operands = (dq, keys, values, taps, embedded, first_grad, normed, patches, vec, head, more)
+    half = pl.BlockSpec((width // 2, columns), lambda i: (0, 0))
     return call(
         functools.partial(embed_back_kernel, len(weights)),
         (MICRO,),
-        [
-            tile(width),
-            pl.BlockSpec((1, 2, rows // 4, width), lambda i: (i, 0, 0, 0)),
-            tile(width),
-            tile(width),
-            whole(taps),
-            tile(width),
-            tile(width),
-            whole(vec),
-        ]
+        [tile(width)] * 3
+        + [whole(taps)]
+        + [tile(width)] * 3
+        + [tile(patch)]
+        + [whole(a) for a in (vec, head, more) + pools]
         + [pl.BlockSpec(memory_space=pl.ANY)] * len(weights),
-        [
-            tile(3 * width),
-            tile(width),
-            pl.BlockSpec((8, width), lambda i: (0, 0)),
-            pl.BlockSpec((8, width), lambda i: (0, 0)),
-        ],
-        [
-            jax.ShapeDtypeStruct((total, 3 * width), bf16),
-            jax.ShapeDtypeStruct((total, width), bf16),
-            jax.ShapeDtypeStruct((8, width), f32),
+        [half, half, pl.BlockSpec((8, width), lambda i: (0, 0))],
+        [
+            jax.ShapeDtypeStruct((width // 2, columns), bf16),
+            jax.ShapeDtypeStruct((width // 2, columns), bf16),
             jax.ShapeDtypeStruct((8, width), f32),
         ],
-        (dq, pool, keys, values, taps, embedded, first_grad, vec) + weights,
+        operands + pools + weights,
         2 * total * width * 3 * width,
         scratch=[
             pltpu.VMEM((width, 2 * width), bf16),
             pltpu.VMEM((width, width), bf16),
+            pltpu.VMEM((MICRO, 2, rows // 4, width), f32),
+            pltpu.VMEM((128, width), f32),
+            pltpu.VMEM((width, total), bf16),
+            pltpu.VMEM((total, 3 * width), bf16),
+            pltpu.VMEM((width, total), bf16),
+            pltpu.VMEM((total, edge), bf16),
             pltpu.SemaphoreType.DMA((2 * len(weights),)),
         ],
         events=events,
     )
 
 
-def squares_kernel(count, *refs):
-    grads = refs[:count]
-    names = refs[count:]
-    rest_ref, share_ref, place_ref = names[:3]
-    attn_out, small_out, total_out = names[3:]
-    attn = grads[0][...].astype(f32)
-    small = grads[count // 2][...].astype(f32)
-    for i in range(1, count // 2):
-        attn = attn + grads[i][...].astype(f32)
-        small = small + grads[count // 2 + i][...].astype(f32)
-    attn_out[...] = attn
-    small_out[...] = small
-    share = share_ref[...] * place_ref[...]
-    total = (
-        jnp.sum(attn * attn)
-        + jnp.sum(small * small)
-        + jnp.sum(rest_ref[...] * rest_ref[...])
-        + jnp.sum(share * share_ref[...])
-    )
-    total_out[...] = jnp.zeros_like(total_out) + total
-
-
-def squares_of(attn, small, rest, share, place):
-    operands = attn + small + (rest, share, place)
+def squares_kernel(*refs):
+    grads, flat_ref, outs = refs[:6], refs[6], refs[7:]
+    total = 0.0
+    for i in range(3):
+        found = grads[2 * i][...].astype(f32) + grads[2 * i + 1][...].astype(f32)
+        outs[i][...] = found
+        total = total + jnp.sum(found * found)
+    rows = flat_ref.shape[0]
+    outs[3][...] = jnp.zeros_like(outs[3]) + total
+    outs[3][:rows] = flat_ref[...]
+
+
+def squares_of(attn, small, rest, flat):
+    operands = tuple(attn) + tuple(small) + tuple(rest) + (flat,)
+    rows = flat.shape[0] + (-flat.shape[0] % 8)
+    rows += 8 * (rows == flat.shape[0])
+    shapes = [jax.ShapeDtypeStruct(g[0].shape, f32) for g in (attn, small, rest)]
+    shapes.append(jax.ShapeDtypeStruct((rows, flat.shape[1]), f32))
     return call(
-        functools.partial(squares_kernel, len(attn) + len(small)),
+        squares_kernel,
         (1,),
         [whole(o) for o in operands],
-        [whole(attn[0]), whole(small[0]), pl.BlockSpec((8, 128), lambda i: (0, 0))],
-        [
-            jax.ShapeDtypeStruct(attn[0].shape, f32),
-            jax.ShapeDtypeStruct(small[0].shape, f32),
-            jax.ShapeDtypeStruct((8, 128), f32),
-        ],
+        [whole(o) for o in shapes],
+        shapes,
         operands,
         0,
     )
 
 
-def update_kernel(rates, one_ref, two_ref, boxes_ref, *refs):
+def update_kernel(rates, patch, odd_ref, one_ref, two_ref, *refs):
     count = len(rates)
-    grads, weights, moments, averages = (refs[i * count : (i + 1) * count] for i in range(4))
-    outs = refs[4 * count :]
-    boxes = boxes_ref[0:1, 0:1]
-    norm = jnp.sqrt(one_ref[0:1, 0:1] + two_ref[0:1, 0:1]) / boxes
-    outs[0][...] = norm
+    attn_ref, small_ref, rest_ref = refs[:3]
+    weights, moments, averages = (refs[3 + i * count : 3 + (i + 1) * count] for i in range(3))
+    outs = refs[3 + 3 * count :]
+    heads = weights[6].shape[0] * 3
+    blocks = []
+    square = one_ref[52:53, 0:1] + two_ref[52:53, 0:1]
+    spot = lax.broadcasted_iota(jnp.int32, (13, one_ref.shape[1]), 1)
+    row = lax.broadcasted_iota(jnp.int32, (13, one_ref.shape[1]), 0)
+    counted = (row < 12) | (spot < heads)
+    for c in range(4):
+        far = 13 * (c ^ 2)
+        block = one_ref[13 * c : 13 * c + 13] + two_ref[far : far + 13]
+        kept = jnp.where(counted, block, 0.0)
+        square = square + jnp.sum(kept * kept)
+        blocks.append(block)
+    mine = jnp.where(odd_ref[0] == 1, blocks[1], blocks[0])
+    boxes = blocks[0][12:13, heads + 1 : heads + 2]
+    norm = jnp.sqrt(square) / boxes
+    lane = lax.broadcasted_iota(jnp.int32, (1, 128), 1)
+    loss = blocks[0][12:13, heads : heads + 1]
+    outs[0][...] = jnp.where(lane == 0, loss, jnp.where(lane == 1, boxes, norm))
     scaling = jnp.minimum(1.0, THRESHOLD / norm) / boxes
-    for i, rate in enumerate(rates):
-        factor = scaling if weights[i].ndim == 2 else scaling[None]
-        grad = grads[i][...] * factor
-        moment = MOMENTUM * moments[i][...] + grad
-        updated = weights[i][...] - rate * (grad + MOMENTUM * moment)
-        outs[1 + i][...] = updated
-        outs[1 + count + i][...] = moment
-        outs[1 + 2 * count + i][...] = AVERAGING * averages[i][...] + (1.0 - AVERAGING) * updated
+    hidden = weights[0].shape[1] - attn_ref.shape[1]
+    edge = small_ref.shape[1] - 128
+    classes = weights[3].shape[1]
+    tail = small_ref[:, edge:]
+
+    def step(i, at, grad):
+        grad = grad * scaling
+        moment = MOMENTUM * moments[i][at] + grad
+        updated = weights[i][at] - rates[i] * (grad + MOMENTUM * moment)
+        outs[1 + i][at] = updated
+        outs[1 + count + i][at] = moment
+        outs[1 + 2 * count + i][at] = AVERAGING * averages[i][at] + (1.0 - AVERAGING) * updated
         if i < 2:
-            outs[1 + 3 * count + i][...] = updated.astype(bf16)
-
-
-def update(one, two, boxes, grads, weights, moments, averages, rates):
-    operands = (one, two, boxes) + grads + weights + moments + averages
+            outs[1 + 3 * count + i][at] = updated.astype(bf16)
+
+    step(0, ..., jnp.concatenate([attn_ref[...], rest_ref[:, :hidden]], axis=1))
+    step(1, ..., rest_ref[:, hidden:])
+    step(2, ..., small_ref[:, :patch])
+    step(3, ..., tail[:, 8 : 8 + classes])
+    step(4, ..., tail.T[:7])
+    for t in range(6):
+        step(5, t, mine[2 * t : 2 * t + 2])
+    for h in range(heads // 3):
+        step(6, slice(h, h + 1), mine[12:13, 3 * h : 3 * h + 3])
+
+
+def update(odd, one, two, grads, patch, weights, moments, averages, rates):
+    operands = (odd, one, two) + grads + weights + moments + averages
     kept = [jax.ShapeDtypeStruct(w.shape, f32) for w in weights]
-    shapes = [jax.ShapeDtypeStruct((1, 1), f32)] + kept * 3
+    shapes = [jax.ShapeDtypeStruct((1, 128), f32)] + kept * 3
     shapes = shapes + [jax.ShapeDtypeStruct(w.shape, bf16) for w in weights[:2]]
     return call(
-        functools.partial(update_kernel, rates),
+        functools.partial(update_kernel, rates, patch),
         (1,),
-        [whole(o) for o in operands],
+        [pl.BlockSpec(memory_space=pltpu.SMEM)] + [whole(o) for o in operands[1:]],
         [pl.BlockSpec(o.shape, lambda i, n=len(o.shape): (0,) * n) for o in shapes],
         shapes,
         operands,
@@ -928,17 +1042,26 @@
     )
     taps_pos = jnp.concatenate(in_three(taps_pos)).reshape(sub, -1)
     small = jnp.concatenate([jnp.concatenate(columns_in).T, taps_pos], axis=1).astype(bf16)
+    strip = -(-small.shape[1] // 512) * 128
+    small = jnp.pad(small, ((0, 0), (0, 4 * strip - small.shape[1])))
+    small = jnp.concatenate([small[:, i * strip : (i + 1) * strip] for i in range(4)])
     up_low = up_weight.astype(bf16)
     down_low = down_weight.astype(bf16)
-    pieces = gather_mp(up_low[:, : 3 * head_cols])
-    small = gather_mp(small)
-    place = jnp.arange(4 * sub)
-    small_mine = product(
-        one_hot_rows(((place // sub) ^ mp_index) * sub + place % sub, 4 * sub),
-        jnp.concatenate([p[:, : edge + 128] for p in small]),
+    pieces = gather_mp(jnp.concatenate([up_low[:, : 3 * head_cols], small], axis=1))
+    place = jnp.arange(16 * sub)
+    source = (
+        (((place // sub) % 4) ^ mp_index) * 4 * sub + place // (4 * sub) * sub + place % sub
+    )
+    small = product(
+        one_hot_rows(source, 16 * sub), jnp.concatenate([p[:, 3 * head_cols :] for p in pieces])
     ).astype(bf16)
-    taps_pos = jnp.stack(pick([p[:, edge + 128 :] for p in small])).reshape(4, 3, 13, head_cols)
-    taps_pos = jnp.sum(taps_pos.astype(f32), axis=1)
+    small = jnp.concatenate(
+        [small[i * 4 * sub : (i + 1) * 4 * sub] for i in range(4)], axis=1
+    )
+    small_mine = small[:, : edge + 128]
+    taps_pos = small[:, edge + 128 : edge + 128 + 39 * head_cols // sub]
+    taps_pos = jnp.sum(taps_pos.reshape(4, 3, 13, head_cols).astype(f32), axis=1)
+    taps_pos = jnp.where(upper == 2, jnp.roll(taps_pos, 2, axis=0), taps_pos)
     conv_all = taps_pos[:, :12].transpose(1, 0, 2).reshape(2, 6, width)
     rel_bias = taps_pos[:, 12, : position_bias.size].reshape(heads, 3)
     weights = jnp.concatenate(
@@ -947,23 +1070,18 @@
         axis=1,
     )
     weights = spread_core(spread_dp(weights))
-    q_pieces = pieces
     pieces = gather_mp(
         after(
-            jnp.concatenate([down_low, up_low[:, 3 * head_cols :]], axis=1), *pieces, *small
+            jnp.concatenate(
+                [down_low[:, head_cols:], up_low[:, 3 * head_cols :], down_low[:, :head_cols]],
+                axis=1,
+            ),
+            *pieces,
         )
     )
-    patches_t = regroup(after(patches.transpose(0, 2, 1), *q_pieces, *small))
-    pieces = [after(p, *weights, patches_t) for p in pieces]
-    edges = (head_cols, head_cols + hidden_cols, head_cols + 2 * hidden_cols)
-    rest = spread_dp(
-        jnp.concatenate(
-            [p[:, edges[0] : edges[1]] for p in pieces]
-            + [p[:, edges[1] :] for p in pieces]
-            + pick([p[:, : edges[0]] for p in pieces]),
-            axis=1,
-        )
-    )
+    rest = join(2 * hidden_cols, across[None], pieces)
+    patches_t = regroup(after(patches.transpose(0, 2, 1), rest))
+    rest = [rest, swap_dp(rest, 2), swap_dp(rest, 4)]
 
     place = jnp.arange(rows)
     token = 8 * (place % eighth) + 4 * ((place // eighth) % 2) + place // (2 * eighth)
@@ -982,28 +1100,15 @@
         pools,
         vectors,
         head_low,
-    ) = embed(patches_t, token_order, conv_all, weights, classes)
-    stored = []
-    for m in range(MICRO):
-        one = swap_dp(pools[m : m + 1], 1)
-        two = swap_mp(pools[m : m + 1], 1)
-        three = swap_dp(two, 1)
-        stored.append([(pools, m), (one, 0), (two, 0), (three, 0)])
-    memory_t = regroup(after(memory.transpose(0, 1, 3, 2), patches_t))
-    mem_two = swap_mp(memory_t, 1)
-    mem_parts = (memory_t, swap_dp(memory_t, 1), mem_two, swap_dp(mem_two, 1))
-    mem_full = memory_in(
-        jnp.stack(
-            [
-                (((c ^ upper) // 2) ^ core) + 2 * (((c ^ upper) % 2) ^ across)
-                for c in range(4)
-            ]
-        ),
-        mem_order,
-        mem_parts,
-    )
-
-    stored = [[(mem_full, 0)], [(mem_full, 1)]] + stored
+    ) = embed(patches_t, token_order, conv_all, weights, classes, events=tuple(rest[1:]))
+    rest_late = after(rest[0], *rest[1:])
+    rest_late = [swap_dp(rest_late, b) for b in range(6, dp_count, 2)]
+    two = swap_mp(pools, 1)
+    gathered = (pools, swap_dp(pools, 1), two, swap_dp(two, 1))
+    stored = [[(a, m) for a in gathered] for m in range(MICRO)]
+    memory_t = regroup(after(memory.transpose(0, 1, 3, 2), pools))
+    mem_two = swap_mp(after(memory_t, two), 1)
+    stored = [None, None] + stored
 
     part_quarter = [2 * (core ^ (s % 2)) + (across ^ (s // 2)) for s in range(4)]
     pool_place = jnp.arange(pooled)
@@ -1029,10 +1134,48 @@
     attended, saved = None, {}
     for m in (2, 1, 0):
         attended, probs, keys, values = attend(
-            m, query, conv_all, key_bias(m), stored[m + 2], stored[m + 1], stored[m], attended
+            m, query, conv_all, key_bias(m), stored[m + 2], stored[m + 1], stored[m], attended,
+            events=tuple(rest_late) if m == 0 else (),
         )
         saved[m] = (keys, values, probs)
-    rest = spread_core([after(p, attended) for p in rest])
+        if m == 2:
+            rest_core = [swap_dp(after(p, attended), 1) for p in rest]
+        if m == 1:
+            late_core = [swap_dp(after(p, attended), 1) for p in rest_late]
+        if m > 1:
+            target_row = jnp.arange(4 * pooled)
+            target_quarter, target_rest = target_row // pooled, target_row % pooled
+            source_row = (
+                (((target_quarter // 2) ^ core) + 2 * ((target_quarter % 2) ^ across)) * pooled
+                + (target_rest % 2) * half_pool
+                + target_rest // 2
+            )
+            new_memory = memory_out(
+                (quarter ^ upper)[None],
+                one_hot_rows(source_row, 4 * pooled).T,
+                stored[3] + stored[4],
+            )
+            mem_two = after(mem_two, attended)
+            mem_parts = (
+                memory_t,
+                swap_dp(after(memory_t, attended), 1),
+                mem_two,
+                swap_dp(mem_two, 1),
+            )
+            mem_full = memory_in(
+                jnp.stack(
+                    [
+                        (((c ^ upper) // 2) ^ core) + 2 * (((c ^ upper) % 2) ^ across)
+                        for c in range(4)
+                    ]
+                ),
+                mem_order,
+                mem_parts,
+                events=(new_memory,),
+            )
+            new_memory = regroup(new_memory)
+            stored[:2] = [[(mem_full, 0)], [(mem_full, 1)]]
+    rest = one_or_all(rest + rest_late + rest_core + late_core)
 
     position = quarter * rows + token
     within = position % FRAME
@@ -1046,22 +1189,9 @@
         f32
     )
     select = inside.astype(f32) / denominator[:, :, None]
-    target_row = jnp.arange(4 * pooled)
-    target_quarter, target_rest = target_row // pooled, target_row % pooled
-    source_row = (
-        (((target_quarter // 2) ^ core) + 2 * ((target_quarter % 2) ^ across)) * pooled
-        + (target_rest % 2) * half_pool
-        + target_rest // 2
-    )
-    new_memory = memory_out(
-        (quarter ^ upper)[None],
-        one_hot_rows(source_row, 4 * pooled).T,
-        stored[3] + stored[4],
-    )
     first_res, normed_mlp, active, slope, second_res, feature = mlp(
-        attended, embedded, vectors, select, rest, events=(new_memory,)
-    )
-    new_memory = regroup(new_memory)
+        attended, embedded, vectors, select, rest
+    )
     feature = after(feature.reshape(MICRO * boxes, width), new_memory)
     feature = group_sum_features(feature).astype(bf16)
     logits = contract_last(feature, head_low)
@@ -1071,7 +1201,7 @@
     loss_part = jnp.sum((jax.nn.softplus(logits) - target * logits) * keep) * lead
     grad_logits = ((jax.nn.sigmoid(logits) - target) * keep).astype(bf16)
 
-    grad_head = contract_rows(feature, grad_logits) * lead
+    grad_head = contract_rows(grad_logits, feature) * lead
     grad_feature = product(grad_logits, head_low).reshape(MICRO, boxes, width)
     grad_branch, grad_hidden, grad_attn, grad_first, grad_attended, sums = mlp_back(
         grad_feature, select, second_res, first_res, slope, vectors, rest
@@ -1088,91 +1218,87 @@
 
     dq, pool_grads, bias_grad, mem_taps = None, [], 0.0, 0.0
     events = tuple(rest_pieces)
+    rest_found = trade_dp(rest_pieces, 1, 3)
     for m in range(MICRO):
         keys, values, probs = saved[m]
         dq, kept, sent, taps_part, bias_part = attend_back(
             m, query, keys, values, probs, grad_attended, stored[m + 1], stored[m], dq, events
         )
         got = swap_dp(sent, 1)
-        away = (kept[:, 1].astype(f32) + got[:, 1].astype(f32)).astype(bf16)
-        mine = kept[:, 0].astype(f32) + got[:, 0].astype(f32)
-        pool_grads.append(mine + swap_mp(away, 1).astype(f32))
+        away = (kept[1].astype(f32) + got[1].astype(f32)).astype(bf16)
+        pool_grads.extend([kept, got, swap_mp(away, 1)])
         bias_grad = bias_grad + bias_part
         mem_taps = mem_taps + taps_part
         events = (away,)
-    projected_grad, embedded_grad, embed_sums, taps_grad = embed_back(
+        if m == 1:
+            events = (away, pool_grads[2]) + tuple(rest_found)
+            rest_pieces[3:] = [after(p, *rest_found) for p in rest_pieces[3:]]
+            rest_found += trade_dp(rest_pieces, 3, None)
+    rest_total = sum((f.astype(f32) for f in rest_found), rest_pieces[0].astype(f32))
+    units = 4 * hidden_cols
+    rest_pieces = []
+    out_blocks = pick(
+        [
+            rest_total[:, 2 * units + c * head_cols : 2 * units + (c + 1) * head_cols]
+            for c in range(4)
+        ]
+    )
+    for s in range(4):
+        piece = jnp.concatenate(
+            [
+                rest_total[:, units + s * hidden_cols : units + (s + 1) * hidden_cols],
+                out_blocks[s],
+                rest_total[:, s * hidden_cols : (s + 1) * hidden_cols],
+            ],
+            axis=1,
+        )
+        rest_pieces.append(piece)
+    rest_near, rest_far, rest_got = halve_mp(rest_pieces)
+    attn_near, attn_far, taps_grad = embed_back(
         dq,
-        jnp.stack(pool_grads),
         raw_keys,
         raw_values,
         conv_all,
         embedded,
         grad_first,
+        normed,
+        patches_in,
         vectors,
+        grad_head,
+        sums,
+        tuple(pool_grads),
         weights,
-    )
-    rest_total = collect_dp(rest_pieces)
-    grad_vectors = jnp.concatenate([embed_sums[:3], sums[:4]])
-
-    def small_grad(at):
-        return jnp.concatenate(
-            [
-                contract_rows(embedded_grad[:, at : at + half], patches_in),
-                grad_head[at : at + half],
-                grad_vectors[:, at : at + half].T,
-            ],
-            axis=1,
-        ).astype(bf16)
-
-    attn_far = [small_grad(half), weight_grad(normed, projected_grad, half)]
-    attn_near = [small_grad(0), weight_grad(normed, projected_grad, 0)]
-    rest_total = after(rest_total, *attn_far)
-    units = 4 * hidden_cols
-    rest_pieces = []
-    out_blocks = pick(
-        [
-            rest_total[:, 2 * units + c * head_cols : 2 * units + (c + 1) * head_cols]
-            for c in range(4)
-        ]
-    )
-    for s in range(4):
-        piece = jnp.concatenate(
-            [
-                out_blocks[s],
-                rest_total[:, s * hidden_cols : (s + 1) * hidden_cols],
-                rest_total[:, units + s * hidden_cols : units + (s + 1) * hidden_cols],
-            ],
-            axis=1,
-        )
-        rest_pieces.append(piece if s == 0 else piece.astype(bf16))
-    rest_mine = scatter_mp(rest_pieces)
-    attn_total = collect_dp(halve_dp(attn_near, attn_far))
-    small_size = patch + classes + 7
-    small_total = attn_total[:, :small_size].astype(bf16)
-    small_parts = trade_mp(
+        events=(rest_near,) + rest_far,
+    )
+    attn_pieces = halve_dp([attn_near], [attn_far])
+    attn_found = trade_dp(attn_pieces, 1, None)
+    rest_got = after(rest_got, *attn_pieces)
+    columns = rest_near.shape[1]
+    far = (rest_far[0].astype(f32) + rest_got[:, columns:].astype(f32)).astype(bf16)
+    rest_mine = (rest_near + rest_got[:, :columns].astype(f32), swap_mp(far, 2))
+    attn_found[-1] = after(attn_found[-1], far)
+    attn_total = sum((f.astype(f32) for f in attn_found), attn_pieces[0].astype(f32))
+    small_total = attn_total[:, 3 * width :]
+    small_parts = halve_more(*halve_mp(
         [
             lax.dynamic_slice_in_dim(small_total, (mp_index ^ s) * sub, sub, axis=0)
             for s in range(4)
         ]
-    )
-    attn_parts = trade_mp(
+    ))
+    attn_parts = halve_more(*halve_mp(
         pick(
             [
                 jnp.concatenate(
                     [
-                        attn_total[
-                            :,
-                            small_size + (4 * j + c) * head_cols : small_size
-                            + (4 * j + c + 1) * head_cols,
-                        ]
+                        attn_total[:, (4 * j + c) * head_cols : (4 * j + c + 1) * head_cols]
                         for j in range(3)
                     ],
                     axis=1,
-                ).astype(bf16)
+                )
                 for c in range(4)
             ]
         )
-    )
+    ))
 
     count_local = jnp.sum(box_count).astype(f32) * (mp_index == 0).astype(f32)
     taps_rows = jnp.stack(
@@ -1192,32 +1318,18 @@
     )
     last = jnp.pad(last, ((0, 0), (0, head_cols - last.shape[1])))
     flat = jnp.concatenate([taps_rows, last[None]]).transpose(1, 0, 2)
-    flat = sum_dp(flat)
-    flat = scatter_mp(pick([flat[c] for c in range(4)]))
-    loss_global = flat[12, own_heads * 3]
-    box_total = flat[12, own_heads * 3 + 1]
-    spot_row = jnp.arange(13)[:, None]
-    spot_column = jnp.arange(head_cols)[None, :]
-    counted = ((spot_row < 12) | (spot_column < own_heads * 3)).astype(f32) / dp_count
-    attn_mine, small_mine, squares = squares_of(attn_parts, small_parts, rest_mine, flat, counted)
+    attn_mine, small_mine, rest_mine, both = squares_of(
+        attn_parts, small_parts, rest_mine, flat.reshape(52, head_cols)
+    )
     for bit in range(dp_bits()):
-        squares = squares + swap_dp(squares, 1 << bit)
-    squares = squares + swap_mp(squares, 1)
-    squares_two = swap_mp(squares, 2)
+        both = both + swap_dp(both, 1 << bit)
+    both = both + swap_mp(both, 1)
+    both_two = swap_mp(both, 2)
 
     def turned(arrays):
         up, down, embed_part, head, vector, conv, position = arrays
         return (up, down, embed_part.T, head.T, vector, conv.transpose(1, 0, 2), position)
 
-    grads = (
-        jnp.concatenate([attn_mine, rest_mine[:, head_cols + hidden_cols :]], axis=1),
-        rest_mine[:, : head_cols + hidden_cols],
-        small_mine[:, :patch],
-        small_mine[:, patch : patch + classes],
-        small_mine[:, patch + classes :].T,
-        flat[:12].reshape(6, 2, head_cols),
-        flat[12, : own_heads * 3].reshape(own_heads, 3),
-    )
     masters = (
         up_weight,
         down_weight,
@@ -1247,16 +1359,17 @@
     )
     rates = (LEARNING,) * 4 + (VECTOR_LEARNING,) * 3
     made = update(
-        squares,
-        squares_two,
-        box_total.reshape(1, 1),
-        grads,
+        across[None],
+        both,
+        both_two,
+        (attn_mine, small_mine, rest_mine),
+        patch,
         turned(masters),
         turned(moments),
         turned(averages),
         rates,
     )
-    grad_norm = made[0].reshape(())
+    loss_global, box_total, grad_norm = (made[0][0, i] for i in range(3))
     results = []
     for i in range(3):
         results.extend(turned(made[1 + 7 * i : 8 + 7 * i]))

time: 541 us -> 489 us (0.904)
  other arithmetic: 60.2 us -> 37.4 us
  local copies, waits for them, and re-layouts: 43.1 us -> 22.9 us
  matrix products: 39.9 us -> 24.1 us
  starting transfers between devices: 88.3 us -> 75.2 us
  waiting for transfers between devices: 106 us -> 116 us
  Pallas kernels: 180 us -> 189 us
    ppermute x31 -> x20, waiting for transfers between devices: 47.5 us -> 75.9 us  [swap_mp(): return lax.ppermute(inputs, 'mp', [(i, i ^ mask) for i in range(size)])]
    ppermute x43 -> x35, waiting for transfers between devices: 58.2 us -> 40.3 us  [swap_dp(): return lax.ppermute(inputs, 'dp', [(i, i ^ mask) for i in range(size)])]
    dot_general x11 -> x7, matrix products: 38.1 us -> 22.2 us  [contract_rows(): lax.dot_general(first_operand, second_operand, (((0,), (0,)), ((), ())),...]
    slice x23 -> x11, local copies, waits for them, and re-layouts: 15.7 us -> 1.81 us  [the longest x1 1.29 us: shards(): loss_global, box_total, grad_norm = (made[0][0, i] for i in range(3))]
    ppermute x31 -> x20, starting transfers between devices: 47.8 us -> 34.4 us  [swap_mp(): return lax.ppermute(inputs, 'mp', [(i, i ^ mask) for i in range(size)])]
    pallas_call x14 -> x15, Pallas kernels: 180 us -> 189 us  [call(): pl.pallas_call(run, grid=grid, in_specs=list(in_specs) + [pl.BlockSpec(me...]
    another operation x17 -> x11, other arithmetic: 15.8 us -> 6.42 us
    convert_element_type x3 -> x7, other arithmetic: 3.21 us -> 11.9 us  [the longest x3 5.8 us: shards(): away = (kept[1].astype(f32) + got[1].astype(f32)).astype(bf16)]
  transfers between devices with their start and end apart: 78 -> 59, of which waited for: 24 -> 29; matrix products, arithmetic and copies ran while one was open for 22% -> 13% of each run, Pallas kernels for 22% -> 27%
where the time goes in v4:
time: 489 us; the launch traced here: 482 us
  Pallas kernels  189 us (39%)
  waiting for transfers between devices  116 us (24%)
  starting transfers between devices  75.2 us (15%)
  other arithmetic  37.4 us (8%)
  matrix products  24.1 us (5%)
  local copies, waits for them, and re-layouts  22.9 us (5%)
  between operations  16.6 us (3%)
    pallas_call x15, Pallas kernels, call(): pl.pallas_call(run, grid=grid, in_specs=list(in_specs) + [pl.BlockSpec(me...  189 us
    ppermute x20, waiting for transfers between devices, swap_mp(): return lax.ppermute(inputs, 'mp', [(i, i ^ mask) for i in range(size)])  75.9 us
    ppermute x35, waiting for transfers between devices, swap_dp(): return lax.ppermute(inputs, 'dp', [(i, i ^ mask) for i in range(size)])  40.3 us
    ppermute x20, starting transfers between devices, swap_mp(): return lax.ppermute(inputs, 'mp', [(i, i ^ mask) for i in range(size)])  34.4 us
    ppermute x35, starting transfers between devices, swap_dp(): return lax.ppermute(inputs, 'dp', [(i, i ^ mask) for i in range(size)])  27.6 us
    dot_general x7, matrix products, contract_rows(): lax.dot_general(first_operand, second_operand, (((0,), (0,)), ((), ())),...  22.2 us
    ppermute x4, starting transfers between devices, regroup(): return lax.ppermute(inputs, ('dp', 'mp'), pairs)  13.2 us
    unnamed x116, local copies, waits for them, and re-layouts  10.5 us
  transfers between devices with their start and end apart: 59, of which 29 were waited for; matrix products, arithmetic and copies ran while one was open for 13% of the time, Pallas kernels for 27%

profile of v4, /device:TPU:0, one launch (start us, length us, event | category | flops | bytes accessed | tf_op | source)
XLA Modules:
  0.0 481.8 jit_solution(16704485062214585461)
XLA Ops:
  6.9 3.1 collective-permute-start
  9.9 2.6 collective-permute-start.1
  12.9 4.1 collective-permute-done
  17.0 8.5 %collective-permute-done.1 = bf16[96,832]{1,0:T(8,128)(2,1)S(1)} collective-permute-done((bf16[96,832]{1,0:T(8,128)(2,1)S(1)}, bf16[96,832]{1,0:T(8,128)(2,1)S(1)}, u32[]{:S(2)}, u32[]{:S(2)}) %collective-permute-start.1) | collective-permute-done | bytes 159776 | tf_op jit(solution)/shard_map/ppermute | solution.py:50
  25.5 2.8 collective-permute-start.3
  29.8 1.6 collective-permute-start.7
  35.4 1.8 collective-permute-done.3.refs_2_
  37.2 5.3 %collective-permute-start.9 = (bf16[96,2944]{1,0:T(8,128)(2,1)S(1)}, bf16[96,2944]{1,0:T(8,128)(2,1)}, u32[]{:S(2)}, u32[]{:S(2)}) collective-permute-start(bf16[96,2944]{1,0:T(8,128)(2,1)S(1)} %concatenate.156.refs_3_.refs_20_), channel_id=1, source_target_pairs={{0,24},{4,28},{8,16},{12,20},{16,8},{20,12},{24,0},{28,4},{1,25},{... | collective-permute-start | bytes 1695752 | tf_op jit(solution)/shard_map/ppermute | solution.py:45
  43.0 15.5 %collective-permute-done.4.refs_3_ = bf16[96,1728]{1,0:T(8,128)(2,1)S(1)} collective-permute-done((bf16[96,1728]{1,0:T(8,128)(2,1)S(1)}, bf16[96,1728]{1,0:T(8,128)(2,1)S(1)}, u32[]{:S(2)}, u32[]{:S(2)}) %collective-permute-start.4) | collective-permute-done | bytes 331808 | tf_op jit(solution)/shard_map/ppermute | solution.py:50
  59.3 2.5 shard_map.466.refs_4_.refs_6_
  64.4 9.4 %collective-permute-start.6 = (bf16[3,441,384]{2,1,0:T(8,128)(2,1)}, bf16[3,441,384]{2,1,0:T(8,128)(2,1)}, u32[]{:S(2)}, u32[]{:S(2)}) collective-permute-start(bf16[3,441,384]{2,1,0:T(8,128)(2,1)} %bitcast.111), channel_id=1, source_target_pairs={{0,0},{1,1},{2,4},{3,5},{4,2},{5,3},{6,6},{7,7},{8,8},{9,9},{10,12... | collective-permute-start | bytes 3048200 | tf_op jit(solution)/shard_map/ppermute | solution.py:64
  79.7 9.4 %collective-permute-done.14.refs_11_.refs_5_.refs_7_ = bf16[96,6912]{1,0:T(8,128)(2,1)S(1)} collective-permute-done((bf16[96,6912]{1,0:T(8,128)(2,1)}, bf16[96,6912]{1,0:T(8,128)(2,1)S(1)}, u32[]{:S(2)}, u32[]{:S(2)}) %collective-permute-start.14) | collective-permute-done | bytes 1327136 | tf_op jit(solution)/shard_map/ppermute | solution.py:45
  91.4 12.7 %shard_map.467 = (bf16[1152,441]{1,0:T(8,128)(2,1)}, f32[1152,768]{1,0:T(8,128)}, bf16[1152,768]{1,0:T(8,128)(2,1)}, bf16[1152,768]{1,0:T(8,128)(2,1)}, bf16[115...) custom-call(bf16[3,441,384]{2,1,0:T(8,128)(2,1)} %collective-permute, ...), custom_call_target="tpu_custom_call" | custom-call | flops 1000 | bytes 1000 | tf_op jit(solution)/shard_map/pallas_call | solution.py:143
  104.1 7.8 %collective-permute-start.18 = (bf16[3,2,96,768]{3,2,1,0:T(8,128)(2,1)}, bf16[3,2,96,768]{3,2,1,0:T(8,128)(2,1)S(1)}, u32[]{:S(2)}, u32[]{:S(2)}) collective-permute-start(bf16[3,2,96,768]{3,2,1,0:T(8,128)(2,1)} %get-tuple-element.124.refs_3_.refs_7_.refs_11_.refs_2_.refs_6_.refs_5_.refs_9_), channel_id=1, source_target_pairs={{0,1},{1,0},{2,3},{3,2},{4,5},{5,4},{6,7},{7,6},{8,9},{9,8},{10,11... | collective-permute-start | bytes 2654216 | tf_op jit(solution)/shard_map/ppermute | solution.py:50
  115.3 2.2 collective-permute-start.20
  128.1 1.9 collective-permute-start.17
  130.0 8.7 %collective-permute-done.18.refs_5_.refs_9_.refs_13_.refs_4_.refs_8_.refs_7_.refs_11_ = bf16[3,2,96,768]{3,2,1,0:T(8,128)(2,1)S(1)} collective-permute-done((bf16[3,2,96,768]{3,2,1,0:T(8,128)(2,1)}, bf16[3,2,96,768]{3,2,1,0:T(8,128)(2,1)S(1)}, u32[]{:S(2)}, u32[]{:S(2)}) %collective-permute-start.18) | collective-permute-done | bytes 884768 | tf_op jit(solution)/shard_map/ppermute | solution.py:50
  142.0 10.1 %shard_map.468 = (bf16[1152,768]{1,0:T(8,128)(2,1)}, bf16[12,384,768]{2,1,0:T(8,128)(2,1)}, bf16[768,768]{1,0:T(8,128)(2,1)}, bf16[768,768]{1,0:T(8,128)(2,1)}) custom-call(bf16[1152,768]{1,0:T(8,128)(2,1)} %get-tuple-element.123.refs_0_, f32[2,6,768]{2,1,0:T(8,128)} %reshape.667.refs_2_.refs_1_.refs_3_, f32[3,4,768]{2,1,0:T(4,128)} %pad_maximum_fusion.16.refs_2_, ...), custom_call_target="tpu_custom_call" | custom-call | flops 1000 | bytes 1000 | tf_op jit(solution)/shard_map/pallas_call | solution.py:143
  152.3 2.4 collective-permute-done.22.refs_4_
  158.1 4.2 shard_map.469.refs_6_
  164.0 5.2 %shard_map.470.refs_11_.refs_7_.refs_8_.refs_5_.refs_6_.refs_9_ = bf16[2,2,384,768]{3,2,1,0:T(8,128)(2,1)} custom-call(s32[4]{0:T(128)} %pad_add_fusion.2.refs_0_, bf16[384,384]{1,0:T(8,128)(2,1)} %fusion.7.refs_1_, bf16[2,2,192,384]{3,2,1,0:T(8,128)(2,1)} %copy-done.23, bf16[2,2,192,384]{3,2,1,0:T(8,128)(2,1)} %copy-done.24, ...), custom_call_target="tpu_custom_call" | custom-call | flops 1000 | bytes 1000 | tf_op jit(solution)/shard_map/pallas_call | solution.py:143
  169.8 10.1 %shard_map.471 = (bf16[1152,768]{1,0:T(8,128)(2,1)}, bf16[12,384,768]{2,1,0:T(8,128)(2,1)}, bf16[768,768]{1,0:T(8,128)(2,1)}, bf16[768,768]{1,0:T(8,128)(2,1)}) custom-call(bf16[1152,768]{1,0:T(8,128)(2,1)} %get-tuple-element.123.refs_0_, f32[2,6,768]{2,1,0:T(8,128)} %reshape.667.refs_2_.refs_1_.refs_3_, ...), custom_call_target="tpu_custom_call", output_to_operand_aliasing={{0}: (12, {})} | custom-call | flops 1000 | bytes 1000 | tf_op jit(solution)/shard_map/pallas_call | solution.py:143
  183.1 10.0 %shard_map.472 = (bf16[1152,768]{1,0:T(8,128)(2,1)}, bf16[12,384,768]{2,1,0:T(8,128)(2,1)}, bf16[768,768]{1,0:T(8,128)(2,1)}, bf16[768,768]{1,0:T(8,128)(2,1)}) custom-call(bf16[1152,768]{1,0:T(8,128)(2,1)} %get-tuple-element.123.refs_0_, f32[2,6,768]{2,1,0:T(8,128)} %reshape.667.refs_2_.refs_1_.refs_3_, ...), custom_call_target="tpu_custom_call", output_to_operand_aliasing={{0}: (9, {})} | custom-call | flops 1000 | bytes 1000 | tf_op jit(solution)/shard_map/pallas_call | solution.py:143
  193.1 34.0 %shard_map.473 = (f32[1152,768]{1,0:T(8,128)}, bf16[1152,768]{1,0:T(8,128)(2,1)}, bf16[1152,3072]{1,0:T(8,128)(2,1)}, bf16[1152,3072]{1,0:T(8,128)(2,1)}, f32[1152,768]{1,0:T(8,128)}, /*index=5*/f32[3,8,768]{2,1,0:T(8,128)}) custom-call(bf16[1152,768]{1,0:T(8,128)(2,1)} %get-tuple-element.135.refs_0_, f32[1152,768]{1,0:T(8,128)} %get-tuple-element.136.refs_1_.refs_4_, ...), custom_call_target="tpu_custom_call" | custom-call | flops 1000 | bytes 1000 | tf_op jit(solution)/shard_map/pallas_call | solution.py:143
  227.1 1.7 collective-permute-start.30
  231.6 3.8 collective-permute-done.31
  237.0 28.9 %shard_map.474 = (bf16[1152,768]{1,0:T(8,128)(2,1)}, bf16[1152,3072]{1,0:T(8,128)(2,1)}, bf16[1152,768]{1,0:T(8,128)(2,1)}, f32[1152,768]{1,0:T(8,128)}, bf16[1152,768]{1,0:T(8,128)(2,1)}, /*index=5*/f32[8,768]{1,0:T(8,128)}) custom-call(f32[3,8,768]{2,1,0:T(8,128)} %convolution_bitcast_fusion.refs_0_, f32[3,8,384]{2,1,0:T(8,128)} %convert_divide_fusion.refs_3_.refs_1_, ...), custom_call_target="tpu_custom_call" | custom-call | flops 1000 | bytes 1000 | tf_op jit(solution)/shard_map/pallas_call | solution.py:143
  266.0 2.3 convolution_convert_fusion.4
  268.4 6.4 %convolution_convert_fusion = bf16[384,3072]{1,0:T(8,128)(2,1)S(1)} fusion(bf16[1152,3072]{1,0:T(8,128)(2,1)} %get-tuple-element.158, bf16[1152,768]{1,0:T(8,128)(2,1)S(1)} %copy-done.48), kind=kOutput, calls=%fused_computation | convolution fusion | flops 2719088640 | bytes 10321920 | tf_op jit(solution)/shard_map/dot_general | solution.py:38
  275.4 3.9 convolution_convert_fusion.2
  280.4 3.5 convolution_convert_fusion.1
  283.9 3.5 convolution_convert_fusion.3
  292.3 2.5 collective-permute-start.39
  297.0 13.8 %shard_map.475 = (bf16[1152,768]{1,0:T(8,128)(2,1)}, bf16[2,2,96,768]{3,2,1,0:T(8,128)(2,1)}, bf16[2,2,96,768]{3,2,1,0:T(8,128)(2,1)}, f32[2,2,768]{2,1,0:T(2,128)}, f32[3,4,128]{2,1,0:T(4,128)}) custom-call(bf16[1152,768]{1,0:T(8,128)(2,1)} %get-tuple-element.123.refs_0_, bf16[768,768]{1,0:T(8,128)(2,1)} %get-tuple-element.152.refs_1_, ...), custom_call_target="tpu_custom_call" | custom-call | flops 1000 | bytes 1000 | tf_op jit(solution)/shard_map/pallas_call | solution.py:143
  310.9 2.2 collective-permute-done.35.refs_12_
  313.1 1.9 fusion.9.refs_11_
  315.1 13.8 %shard_map.476 = (bf16[1152,768]{1,0:T(8,128)(2,1)}, bf16[2,2,96,768]{3,2,1,0:T(8,128)(2,1)}, bf16[2,2,96,768]{3,2,1,0:T(8,128)(2,1)}, f32[2,2,768]{2,1,0:T(2,128)}, f32[3,4,128]{2,1,0:T(4,128)}) custom-call(bf16[1152,768]{1,0:T(8,128)(2,1)} %get-tuple-element.123.refs_0_, ...), custom_call_target="tpu_custom_call", output_to_operand_aliasing={{0}: (10, {})} | custom-call | flops 1000 | bytes 1000 | tf_op jit(solution)/shard_map/pallas_call | solution.py:143
  331.1 1.9 fusion.10.refs_14_
  333.1 5.5 %collective-permute-done.37.refs_15_.refs_13_ = bf16[2,96,768]{2,1,0:T(8,128)(2,1)S(1)} collective-permute-done((bf16[2,96,768]{2,1,0:T(8,128)(2,1)S(1)}, bf16[2,96,768]{2,1,0:T(8,128)(2,1)S(1)}, u32[]{:S(2)}, u32[]{:S(2)}) %collective-permute-start.37) | collective-permute-done | bytes 294944 | tf_op jit(solution)/shard_map/ppermute | solution.py:50
  339.3 13.7 %shard_map.477 = (bf16[1152,768]{1,0:T(8,128)(2,1)}, bf16[2,2,96,768]{3,2,1,0:T(8,128)(2,1)}, bf16[2,2,96,768]{3,2,1,0:T(8,128)(2,1)}, f32[2,2,768]{2,1,0:T(2,128)}, f32[3,4,128]{2,1,0:T(4,128)}) custom-call(bf16[1152,768]{1,0:T(8,128)(2,1)} %get-tuple-element.123.refs_0_, ...), custom_call_target="tpu_custom_call", output_to_operand_aliasing={{0}: (13, {})} | custom-call | flops 1000 | bytes 1000 | tf_op jit(solution)/shard_map/pallas_call | solution.py:143
  353.1 1.7 convolution_multiply_fusion.refs_9_
  355.3 1.9 fusion.11
  358.7 3.0 collective-permute-done.43
  361.8 2.8 fusion.66
  368.1 2.5 collective-permute-done.42.refs_19_
  370.6 23.3 %shard_map.478 = (bf16[384,2944]{1,0:T(8,128)(2,1)}, bf16[384,2944]{1,0:T(8,128)(2,1)}, f32[8,768]{1,0:T(8,128)}) custom-call(bf16[1152,768]{1,0:T(8,128)(2,1)} %get-tuple-element.166.refs_0_, bf16[1152,768]{1,0:T(8,128)(2,1)} %get-tuple-element.167.refs_1_, bf16[1152,768]{1,0:T(8,128)(2,1)} %get-tuple-element.168.refs_2_, ...), custom_call_target="tpu_custom_call" | custom-call | flops 1000 | bytes 1000 | tf_op jit(solution)/shard_map/pallas_call | solution.py:143
  398.8 3.9 add_convert_fusion.9
  402.6 2.5 collective-permute-start.47
  406.3 7.4 %collective-permute-done.48 = bf16[96,3456]{1,0:T(8,128)(2,1)S(1)} collective-permute-done((bf16[96,3456]{1,0:T(8,128)(2,1)S(1)}, bf16[96,3456]{1,0:T(8,128)(2,1)S(1)}, u32[]{:S(2)}, u32[]{:S(2)}) %collective-permute-start.48) | collective-permute-done | bytes 663584 | tf_op jit(solution)/shard_map/ppermute | solution.py:50
  414.7 2.7 collective-permute-start.53
  417.4 2.2 collective-permute-done.47
  419.5 11.3 %collective-permute-done.46 = bf16[96,2944]{1,0:T(8,128)(2,1)} collective-permute-done((bf16[96,2944]{1,0:T(8,128)(2,1)}, bf16[96,2944]{1,0:T(8,128)(2,1)}, u32[]{:S(2)}, u32[]{:S(2)}) %collective-permute-start.46) | collective-permute-done | bytes 565280 | tf_op jit(solution)/shard_map/ppermute | solution.py:45
  430.8 1.7 convert_add_fusion.1
  435.3 2.4 collective-permute-done.51
  438.4 2.7 collective-permute-start.52
  442.8 2.7 collective-permute-start.50
  446.2 4.5 collective-permute-done.50.refs_1_
  451.4 2.5 shard_map.479
  457.4 2.9 collective-permute-done.55
  461.7 2.9 collective-permute-done.56
  464.7 4.2 collective-permute-done.57
  468.9 1.6 collective-permute-start.58
  470.5 3.9 collective-permute-done.58.refs_2_
  475.0 4.5 shard_map.480
  (343 shorter events, 78.5 us)
Async XLA Ops:
  6.9 10.2 %collective-permute-start = (bf16[96,832]{1,0:T(8,128)(2,1)S(1)}, bf16[96,832]{1,0:T(8,128)(2,1)S(1)}, u32[]{:S(2)}, u32[]{:S(2)}) collective-permute-start(bf16[96,832]{1,0:T(8,128)(2,1)S(1)} %maximum_maximum_fusion), channel_id=1, source_target_pairs={{0,1},{1,0},{2,3},{3,2},{4,5},{5,4},{6,7},{7,6},{8,9},{9,8},{10,11... | collective-permute-start | bytes 479240 | tf_op jit(solution)/shard_map/ppermute | solution.py:50
  9.9 15.6 %collective-permute-start.1 = (bf16[96,832]{1,0:T(8,128)(2,1)S(1)}, bf16[96,832]{1,0:T(8,128)(2,1)S(1)}, u32[]{:S(2)}, u32[]{:S(2)}) collective-permute-start(bf16[96,832]{1,0:T(8,128)(2,1)S(1)} %maximum_maximum_fusion), channel_id=1, source_target_pairs={{0,2},{1,3},{2,0},{3,1},{4,6},{5,7},{6,4},{7,5},{8,10},{9,11},{10,... | collective-permute-start | bytes 479240 | tf_op jit(solution)/shard_map/ppermute | solution.py:50
  12.5 13.0 %collective-permute-start.2 = (bf16[96,832]{1,0:T(8,128)(2,1)S(1)}, bf16[96,832]{1,0:T(8,128)(2,1)S(1)}, u32[]{:S(2)}, u32[]{:S(2)}) collective-permute-start(bf16[96,832]{1,0:T(8,128)(2,1)S(1)} %maximum_maximum_fusion), channel_id=1, source_target_pairs={{0,3},{1,2},{2,1},{3,0},{4,7},{5,6},{6,5},{7,4},{8,11},{9,10},{10,... | collective-permute-start | bytes 479240 | tf_op jit(solution)/shard_map/ppermute | solution.py:50
  25.5 11.7 %collective-permute-start.3 = (bf16[96,1728]{1,0:T(8,128)(2,1)S(1)}, bf16[96,1728]{1,0:T(8,128)(2,1)S(1)}, u32[]{:S(2)}, u32[]{:S(2)}) collective-permute-start(bf16[96,1728]{1,0:T(8,128)(2,1)S(1)} %pad_maximum_fusion.4.refs_1_), channel_id=1, source_target_pairs={{0,1},{1,0},{2,3},{3,2},{4,5},{5,4},{6,7},{7,6},{8,9},{9,8},{10,11... | collective-permute-start | bytes 995336 | tf_op jit(solution)/shard_map/ppermute | solution.py:50
  29.8 46.7 %copy-start.10 = (bf16[96,2944]{1,0:T(8,128)(2,1)}, bf16[96,2944]{1,0:T(8,128)(2,1)S(1)}, u32[]{:S(2)}) copy-start(bf16[96,2944]{1,0:T(8,128)(2,1)S(1)} %concatenate.156.refs_3_.refs_20_) | copy-start | bytes 1695748
  29.8 34.1 %collective-permute-start.7 = (bf16[96,2944]{1,0:T(8,128)(2,1)S(1)}, bf16[96,2944]{1,0:T(8,128)(2,1)}, u32[]{:S(2)}, u32[]{:S(2)}) collective-permute-start(bf16[96,2944]{1,0:T(8,128)(2,1)S(1)} %concatenate.156.refs_3_.refs_20_), channel_id=1, source_target_pairs={{0,8},{4,12},{8,0},{12,4},{16,24},{20,28},{24,16},{28,20},{1,9},{5... | collective-permute-start | bytes 1695752 | tf_op jit(solution)/shard_map/ppermute | solution.py:45
  31.4 32.5 %collective-permute-start.8 = (bf16[96,2944]{1,0:T(8,128)(2,1)S(1)}, bf16[96,2944]{1,0:T(8,128)(2,1)}, u32[]{:S(2)}, u32[]{:S(2)}) collective-permute-start(bf16[96,2944]{1,0:T(8,128)(2,1)S(1)} %concatenate.156.refs_3_.refs_20_), channel_id=1, source_target_pairs={{0,16},{4,20},{8,24},{12,28},{16,0},{20,4},{24,8},{28,12},{1,17},{... | collective-permute-start | bytes 1695752 | tf_op jit(solution)/shard_map/ppermute | solution.py:45
  32.9 25.6 %collective-permute-start.4 = (bf16[96,1728]{1,0:T(8,128)(2,1)S(1)}, bf16[96,1728]{1,0:T(8,128)(2,1)S(1)}, u32[]{:S(2)}, u32[]{:S(2)}) collective-permute-start(bf16[96,1728]{1,0:T(8,128)(2,1)S(1)} %pad_maximum_fusion.4.refs_1_), channel_id=1, source_target_pairs={{0,2},{1,3},{2,0},{3,1},{4,6},{5,7},{6,4},{7,5},{8,10},{9,11},{10,... | collective-permute-start | bytes 995336 | tf_op jit(solution)/shard_map/ppermute | solution.py:50
  33.9 24.6 %collective-permute-start.5 = (bf16[96,1728]{1,0:T(8,128)(2,1)S(1)}, bf16[96,1728]{1,0:T(8,128)(2,1)S(1)}, u32[]{:S(2)}, u32[]{:S(2)}) collective-permute-start(bf16[96,1728]{1,0:T(8,128)(2,1)S(1)} %pad_maximum_fusion.4.refs_1_), channel_id=1, source_target_pairs={{0,3},{1,2},{2,1},{3,0},{4,7},{5,6},{6,5},{7,4},{8,11},{9,10},{10,... | collective-permute-start | bytes 995336 | tf_op jit(solution)/shard_map/ppermute | solution.py:50
  37.2 27.2 %collective-permute-start.9 = (bf16[96,2944]{1,0:T(8,128)(2,1)S(1)}, bf16[96,2944]{1,0:T(8,128)(2,1)}, u32[]{:S(2)}, u32[]{:S(2)}) collective-permute-start(bf16[96,2944]{1,0:T(8,128)(2,1)S(1)} %concatenate.156.refs_3_.refs_20_), channel_id=1, source_target_pairs={{0,24},{4,28},{8,16},{12,20},{16,8},{20,12},{24,0},{28,4},{1,25},{... | collective-permute-start | bytes 1695752 | tf_op jit(solution)/shard_map/ppermute | solution.py:45
  61.8 27.3 %collective-permute-start.14 = (bf16[96,6912]{1,0:T(8,128)(2,1)}, bf16[96,6912]{1,0:T(8,128)(2,1)S(1)}, u32[]{:S(2)}, u32[]{:S(2)}) collective-permute-start(bf16[96,6912]{1,0:T(8,128)(2,1)} %shard_map.466.refs_4_.refs_6_), channel_id=1, source_target_pairs={{0,8},{4,12},{8,0},{12,4},{16,24},{20,28},{24,16},{28,20},{1,9},{5... | collective-permute-start | bytes 3981320 | tf_op jit(solution)/shard_map/ppermute | solution.py:45
  62.9 26.3 %collective-permute-start.15 = (bf16[96,6912]{1,0:T(8,128)(2,1)}, bf16[96,6912]{1,0:T(8,128)(2,1)S(1)}, u32[]{:S(2)}, u32[]{:S(2)}) collective-permute-start(bf16[96,6912]{1,0:T(8,128)(2,1)} %shard_map.466.refs_4_.refs_6_), channel_id=1, source_target_pairs={{0,16},{4,20},{8,24},{12,28},{16,0},{20,4},{24,8},{28,12},{1,17},{... | collective-permute-start | bytes 3981320 | tf_op jit(solution)/shard_map/ppermute | solution.py:45
  63.9 12.6 %collective-permute-start.10 = (bf16[96,2944]{1,0:T(8,128)(2,1)S(1)}, bf16[96,2944]{1,0:T(8,128)(2,1)}, u32[]{:S(2)}, u32[]{:S(2)}) collective-permute-start(bf16[96,2944]{1,0:T(8,128)(2,1)S(1)} %concatenate.156.refs_3_.refs_20_), channel_id=1, source_target_pairs={{0,4},{4,0},{8,12},{12,8},{16,20},{20,16},{24,28},{28,24},{1,5},{5... | collective-permute-start | bytes 1695752 | tf_op jit(solution)/shard_map/ppermute | solution.py:45
  63.9 12.7 %collective-permute-start.11 = (bf16[96,2944]{1,0:T(8,128)(2,1)}, bf16[96,2944]{1,0:T(8,128)(2,1)}, u32[]{:S(2)}, u32[]{:S(2)}) collective-permute-start(bf16[96,2944]{1,0:T(8,128)(2,1)} %collective-permute-done.7.refs_4_.refs_21_), channel_id=1, source_target_pairs={{0,4},{4,0},{8,12},{12,8},{16,20},{20,16},{24,28},{28,24},{1,5},{5... | collective-permute-start | bytes 1695752 | tf_op jit(solution)/shard_map/ppermute | solution.py:45
  64.4 15.3 %collective-permute-start.6 = (bf16[3,441,384]{2,1,0:T(8,128)(2,1)}, bf16[3,441,384]{2,1,0:T(8,128)(2,1)}, u32[]{:S(2)}, u32[]{:S(2)}) collective-permute-start(bf16[3,441,384]{2,1,0:T(8,128)(2,1)} %bitcast.111), channel_id=1, source_target_pairs={{0,0},{1,1},{2,4},{3,5},{4,2},{5,3},{6,6},{7,7},{8,8},{9,9},{10,12... | collective-permute-start | bytes 3048200 | tf_op jit(solution)/shard_map/ppermute | solution.py:64
  76.5 2.2 collective-permute-start.12
  76.6 3.1 collective-permute-start.13
  78.8 33.3 %collective-permute-start.16 = (s32[16,128]{1,0:T(8,128)S(1)}, s32[16,128]{1,0:T(8,128)S(1)}, u32[]{:S(2)}, u32[]{:S(2)}) collective-permute-start(s32[16,128]{1,0:T(8,128)S(1)} %pad_bitcast_fusion), channel_id=1, source_target_pairs={{0,0},{1,1},{2,4},{3,5},{4,2},{5,3},{6,6},{7,7},{8,8},{9,9},{10,12... | collective-permute-start | bytes 24584 | tf_op jit(solution)/shard_map/ppermute | solution.py:64
  104.1 34.6 %collective-permute-start.18 = (bf16[3,2,96,768]{3,2,1,0:T(8,128)(2,1)}, bf16[3,2,96,768]{3,2,1,0:T(8,128)(2,1)S(1)}, u32[]{:S(2)}, u32[]{:S(2)}) collective-permute-start(bf16[3,2,96,768]{3,2,1,0:T(8,128)(2,1)} %get-tuple-element.124.refs_3_.refs_7_.refs_11_.refs_2_.refs_6_.refs_5_.refs_9_), channel_id=1, source_target_pairs={{0,1},{1,0},{2,3},{3,2},{4,5},{5,4},{6,7},{7,6},{8,9},{9,8},{10,11... | collective-permute-start | bytes 2654216 | tf_op jit(solution)/shard_map/ppermute | solution.py:50
  115.3 23.9 %collective-permute-start.20 = (bf16[2,2,192,384]{3,2,1,0:T(8,128)(2,1)}, bf16[2,2,192,384]{3,2,1,0:T(8,128)(2,1)S(1)}, u32[]{:S(2)}, u32[]{:S(2)}) collective-permute-start(bf16[2,2,192,384]{3,2,1,0:T(8,128)(2,1)} %bitcast.112), channel_id=1, source_target_pairs={{0,0},{1,1},{2,4},{3,5},{4,2},{5,3},{6,6},{7,7},{8,8},{9,9},{10,12... | collective-permute-start | bytes 1769480 | tf_op jit(solution)/shard_map/ppermute | solution.py:64
  128.1 12.4 %collective-permute-start.17 = (bf16[3,2,96,768]{3,2,1,0:T(8,128)(2,1)}, bf16[3,2,96,768]{3,2,1,0:T(8,128)(2,1)S(1)}, u32[]{:S(2)}, u32[]{:S(2)}) collective-permute-start(bf16[3,2,96,768]{3,2,1,0:T(8,128)(2,1)} %get-tuple-element.124.refs_3_.refs_7_.refs_11_.refs_2_.refs_6_.refs_5_.refs_9_), channel_id=1, source_target_pairs={{0,4},{4,0},{8,12},{12,8},{16,20},{20,16},{24,28},{28,24},{1,5},{5... | collective-permute-start | bytes 2654216 | tf_op jit(solution)/shard_map/ppermute | solution.py:45
  138.6 2.4 collective-permute-start.19
  138.9 41.0 %collective-permute-start.24 = (bf16[96,6912]{1,0:T(8,128)(2,1)}, bf16[96,6912]{1,0:T(8,128)(2,1)}, u32[]{:S(2)}, u32[]{:S(2)}) collective-permute-start(bf16[96,6912]{1,0:T(8,128)(2,1)} %shard_map.466.refs_4_.refs_6_), channel_id=1, source_target_pairs={{0,24},{4,28},{8,16},{12,20},{16,8},{20,12},{24,0},{28,4},{1,25},{... | collective-permute-start | bytes 3981320 | tf_op jit(solution)/shard_map/ppermute | solution.py:45
  139.2 15.5 %collective-permute-start.22 = (bf16[2,2,192,384]{3,2,1,0:T(8,128)(2,1)S(1)}, bf16[2,2,192,384]{3,2,1,0:T(8,128)(2,1)}, u32[]{:S(2)}, u32[]{:S(2)}) collective-permute-start(bf16[2,2,192,384]{3,2,1,0:T(8,128)(2,1)S(1)} %collective-permute-done.20.refs_2_), channel_id=1, source_target_pairs={{0,1},{1,0},{2,3},{3,2},{4,5},{5,4},{6,7},{7,6},{8,9},{9,8},{10,11... | collective-permute-start | bytes 1769480 | tf_op jit(solution)/shard_map/ppermute | solution.py:50
  152.1 10.2 %collective-permute-start.21 = (bf16[2,2,192,384]{3,2,1,0:T(8,128)(2,1)S(1)}, bf16[2,2,192,384]{3,2,1,0:T(8,128)(2,1)S(1)}, u32[]{:S(2)}, u32[]{:S(2)}) collective-permute-start(bf16[2,2,192,384]{3,2,1,0:T(8,128)(2,1)S(1)} %collective-permute-done.20.refs_2_), channel_id=1, source_target_pairs={{0,4},{4,0},{8,12},{12,8},{16,20},{20,16},{24,28},{28,24},{1,5},{5... | collective-permute-start | bytes 1769480 | tf_op jit(solution)/shard_map/ppermute | solution.py:45
  154.7 7.7 %collective-permute-start.23 = (bf16[2,2,192,384]{3,2,1,0:T(8,128)(2,1)}, bf16[2,2,192,384]{3,2,1,0:T(8,128)(2,1)S(1)}, u32[]{:S(2)}, u32[]{:S(2)}) collective-permute-start(bf16[2,2,192,384]{3,2,1,0:T(8,128)(2,1)} %collective-permute-done.22.refs_4_), channel_id=1, source_target_pairs={{0,4},{4,0},{8,12},{12,8},{16,20},{20,16},{24,28},{28,24},{1,5},{5... | collective-permute-start | bytes 1769480 | tf_op jit(solution)/shard_map/ppermute | solution.py:45
  157.6 35.4 %collective-permute-start.25 = (bf16[96,6912]{1,0:T(8,128)(2,1)}, bf16[96,6912]{1,0:T(8,128)(2,1)}, u32[]{:S(2)}, u32[]{:S(2)}) collective-permute-start(bf16[96,6912]{1,0:T(8,128)(2,1)} %shard_map.466.refs_4_.refs_6_), channel_id=1, source_target_pairs={{0,4},{4,0},{8,12},{12,8},{16,20},{20,16},{24,28},{28,24},{1,5},{5... | collective-permute-start | bytes 3981320 | tf_op jit(solution)/shard_map/ppermute | solution.py:45
  158.1 34.9 %collective-permute-start.26 = (bf16[96,6912]{1,0:T(8,128)(2,1)}, bf16[96,6912]{1,0:T(8,128)(2,1)}, u32[]{:S(2)}, u32[]{:S(2)}) collective-permute-start(bf16[96,6912]{1,0:T(8,128)(2,1)} %copy-done.4), channel_id=1, source_target_pairs={{0,4},{4,0},{8,12},{12,8},{16,20},{20,16},{24,28},{28,24},{1,5},{5... | collective-permute-start | bytes 3981320 | tf_op jit(solution)/shard_map/ppermute | solution.py:45
  169.2 23.9 %collective-permute-start.27 = (bf16[96,6912]{1,0:T(8,128)(2,1)S(1)}, bf16[96,6912]{1,0:T(8,128)(2,1)}, u32[]{:S(2)}, u32[]{:S(2)}) collective-permute-start(bf16[96,6912]{1,0:T(8,128)(2,1)S(1)} %copy-done.6), channel_id=1, source_target_pairs={{0,4},{4,0},{8,12},{12,8},{16,20},{20,16},{24,28},{28,24},{1,5},{5... | collective-permute-start | bytes 3981320 | tf_op jit(solution)/shard_map/ppermute | solution.py:45
  179.9 13.2 %collective-permute-start.28 = (bf16[96,6912]{1,0:T(8,128)(2,1)}, bf16[96,6912]{1,0:T(8,128)(2,1)}, u32[]{:S(2)}, u32[]{:S(2)}) collective-permute-start(bf16[96,6912]{1,0:T(8,128)(2,1)} %collective-permute-done.24.refs_10_.refs_7_.refs_9_), channel_id=1, source_target_pairs={{0,4},{4,0},{8,12},{12,8},{16,20},{20,16},{24,28},{28,24},{1,5},{5... | collective-permute-start | bytes 3981320 | tf_op jit(solution)/shard_map/ppermute | solution.py:45
  180.5 46.6 %collective-permute-start.29 = (bf16[2,2,192,384]{3,2,1,0:T(8,128)(2,1)S(1)}, bf16[2,2,192,384]{3,2,1,0:T(8,128)(2,1)S(1)}, u32[]{:S(2)}, u32[]{:S(2)}) collective-permute-start(bf16[2,2,192,384]{3,2,1,0:T(8,128)(2,1)S(1)} %copy-done.12), channel_id=1, source_target_pairs={{0,0},{1,1},{2,4},{3,5},{4,2},{5,3},{6,6},{7,7},{8,8},{9,9},{10,12... | collective-permute-start | bytes 1769480 | tf_op jit(solution)/shard_map/ppermute | solution.py:64
  193.1 42.4 %copy-start.34 = (bf16[80,768]{1,0:T(8,128)(2,1)S(1)}, bf16[80,768]{1,0:T(8,128)(2,1)}, u32[]{:S(2)}) copy-start(bf16[80,768]{1,0:T(8,128)(2,1)} %get-tuple-element.144) | copy-start | bytes 368644
  227.1 38.9 %copy-start.26 = (bf16[2,2,192,384]{3,2,1,0:T(8,128)(2,1)}, bf16[2,2,192,384]{3,2,1,0:T(8,128)(2,1)S(1)}, u32[]{:S(2)}) copy-start(bf16[2,2,192,384]{3,2,1,0:T(8,128)(2,1)S(1)} %collective-permute-done.29) | copy-start | bytes 1769476
  227.1 2.8 collective-permute-start.30
  230.8 4.6 collective-permute-start.31
  237.0 29.0 %copy-start.3 = (bf16[1152,768]{1,0:T(8,128)(2,1)S(1)}, bf16[1152,768]{1,0:T(8,128)(2,1)}, u32[]{:S(2)}) copy-start(bf16[1152,768]{1,0:T(8,128)(2,1)} %get-tuple-element.135.refs_0_) | copy-start | bytes 5308420
  268.3 19.1 %collective-permute-start.34 = (bf16[384,768]{1,0:T(8,128)(2,1)S(1)}, bf16[384,768]{1,0:T(8,128)(2,1)S(1)}, u32[]{:S(2)}, u32[]{:S(2)}) collective-permute-start(bf16[384,768]{1,0:T(8,128)(2,1)S(1)} %convolution_convert_fusion.4), channel_id=1, source_target_pairs={{0,4},{4,0},{8,12},{12,8},{16,20},{20,16},{24,28},{28,24},{1,5},{5... | collective-permute-start | bytes 1769480 | tf_op jit(solution)/shard_map/ppermute | solution.py:45
  274.9 12.7 %collective-permute-start.33 = (bf16[384,3072]{1,0:T(8,128)(2,1)S(1)}, bf16[384,3072]{1,0:T(8,128)(2,1)S(1)}, u32[]{:S(2)}, u32[]{:S(2)}) collective-permute-start(bf16[384,3072]{1,0:T(8,128)(2,1)S(1)} %convolution_convert_fusion), channel_id=1, source_target_pairs={{0,4},{4,0},{8,12},{12,8},{16,20},{20,16},{24,28},{28,24},{1,5},{5... | collective-permute-start | bytes 7077896 | tf_op jit(solution)/shard_map/ppermute | solution.py:45
  279.3 9.1 %collective-permute-start.32 = (bf16[384,3072]{1,0:T(8,128)(2,1)S(1)}, bf16[384,3072]{1,0:T(8,128)(2,1)S(1)}, u32[]{:S(2)}, u32[]{:S(2)}) collective-permute-start(bf16[384,3072]{1,0:T(8,128)(2,1)S(1)} %convolution_convert_fusion.2), channel_id=1, source_target_pairs={{0,4},{4,0},{8,12},{12,8},{16,20},{20,16},{24,28},{28,24},{1,5},{5... | collective-permute-start | bytes 7077896 | tf_op jit(solution)/shard_map/ppermute | solution.py:45
  290.5 38.6 %collective-permute-start.38 = (bf16[96,6912]{1,0:T(8,128)(2,1)}, bf16[96,6912]{1,0:T(8,128)(2,1)S(1)}, u32[]{:S(2)}, u32[]{:S(2)}) collective-permute-start(bf16[96,6912]{1,0:T(8,128)(2,1)} %pad_maximum_fusion.1.refs_8_), channel_id=1, source_target_pairs={{0,8},{4,12},{8,0},{12,4},{16,24},{20,28},{24,16},{28,20},{1,9},{5... | collective-permute-start | bytes 3981320 | tf_op jit(solution)/shard_map/ppermute | solution.py:45
  292.3 36.8 %collective-permute-start.39 = (bf16[96,6912]{1,0:T(8,128)(2,1)}, bf16[96,6912]{1,0:T(8,128)(2,1)}, u32[]{:S(2)}, u32[]{:S(2)}) collective-permute-start(bf16[96,6912]{1,0:T(8,128)(2,1)} %pad_maximum_fusion.2.refs_9_), channel_id=1, source_target_pairs={{0,16},{4,20},{8,24},{12,28},{16,0},{20,4},{24,8},{28,12},{1,17},{... | collective-permute-start | bytes 3981320 | tf_op jit(solution)/shard_map/ppermute | solution.py:45
  310.9 2.3 collective-permute-start.35
  328.9 2.3 collective-permute-start.36
  329.1 32.7 %collective-permute-start.43 = (bf16[96,6912]{1,0:T(8,128)(2,1)}, bf16[96,6912]{1,0:T(8,128)(2,1)}, u32[]{:S(2)}, u32[]{:S(2)}) collective-permute-start(bf16[96,6912]{1,0:T(8,128)(2,1)} %pad_maximum_fusion.3.refs_10_), channel_id=1, source_target_pairs={{0,24},{4,28},{8,16},{12,20},{16,8},{20,12},{24,0},{28,4},{1,25},{... | collective-permute-start | bytes 3981320 | tf_op jit(solution)/shard_map/ppermute | solution.py:45
  329.6 9.0 %collective-permute-start.37 = (bf16[2,96,768]{2,1,0:T(8,128)(2,1)S(1)}, bf16[2,96,768]{2,1,0:T(8,128)(2,1)S(1)}, u32[]{:S(2)}, u32[]{:S(2)}) collective-permute-start(bf16[2,96,768]{2,1,0:T(8,128)(2,1)S(1)} %copy-done.21), channel_id=1, source_target_pairs={{0,1},{1,0},{2,3},{3,2},{4,5},{5,4},{6,7},{7,6},{8,9},{9,8},{10,11... | collective-permute-start | bytes 884744 | tf_op jit(solution)/shard_map/ppermute | solution.py:50
  353.0 2.3 collective-permute-start.41
  354.8 13.4 %collective-permute-start.40 = (bf16[2,96,768]{2,1,0:T(8,128)(2,1)S(1)}, bf16[2,96,768]{2,1,0:T(8,128)(2,1)}, u32[]{:S(2)}, u32[]{:S(2)}) collective-permute-start(bf16[2,96,768]{2,1,0:T(8,128)(2,1)S(1)} %copy-done.20), channel_id=1, source_target_pairs={{0,1},{1,0},{2,3},{3,2},{4,5},{5,4},{6,7},{7,6},{8,9},{9,8},{10,11... | collective-permute-start | bytes 884744 | tf_op jit(solution)/shard_map/ppermute | solution.py:50
  357.2 13.4 %collective-permute-start.42 = (bf16[2,96,768]{2,1,0:T(8,128)(2,1)}, bf16[2,96,768]{2,1,0:T(8,128)(2,1)}, u32[]{:S(2)}, u32[]{:S(2)}) collective-permute-start(bf16[2,96,768]{2,1,0:T(8,128)(2,1)} %fusion.11), channel_id=1, source_target_pairs={{0,1},{1,0},{2,3},{3,2},{4,5},{5,4},{6,7},{7,6},{8,9},{9,8},{10,11... | collective-permute-start | bytes 884744 | tf_op jit(solution)/shard_map/ppermute | solution.py:50
  370.6 25.6 %copy-start.11 = (bf16[96,3456]{1,0:T(8,128)(2,1)S(1)}, bf16[96,3456]{1,0:T(8,128)(2,1)}, u32[]{:S(2)}) copy-start(bf16[96,3456]{1,0:T(8,128)(2,1)} %concatenate.170.refs_30_) | copy-start | bytes 1990660
  394.0 4.8 collective-permute-start.44
  396.3 17.4 %collective-permute-start.48 = (bf16[96,3456]{1,0:T(8,128)(2,1)S(1)}, bf16[96,3456]{1,0:T(8,128)(2,1)S(1)}, u32[]{:S(2)}, u32[]{:S(2)}) collective-permute-start(bf16[96,3456]{1,0:T(8,128)(2,1)S(1)} %copy-done.11), channel_id=1, source_target_pairs={{0,1},{1,0},{2,3},{3,2},{4,5},{5,4},{6,7},{7,6},{8,9},{9,8},{10,11... | collective-permute-start | bytes 1990664 | tf_op jit(solution)/shard_map/ppermute | solution.py:50
  402.6 16.9 %collective-permute-start.47 = (bf16[96,2944]{1,0:T(8,128)(2,1)}, bf16[96,2944]{1,0:T(8,128)(2,1)}, u32[]{:S(2)}, u32[]{:S(2)}) collective-permute-start(bf16[96,2944]{1,0:T(8,128)(2,1)} %get-tuple-element.235), channel_id=1, source_target_pairs={{0,24},{4,28},{8,16},{12,20},{16,8},{20,12},{24,0},{28,4},{1,25},{... | collective-permute-start | bytes 1695752 | tf_op jit(solution)/shard_map/ppermute | solution.py:45
  405.2 25.6 %collective-permute-start.46 = (bf16[96,2944]{1,0:T(8,128)(2,1)}, bf16[96,2944]{1,0:T(8,128)(2,1)}, u32[]{:S(2)}, u32[]{:S(2)}) collective-permute-start(bf16[96,2944]{1,0:T(8,128)(2,1)} %get-tuple-element.234), channel_id=1, source_target_pairs={{0,16},{4,20},{8,24},{12,28},{16,0},{20,4},{24,8},{28,12},{1,17},{... | collective-permute-start | bytes 1695752 | tf_op jit(solution)/shard_map/ppermute | solution.py:45
  405.2 25.6 %collective-permute-start.45 = (bf16[96,2944]{1,0:T(8,128)(2,1)}, bf16[96,2944]{1,0:T(8,128)(2,1)}, u32[]{:S(2)}, u32[]{:S(2)}) collective-permute-start(bf16[96,2944]{1,0:T(8,128)(2,1)} %get-tuple-element.236), channel_id=1, source_target_pairs={{0,8},{4,12},{8,0},{12,4},{16,24},{20,28},{24,16},{28,20},{1,9},{5... | collective-permute-start | bytes 1695752 | tf_op jit(solution)/shard_map/ppermute | solution.py:45
  414.7 31.5 %collective-permute-start.53 = (bf16[96,1728]{1,0:T(8,128)(2,1)S(1)}, bf16[96,1728]{1,0:T(8,128)(2,1)S(1)}, u32[]{:S(2)}, u32[]{:S(2)}) collective-permute-start(bf16[96,1728]{1,0:T(8,128)(2,1)S(1)} %get-tuple-element.267), channel_id=1, source_target_pairs={{0,2},{1,3},{2,0},{3,1},{4,6},{5,7},{6,4},{7,5},{8,10},{9,11},{10,... | collective-permute-start | bytes 995336 | tf_op jit(solution)/shard_map/ppermute | solution.py:50
  432.8 4.9 %collective-permute-start.51 = (bf16[24,1280]{1,0:T(8,128)(2,1)S(1)}, bf16[24,1280]{1,0:T(8,128)(2,1)S(1)}, u32[]{:S(2)}, u32[]{:S(2)}) collective-permute-start(bf16[24,1280]{1,0:T(8,128)(2,1)S(1)} %pad_maximum_fusion.13), channel_id=1, source_target_pairs={{0,1},{1,0},{2,3},{3,2},{4,5},{5,4},{6,7},{7,6},{8,9},{9,8},{10,11... | collective-permute-start | bytes 184328 | tf_op jit(solution)/shard_map/ppermute | solution.py:50
  433.7 8.1 %collective-permute-start.49 = (bf16[96,1152]{1,0:T(8,128)(2,1)S(1)}, bf16[96,1152]{1,0:T(8,128)(2,1)S(1)}, u32[]{:S(2)}, u32[]{:S(2)}) collective-permute-start(bf16[96,1152]{1,0:T(8,128)(2,1)S(1)} %pad_maximum_fusion.9), channel_id=1, source_target_pairs={{0,1},{1,0},{2,3},{3,2},{4,5},{5,4},{6,7},{7,6},{8,9},{9,8},{10,11... | collective-permute-start | bytes 663560 | tf_op jit(solution)/shard_map/ppermute | solution.py:50
  438.4 7.8 %collective-permute-start.52 = (bf16[24,640]{1,0:T(8,128)(2,1)S(1)}, bf16[24,640]{1,0:T(8,128)(2,1)S(1)}, u32[]{:S(2)}, u32[]{:S(2)}) collective-permute-start(bf16[24,640]{1,0:T(8,128)(2,1)S(1)} %get-tuple-element.272), channel_id=1, source_target_pairs={{0,2},{1,3},{2,0},{3,1},{4,6},{5,7},{6,4},{7,5},{8,10},{9,11},{10,... | collective-permute-start | bytes 92168 | tf_op jit(solution)/shard_map/ppermute | solution.py:50
  442.8 7.9 %collective-permute-start.50 = (bf16[96,576]{1,0:T(8,128)(2,1)S(1)}, bf16[96,576]{1,0:T(8,128)(2,1)S(1)}, u32[]{:S(2)}, u32[]{:S(2)}) collective-permute-start(bf16[96,576]{1,0:T(8,128)(2,1)S(1)} %get-tuple-element.276), channel_id=1, source_target_pairs={{0,2},{1,3},{2,0},{3,1},{4,6},{5,7},{6,4},{7,5},{8,10},{9,11},{10,... | collective-permute-start | bytes 331784 | tf_op jit(solution)/shard_map/ppermute | solution.py:50
  453.9 1.5 collective-permute-start.54
  456.2 4.2 collective-permute-start.55
  460.4 4.2 collective-permute-start.56
  464.6 4.2 collective-permute-start.57
  468.9 5.5 %collective-permute-start.58 = (f32[56,192]{1,0:T(8,128)S(1)}, f32[56,192]{1,0:T(8,128)S(1)}, u32[]{:S(2)}, u32[]{:S(2)}) collective-permute-start(f32[56,192]{1,0:T(8,128)S(1)} %add.706.refs_1_), channel_id=1, source_target_pairs={{0,2},{1,3},{2,0},{3,1},{4,6},{5,7},{6,4},{7,5},{8,10},{9,11},{10,... | collective-permute-start | bytes 129032 | tf_op jit(solution)/shard_map/ppermute | solution.py:50
  (49 other events, 501.0 us)

commit v5 on v4

--- a/solution.py
+++ b/solution.py
@@ -203,48 +203,59 @@
     )
 
 
-def memory_in_kernel(index_ref, order_ref, one_ref, two_ref, three_ref, four_ref, out_ref):
-    parts = [r[0, 0] for r in (one_ref, two_ref, three_ref, four_ref)]
-    blocks = []
+def memory_in_kernel(index_ref, order_ref, *refs):
+    parts, (out_ref, held, sems) = refs[:4], refs[4:]
+    columns = parts[0].shape[2]
+
+    def copy(p, c):
+        target = held.at[:, :, c * columns : (c + 1) * columns]
+        return pltpu.make_async_copy(parts[p], target, sems.at[c])
+
     for c in range(4):
-        s = index_ref[c]
-        chosen = parts[3]
-        for p in (2, 1, 0):
-            chosen = jnp.where(s == p, parts[p], chosen)
-        blocks.append(chosen)
-    out_ref[0, 0] = contract_last(order_ref[...], jnp.concatenate(blocks)).astype(bf16)
+        for p in range(4):
+
+            @pl.when(index_ref[c] == p)
+            def _(p=p, c=c):
+                copy(p, c).start()
+
+    for c in range(4):
+        copy(0, c).wait()
+    order = order_ref[...]
+    for m in range(2):
+        for ch in range(2):
+            out_ref[m, ch] = contract_last(order, held[m, ch]).astype(bf16)
 
 
 def memory_in(index, order, parts, events=()):
     _, _, columns, rows = parts[0].shape
     return call(
         memory_in_kernel,
-        (2, 2),
-        [pl.BlockSpec(memory_space=pltpu.SMEM), pl.BlockSpec((rows, rows), lambda i, j: (0, 0))]
-        + [pl.BlockSpec((1, 1, columns, rows), lambda i, j: (i, j, 0, 0))] * 4,
-        pl.BlockSpec((1, 1, rows, 4 * columns), lambda i, j: (i, j, 0, 0)),
+        (1,),
+        [pl.BlockSpec(memory_space=pltpu.SMEM), whole(order)]
+        + [pl.BlockSpec(memory_space=pl.ANY)] * 4,
+        pl.BlockSpec((2, 2, rows, 4 * columns), lambda i: (0, 0, 0, 0)),
         jax.ShapeDtypeStruct((2, 2, rows, 4 * columns), bf16),
         (index, order) + tuple(parts),
-        8 * rows * rows * 4 * columns,
+        0,
+        scratch=[
+            pltpu.VMEM((2, 2, 4 * columns, rows), bf16),
+            pltpu.SemaphoreType.DMA((4,)),
+        ],
         events=events,
     )
 
 
 def memory_out_kernel(index_ref, order_ref, *refs):
-    out_ref = refs[-1]
-    chosen = index_ref[0]
+    out_ref, turned = refs[-2:]
+    columns = turned.shape[0] // 4
+    at = pl.multiple_of(index_ref[0] * columns, 64)
     for m in range(2):
         rows = jnp.concatenate([r[0, 0] for r in refs[4 * m : 4 * m + 4]])
-        turned = contract_rows(rows, order_ref[...]).astype(bf16)
-        columns = turned.shape[0] // 4
-        blocks = [turned[c * columns : (c + 1) * columns] for c in range(4)]
-        block = blocks[3]
-        for c in (2, 1, 0):
-            block = jnp.where(chosen == c, blocks[c], block)
-        out_ref[m, 0] = block
-
-
-def memory_out(index, order, parts):
+        turned[...] = contract_rows(rows, order_ref[...])
+        out_ref[m, 0] = turned[pl.ds(at, columns)].astype(bf16)
+
+
+def memory_out(index, order, parts, events=()):
     _, _, rows, width = parts[0][0].shape
     return call(
         memory_out_kernel,
@@ -258,6 +269,8 @@
         jax.ShapeDtypeStruct((2, 2, width // 4, 4 * rows), bf16),
         (index, order) + tuple(a for a, _ in parts),
         8 * (4 * rows) ** 2 * width,
+        scratch=[pltpu.VMEM((width, 4 * rows), f32)],
+        events=events,
     )
 
 
@@ -386,9 +399,15 @@
     lane = lax.broadcasted_iota(jnp.int32, (rows, width), 1) // size
     scaled = query * (size**-0.5)
     total = query.astype(f32)
+    def score(h):
+        own = jnp.where(lane == h, scaled, jnp.zeros_like(scaled))
+        return product(own, keys_t) + bias_ref[0, h : h + 1, :]
+
+    following = score(0)
     for h in range(QUAD):
-        own = jnp.where(lane == h, scaled, jnp.zeros_like(scaled))
-        scores = product(own, keys_t) + bias_ref[0, h : h + 1, :]
+        scores = following
+        if h + 1 < QUAD:
+            following = score(h + 1)
         top = jnp.max(scores, axis=-1, keepdims=True)
         exponent = jnp.exp(scores - top)
         denominator = jnp.sum(exponent, axis=-1, keepdims=True)
@@ -464,11 +483,18 @@
     half = count // 2
     spot = lax.broadcasted_iota(jnp.int32, (1, 128), 1)
     key_parts, value_parts = [], []
+    def pull(h):
+        own = jnp.where(lane == h, grad, jnp.zeros_like(grad))
+        return product(own, values_t)
+
+    following = pull(0)
     for h in range(QUAD):
-        own = jnp.where(lane == h, grad, jnp.zeros_like(grad))
+        current = following
+        if h + 1 < QUAD:
+            following = pull(h + 1)
         probs_low = prob_ref[h]
         probs = probs_low.astype(f32)
-        pulled = probs * product(own, values_t)
+        pulled = probs * current
         shift = jnp.sum(pulled, axis=-1, keepdims=True)
         score_grad = (pulled - probs * shift).astype(bf16)
         total = total + jnp.where(lane == h, product(score_grad, keys), 0.0)
@@ -603,9 +629,16 @@
         finish(copies)
 
     chunk = units // 4
+
+    def entry(s):
+        return product(normed, both_s[:, (2 * s + 1) * chunk : (2 * s + 2) * chunk])
+
+    following = entry(0)
     for s in range(4):
         at = s * chunk
-        hidden = product(normed, both_s[:, 2 * at + chunk : 2 * at + 2 * chunk])
+        hidden = following
+        if s < 3:
+            following = entry(s + 1)
         value, slope = gelu_pair(hidden)
         value = value.astype(bf16)
         active_ref[:, at : at + chunk] = value
@@ -693,6 +726,7 @@
 
     chunk = units // 4
     normed_grad = jnp.zeros(second_grad.shape, f32)
+
     for s in range(4):
         at = s * chunk
         active_grad = product(branch, both_s[:, 2 * at : 2 * at + chunk])
@@ -1070,18 +1104,16 @@
         axis=1,
     )
     weights = spread_core(spread_dp(weights))
+    patches_t = regroup(after(patches.transpose(0, 2, 1), *pieces))
     pieces = gather_mp(
         after(
             jnp.concatenate(
                 [down_low[:, head_cols:], up_low[:, 3 * head_cols :], down_low[:, :head_cols]],
                 axis=1,
             ),
-            *pieces,
+            patches_t,
         )
     )
-    rest = join(2 * hidden_cols, across[None], pieces)
-    patches_t = regroup(after(patches.transpose(0, 2, 1), rest))
-    rest = [rest, swap_dp(rest, 2), swap_dp(rest, 4)]
 
     place = jnp.arange(rows)
     token = 8 * (place % eighth) + 4 * ((place // eighth) % 2) + place // (2 * eighth)
@@ -1090,26 +1122,6 @@
     half_mem = mem_rows // 2
     mem_place = jnp.arange(mem_rows)
     mem_order = one_hot_rows(2 * (mem_place % half_mem) + mem_place // half_mem, mem_rows)
-    (
-        patches_in,
-        embedded,
-        normed,
-        query,
-        raw_keys,
-        raw_values,
-        pools,
-        vectors,
-        head_low,
-    ) = embed(patches_t, token_order, conv_all, weights, classes, events=tuple(rest[1:]))
-    rest_late = after(rest[0], *rest[1:])
-    rest_late = [swap_dp(rest_late, b) for b in range(6, dp_count, 2)]
-    two = swap_mp(pools, 1)
-    gathered = (pools, swap_dp(pools, 1), two, swap_dp(two, 1))
-    stored = [[(a, m) for a in gathered] for m in range(MICRO)]
-    memory_t = regroup(after(memory.transpose(0, 1, 3, 2), pools))
-    mem_two = swap_mp(after(memory_t, two), 1)
-    stored = [None, None] + stored
-
     part_quarter = [2 * (core ^ (s % 2)) + (across ^ (s // 2)) for s in range(4)]
     pool_place = jnp.arange(pooled)
     pool_token = 2 * (pool_place % half_pool) + pool_place // half_pool
@@ -1131,11 +1143,37 @@
             axis=1,
         ).reshape(heads // QUAD, QUAD, -1)
 
+    biases = [key_bias(m) for m in range(MICRO)]
+
+    (
+        patches_in,
+        embedded,
+        normed,
+        query,
+        raw_keys,
+        raw_values,
+        pools,
+        vectors,
+        head_low,
+    ) = embed(patches_t, token_order, conv_all, weights, classes)
+    two = swap_mp(pools, 1)
+    rest = join(2 * hidden_cols, across[None], [after(p, pools) for p in pieces])
+    rest = [rest, swap_dp(rest, 2), swap_dp(rest, 4)]
+    rest_late = after(rest[0], *rest[1:])
+    rest_late = [swap_dp(rest_late, b) for b in range(6, dp_count, 2)]
+    gathered = (pools, swap_dp(pools, 1), two, swap_dp(after(two, *biases), 1))
+    stored = [[(a, m) for a in gathered] for m in range(MICRO)]
+    memory_t = regroup(after(memory.transpose(0, 1, 3, 2), rest[0]))
+    mem_two = swap_mp(after(memory_t, two), 1)
+    stored = [None, None] + stored
+
     attended, saved = None, {}
     for m in (2, 1, 0):
         attended, probs, keys, values = attend(
-            m, query, conv_all, key_bias(m), stored[m + 2], stored[m + 1], stored[m], attended,
+            m, query, conv_all, biases[m], stored[m + 2], stored[m + 1], stored[m], attended,
             events=tuple(rest_late) if m == 0 else (),
+        ) if m < 2 else attend(
+            m, after(query, *rest[1:]), conv_all, biases[m], stored[m + 2], stored[m + 1], stored[m], attended,
         )
         saved[m] = (keys, values, probs)
         if m == 2:
@@ -1143,18 +1181,6 @@
         if m == 1:
             late_core = [swap_dp(after(p, attended), 1) for p in rest_late]
         if m > 1:
-            target_row = jnp.arange(4 * pooled)
-            target_quarter, target_rest = target_row // pooled, target_row % pooled
-            source_row = (
-                (((target_quarter // 2) ^ core) + 2 * ((target_quarter % 2) ^ across)) * pooled
-                + (target_rest % 2) * half_pool
-                + target_rest // 2
-            )
-            new_memory = memory_out(
-                (quarter ^ upper)[None],
-                one_hot_rows(source_row, 4 * pooled).T,
-                stored[3] + stored[4],
-            )
             mem_two = after(mem_two, attended)
             mem_parts = (
                 memory_t,
@@ -1171,9 +1197,7 @@
                 ),
                 mem_order,
                 mem_parts,
-                events=(new_memory,),
             )
-            new_memory = regroup(new_memory)
             stored[:2] = [[(mem_full, 0)], [(mem_full, 1)]]
     rest = one_or_all(rest + rest_late + rest_core + late_core)
 
@@ -1192,7 +1216,20 @@
     first_res, normed_mlp, active, slope, second_res, feature = mlp(
         attended, embedded, vectors, select, rest
     )
-    feature = after(feature.reshape(MICRO * boxes, width), new_memory)
+    target_row = jnp.arange(4 * pooled)
+    target_quarter, target_rest = target_row // pooled, target_row % pooled
+    source_row = (
+        (((target_quarter // 2) ^ core) + 2 * ((target_quarter % 2) ^ across)) * pooled
+        + (target_rest % 2) * half_pool
+        + target_rest // 2
+    )
+    new_memory = memory_out(
+        (quarter ^ upper)[None],
+        one_hot_rows(source_row, 4 * pooled).T,
+        stored[3] + stored[4],
+        events=(feature,),
+    )
+    feature = feature.reshape(MICRO * boxes, width)
     feature = group_sum_features(feature).astype(bf16)
     logits = contract_last(feature, head_low)
     target = labels.astype(f32)
@@ -1204,8 +1241,11 @@
     grad_head = contract_rows(grad_logits, feature) * lead
     grad_feature = product(grad_logits, head_low).reshape(MICRO, boxes, width)
     grad_branch, grad_hidden, grad_attn, grad_first, grad_attended, sums = mlp_back(
-        grad_feature, select, second_res, first_res, slope, vectors, rest
-    )
+        grad_feature, select, second_res, first_res, slope, vectors, rest, (new_memory,)
+    )
+    new_memory = regroup(new_memory)
+    grad_branch = after(grad_branch, new_memory)
+
     half = width // 2
 
     def weight_grad(left, right, at):

time: 489 us -> 474 us (0.969)
  starting transfers between devices: 75.2 us -> 67.4 us
  waiting for transfers between devices: 116 us -> 109 us
  Pallas kernels: 189 us -> 183 us
    ppermute x20, waiting for transfers between devices: 75.9 us -> 68 us  [swap_mp(): return lax.ppermute(inputs, 'mp', [(i, i ^ mask) for i in range(size)])]
    ppermute x20, starting transfers between devices: 34.4 us -> 27.7 us  [swap_mp(): return lax.ppermute(inputs, 'mp', [(i, i ^ mask) for i in range(size)])]
    pallas_call x15, Pallas kernels: 189 us -> 183 us  [call(): pl.pallas_call(run, grid=grid, in_specs=list(in_specs) + [pl.BlockSpec(me...]
    ppermute x35, starting transfers between devices: 27.6 us -> 21.7 us  [swap_dp(): return lax.ppermute(inputs, 'dp', [(i, i ^ mask) for i in range(size)])]
    unnamed x116 -> x124, local copies, waits for them, and re-layouts: 10.5 us -> 11.1 us
  transfers between devices with their start and end apart: 59 -> 59, of which waited for: 29 -> 27; matrix products, arithmetic and copies ran while one was open for 13% -> 15% of each run, Pallas kernels for 27% -> 25%
where the time goes in v5:
time: 474 us; the launch traced here: 466 us
  Pallas kernels  183 us (39%)
  waiting for transfers between devices  109 us (23%)
  starting transfers between devices  67.4 us (14%)
  other arithmetic  41.4 us (9%)
  local copies, waits for them, and re-layouts  25.4 us (5%)
  matrix products  23.8 us (5%)
  between operations  16.5 us (3%)
    pallas_call x15, Pallas kernels, call(): pl.pallas_call(run, grid=grid, in_specs=list(in_specs) + [pl.BlockSpec(me...  183 us
    ppermute x20, waiting for transfers between devices, swap_mp(): return lax.ppermute(inputs, 'mp', [(i, i ^ mask) for i in range(size)])  68 us
    ppermute x35, waiting for transfers between devices, swap_dp(): return lax.ppermute(inputs, 'dp', [(i, i ^ mask) for i in range(size)])  41 us
    ppermute x20, starting transfers between devices, swap_mp(): return lax.ppermute(inputs, 'mp', [(i, i ^ mask) for i in range(size)])  27.7 us
    dot_general x7, matrix products, contract_rows(): lax.dot_general(first_operand, second_operand, (((0,), (0,)), ((), ())),...  22 us
    ppermute x35, starting transfers between devices, swap_dp(): return lax.ppermute(inputs, 'dp', [(i, i ^ mask) for i in range(size)])  21.7 us
    ppermute x4, starting transfers between devices, regroup(): return lax.ppermute(inputs, ('dp', 'mp'), pairs)  18 us
    unnamed x124, local copies, waits for them, and re-layouts  11.1 us
  transfers between devices with their start and end apart: 59, of which 27 were waited for; matrix products, arithmetic and copies ran while one was open for 15% of the time, Pallas kernels for 25%

profile of v5, /device:TPU:0, one launch (start us, length us, event | category | flops | bytes accessed | tf_op | source)
XLA Modules:
  0.0 466.3 jit_solution(17159998332342622930)
XLA Ops:
  6.9 3.1 collective-permute-start
  10.0 2.6 collective-permute-start.1
  15.6 1.5 collective-permute-done
  17.2 8.5 %collective-permute-done.1 = bf16[96,832]{1,0:T(8,128)(2,1)S(1)} collective-permute-done((bf16[96,832]{1,0:T(8,128)(2,1)S(1)}, bf16[96,832]{1,0:T(8,128)(2,1)S(1)}, u32[]{:S(2)}, u32[]{:S(2)}) %collective-permute-start.1) | collective-permute-done | bytes 159776 | tf_op jit(solution)/shard_map/ppermute | solution.py:50
  27.8 1.6 collective-permute-start.4
  29.4 9.4 %collective-permute-start.3 = (bf16[3,441,384]{2,1,0:T(8,128)(2,1)}, bf16[3,441,384]{2,1,0:T(8,128)(2,1)}, u32[]{:S(2)}, u32[]{:S(2)}) collective-permute-start(bf16[3,441,384]{2,1,0:T(8,128)(2,1)} %bitcast.1), channel_id=1, source_target_pairs={{0,0},{1,1},{2,4},{3,5},{4,2},{5,3},{6,6},{7,7},{8,8},{9,9},{10,12... | collective-permute-start | bytes 3048200 | tf_op jit(solution)/shard_map/ppermute | solution.py:64
  39.9 1.5 collective-permute-start.5
  56.2 6.9 %collective-permute-done.5.refs_5_.refs_22_ = bf16[96,2944]{1,0:T(8,128)(2,1)S(1)} collective-permute-done((bf16[96,2944]{1,0:T(8,128)(2,1)S(1)}, bf16[96,2944]{1,0:T(8,128)(2,1)S(1)}, u32[]{:S(2)}, u32[]{:S(2)}) %collective-permute-start.5) | collective-permute-done | bytes 565280 | tf_op jit(solution)/shard_map/ppermute | solution.py:45
  64.1 4.0 collective-permute-start.13
  68.8 1.5 reshape.667.refs_2_.refs_1_.refs_3_
  70.4 12.7 %shard_map.466 = (bf16[1152,441]{1,0:T(8,128)(2,1)}, f32[1152,768]{1,0:T(8,128)}, bf16[1152,768]{1,0:T(8,128)(2,1)}, bf16[1152,768]{1,0:T(8,128)(2,1)}, bf16[115...) custom-call(bf16[3,441,384]{2,1,0:T(8,128)(2,1)} %collective-permute, ...), custom_call_target="tpu_custom_call" | custom-call | flops 1000 | bytes 1000 | tf_op jit(solution)/shard_map/pallas_call | solution.py:143
  83.1 7.6 %collective-permute-done.12.refs_3_ = bf16[96,1728]{1,0:T(8,128)(2,1)} collective-permute-done((bf16[96,1728]{1,0:T(8,128)(2,1)}, bf16[96,1728]{1,0:T(8,128)(2,1)}, u32[]{:S(2)}, u32[]{:S(2)}) %collective-permute-start.12) | collective-permute-done | bytes 331808 | tf_op jit(solution)/shard_map/ppermute | solution.py:50
  90.7 2.5 shard_map.467.refs_4_.refs_6_
  93.8 1.5 collective-permute-start.15
  98.1 7.1 %collective-permute-start.18 = (bf16[3,2,96,768]{3,2,1,0:T(8,128)(2,1)S(1)}, bf16[3,2,96,768]{3,2,1,0:T(8,128)(2,1)S(1)}, u32[]{:S(2)}, u32[]{:S(2)}) collective-permute-start(bf16[3,2,96,768]{3,2,1,0:T(8,128)(2,1)S(1)} %copy-done), channel_id=1, source_target_pairs={{0,1},{1,0},{2,3},{3,2},{4,5},{5,4},{6,7},{7,6},{8,9},{9,8},{10,11... | collective-permute-start | bytes 2654216 | tf_op jit(solution)/shard_map/ppermute | solution.py:50
  105.8 6.2 %collective-permute-start.20 = (bf16[2,2,192,384]{3,2,1,0:T(8,128)(2,1)}, bf16[2,2,192,384]{3,2,1,0:T(8,128)(2,1)}, u32[]{:S(2)}, u32[]{:S(2)}) collective-permute-start(bf16[2,2,192,384]{3,2,1,0:T(8,128)(2,1)} %bitcast.17), channel_id=1, source_target_pairs={{0,0},{1,1},{2,4},{3,5},{4,2},{5,3},{6,6},{7,7},{8,8},{9,9},{10,12... | collective-permute-start | bytes 1769480 | tf_op jit(solution)/shard_map/ppermute | solution.py:64
  114.1 15.9 %collective-permute-done.18.refs_5_.refs_9_.refs_13_.refs_4_.refs_8_.refs_7_.refs_11_ = bf16[3,2,96,768]{3,2,1,0:T(8,128)(2,1)S(1)} collective-permute-done((bf16[3,2,96,768]{3,2,1,0:T(8,128)(2,1)S(1)}, bf16[3,2,96,768]{3,2,1,0:T(8,128)(2,1)S(1)}, u32[]{:S(2)}, u32[]{:S(2)}) %collective-permute-start.18) | collective-permute-done | bytes 884768 | tf_op jit(solution)/shard_map/ppermute | solution.py:50
  130.0 1.5 collective-permute-start.24
  131.5 2.0 collective-permute-start.22
  135.4 10.1 %shard_map.468 = (bf16[1152,768]{1,0:T(8,128)(2,1)}, bf16[12,384,768]{2,1,0:T(8,128)(2,1)}, bf16[768,768]{1,0:T(8,128)(2,1)}, bf16[768,768]{1,0:T(8,128)(2,1)}) custom-call(bf16[1152,768]{1,0:T(8,128)(2,1)} %get-tuple-element.135.refs_0_, f32[2,6,768]{2,1,0:T(8,128)} %reshape.667.refs_2_.refs_1_.refs_3_, f32[3,4,768]{2,1,0:T(4,128)} %pad_maximum_fusion.16.refs_2_, ...), custom_call_target="tpu_custom_call" | custom-call | flops 1000 | bytes 1000 | tf_op jit(solution)/shard_map/pallas_call | solution.py:143
  145.6 1.7 collective-permute-done.22.refs_4_
  150.9 5.5 %shard_map.469.refs_11_.refs_7_.refs_8_.refs_5_.refs_6_.refs_9_ = bf16[2,2,384,768]{3,2,1,0:T(8,128)(2,1)} custom-call(s32[4]{0:T(128)} %pad_add_fusion.2.refs_0_, bf16[384,384]{1,0:T(8,128)(2,1)} %fusion.7.refs_1_, bf16[2,2,192,384]{3,2,1,0:T(8,128)(2,1)} %collective-permute-done.20.refs_2_, bf16[2,2,192,384]{3,2,1,0:T(8,128)(2,1)} %copy-done.27, ...), custom_call_target="tpu_custom_call" | custom-call | flops 1000 | bytes 1000 | tf_op jit(solution)/shard_map/pallas_call | solution.py:143
  157.0 10.0 %shard_map.470 = (bf16[1152,768]{1,0:T(8,128)(2,1)}, bf16[12,384,768]{2,1,0:T(8,128)(2,1)}, bf16[768,768]{1,0:T(8,128)(2,1)}, bf16[768,768]{1,0:T(8,128)(2,1)}) custom-call(bf16[1152,768]{1,0:T(8,128)(2,1)} %get-tuple-element.135.refs_0_, f32[2,6,768]{2,1,0:T(8,128)} %reshape.667.refs_2_.refs_1_.refs_3_, ...), custom_call_target="tpu_custom_call", output_to_operand_aliasing={{0}: (12, {})} | custom-call | flops 1000 | bytes 1000 | tf_op jit(solution)/shard_map/pallas_call | solution.py:143
  169.3 9.9 %shard_map.471 = (bf16[1152,768]{1,0:T(8,128)(2,1)}, bf16[12,384,768]{2,1,0:T(8,128)(2,1)}, bf16[768,768]{1,0:T(8,128)(2,1)}, bf16[768,768]{1,0:T(8,128)(2,1)}) custom-call(bf16[1152,768]{1,0:T(8,128)(2,1)} %get-tuple-element.135.refs_0_, f32[2,6,768]{2,1,0:T(8,128)} %reshape.667.refs_2_.refs_1_.refs_3_, ...), custom_call_target="tpu_custom_call", output_to_operand_aliasing={{0}: (9, {})} | custom-call | flops 1000 | bytes 1000 | tf_op jit(solution)/shard_map/pallas_call | solution.py:143
  180.3 34.4 %shard_map.472 = (f32[1152,768]{1,0:T(8,128)}, bf16[1152,768]{1,0:T(8,128)(2,1)}, bf16[1152,3072]{1,0:T(8,128)(2,1)}, bf16[1152,3072]{1,0:T(8,128)(2,1)}, f32[1152,768]{1,0:T(8,128)}, /*index=5*/f32[3,8,768]{2,1,0:T(8,128)}) custom-call(bf16[1152,768]{1,0:T(8,128)(2,1)} %get-tuple-element.147.refs_0_, f32[1152,768]{1,0:T(8,128)} %get-tuple-element.148.refs_1_.refs_4_, ...), custom_call_target="tpu_custom_call" | custom-call | flops 1000 | bytes 1000 | tf_op jit(solution)/shard_map/pallas_call | solution.py:143
  217.9 4.3 shard_map.473.refs_14_
  222.1 1.7 collective-permute-start.31
  225.4 28.8 %shard_map.474 = (bf16[1152,768]{1,0:T(8,128)(2,1)}, bf16[1152,3072]{1,0:T(8,128)(2,1)}, bf16[1152,768]{1,0:T(8,128)(2,1)}, f32[1152,768]{1,0:T(8,128)}, bf16[1152,768]{1,0:T(8,128)(2,1)}, /*index=5*/f32[8,768]{1,0:T(8,128)}) custom-call(f32[3,8,768]{2,1,0:T(8,128)} %convolution_bitcast_fusion.refs_0_, f32[3,8,384]{2,1,0:T(8,128)} %convert_divide_fusion.refs_3_.refs_1_, ...), custom_call_target="tpu_custom_call" | custom-call | flops 1000 | bytes 1000 | tf_op jit(solution)/shard_map/pallas_call | solution.py:143
  254.2 2.3 convolution_convert_fusion.4
  256.5 2.4 collective-permute-start.34
  259.0 6.4 %convolution_convert_fusion = bf16[384,3072]{1,0:T(8,128)(2,1)S(1)} fusion(bf16[1152,3072]{1,0:T(8,128)(2,1)} %get-tuple-element.170, bf16[1152,768]{1,0:T(8,128)(2,1)S(1)} %copy-done.52), kind=kOutput, calls=%fused_computation | convolution fusion | flops 2719088640 | bytes 10321920 | tf_op jit(solution)/shard_map/dot_general | solution.py:38
  266.9 3.7 convolution_convert_fusion.2
  270.8 3.5 convolution_convert_fusion.1
  274.3 3.5 convolution_convert_fusion.3
  282.5 1.5 collective-permute-start.39
  286.4 11.3 %shard_map.475 = (bf16[1152,768]{1,0:T(8,128)(2,1)}, bf16[2,2,96,768]{3,2,1,0:T(8,128)(2,1)}, bf16[2,2,96,768]{3,2,1,0:T(8,128)(2,1)}, f32[2,2,768]{2,1,0:T(2,128)}, f32[3,4,128]{2,1,0:T(4,128)}) custom-call(bf16[1152,768]{1,0:T(8,128)(2,1)} %get-tuple-element.135.refs_0_, bf16[768,768]{1,0:T(8,128)(2,1)} %get-tuple-element.163.refs_1_, ...), custom_call_target="tpu_custom_call" | custom-call | flops 1000 | bytes 1000 | tf_op jit(solution)/shard_map/pallas_call | solution.py:143
  297.7 2.2 collective-permute-done.35.refs_12_
  299.9 1.9 fusion.9.refs_11_
  301.9 11.8 %shard_map.476 = (bf16[1152,768]{1,0:T(8,128)(2,1)}, bf16[2,2,96,768]{3,2,1,0:T(8,128)(2,1)}, bf16[2,2,96,768]{3,2,1,0:T(8,128)(2,1)}, f32[2,2,768]{2,1,0:T(2,128)}, f32[3,4,128]{2,1,0:T(4,128)}) custom-call(bf16[1152,768]{1,0:T(8,128)(2,1)} %get-tuple-element.135.refs_0_, ...), custom_call_target="tpu_custom_call", output_to_operand_aliasing={{0}: (10, {})} | custom-call | flops 1000 | bytes 1000 | tf_op jit(solution)/shard_map/pallas_call | solution.py:143
  313.9 2.4 collective-permute-start.43
  316.7 1.9 fusion.10.refs_14_
  318.6 5.8 %collective-permute-done.37.refs_15_.refs_13_ = bf16[2,96,768]{2,1,0:T(8,128)(2,1)S(1)} collective-permute-done((bf16[2,96,768]{2,1,0:T(8,128)(2,1)S(1)}, bf16[2,96,768]{2,1,0:T(8,128)(2,1)S(1)}, u32[]{:S(2)}, u32[]{:S(2)}) %collective-permute-start.37) | collective-permute-done | bytes 294944 | tf_op jit(solution)/shard_map/ppermute | solution.py:50
  325.1 11.3 %shard_map.477 = (bf16[1152,768]{1,0:T(8,128)(2,1)}, bf16[2,2,96,768]{3,2,1,0:T(8,128)(2,1)}, bf16[2,2,96,768]{3,2,1,0:T(8,128)(2,1)}, f32[2,2,768]{2,1,0:T(2,128)}, f32[3,4,128]{2,1,0:T(4,128)}) custom-call(bf16[1152,768]{1,0:T(8,128)(2,1)} %get-tuple-element.135.refs_0_, ...), custom_call_target="tpu_custom_call", output_to_operand_aliasing={{0}: (13, {})} | custom-call | flops 1000 | bytes 1000 | tf_op jit(solution)/shard_map/pallas_call | solution.py:143
  336.5 1.7 convolution_multiply_fusion.refs_9_
  338.7 1.9 fusion.11
  340.7 1.5 collective-permute-start.42
  342.2 4.4 collective-permute-done.43
  346.6 2.8 fusion.66
  354.1 23.3 %shard_map.478 = (bf16[384,2944]{1,0:T(8,128)(2,1)}, bf16[384,2944]{1,0:T(8,128)(2,1)}, f32[8,768]{1,0:T(8,128)}) custom-call(bf16[1152,768]{1,0:T(8,128)(2,1)} %get-tuple-element.178.refs_0_, bf16[1152,768]{1,0:T(8,128)(2,1)} %get-tuple-element.179.refs_1_, bf16[1152,768]{1,0:T(8,128)(2,1)} %get-tuple-element.180.refs_2_, ...), custom_call_target="tpu_custom_call" | custom-call | flops 1000 | bytes 1000 | tf_op jit(solution)/shard_map/pallas_call | solution.py:143
  383.6 3.9 add_convert_fusion.9
  391.1 6.2 %collective-permute-done.48 = bf16[96,3456]{1,0:T(8,128)(2,1)} collective-permute-done((bf16[96,3456]{1,0:T(8,128)(2,1)S(1)}, bf16[96,3456]{1,0:T(8,128)(2,1)}, u32[]{:S(2)}, u32[]{:S(2)}) %collective-permute-start.48) | collective-permute-done | bytes 663584 | tf_op jit(solution)/shard_map/ppermute | solution.py:50
  397.3 2.1 convert_add_fusion.2
  400.2 4.2 collective-permute-done.47
  404.3 11.3 %collective-permute-done.46 = bf16[96,2944]{1,0:T(8,128)(2,1)} collective-permute-done((bf16[96,2944]{1,0:T(8,128)(2,1)}, bf16[96,2944]{1,0:T(8,128)(2,1)}, u32[]{:S(2)}, u32[]{:S(2)}) %collective-permute-start.46) | collective-permute-done | bytes 565280 | tf_op jit(solution)/shard_map/ppermute | solution.py:45
  415.7 1.7 convert_add_fusion.1
  420.2 2.4 collective-permute-done.51
  424.0 2.7 collective-permute-done.49
  429.8 5.7 %collective-permute-done.50.refs_1_ = bf16[96,576]{1,0:T(8,128)(2,1)S(1)} collective-permute-done((bf16[96,576]{1,0:T(8,128)(2,1)S(1)}, bf16[96,576]{1,0:T(8,128)(2,1)S(1)}, u32[]{:S(2)}, u32[]{:S(2)}) %collective-permute-start.50) | collective-permute-done | bytes 110624 | tf_op jit(solution)/shard_map/ppermute | solution.py:50
  436.1 2.5 shard_map.479
  441.5 3.6 collective-permute-done.55
  445.2 4.1 collective-permute-done.56
  449.4 4.2 collective-permute-done.57
  454.2 4.7 %collective-permute-done.58.refs_2_ = f32[56,192]{1,0:T(8,128)S(1)} collective-permute-done((f32[56,192]{1,0:T(8,128)S(1)}, f32[56,192]{1,0:T(8,128)S(1)}, u32[]{:S(2)}, u32[]{:S(2)}) %collective-permute-start.58) | collective-permute-done | bytes 43040 | tf_op jit(solution)/shard_map/ppermute | solution.py:50
  459.4 4.5 shard_map.480
  (349 shorter events, 74.6 us)
Async XLA Ops:
  6.9 10.2 %collective-permute-start = (bf16[96,832]{1,0:T(8,128)(2,1)S(1)}, bf16[96,832]{1,0:T(8,128)(2,1)S(1)}, u32[]{:S(2)}, u32[]{:S(2)}) collective-permute-start(bf16[96,832]{1,0:T(8,128)(2,1)S(1)} %maximum_maximum_fusion), channel_id=1, source_target_pairs={{0,1},{1,0},{2,3},{3,2},{4,5},{5,4},{6,7},{7,6},{8,9},{9,8},{10,11... | collective-permute-start | bytes 479240 | tf_op jit(solution)/shard_map/ppermute | solution.py:50
  10.0 15.7 %collective-permute-start.1 = (bf16[96,832]{1,0:T(8,128)(2,1)S(1)}, bf16[96,832]{1,0:T(8,128)(2,1)S(1)}, u32[]{:S(2)}, u32[]{:S(2)}) collective-permute-start(bf16[96,832]{1,0:T(8,128)(2,1)S(1)} %maximum_maximum_fusion), channel_id=1, source_target_pairs={{0,2},{1,3},{2,0},{3,1},{4,6},{5,7},{6,4},{7,5},{8,10},{9,11},{10,... | collective-permute-start | bytes 479240 | tf_op jit(solution)/shard_map/ppermute | solution.py:50
  12.6 13.2 %collective-permute-start.2 = (bf16[96,832]{1,0:T(8,128)(2,1)S(1)}, bf16[96,832]{1,0:T(8,128)(2,1)S(1)}, u32[]{:S(2)}, u32[]{:S(2)}) collective-permute-start(bf16[96,832]{1,0:T(8,128)(2,1)S(1)} %maximum_maximum_fusion), channel_id=1, source_target_pairs={{0,3},{1,2},{2,1},{3,0},{4,7},{5,6},{6,5},{7,4},{8,11},{9,10},{10,... | collective-permute-start | bytes 479240 | tf_op jit(solution)/shard_map/ppermute | solution.py:50
  13.0 28.9 %collective-permute-start.16 = (s32[16,128]{1,0:T(8,128)S(1)}, s32[16,128]{1,0:T(8,128)S(1)}, u32[]{:S(2)}, u32[]{:S(2)}) collective-permute-start(s32[16,128]{1,0:T(8,128)S(1)} %pad_bitcast_fusion), channel_id=1, source_target_pairs={{0,0},{1,1},{2,4},{3,5},{4,2},{5,3},{6,6},{7,7},{8,8},{9,9},{10,12... | collective-permute-start | bytes 24584 | tf_op jit(solution)/shard_map/ppermute | solution.py:64
  27.8 42.5 %copy-start.9 = (bf16[96,2944]{1,0:T(8,128)(2,1)}, bf16[96,2944]{1,0:T(8,128)(2,1)S(1)}, u32[]{:S(2)}) copy-start(bf16[96,2944]{1,0:T(8,128)(2,1)S(1)} %concatenate.155.refs_3_.refs_20_) | copy-start | bytes 1695748
  27.8 25.2 %collective-permute-start.4 = (bf16[96,2944]{1,0:T(8,128)(2,1)S(1)}, bf16[96,2944]{1,0:T(8,128)(2,1)S(1)}, u32[]{:S(2)}, u32[]{:S(2)}) collective-permute-start(bf16[96,2944]{1,0:T(8,128)(2,1)S(1)} %concatenate.155.refs_3_.refs_20_), channel_id=1, source_target_pairs={{0,8},{4,12},{8,0},{12,4},{16,24},{20,28},{24,16},{28,20},{1,9},{5... | collective-permute-start | bytes 1695752 | tf_op jit(solution)/shard_map/ppermute | solution.py:45
  29.4 34.3 %collective-permute-start.3 = (bf16[3,441,384]{2,1,0:T(8,128)(2,1)}, bf16[3,441,384]{2,1,0:T(8,128)(2,1)}, u32[]{:S(2)}, u32[]{:S(2)}) collective-permute-start(bf16[3,441,384]{2,1,0:T(8,128)(2,1)} %bitcast.1), channel_id=1, source_target_pairs={{0,0},{1,1},{2,4},{3,5},{4,2},{5,3},{6,6},{7,7},{8,8},{9,9},{10,12... | collective-permute-start | bytes 3048200 | tf_op jit(solution)/shard_map/ppermute | solution.py:64
  39.9 23.2 %collective-permute-start.5 = (bf16[96,2944]{1,0:T(8,128)(2,1)S(1)}, bf16[96,2944]{1,0:T(8,128)(2,1)S(1)}, u32[]{:S(2)}, u32[]{:S(2)}) collective-permute-start(bf16[96,2944]{1,0:T(8,128)(2,1)S(1)} %concatenate.155.refs_3_.refs_20_), channel_id=1, source_target_pairs={{0,16},{4,20},{8,24},{12,28},{16,0},{20,4},{24,8},{28,12},{1,17},{... | collective-permute-start | bytes 1695752 | tf_op jit(solution)/shard_map/ppermute | solution.py:45
  41.4 21.7 %collective-permute-start.6 = (bf16[96,2944]{1,0:T(8,128)(2,1)S(1)}, bf16[96,2944]{1,0:T(8,128)(2,1)S(1)}, u32[]{:S(2)}, u32[]{:S(2)}) collective-permute-start(bf16[96,2944]{1,0:T(8,128)(2,1)S(1)} %concatenate.155.refs_3_.refs_20_), channel_id=1, source_target_pairs={{0,24},{4,28},{8,16},{12,20},{16,8},{20,12},{24,0},{28,4},{1,25},{... | collective-permute-start | bytes 1695752 | tf_op jit(solution)/shard_map/ppermute | solution.py:45
  53.0 10.7 %collective-permute-start.7 = (bf16[96,2944]{1,0:T(8,128)(2,1)S(1)}, bf16[96,2944]{1,0:T(8,128)(2,1)S(1)}, u32[]{:S(2)}, u32[]{:S(2)}) collective-permute-start(bf16[96,2944]{1,0:T(8,128)(2,1)S(1)} %concatenate.155.refs_3_.refs_20_), channel_id=1, source_target_pairs={{0,4},{4,0},{8,12},{12,8},{16,20},{20,16},{24,28},{28,24},{1,5},{5... | collective-permute-start | bytes 1695752 | tf_op jit(solution)/shard_map/ppermute | solution.py:45
  53.0 11.0 %collective-permute-start.8 = (bf16[96,2944]{1,0:T(8,128)(2,1)S(1)}, bf16[96,2944]{1,0:T(8,128)(2,1)S(1)}, u32[]{:S(2)}, u32[]{:S(2)}) collective-permute-start(bf16[96,2944]{1,0:T(8,128)(2,1)S(1)} %collective-permute-done.4.refs_4_.refs_21_), channel_id=1, source_target_pairs={{0,4},{4,0},{8,12},{12,8},{16,20},{20,16},{24,28},{28,24},{1,5},{5... | collective-permute-start | bytes 1695752 | tf_op jit(solution)/shard_map/ppermute | solution.py:45
  63.1 7.2 %collective-permute-start.9 = (bf16[96,2944]{1,0:T(8,128)(2,1)S(1)}, bf16[96,2944]{1,0:T(8,128)(2,1)}, u32[]{:S(2)}, u32[]{:S(2)}) collective-permute-start(bf16[96,2944]{1,0:T(8,128)(2,1)S(1)} %collective-permute-done.5.refs_5_.refs_22_), channel_id=1, source_target_pairs={{0,4},{4,0},{8,12},{12,8},{16,20},{20,16},{24,28},{28,24},{1,5},{5... | collective-permute-start | bytes 1695752 | tf_op jit(solution)/shard_map/ppermute | solution.py:45
  63.1 7.2 %collective-permute-start.10 = (bf16[96,2944]{1,0:T(8,128)(2,1)S(1)}, bf16[96,2944]{1,0:T(8,128)(2,1)}, u32[]{:S(2)}, u32[]{:S(2)}) collective-permute-start(bf16[96,2944]{1,0:T(8,128)(2,1)S(1)} %collective-permute-done.6.refs_6_.refs_23_), channel_id=1, source_target_pairs={{0,4},{4,0},{8,12},{12,8},{16,20},{20,16},{24,28},{28,24},{1,5},{5... | collective-permute-start | bytes 1695752 | tf_op jit(solution)/shard_map/ppermute | solution.py:45
  63.6 19.5 %collective-permute-start.11 = (bf16[96,1728]{1,0:T(8,128)(2,1)}, bf16[96,1728]{1,0:T(8,128)(2,1)}, u32[]{:S(2)}, u32[]{:S(2)}) collective-permute-start(bf16[96,1728]{1,0:T(8,128)(2,1)} %pad_maximum_fusion.4.refs_1_), channel_id=1, source_target_pairs={{0,1},{1,0},{2,3},{3,2},{4,5},{5,4},{6,7},{7,6},{8,9},{9,8},{10,11... | collective-permute-start | bytes 995336 | tf_op jit(solution)/shard_map/ppermute | solution.py:50
  63.7 27.0 %collective-permute-start.12 = (bf16[96,1728]{1,0:T(8,128)(2,1)}, bf16[96,1728]{1,0:T(8,128)(2,1)}, u32[]{:S(2)}, u32[]{:S(2)}) collective-permute-start(bf16[96,1728]{1,0:T(8,128)(2,1)} %pad_maximum_fusion.4.refs_1_), channel_id=1, source_target_pairs={{0,2},{1,3},{2,0},{3,1},{4,6},{5,7},{6,4},{7,5},{8,10},{9,11},{10,... | collective-permute-start | bytes 995336 | tf_op jit(solution)/shard_map/ppermute | solution.py:50
  64.1 26.7 %collective-permute-start.13 = (bf16[96,1728]{1,0:T(8,128)(2,1)}, bf16[96,1728]{1,0:T(8,128)(2,1)}, u32[]{:S(2)}, u32[]{:S(2)}) collective-permute-start(bf16[96,1728]{1,0:T(8,128)(2,1)} %pad_maximum_fusion.4.refs_1_), channel_id=1, source_target_pairs={{0,3},{1,2},{2,1},{3,0},{4,7},{5,6},{6,5},{7,4},{8,11},{9,10},{10,... | collective-permute-start | bytes 995336 | tf_op jit(solution)/shard_map/ppermute | solution.py:50
  93.2 36.8 %collective-permute-start.14 = (bf16[96,6912]{1,0:T(8,128)(2,1)}, bf16[96,6912]{1,0:T(8,128)(2,1)}, u32[]{:S(2)}, u32[]{:S(2)}) collective-permute-start(bf16[96,6912]{1,0:T(8,128)(2,1)} %shard_map.467.refs_4_.refs_6_), channel_id=1, source_target_pairs={{0,8},{4,12},{8,0},{12,4},{16,24},{20,28},{24,16},{28,20},{1,9},{5... | collective-permute-start | bytes 3981320 | tf_op jit(solution)/shard_map/ppermute | solution.py:45
  93.8 36.3 %collective-permute-start.15 = (bf16[96,6912]{1,0:T(8,128)(2,1)}, bf16[96,6912]{1,0:T(8,128)(2,1)}, u32[]{:S(2)}, u32[]{:S(2)}) collective-permute-start(bf16[96,6912]{1,0:T(8,128)(2,1)} %shard_map.467.refs_4_.refs_6_), channel_id=1, source_target_pairs={{0,16},{4,20},{8,24},{12,28},{16,0},{20,4},{24,8},{28,12},{1,17},{... | collective-permute-start | bytes 3981320 | tf_op jit(solution)/shard_map/ppermute | solution.py:45
  98.1 31.9 %collective-permute-start.18 = (bf16[3,2,96,768]{3,2,1,0:T(8,128)(2,1)S(1)}, bf16[3,2,96,768]{3,2,1,0:T(8,128)(2,1)S(1)}, u32[]{:S(2)}, u32[]{:S(2)}) collective-permute-start(bf16[3,2,96,768]{3,2,1,0:T(8,128)(2,1)S(1)} %copy-done), channel_id=1, source_target_pairs={{0,1},{1,0},{2,3},{3,2},{4,5},{5,4},{6,7},{7,6},{8,9},{9,8},{10,11... | collective-permute-start | bytes 2654216 | tf_op jit(solution)/shard_map/ppermute | solution.py:50
  105.8 25.7 %collective-permute-start.20 = (bf16[2,2,192,384]{3,2,1,0:T(8,128)(2,1)}, bf16[2,2,192,384]{3,2,1,0:T(8,128)(2,1)}, u32[]{:S(2)}, u32[]{:S(2)}) collective-permute-start(bf16[2,2,192,384]{3,2,1,0:T(8,128)(2,1)} %bitcast.17), channel_id=1, source_target_pairs={{0,0},{1,1},{2,4},{3,5},{4,2},{5,3},{6,6},{7,7},{8,8},{9,9},{10,12... | collective-permute-start | bytes 1769480 | tf_op jit(solution)/shard_map/ppermute | solution.py:64
  114.1 19.4 %collective-permute-start.17 = (bf16[3,2,96,768]{3,2,1,0:T(8,128)(2,1)S(1)}, bf16[3,2,96,768]{3,2,1,0:T(8,128)(2,1)S(1)}, u32[]{:S(2)}, u32[]{:S(2)}) collective-permute-start(bf16[3,2,96,768]{3,2,1,0:T(8,128)(2,1)S(1)} %copy-done), channel_id=1, source_target_pairs={{0,4},{4,0},{8,12},{12,8},{16,20},{20,16},{24,28},{28,24},{1,5},{5... | collective-permute-start | bytes 2654216 | tf_op jit(solution)/shard_map/ppermute | solution.py:45
  130.0 3.5 collective-permute-start.19
  130.0 36.9 %collective-permute-start.24 = (bf16[96,6912]{1,0:T(8,128)(2,1)}, bf16[96,6912]{1,0:T(8,128)(2,1)}, u32[]{:S(2)}, u32[]{:S(2)}) collective-permute-start(bf16[96,6912]{1,0:T(8,128)(2,1)} %shard_map.467.refs_4_.refs_6_), channel_id=1, source_target_pairs={{0,24},{4,28},{8,16},{12,20},{16,8},{20,12},{24,0},{28,4},{1,25},{... | collective-permute-start | bytes 3981320 | tf_op jit(solution)/shard_map/ppermute | solution.py:45
  131.5 15.7 %collective-permute-start.22 = (bf16[2,2,192,384]{3,2,1,0:T(8,128)(2,1)}, bf16[2,2,192,384]{3,2,1,0:T(8,128)(2,1)}, u32[]{:S(2)}, u32[]{:S(2)}) collective-permute-start(bf16[2,2,192,384]{3,2,1,0:T(8,128)(2,1)} %collective-permute-done.20.refs_2_), channel_id=1, source_target_pairs={{0,1},{1,0},{2,3},{3,2},{4,5},{5,4},{6,7},{7,6},{8,9},{9,8},{10,11... | collective-permute-start | bytes 1769480 | tf_op jit(solution)/shard_map/ppermute | solution.py:50
  145.5 3.7 collective-permute-start.21
  147.3 2.2 collective-permute-start.23
  148.7 30.5 %collective-permute-start.25 = (bf16[96,6912]{1,0:T(8,128)(2,1)}, bf16[96,6912]{1,0:T(8,128)(2,1)S(1)}, u32[]{:S(2)}, u32[]{:S(2)}) collective-permute-start(bf16[96,6912]{1,0:T(8,128)(2,1)} %shard_map.467.refs_4_.refs_6_), channel_id=1, source_target_pairs={{0,4},{4,0},{8,12},{12,8},{16,20},{20,16},{24,28},{28,24},{1,5},{5... | collective-permute-start | bytes 3981320 | tf_op jit(solution)/shard_map/ppermute | solution.py:45
  149.2 30.0 %collective-permute-start.26 = (bf16[96,6912]{1,0:T(8,128)(2,1)}, bf16[96,6912]{1,0:T(8,128)(2,1)}, u32[]{:S(2)}, u32[]{:S(2)}) collective-permute-start(bf16[96,6912]{1,0:T(8,128)(2,1)} %collective-permute-done.14.refs_5_.refs_7_), channel_id=1, source_target_pairs={{0,4},{4,0},{8,12},{12,8},{16,20},{20,16},{24,28},{28,24},{1,5},{5... | collective-permute-start | bytes 3981320 | tf_op jit(solution)/shard_map/ppermute | solution.py:45
  156.4 22.9 %collective-permute-start.27 = (bf16[96,6912]{1,0:T(8,128)(2,1)}, bf16[96,6912]{1,0:T(8,128)(2,1)}, u32[]{:S(2)}, u32[]{:S(2)}) collective-permute-start(bf16[96,6912]{1,0:T(8,128)(2,1)} %collective-permute-done.15.refs_6_.refs_8_), channel_id=1, source_target_pairs={{0,4},{4,0},{8,12},{12,8},{16,20},{20,16},{24,28},{28,24},{1,5},{5... | collective-permute-start | bytes 3981320 | tf_op jit(solution)/shard_map/ppermute | solution.py:45
  167.0 12.3 %collective-permute-start.28 = (bf16[96,6912]{1,0:T(8,128)(2,1)}, bf16[96,6912]{1,0:T(8,128)(2,1)}, u32[]{:S(2)}, u32[]{:S(2)}) collective-permute-start(bf16[96,6912]{1,0:T(8,128)(2,1)} %collective-permute-done.24.refs_10_.refs_7_.refs_9_), channel_id=1, source_target_pairs={{0,4},{4,0},{8,12},{12,8},{16,20},{20,16},{24,28},{28,24},{1,5},{5... | collective-permute-start | bytes 3981320 | tf_op jit(solution)/shard_map/ppermute | solution.py:45
  214.7 1.7 collective-permute-start.29
  217.3 6.6 %collective-permute-start.30 = (f32[24,768]{1,0:T(8,128)S(1)}, f32[24,768]{1,0:T(8,128)S(1)}, u32[]{:S(2)}, u32[]{:S(2)}) collective-permute-start(f32[24,768]{1,0:T(8,128)S(1)} %maximum_add_fusion), channel_id=1, source_target_pairs={{0,1},{1,0},{2,3},{3,2},{4,5},{5,4},{6,7},{7,6},{8,9},{9,8},{10,11... | collective-permute-start | bytes 221192 | tf_op jit(solution)/shard_map/ppermute | solution.py:50
  222.1 44.3 %collective-permute-start.31 = (bf16[2,2,192,384]{3,2,1,0:T(8,128)(2,1)}, bf16[2,2,192,384]{3,2,1,0:T(8,128)(2,1)S(1)}, u32[]{:S(2)}, u32[]{:S(2)}) collective-permute-start(bf16[2,2,192,384]{3,2,1,0:T(8,128)(2,1)} %shard_map.473.refs_14_), channel_id=1, source_target_pairs={{0,0},{1,1},{2,4},{3,5},{4,2},{5,3},{6,6},{7,7},{8,8},{9,9},{10,12... | collective-permute-start | bytes 1769480 | tf_op jit(solution)/shard_map/ppermute | solution.py:64
  225.4 28.8 %copy-start.4 = (bf16[1152,768]{1,0:T(8,128)(2,1)S(1)}, bf16[1152,768]{1,0:T(8,128)(2,1)}, u32[]{:S(2)}) copy-start(bf16[1152,768]{1,0:T(8,128)(2,1)} %get-tuple-element.147.refs_0_) | copy-start | bytes 5308420
  256.5 21.2 %collective-permute-start.34 = (bf16[384,768]{1,0:T(8,128)(2,1)S(1)}, bf16[384,768]{1,0:T(8,128)(2,1)S(1)}, u32[]{:S(2)}, u32[]{:S(2)}) collective-permute-start(bf16[384,768]{1,0:T(8,128)(2,1)S(1)} %convolution_convert_fusion.4), channel_id=1, source_target_pairs={{0,4},{4,0},{8,12},{12,8},{16,20},{20,16},{24,28},{28,24},{1,5},{5... | collective-permute-start | bytes 1769480 | tf_op jit(solution)/shard_map/ppermute | solution.py:45
  265.4 12.5 %collective-permute-start.33 = (bf16[384,3072]{1,0:T(8,128)(2,1)S(1)}, bf16[384,3072]{1,0:T(8,128)(2,1)S(1)}, u32[]{:S(2)}, u32[]{:S(2)}) collective-permute-start(bf16[384,3072]{1,0:T(8,128)(2,1)S(1)} %convolution_convert_fusion), channel_id=1, source_target_pairs={{0,4},{4,0},{8,12},{12,8},{16,20},{20,16},{24,28},{28,24},{1,5},{5... | collective-permute-start | bytes 7077896 | tf_op jit(solution)/shard_map/ppermute | solution.py:45
  270.5 8.2 %collective-permute-start.32 = (bf16[384,3072]{1,0:T(8,128)(2,1)S(1)}, bf16[384,3072]{1,0:T(8,128)(2,1)S(1)}, u32[]{:S(2)}, u32[]{:S(2)}) collective-permute-start(bf16[384,3072]{1,0:T(8,128)(2,1)S(1)} %convolution_convert_fusion.2), channel_id=1, source_target_pairs={{0,4},{4,0},{8,12},{12,8},{16,20},{20,16},{24,28},{28,24},{1,5},{5... | collective-permute-start | bytes 7077896 | tf_op jit(solution)/shard_map/ppermute | solution.py:45
  280.8 33.1 %collective-permute-start.38 = (bf16[96,6912]{1,0:T(8,128)(2,1)}, bf16[96,6912]{1,0:T(8,128)(2,1)S(1)}, u32[]{:S(2)}, u32[]{:S(2)}) collective-permute-start(bf16[96,6912]{1,0:T(8,128)(2,1)} %pad_maximum_fusion.1.refs_8_), channel_id=1, source_target_pairs={{0,8},{4,12},{8,0},{12,4},{16,24},{20,28},{24,16},{28,20},{1,9},{5... | collective-permute-start | bytes 3981320 | tf_op jit(solution)/shard_map/ppermute | solution.py:45
  282.5 31.4 %collective-permute-start.39 = (bf16[96,6912]{1,0:T(8,128)(2,1)}, bf16[96,6912]{1,0:T(8,128)(2,1)}, u32[]{:S(2)}, u32[]{:S(2)}) collective-permute-start(bf16[96,6912]{1,0:T(8,128)(2,1)} %pad_maximum_fusion.2.refs_9_), channel_id=1, source_target_pairs={{0,16},{4,20},{8,24},{12,28},{16,0},{20,4},{24,8},{28,12},{1,17},{... | collective-permute-start | bytes 3981320 | tf_op jit(solution)/shard_map/ppermute | solution.py:45
  297.7 2.3 collective-permute-start.35
  313.7 3.0 collective-permute-start.36
  313.9 32.6 %collective-permute-start.43 = (bf16[96,6912]{1,0:T(8,128)(2,1)}, bf16[96,6912]{1,0:T(8,128)(2,1)}, u32[]{:S(2)}, u32[]{:S(2)}) collective-permute-start(bf16[96,6912]{1,0:T(8,128)(2,1)} %pad_maximum_fusion.3.refs_10_), channel_id=1, source_target_pairs={{0,24},{4,28},{8,16},{12,20},{16,8},{20,12},{24,0},{28,4},{1,25},{... | collective-permute-start | bytes 3981320 | tf_op jit(solution)/shard_map/ppermute | solution.py:45
  316.4 8.0 %collective-permute-start.37 = (bf16[2,96,768]{2,1,0:T(8,128)(2,1)S(1)}, bf16[2,96,768]{2,1,0:T(8,128)(2,1)S(1)}, u32[]{:S(2)}, u32[]{:S(2)}) collective-permute-start(bf16[2,96,768]{2,1,0:T(8,128)(2,1)S(1)} %copy-done.23), channel_id=1, source_target_pairs={{0,1},{1,0},{2,3},{3,2},{4,5},{5,4},{6,7},{7,6},{8,9},{9,8},{10,11... | collective-permute-start | bytes 884744 | tf_op jit(solution)/shard_map/ppermute | solution.py:50
  336.5 2.3 collective-permute-start.41
  338.2 14.7 %collective-permute-start.40 = (bf16[2,96,768]{2,1,0:T(8,128)(2,1)S(1)}, bf16[2,96,768]{2,1,0:T(8,128)(2,1)}, u32[]{:S(2)}, u32[]{:S(2)}) collective-permute-start(bf16[2,96,768]{2,1,0:T(8,128)(2,1)S(1)} %copy-done.22), channel_id=1, source_target_pairs={{0,1},{1,0},{2,3},{3,2},{4,5},{5,4},{6,7},{7,6},{8,9},{9,8},{10,11... | collective-permute-start | bytes 884744 | tf_op jit(solution)/shard_map/ppermute | solution.py:50
  340.7 13.4 %collective-permute-start.42 = (bf16[2,96,768]{2,1,0:T(8,128)(2,1)}, bf16[2,96,768]{2,1,0:T(8,128)(2,1)}, u32[]{:S(2)}, u32[]{:S(2)}) collective-permute-start(bf16[2,96,768]{2,1,0:T(8,128)(2,1)} %fusion.11), channel_id=1, source_target_pairs={{0,1},{1,0},{2,3},{3,2},{4,5},{5,4},{6,7},{7,6},{8,9},{9,8},{10,11... | collective-permute-start | bytes 884744 | tf_op jit(solution)/shard_map/ppermute | solution.py:50
  354.1 25.7 %copy-start.38 = (f32[2,2,768]{2,1,0:T(2,128)S(1)}, f32[2,2,768]{2,1,0:T(2,128)}, u32[]{:S(2)}) copy-start(f32[2,2,768]{2,1,0:T(2,128)} %get-tuple-element.193) | copy-start | bytes 36868
  354.1 25.7 %copy-start.39 = (f32[2,2,768]{2,1,0:T(2,128)S(1)}, f32[2,2,768]{2,1,0:T(2,128)}, u32[]{:S(2)}) copy-start(f32[2,2,768]{2,1,0:T(2,128)} %get-tuple-element.194) | copy-start | bytes 36868
  354.1 25.7 %copy-start.10 = (bf16[96,3456]{1,0:T(8,128)(2,1)S(1)}, bf16[96,3456]{1,0:T(8,128)(2,1)}, u32[]{:S(2)}) copy-start(bf16[96,3456]{1,0:T(8,128)(2,1)} %concatenate.170.refs_30_) | copy-start | bytes 1990660
  377.5 4.7 %collective-permute-start.44 = (bf16[384,2944]{1,0:T(8,128)(2,1)}, bf16[384,2944]{1,0:T(8,128)(2,1)S(1)}, u32[]{:S(2)}, u32[]{:S(2)}) collective-permute-start(bf16[384,2944]{1,0:T(8,128)(2,1)} %get-tuple-element.189), channel_id=1, source_target_pairs={{0,4},{4,0},{8,12},{12,8},{16,20},{20,16},{24,28},{28,24},{1,5},{5... | collective-permute-start | bytes 6782984 | tf_op jit(solution)/shard_map/ppermute | solution.py:45
  379.8 17.5 %collective-permute-start.48 = (bf16[96,3456]{1,0:T(8,128)(2,1)S(1)}, bf16[96,3456]{1,0:T(8,128)(2,1)}, u32[]{:S(2)}, u32[]{:S(2)}) collective-permute-start(bf16[96,3456]{1,0:T(8,128)(2,1)S(1)} %copy-done.10), channel_id=1, source_target_pairs={{0,1},{1,0},{2,3},{3,2},{4,5},{5,4},{6,7},{7,6},{8,9},{9,8},{10,11... | collective-permute-start | bytes 1990664 | tf_op jit(solution)/shard_map/ppermute | solution.py:50
  387.4 16.9 %collective-permute-start.47 = (bf16[96,2944]{1,0:T(8,128)(2,1)}, bf16[96,2944]{1,0:T(8,128)(2,1)}, u32[]{:S(2)}, u32[]{:S(2)}) collective-permute-start(bf16[96,2944]{1,0:T(8,128)(2,1)} %get-tuple-element.247), channel_id=1, source_target_pairs={{0,24},{4,28},{8,16},{12,20},{16,8},{20,12},{24,0},{28,4},{1,25},{... | collective-permute-start | bytes 1695752 | tf_op jit(solution)/shard_map/ppermute | solution.py:45
  388.9 26.7 %collective-permute-start.46 = (bf16[96,2944]{1,0:T(8,128)(2,1)}, bf16[96,2944]{1,0:T(8,128)(2,1)}, u32[]{:S(2)}, u32[]{:S(2)}) collective-permute-start(bf16[96,2944]{1,0:T(8,128)(2,1)} %get-tuple-element.246), channel_id=1, source_target_pairs={{0,16},{4,20},{8,24},{12,28},{16,0},{20,4},{24,8},{28,12},{1,17},{... | collective-permute-start | bytes 1695752 | tf_op jit(solution)/shard_map/ppermute | solution.py:45
  389.4 26.3 %collective-permute-start.45 = (bf16[96,2944]{1,0:T(8,128)(2,1)S(1)}, bf16[96,2944]{1,0:T(8,128)(2,1)}, u32[]{:S(2)}, u32[]{:S(2)}) collective-permute-start(bf16[96,2944]{1,0:T(8,128)(2,1)S(1)} %get-tuple-element.248), channel_id=1, source_target_pairs={{0,8},{4,12},{8,0},{12,4},{16,24},{20,28},{24,16},{28,20},{1,9},{5... | collective-permute-start | bytes 1695752 | tf_op jit(solution)/shard_map/ppermute | solution.py:45
  399.4 30.4 %collective-permute-start.53 = (bf16[96,1728]{1,0:T(8,128)(2,1)S(1)}, bf16[96,1728]{1,0:T(8,128)(2,1)S(1)}, u32[]{:S(2)}, u32[]{:S(2)}) collective-permute-start(bf16[96,1728]{1,0:T(8,128)(2,1)S(1)} %get-tuple-element.279), channel_id=1, source_target_pairs={{0,2},{1,3},{2,0},{3,1},{4,6},{5,7},{6,4},{7,5},{8,10},{9,11},{10,... | collective-permute-start | bytes 995336 | tf_op jit(solution)/shard_map/ppermute | solution.py:50
  417.7 4.9 %collective-permute-start.51 = (bf16[24,1280]{1,0:T(8,128)(2,1)S(1)}, bf16[24,1280]{1,0:T(8,128)(2,1)S(1)}, u32[]{:S(2)}, u32[]{:S(2)}) collective-permute-start(bf16[24,1280]{1,0:T(8,128)(2,1)S(1)} %pad_maximum_fusion.13), channel_id=1, source_target_pairs={{0,1},{1,0},{2,3},{3,2},{4,5},{5,4},{6,7},{7,6},{8,9},{9,8},{10,11... | collective-permute-start | bytes 184328 | tf_op jit(solution)/shard_map/ppermute | solution.py:50
  418.8 8.0 %collective-permute-start.49 = (bf16[96,1152]{1,0:T(8,128)(2,1)S(1)}, bf16[96,1152]{1,0:T(8,128)(2,1)S(1)}, u32[]{:S(2)}, u32[]{:S(2)}) collective-permute-start(bf16[96,1152]{1,0:T(8,128)(2,1)S(1)} %pad_maximum_fusion.9), channel_id=1, source_target_pairs={{0,1},{1,0},{2,3},{3,2},{4,5},{5,4},{6,7},{7,6},{8,9},{9,8},{10,11... | collective-permute-start | bytes 663560 | tf_op jit(solution)/shard_map/ppermute | solution.py:50
  423.3 6.5 %collective-permute-start.52 = (bf16[24,640]{1,0:T(8,128)(2,1)S(1)}, bf16[24,640]{1,0:T(8,128)(2,1)S(1)}, u32[]{:S(2)}, u32[]{:S(2)}) collective-permute-start(bf16[24,640]{1,0:T(8,128)(2,1)S(1)} %get-tuple-element.284), channel_id=1, source_target_pairs={{0,2},{1,3},{2,0},{3,1},{4,6},{5,7},{6,4},{7,5},{8,10},{9,11},{10,... | collective-permute-start | bytes 92168 | tf_op jit(solution)/shard_map/ppermute | solution.py:50
  427.7 7.8 %collective-permute-start.50 = (bf16[96,576]{1,0:T(8,128)(2,1)S(1)}, bf16[96,576]{1,0:T(8,128)(2,1)S(1)}, u32[]{:S(2)}, u32[]{:S(2)}) collective-permute-start(bf16[96,576]{1,0:T(8,128)(2,1)S(1)} %get-tuple-element.288), channel_id=1, source_target_pairs={{0,2},{1,3},{2,0},{3,1},{4,6},{5,7},{6,4},{7,5},{8,10},{9,11},{10,... | collective-permute-start | bytes 331784 | tf_op jit(solution)/shard_map/ppermute | solution.py:50
  438.6 1.5 collective-permute-start.54
  440.9 4.2 collective-permute-start.55
  445.1 4.2 collective-permute-start.56
  449.4 4.2 collective-permute-start.57
  453.6 5.2 %collective-permute-start.58 = (f32[56,192]{1,0:T(8,128)S(1)}, f32[56,192]{1,0:T(8,128)S(1)}, u32[]{:S(2)}, u32[]{:S(2)}) collective-permute-start(f32[56,192]{1,0:T(8,128)S(1)} %add.706.refs_1_), channel_id=1, source_target_pairs={{0,2},{1,3},{2,0},{3,1},{4,6},{5,7},{6,4},{7,5},{8,10},{9,11},{10,... | collective-permute-start | bytes 129032 | tf_op jit(solution)/shard_map/ppermute | solution.py:50
  (53 other events, 504.7 us)

commit v6 on v5

--- a/solution.py
+++ b/solution.py
@@ -912,7 +912,7 @@
     outs[3][:rows] = flat_ref[...]
 
 
-def squares_of(attn, small, rest, flat):
+def squares_of(attn, small, rest, flat, events=()):
     operands = tuple(attn) + tuple(small) + tuple(rest) + (flat,)
     rows = flat.shape[0] + (-flat.shape[0] % 8)
     rows += 8 * (rows == flat.shape[0])
@@ -926,6 +926,7 @@
         shapes,
         operands,
         0,
+        events=events,
     )
 
 
@@ -949,9 +950,9 @@
     mine = jnp.where(odd_ref[0] == 1, blocks[1], blocks[0])
     boxes = blocks[0][12:13, heads + 1 : heads + 2]
     norm = jnp.sqrt(square) / boxes
-    lane = lax.broadcasted_iota(jnp.int32, (1, 128), 1)
-    loss = blocks[0][12:13, heads : heads + 1]
-    outs[0][...] = jnp.where(lane == 0, loss, jnp.where(lane == 1, boxes, norm))
+    outs[-3][...] = blocks[0][12:13, heads : heads + 1]
+    outs[-2][...] = boxes
+    outs[-1][...] = norm
     scaling = jnp.minimum(1.0, THRESHOLD / norm) / boxes
     hidden = weights[0].shape[1] - attn_ref.shape[1]
     edge = small_ref.shape[1] - 128
@@ -962,11 +963,11 @@
         grad = grad * scaling
         moment = MOMENTUM * moments[i][at] + grad
         updated = weights[i][at] - rates[i] * (grad + MOMENTUM * moment)
-        outs[1 + i][at] = updated
-        outs[1 + count + i][at] = moment
-        outs[1 + 2 * count + i][at] = AVERAGING * averages[i][at] + (1.0 - AVERAGING) * updated
+        outs[i][at] = updated
+        outs[count + i][at] = moment
+        outs[2 * count + i][at] = AVERAGING * averages[i][at] + (1.0 - AVERAGING) * updated
         if i < 2:
-            outs[1 + 3 * count + i][at] = updated.astype(bf16)
+            outs[3 * count + i][at] = updated.astype(bf16)
 
     step(0, ..., jnp.concatenate([attn_ref[...], rest_ref[:, :hidden]], axis=1))
     step(1, ..., rest_ref[:, hidden:])
@@ -982,8 +983,8 @@
 def update(odd, one, two, grads, patch, weights, moments, averages, rates):
     operands = (odd, one, two) + grads + weights + moments + averages
     kept = [jax.ShapeDtypeStruct(w.shape, f32) for w in weights]
-    shapes = [jax.ShapeDtypeStruct((1, 128), f32)] + kept * 3
-    shapes = shapes + [jax.ShapeDtypeStruct(w.shape, bf16) for w in weights[:2]]
+    shapes = kept * 3 + [jax.ShapeDtypeStruct(w.shape, bf16) for w in weights[:2]]
+    shapes = shapes + [jax.ShapeDtypeStruct((1, 1), f32)] * 3
     return call(
         functools.partial(update_kernel, rates, patch),
         (1,),
@@ -1137,7 +1138,7 @@
         ]
         return jnp.concatenate(
             [
-                jnp.where((index < limit)[None, :], rel_bias[:, g : g + 1], -1e30)
+                jnp.where((index < limit)[None, :], rel_bias[:, g : g + 1], -3e38)
                 for g, (index, limit) in enumerate(sides)
             ],
             axis=1,
@@ -1169,11 +1170,16 @@
 
     attended, saved = None, {}
     for m in (2, 1, 0):
+        arrived = {2: rest[1:], 1: [], 0: rest_late}[m]
         attended, probs, keys, values = attend(
-            m, query, conv_all, biases[m], stored[m + 2], stored[m + 1], stored[m], attended,
-            events=tuple(rest_late) if m == 0 else (),
-        ) if m < 2 else attend(
-            m, after(query, *rest[1:]), conv_all, biases[m], stored[m + 2], stored[m + 1], stored[m], attended,
+            m,
+            after(query, *arrived) if arrived else query,
+            conv_all,
+            biases[m],
+            stored[m + 2],
+            stored[m + 1],
+            stored[m],
+            attended,
         )
         saved[m] = (keys, values, probs)
         if m == 2:
@@ -1262,7 +1268,15 @@
     for m in range(MICRO):
         keys, values, probs = saved[m]
         dq, kept, sent, taps_part, bias_part = attend_back(
-            m, query, keys, values, probs, grad_attended, stored[m + 1], stored[m], dq, events
+            m,
+            query,
+            keys,
+            values,
+            probs,
+            after(grad_attended, *events),
+            stored[m + 1],
+            stored[m],
+            dq,
         )
         got = swap_dp(sent, 1)
         away = (kept[1].astype(f32) + got[1].astype(f32)).astype(bf16)
@@ -1295,7 +1309,7 @@
         rest_pieces.append(piece)
     rest_near, rest_far, rest_got = halve_mp(rest_pieces)
     attn_near, attn_far, taps_grad = embed_back(
-        dq,
+        after(dq, rest_near, *rest_far),
         raw_keys,
         raw_values,
         conv_all,
@@ -1308,7 +1322,7 @@
         sums,
         tuple(pool_grads),
         weights,
-        events=(rest_near,) + rest_far,
+        events=(),
     )
     attn_pieces = halve_dp([attn_near], [attn_far])
     attn_found = trade_dp(attn_pieces, 1, None)
@@ -1359,10 +1373,10 @@
     last = jnp.pad(last, ((0, 0), (0, head_cols - last.shape[1])))
     flat = jnp.concatenate([taps_rows, last[None]]).transpose(1, 0, 2)
     attn_mine, small_mine, rest_mine, both = squares_of(
-        attn_parts, small_parts, rest_mine, flat.reshape(52, head_cols)
-    )
-    for bit in range(dp_bits()):
-        both = both + swap_dp(both, 1 << bit)
+        attn_parts, small_parts, rest_mine, flat.reshape(52, head_cols), (new_memory,)
+    )
+    both = both + swap_dp(both, 1)
+    both = both + sum(swap_dp(both, b) for b in range(2, dp_count, 2))
     both = both + swap_mp(both, 1)
     both_two = swap_mp(both, 2)
 
@@ -1409,13 +1423,13 @@
         turned(averages),
         rates,
     )
-    loss_global, box_total, grad_norm = (made[0][0, i] for i in range(3))
+    loss_global, box_total, grad_norm = (made[23 + i].reshape(()) for i in range(3))
     results = []
     for i in range(3):
-        results.extend(turned(made[1 + 7 * i : 8 + 7 * i]))
+        results.extend(turned(made[7 * i : 7 * i + 7]))
 
     return (
-        (loss_global, box_total, grad_norm, new_memory.transpose(0, 1, 3, 2)) + tuple(results) + tuple(made[22:24])
+        (loss_global, box_total, grad_norm, new_memory.transpose(0, 1, 3, 2)) + tuple(results) + tuple(made[21:23])
     )
 
 

time: 474 us -> 468 us (0.987)
    ppermute x35 -> x36, starting transfers between devices: 21.7 us -> 25 us  [swap_dp(): return lax.ppermute(inputs, 'dp', [(i, i ^ mask) for i in range(size)])]
    ppermute x35 -> x36, waiting for transfers between devices: 41 us -> 39.4 us  [swap_dp(): return lax.ppermute(inputs, 'dp', [(i, i ^ mask) for i in range(size)])]
    unnamed x124 -> x110, local copies, waits for them, and re-layouts: 11.1 us -> 9.62 us
  transfers between devices with their start and end apart: 59 -> 60, of which waited for: 27 -> 28; matrix products, arithmetic and copies ran while one was open for 15% -> 14% of each run, Pallas kernels for 25% -> 25%
where the time goes in v6:
time: 468 us; the launch traced here: 461 us
  Pallas kernels  183 us (39%)
  waiting for transfers between devices  108 us (23%)
  starting transfers between devices  70.3 us (15%)
  other arithmetic  38.3 us (8%)
  matrix products  23.1 us (5%)
  local copies, waits for them, and re-layouts  21.9 us (5%)
  between operations  16.5 us (4%)
    pallas_call x15, Pallas kernels, call(): pl.pallas_call(run, grid=grid, in_specs=list(in_specs) + [pl.BlockSpec(me...  183 us
    ppermute x20, waiting for transfers between devices, swap_mp(): return lax.ppermute(inputs, 'mp', [(i, i ^ mask) for i in range(size)])  68.5 us
    ppermute x36, waiting for transfers between devices, swap_dp(): return lax.ppermute(inputs, 'dp', [(i, i ^ mask) for i in range(size)])  39.4 us
    ppermute x20, starting transfers between devices, swap_mp(): return lax.ppermute(inputs, 'mp', [(i, i ^ mask) for i in range(size)])  27.3 us
    ppermute x36, starting transfers between devices, swap_dp(): return lax.ppermute(inputs, 'dp', [(i, i ^ mask) for i in range(size)])  25 us
    dot_general x7, matrix products, contract_rows(): lax.dot_general(first_operand, second_operand, (((0,), (0,)), ((), ())),...  21.2 us
    ppermute x4, starting transfers between devices, regroup(): return lax.ppermute(inputs, ('dp', 'mp'), pairs)  18 us
    unnamed x110, local copies, waits for them, and re-layouts  9.62 us
  transfers between devices with their start and end apart: 60, of which 28 were waited for; matrix products, arithmetic and copies ran while one was open for 14% of the time, Pallas kernels for 25%

profile of v6, /device:TPU:0, one launch (start us, length us, event | category | flops | bytes accessed | tf_op | source)
XLA Modules:
  0.0 460.7 jit_solution(599870837025994959)
XLA Ops:
  6.9 3.1 collective-permute-start
  10.0 2.6 collective-permute-start.1
  15.6 1.5 collective-permute-done
  17.2 8.5 %collective-permute-done.1 = bf16[96,832]{1,0:T(8,128)(2,1)S(1)} collective-permute-done((bf16[96,832]{1,0:T(8,128)(2,1)S(1)}, bf16[96,832]{1,0:T(8,128)(2,1)S(1)}, u32[]{:S(2)}, u32[]{:S(2)}) %collective-permute-start.1) | collective-permute-done | bytes 159776 | tf_op jit(solution)/shard_map/ppermute | solution.py:50
  27.8 1.6 collective-permute-start.4
  29.4 9.4 %collective-permute-start.3 = (bf16[3,441,384]{2,1,0:T(8,128)(2,1)}, bf16[3,441,384]{2,1,0:T(8,128)(2,1)}, u32[]{:S(2)}, u32[]{:S(2)}) collective-permute-start(bf16[3,441,384]{2,1,0:T(8,128)(2,1)} %bitcast.1), channel_id=1, source_target_pairs={{0,0},{1,1},{2,4},{3,5},{4,2},{5,3},{6,6},{7,7},{8,8},{9,9},{10,12... | collective-permute-start | bytes 3048200 | tf_op jit(solution)/shard_map/ppermute | solution.py:64
  39.8 1.5 collective-permute-start.5
  56.2 7.0 %collective-permute-done.5.refs_5_.refs_22_ = bf16[96,2944]{1,0:T(8,128)(2,1)S(1)} collective-permute-done((bf16[96,2944]{1,0:T(8,128)(2,1)S(1)}, bf16[96,2944]{1,0:T(8,128)(2,1)S(1)}, u32[]{:S(2)}, u32[]{:S(2)}) %collective-permute-start.5) | collective-permute-done | bytes 565280 | tf_op jit(solution)/shard_map/ppermute | solution.py:45
  64.1 4.0 collective-permute-start.13
  68.8 1.5 reshape.676.refs_2_.refs_1_.refs_3_
  70.4 12.7 %shard_map.466 = (bf16[1152,441]{1,0:T(8,128)(2,1)}, f32[1152,768]{1,0:T(8,128)}, bf16[1152,768]{1,0:T(8,128)(2,1)}, bf16[1152,768]{1,0:T(8,128)(2,1)}, bf16[115...) custom-call(bf16[3,441,384]{2,1,0:T(8,128)(2,1)} %collective-permute, ...), custom_call_target="tpu_custom_call" | custom-call | flops 1000 | bytes 1000 | tf_op jit(solution)/shard_map/pallas_call | solution.py:143
  83.1 7.6 %collective-permute-done.12.refs_3_ = bf16[96,1728]{1,0:T(8,128)(2,1)} collective-permute-done((bf16[96,1728]{1,0:T(8,128)(2,1)}, bf16[96,1728]{1,0:T(8,128)(2,1)}, u32[]{:S(2)}, u32[]{:S(2)}) %collective-permute-start.12) | collective-permute-done | bytes 331808 | tf_op jit(solution)/shard_map/ppermute | solution.py:50
  90.7 2.5 shard_map.467.refs_4_.refs_6_
  93.8 1.5 collective-permute-start.15
  98.1 7.1 %collective-permute-start.18 = (bf16[3,2,96,768]{3,2,1,0:T(8,128)(2,1)S(1)}, bf16[3,2,96,768]{3,2,1,0:T(8,128)(2,1)S(1)}, u32[]{:S(2)}, u32[]{:S(2)}) collective-permute-start(bf16[3,2,96,768]{3,2,1,0:T(8,128)(2,1)S(1)} %copy-done), channel_id=1, source_target_pairs={{0,1},{1,0},{2,3},{3,2},{4,5},{5,4},{6,7},{7,6},{8,9},{9,8},{10,11... | collective-permute-start | bytes 2654216 | tf_op jit(solution)/shard_map/ppermute | solution.py:50
  105.8 6.2 %collective-permute-start.21 = (bf16[2,2,192,384]{3,2,1,0:T(8,128)(2,1)}, bf16[2,2,192,384]{3,2,1,0:T(8,128)(2,1)}, u32[]{:S(2)}, u32[]{:S(2)}) collective-permute-start(bf16[2,2,192,384]{3,2,1,0:T(8,128)(2,1)} %bitcast.17), channel_id=1, source_target_pairs={{0,0},{1,1},{2,4},{3,5},{4,2},{5,3},{6,6},{7,7},{8,8},{9,9},{10,12... | collective-permute-start | bytes 1769480 | tf_op jit(solution)/shard_map/ppermute | solution.py:64
  114.2 15.9 %collective-permute-done.18.refs_5_.refs_9_.refs_13_.refs_4_.refs_8_.refs_7_.refs_11_ = bf16[3,2,96,768]{3,2,1,0:T(8,128)(2,1)S(1)} collective-permute-done((bf16[3,2,96,768]{3,2,1,0:T(8,128)(2,1)S(1)}, bf16[3,2,96,768]{3,2,1,0:T(8,128)(2,1)S(1)}, u32[]{:S(2)}, u32[]{:S(2)}) %collective-permute-start.18) | collective-permute-done | bytes 884768 | tf_op jit(solution)/shard_map/ppermute | solution.py:50
  130.0 1.5 collective-permute-start.20
  131.5 2.0 collective-permute-start.23
  135.4 10.0 %shard_map.468 = (bf16[1152,768]{1,0:T(8,128)(2,1)}, bf16[12,384,768]{2,1,0:T(8,128)(2,1)}, bf16[768,768]{1,0:T(8,128)(2,1)}, bf16[768,768]{1,0:T(8,128)(2,1)}) custom-call(bf16[1152,768]{1,0:T(8,128)(2,1)} %get-tuple-element.148.refs_0_, f32[2,6,768]{2,1,0:T(8,128)} %reshape.676.refs_2_.refs_1_.refs_3_, f32[3,4,768]{2,1,0:T(4,128)} %pad_maximum_fusion.16.refs_2_, ...), custom_call_target="tpu_custom_call" | custom-call | flops 1000 | bytes 1000 | tf_op jit(solution)/shard_map/pallas_call | solution.py:143
  145.5 1.8 collective-permute-done.23.refs_4_
  150.9 5.5 %shard_map.469.refs_11_.refs_7_.refs_8_.refs_5_.refs_6_.refs_9_ = bf16[2,2,384,768]{3,2,1,0:T(8,128)(2,1)} custom-call(s32[4]{0:T(128)} %pad_add_fusion.2.refs_0_, bf16[384,384]{1,0:T(8,128)(2,1)} %fusion.7.refs_1_, bf16[2,2,192,384]{3,2,1,0:T(8,128)(2,1)} %collective-permute-done.21.refs_2_, bf16[2,2,192,384]{3,2,1,0:T(8,128)(2,1)} %copy-done.20, ...), custom_call_target="tpu_custom_call" | custom-call | flops 1000 | bytes 1000 | tf_op jit(solution)/shard_map/pallas_call | solution.py:143
  156.9 10.1 %shard_map.470 = (bf16[1152,768]{1,0:T(8,128)(2,1)}, bf16[12,384,768]{2,1,0:T(8,128)(2,1)}, bf16[768,768]{1,0:T(8,128)(2,1)}, bf16[768,768]{1,0:T(8,128)(2,1)}) custom-call(bf16[1152,768]{1,0:T(8,128)(2,1)} %get-tuple-element.148.refs_0_, f32[2,6,768]{2,1,0:T(8,128)} %reshape.676.refs_2_.refs_1_.refs_3_, ...), custom_call_target="tpu_custom_call", output_to_operand_aliasing={{0}: (12, {})} | custom-call | flops 1000 | bytes 1000 | tf_op jit(solution)/shard_map/pallas_call | solution.py:143
  169.4 9.9 %shard_map.471 = (bf16[1152,768]{1,0:T(8,128)(2,1)}, bf16[12,384,768]{2,1,0:T(8,128)(2,1)}, bf16[768,768]{1,0:T(8,128)(2,1)}, bf16[768,768]{1,0:T(8,128)(2,1)}) custom-call(bf16[1152,768]{1,0:T(8,128)(2,1)} %get-tuple-element.148.refs_0_, f32[2,6,768]{2,1,0:T(8,128)} %reshape.676.refs_2_.refs_1_.refs_3_, ...), custom_call_target="tpu_custom_call", output_to_operand_aliasing={{0}: (9, {})} | custom-call | flops 1000 | bytes 1000 | tf_op jit(solution)/shard_map/pallas_call | solution.py:143
  180.4 34.4 %shard_map.472 = (f32[1152,768]{1,0:T(8,128)}, bf16[1152,768]{1,0:T(8,128)(2,1)}, bf16[1152,3072]{1,0:T(8,128)(2,1)}, bf16[1152,3072]{1,0:T(8,128)(2,1)}, f32[1152,768]{1,0:T(8,128)}, /*index=5*/f32[3,8,768]{2,1,0:T(8,128)}) custom-call(bf16[1152,768]{1,0:T(8,128)(2,1)} %get-tuple-element.155.refs_0_, f32[1152,768]{1,0:T(8,128)} %get-tuple-element.156.refs_1_.refs_4_, ...), custom_call_target="tpu_custom_call" | custom-call | flops 1000 | bytes 1000 | tf_op jit(solution)/shard_map/pallas_call | solution.py:143
  217.9 4.3 shard_map.473.refs_14_
  222.2 1.7 collective-permute-start.31
  225.5 28.8 %shard_map.474 = (bf16[1152,768]{1,0:T(8,128)(2,1)}, bf16[1152,3072]{1,0:T(8,128)(2,1)}, bf16[1152,768]{1,0:T(8,128)(2,1)}, f32[1152,768]{1,0:T(8,128)}, bf16[1152,768]{1,0:T(8,128)(2,1)}, /*index=5*/f32[8,768]{1,0:T(8,128)}) custom-call(f32[3,8,768]{2,1,0:T(8,128)} %convolution_bitcast_fusion.refs_0_, f32[3,8,384]{2,1,0:T(8,128)} %convert_divide_fusion.refs_3_.refs_1_, ...), custom_call_target="tpu_custom_call" | custom-call | flops 1000 | bytes 1000 | tf_op jit(solution)/shard_map/pallas_call | solution.py:143
  254.3 2.3 convolution_convert_fusion.4
  256.6 2.4 collective-permute-start.34
  259.0 6.4 %convolution_convert_fusion = bf16[384,3072]{1,0:T(8,128)(2,1)S(1)} fusion(bf16[1152,3072]{1,0:T(8,128)(2,1)} %get-tuple-element.178, bf16[1152,768]{1,0:T(8,128)(2,1)S(1)} %copy-done.45), kind=kOutput, calls=%fused_computation | convolution fusion | flops 2719088640 | bytes 10321920 | tf_op jit(solution)/shard_map/dot_general | solution.py:38
  266.9 3.7 convolution_convert_fusion.2
  270.9 3.5 convolution_convert_fusion.1
  274.3 3.5 convolution_convert_fusion.3
  282.6 1.5 collective-permute-start.39
  285.2 11.3 %shard_map.475 = (bf16[1152,768]{1,0:T(8,128)(2,1)}, bf16[2,2,96,768]{3,2,1,0:T(8,128)(2,1)}, bf16[2,2,96,768]{3,2,1,0:T(8,128)(2,1)}, f32[2,2,768]{2,1,0:T(2,128)}, f32[3,4,128]{2,1,0:T(4,128)}) custom-call(bf16[1152,768]{1,0:T(8,128)(2,1)} %get-tuple-element.148.refs_0_, bf16[768,768]{1,0:T(8,128)(2,1)} %get-tuple-element.171.refs_1_, ...), custom_call_target="tpu_custom_call" | custom-call | flops 1000 | bytes 1000 | tf_op jit(solution)/shard_map/pallas_call | solution.py:143
  296.6 2.2 collective-permute-done.35.refs_12_
  300.0 11.4 %shard_map.476 = (bf16[1152,768]{1,0:T(8,128)(2,1)}, bf16[2,2,96,768]{3,2,1,0:T(8,128)(2,1)}, bf16[2,2,96,768]{3,2,1,0:T(8,128)(2,1)}, f32[2,2,768]{2,1,0:T(2,128)}, f32[3,4,128]{2,1,0:T(4,128)}) custom-call(bf16[1152,768]{1,0:T(8,128)(2,1)} %get-tuple-element.148.refs_0_, ...), custom_call_target="tpu_custom_call", output_to_operand_aliasing={{0}: (10, {})} | custom-call | flops 1000 | bytes 1000 | tf_op jit(solution)/shard_map/pallas_call | solution.py:143
  312.4 1.5 collective-permute-done.39
  314.0 2.4 collective-permute-start.40
  316.7 1.9 fusion.10
  318.6 5.6 %collective-permute-done.37.refs_13_ = bf16[2,96,768]{2,1,0:T(8,128)(2,1)S(1)} collective-permute-done((bf16[2,96,768]{2,1,0:T(8,128)(2,1)S(1)}, bf16[2,96,768]{2,1,0:T(8,128)(2,1)S(1)}, u32[]{:S(2)}, u32[]{:S(2)}) %collective-permute-start.37) | collective-permute-done | bytes 294944 | tf_op jit(solution)/shard_map/ppermute | solution.py:50
  325.0 11.7 %shard_map.477 = (bf16[1152,768]{1,0:T(8,128)(2,1)}, bf16[2,2,96,768]{3,2,1,0:T(8,128)(2,1)}, bf16[2,2,96,768]{3,2,1,0:T(8,128)(2,1)}, f32[2,2,768]{2,1,0:T(2,128)}, f32[3,4,128]{2,1,0:T(4,128)}) custom-call(bf16[1152,768]{1,0:T(8,128)(2,1)} %get-tuple-element.148.refs_0_, ...), custom_call_target="tpu_custom_call", output_to_operand_aliasing={{0}: (13, {})} | custom-call | flops 1000 | bytes 1000 | tf_op jit(solution)/shard_map/pallas_call | solution.py:143
  339.0 1.9 fusion.11
  341.7 3.8 collective-permute-done.40
  345.4 2.8 fusion.66
  351.1 2.7 collective-permute-done.43.refs_19_
  353.8 23.3 %shard_map.478 = (bf16[384,2944]{1,0:T(8,128)(2,1)}, bf16[384,2944]{1,0:T(8,128)(2,1)}, f32[8,768]{1,0:T(8,128)}) custom-call(bf16[1152,768]{1,0:T(8,128)(2,1)} %get-tuple-element.191.refs_0_, bf16[1152,768]{1,0:T(8,128)(2,1)} %get-tuple-element.192.refs_1_, bf16[1152,768]{1,0:T(8,128)(2,1)} %get-tuple-element.193.refs_2_, ...), custom_call_target="tpu_custom_call" | custom-call | flops 1000 | bytes 1000 | tf_op jit(solution)/shard_map/pallas_call | solution.py:143
  381.9 3.8 add_convert_fusion.9
  386.1 1.5 collective-permute-start.46
  389.3 7.5 %collective-permute-done.48 = bf16[96,3456]{1,0:T(8,128)(2,1)S(1)} collective-permute-done((bf16[96,3456]{1,0:T(8,128)(2,1)S(1)}, bf16[96,3456]{1,0:T(8,128)(2,1)S(1)}, u32[]{:S(2)}, u32[]{:S(2)}) %collective-permute-start.48) | collective-permute-done | bytes 663584 | tf_op jit(solution)/shard_map/ppermute | solution.py:50
  398.2 4.4 collective-permute-done.47
  402.6 10.6 %collective-permute-done.46 = bf16[96,2944]{1,0:T(8,128)(2,1)} collective-permute-done((bf16[96,2944]{1,0:T(8,128)(2,1)}, bf16[96,2944]{1,0:T(8,128)(2,1)}, u32[]{:S(2)}, u32[]{:S(2)}) %collective-permute-start.46) | collective-permute-done | bytes 565280 | tf_op jit(solution)/shard_map/ppermute | solution.py:45
  413.1 1.7 convert_add_fusion.1
  416.0 1.6 collective-permute-start.49
  417.6 2.4 collective-permute-done.51
  424.4 2.0 collective-permute-start.50
  427.1 4.4 collective-permute-done.50.refs_1_
  432.1 2.5 shard_map.479
  436.9 2.4 collective-permute-start.57
  442.0 2.0 collective-permute-done.55
  445.1 4.2 collective-permute-done.58
  449.4 5.0 %collective-permute-done.59.refs_2_ = f32[56,192]{1,0:T(8,128)S(1)} collective-permute-done((f32[56,192]{1,0:T(8,128)S(1)}, f32[56,192]{1,0:T(8,128)S(1)}, u32[]{:S(2)}, u32[]{:S(2)}) %collective-permute-start.59) | collective-permute-done | bytes 43040 | tf_op jit(solution)/shard_map/ppermute | solution.py:50
  455.1 4.6 shard_map.480
  (334 shorter events, 73.9 us)
Async XLA Ops:
  6.9 10.2 %collective-permute-start = (bf16[96,832]{1,0:T(8,128)(2,1)S(1)}, bf16[96,832]{1,0:T(8,128)(2,1)S(1)}, u32[]{:S(2)}, u32[]{:S(2)}) collective-permute-start(bf16[96,832]{1,0:T(8,128)(2,1)S(1)} %maximum_maximum_fusion), channel_id=1, source_target_pairs={{0,1},{1,0},{2,3},{3,2},{4,5},{5,4},{6,7},{7,6},{8,9},{9,8},{10,11... | collective-permute-start | bytes 479240 | tf_op jit(solution)/shard_map/ppermute | solution.py:50
  10.0 15.7 %collective-permute-start.1 = (bf16[96,832]{1,0:T(8,128)(2,1)S(1)}, bf16[96,832]{1,0:T(8,128)(2,1)S(1)}, u32[]{:S(2)}, u32[]{:S(2)}) collective-permute-start(bf16[96,832]{1,0:T(8,128)(2,1)S(1)} %maximum_maximum_fusion), channel_id=1, source_target_pairs={{0,2},{1,3},{2,0},{3,1},{4,6},{5,7},{6,4},{7,5},{8,10},{9,11},{10,... | collective-permute-start | bytes 479240 | tf_op jit(solution)/shard_map/ppermute | solution.py:50
  12.6 13.2 %collective-permute-start.2 = (bf16[96,832]{1,0:T(8,128)(2,1)S(1)}, bf16[96,832]{1,0:T(8,128)(2,1)S(1)}, u32[]{:S(2)}, u32[]{:S(2)}) collective-permute-start(bf16[96,832]{1,0:T(8,128)(2,1)S(1)} %maximum_maximum_fusion), channel_id=1, source_target_pairs={{0,3},{1,2},{2,1},{3,0},{4,7},{5,6},{6,5},{7,4},{8,11},{9,10},{10,... | collective-permute-start | bytes 479240 | tf_op jit(solution)/shard_map/ppermute | solution.py:50
  13.0 28.9 %collective-permute-start.16 = (s32[16,128]{1,0:T(8,128)S(1)}, s32[16,128]{1,0:T(8,128)S(1)}, u32[]{:S(2)}, u32[]{:S(2)}) collective-permute-start(s32[16,128]{1,0:T(8,128)S(1)} %pad_bitcast_fusion), channel_id=1, source_target_pairs={{0,0},{1,1},{2,4},{3,5},{4,2},{5,3},{6,6},{7,7},{8,8},{9,9},{10,12... | collective-permute-start | bytes 24584 | tf_op jit(solution)/shard_map/ppermute | solution.py:64
  27.8 42.5 %copy-start.6 = (bf16[96,2944]{1,0:T(8,128)(2,1)}, bf16[96,2944]{1,0:T(8,128)(2,1)S(1)}, u32[]{:S(2)}) copy-start(bf16[96,2944]{1,0:T(8,128)(2,1)S(1)} %concatenate.155.refs_3_.refs_20_) | copy-start | bytes 1695748
  27.8 25.1 %collective-permute-start.4 = (bf16[96,2944]{1,0:T(8,128)(2,1)S(1)}, bf16[96,2944]{1,0:T(8,128)(2,1)S(1)}, u32[]{:S(2)}, u32[]{:S(2)}) collective-permute-start(bf16[96,2944]{1,0:T(8,128)(2,1)S(1)} %concatenate.155.refs_3_.refs_20_), channel_id=1, source_target_pairs={{0,8},{4,12},{8,0},{12,4},{16,24},{20,28},{24,16},{28,20},{1,9},{5... | collective-permute-start | bytes 1695752 | tf_op jit(solution)/shard_map/ppermute | solution.py:45
  29.4 34.3 %collective-permute-start.3 = (bf16[3,441,384]{2,1,0:T(8,128)(2,1)}, bf16[3,441,384]{2,1,0:T(8,128)(2,1)}, u32[]{:S(2)}, u32[]{:S(2)}) collective-permute-start(bf16[3,441,384]{2,1,0:T(8,128)(2,1)} %bitcast.1), channel_id=1, source_target_pairs={{0,0},{1,1},{2,4},{3,5},{4,2},{5,3},{6,6},{7,7},{8,8},{9,9},{10,12... | collective-permute-start | bytes 3048200 | tf_op jit(solution)/shard_map/ppermute | solution.py:64
  39.8 23.3 %collective-permute-start.5 = (bf16[96,2944]{1,0:T(8,128)(2,1)S(1)}, bf16[96,2944]{1,0:T(8,128)(2,1)S(1)}, u32[]{:S(2)}, u32[]{:S(2)}) collective-permute-start(bf16[96,2944]{1,0:T(8,128)(2,1)S(1)} %concatenate.155.refs_3_.refs_20_), channel_id=1, source_target_pairs={{0,16},{4,20},{8,24},{12,28},{16,0},{20,4},{24,8},{28,12},{1,17},{... | collective-permute-start | bytes 1695752 | tf_op jit(solution)/shard_map/ppermute | solution.py:45
  41.3 21.8 %collective-permute-start.6 = (bf16[96,2944]{1,0:T(8,128)(2,1)S(1)}, bf16[96,2944]{1,0:T(8,128)(2,1)S(1)}, u32[]{:S(2)}, u32[]{:S(2)}) collective-permute-start(bf16[96,2944]{1,0:T(8,128)(2,1)S(1)} %concatenate.155.refs_3_.refs_20_), channel_id=1, source_target_pairs={{0,24},{4,28},{8,16},{12,20},{16,8},{20,12},{24,0},{28,4},{1,25},{... | collective-permute-start | bytes 1695752 | tf_op jit(solution)/shard_map/ppermute | solution.py:45
  52.9 10.8 %collective-permute-start.7 = (bf16[96,2944]{1,0:T(8,128)(2,1)S(1)}, bf16[96,2944]{1,0:T(8,128)(2,1)S(1)}, u32[]{:S(2)}, u32[]{:S(2)}) collective-permute-start(bf16[96,2944]{1,0:T(8,128)(2,1)S(1)} %concatenate.155.refs_3_.refs_20_), channel_id=1, source_target_pairs={{0,4},{4,0},{8,12},{12,8},{16,20},{20,16},{24,28},{28,24},{1,5},{5... | collective-permute-start | bytes 1695752 | tf_op jit(solution)/shard_map/ppermute | solution.py:45
  53.0 11.1 %collective-permute-start.8 = (bf16[96,2944]{1,0:T(8,128)(2,1)S(1)}, bf16[96,2944]{1,0:T(8,128)(2,1)S(1)}, u32[]{:S(2)}, u32[]{:S(2)}) collective-permute-start(bf16[96,2944]{1,0:T(8,128)(2,1)S(1)} %collective-permute-done.4.refs_4_.refs_21_), channel_id=1, source_target_pairs={{0,4},{4,0},{8,12},{12,8},{16,20},{20,16},{24,28},{28,24},{1,5},{5... | collective-permute-start | bytes 1695752 | tf_op jit(solution)/shard_map/ppermute | solution.py:45
  63.1 7.2 %collective-permute-start.9 = (bf16[96,2944]{1,0:T(8,128)(2,1)S(1)}, bf16[96,2944]{1,0:T(8,128)(2,1)}, u32[]{:S(2)}, u32[]{:S(2)}) collective-permute-start(bf16[96,2944]{1,0:T(8,128)(2,1)S(1)} %collective-permute-done.5.refs_5_.refs_22_), channel_id=1, source_target_pairs={{0,4},{4,0},{8,12},{12,8},{16,20},{20,16},{24,28},{28,24},{1,5},{5... | collective-permute-start | bytes 1695752 | tf_op jit(solution)/shard_map/ppermute | solution.py:45
  63.1 7.2 %collective-permute-start.10 = (bf16[96,2944]{1,0:T(8,128)(2,1)S(1)}, bf16[96,2944]{1,0:T(8,128)(2,1)}, u32[]{:S(2)}, u32[]{:S(2)}) collective-permute-start(bf16[96,2944]{1,0:T(8,128)(2,1)S(1)} %collective-permute-done.6.refs_6_.refs_23_), channel_id=1, source_target_pairs={{0,4},{4,0},{8,12},{12,8},{16,20},{20,16},{24,28},{28,24},{1,5},{5... | collective-permute-start | bytes 1695752 | tf_op jit(solution)/shard_map/ppermute | solution.py:45
  63.6 19.5 %collective-permute-start.11 = (bf16[96,1728]{1,0:T(8,128)(2,1)}, bf16[96,1728]{1,0:T(8,128)(2,1)}, u32[]{:S(2)}, u32[]{:S(2)}) collective-permute-start(bf16[96,1728]{1,0:T(8,128)(2,1)} %pad_maximum_fusion.4.refs_1_), channel_id=1, source_target_pairs={{0,1},{1,0},{2,3},{3,2},{4,5},{5,4},{6,7},{7,6},{8,9},{9,8},{10,11... | collective-permute-start | bytes 995336 | tf_op jit(solution)/shard_map/ppermute | solution.py:50
  63.7 27.0 %collective-permute-start.12 = (bf16[96,1728]{1,0:T(8,128)(2,1)}, bf16[96,1728]{1,0:T(8,128)(2,1)}, u32[]{:S(2)}, u32[]{:S(2)}) collective-permute-start(bf16[96,1728]{1,0:T(8,128)(2,1)} %pad_maximum_fusion.4.refs_1_), channel_id=1, source_target_pairs={{0,2},{1,3},{2,0},{3,1},{4,6},{5,7},{6,4},{7,5},{8,10},{9,11},{10,... | collective-permute-start | bytes 995336 | tf_op jit(solution)/shard_map/ppermute | solution.py:50
  64.1 26.7 %collective-permute-start.13 = (bf16[96,1728]{1,0:T(8,128)(2,1)}, bf16[96,1728]{1,0:T(8,128)(2,1)}, u32[]{:S(2)}, u32[]{:S(2)}) collective-permute-start(bf16[96,1728]{1,0:T(8,128)(2,1)} %pad_maximum_fusion.4.refs_1_), channel_id=1, source_target_pairs={{0,3},{1,2},{2,1},{3,0},{4,7},{5,6},{6,5},{7,4},{8,11},{9,10},{10,... | collective-permute-start | bytes 995336 | tf_op jit(solution)/shard_map/ppermute | solution.py:50
  93.2 36.8 %collective-permute-start.14 = (bf16[96,6912]{1,0:T(8,128)(2,1)}, bf16[96,6912]{1,0:T(8,128)(2,1)}, u32[]{:S(2)}, u32[]{:S(2)}) collective-permute-start(bf16[96,6912]{1,0:T(8,128)(2,1)} %shard_map.467.refs_4_.refs_6_), channel_id=1, source_target_pairs={{0,8},{4,12},{8,0},{12,4},{16,24},{20,28},{24,16},{28,20},{1,9},{5... | collective-permute-start | bytes 3981320 | tf_op jit(solution)/shard_map/ppermute | solution.py:45
  93.8 36.3 %collective-permute-start.15 = (bf16[96,6912]{1,0:T(8,128)(2,1)}, bf16[96,6912]{1,0:T(8,128)(2,1)}, u32[]{:S(2)}, u32[]{:S(2)}) collective-permute-start(bf16[96,6912]{1,0:T(8,128)(2,1)} %shard_map.467.refs_4_.refs_6_), channel_id=1, source_target_pairs={{0,16},{4,20},{8,24},{12,28},{16,0},{20,4},{24,8},{28,12},{1,17},{... | collective-permute-start | bytes 3981320 | tf_op jit(solution)/shard_map/ppermute | solution.py:45
  98.1 31.9 %collective-permute-start.18 = (bf16[3,2,96,768]{3,2,1,0:T(8,128)(2,1)S(1)}, bf16[3,2,96,768]{3,2,1,0:T(8,128)(2,1)S(1)}, u32[]{:S(2)}, u32[]{:S(2)}) collective-permute-start(bf16[3,2,96,768]{3,2,1,0:T(8,128)(2,1)S(1)} %copy-done), channel_id=1, source_target_pairs={{0,1},{1,0},{2,3},{3,2},{4,5},{5,4},{6,7},{7,6},{8,9},{9,8},{10,11... | collective-permute-start | bytes 2654216 | tf_op jit(solution)/shard_map/ppermute | solution.py:50
  105.8 25.7 %collective-permute-start.21 = (bf16[2,2,192,384]{3,2,1,0:T(8,128)(2,1)}, bf16[2,2,192,384]{3,2,1,0:T(8,128)(2,1)}, u32[]{:S(2)}, u32[]{:S(2)}) collective-permute-start(bf16[2,2,192,384]{3,2,1,0:T(8,128)(2,1)} %bitcast.17), channel_id=1, source_target_pairs={{0,0},{1,1},{2,4},{3,5},{4,2},{5,3},{6,6},{7,7},{8,8},{9,9},{10,12... | collective-permute-start | bytes 1769480 | tf_op jit(solution)/shard_map/ppermute | solution.py:64
  114.2 19.4 %collective-permute-start.17 = (bf16[3,2,96,768]{3,2,1,0:T(8,128)(2,1)S(1)}, bf16[3,2,96,768]{3,2,1,0:T(8,128)(2,1)S(1)}, u32[]{:S(2)}, u32[]{:S(2)}) collective-permute-start(bf16[3,2,96,768]{3,2,1,0:T(8,128)(2,1)S(1)} %copy-done), channel_id=1, source_target_pairs={{0,4},{4,0},{8,12},{12,8},{16,20},{20,16},{24,28},{28,24},{1,5},{5... | collective-permute-start | bytes 2654216 | tf_op jit(solution)/shard_map/ppermute | solution.py:45
  130.0 3.5 collective-permute-start.19
  130.0 37.0 %collective-permute-start.20 = (bf16[96,6912]{1,0:T(8,128)(2,1)}, bf16[96,6912]{1,0:T(8,128)(2,1)}, u32[]{:S(2)}, u32[]{:S(2)}) collective-permute-start(bf16[96,6912]{1,0:T(8,128)(2,1)} %shard_map.467.refs_4_.refs_6_), channel_id=1, source_target_pairs={{0,24},{4,28},{8,16},{12,20},{16,8},{20,12},{24,0},{28,4},{1,25},{... | collective-permute-start | bytes 3981320 | tf_op jit(solution)/shard_map/ppermute | solution.py:45
  131.5 15.7 %collective-permute-start.23 = (bf16[2,2,192,384]{3,2,1,0:T(8,128)(2,1)}, bf16[2,2,192,384]{3,2,1,0:T(8,128)(2,1)}, u32[]{:S(2)}, u32[]{:S(2)}) collective-permute-start(bf16[2,2,192,384]{3,2,1,0:T(8,128)(2,1)} %collective-permute-done.21.refs_2_), channel_id=1, source_target_pairs={{0,1},{1,0},{2,3},{3,2},{4,5},{5,4},{6,7},{7,6},{8,9},{9,8},{10,11... | collective-permute-start | bytes 1769480 | tf_op jit(solution)/shard_map/ppermute | solution.py:50
  145.4 3.8 collective-permute-start.22
  147.3 2.2 collective-permute-start.24
  148.7 30.6 %collective-permute-start.25 = (bf16[96,6912]{1,0:T(8,128)(2,1)}, bf16[96,6912]{1,0:T(8,128)(2,1)S(1)}, u32[]{:S(2)}, u32[]{:S(2)}) collective-permute-start(bf16[96,6912]{1,0:T(8,128)(2,1)} %shard_map.467.refs_4_.refs_6_), channel_id=1, source_target_pairs={{0,4},{4,0},{8,12},{12,8},{16,20},{20,16},{24,28},{28,24},{1,5},{5... | collective-permute-start | bytes 3981320 | tf_op jit(solution)/shard_map/ppermute | solution.py:45
  149.2 30.1 %collective-permute-start.26 = (bf16[96,6912]{1,0:T(8,128)(2,1)}, bf16[96,6912]{1,0:T(8,128)(2,1)}, u32[]{:S(2)}, u32[]{:S(2)}) collective-permute-start(bf16[96,6912]{1,0:T(8,128)(2,1)} %collective-permute-done.14.refs_5_.refs_7_), channel_id=1, source_target_pairs={{0,4},{4,0},{8,12},{12,8},{16,20},{20,16},{24,28},{28,24},{1,5},{5... | collective-permute-start | bytes 3981320 | tf_op jit(solution)/shard_map/ppermute | solution.py:45
  156.4 23.0 %collective-permute-start.27 = (bf16[96,6912]{1,0:T(8,128)(2,1)}, bf16[96,6912]{1,0:T(8,128)(2,1)}, u32[]{:S(2)}, u32[]{:S(2)}) collective-permute-start(bf16[96,6912]{1,0:T(8,128)(2,1)} %collective-permute-done.15.refs_6_.refs_8_), channel_id=1, source_target_pairs={{0,4},{4,0},{8,12},{12,8},{16,20},{20,16},{24,28},{28,24},{1,5},{5... | collective-permute-start | bytes 3981320 | tf_op jit(solution)/shard_map/ppermute | solution.py:45
  167.0 12.3 %collective-permute-start.28 = (bf16[96,6912]{1,0:T(8,128)(2,1)}, bf16[96,6912]{1,0:T(8,128)(2,1)}, u32[]{:S(2)}, u32[]{:S(2)}) collective-permute-start(bf16[96,6912]{1,0:T(8,128)(2,1)} %collective-permute-done.20.refs_7_.refs_9_), channel_id=1, source_target_pairs={{0,4},{4,0},{8,12},{12,8},{16,20},{20,16},{24,28},{28,24},{1,5},{5... | collective-permute-start | bytes 3981320 | tf_op jit(solution)/shard_map/ppermute | solution.py:45
  214.8 1.7 collective-permute-start.29
  217.3 6.6 %collective-permute-start.30 = (f32[24,768]{1,0:T(8,128)S(1)}, f32[24,768]{1,0:T(8,128)S(1)}, u32[]{:S(2)}, u32[]{:S(2)}) collective-permute-start(f32[24,768]{1,0:T(8,128)S(1)} %maximum_add_fusion), channel_id=1, source_target_pairs={{0,1},{1,0},{2,3},{3,2},{4,5},{5,4},{6,7},{7,6},{8,9},{9,8},{10,11... | collective-permute-start | bytes 221192 | tf_op jit(solution)/shard_map/ppermute | solution.py:50
  222.2 44.3 %collective-permute-start.31 = (bf16[2,2,192,384]{3,2,1,0:T(8,128)(2,1)}, bf16[2,2,192,384]{3,2,1,0:T(8,128)(2,1)S(1)}, u32[]{:S(2)}, u32[]{:S(2)}) collective-permute-start(bf16[2,2,192,384]{3,2,1,0:T(8,128)(2,1)} %shard_map.473.refs_14_), channel_id=1, source_target_pairs={{0,0},{1,1},{2,4},{3,5},{4,2},{5,3},{6,6},{7,7},{8,8},{9,9},{10,12... | collective-permute-start | bytes 1769480 | tf_op jit(solution)/shard_map/ppermute | solution.py:64
  225.5 28.8 %copy-start.4 = (bf16[1152,768]{1,0:T(8,128)(2,1)S(1)}, bf16[1152,768]{1,0:T(8,128)(2,1)}, u32[]{:S(2)}) copy-start(bf16[1152,768]{1,0:T(8,128)(2,1)} %get-tuple-element.155.refs_0_) | copy-start | bytes 5308420
  256.6 21.2 %collective-permute-start.34 = (bf16[384,768]{1,0:T(8,128)(2,1)S(1)}, bf16[384,768]{1,0:T(8,128)(2,1)S(1)}, u32[]{:S(2)}, u32[]{:S(2)}) collective-permute-start(bf16[384,768]{1,0:T(8,128)(2,1)S(1)} %convolution_convert_fusion.4), channel_id=1, source_target_pairs={{0,4},{4,0},{8,12},{12,8},{16,20},{20,16},{24,28},{28,24},{1,5},{5... | collective-permute-start | bytes 1769480 | tf_op jit(solution)/shard_map/ppermute | solution.py:45
  265.5 12.5 %collective-permute-start.33 = (bf16[384,3072]{1,0:T(8,128)(2,1)S(1)}, bf16[384,3072]{1,0:T(8,128)(2,1)S(1)}, u32[]{:S(2)}, u32[]{:S(2)}) collective-permute-start(bf16[384,3072]{1,0:T(8,128)(2,1)S(1)} %convolution_convert_fusion), channel_id=1, source_target_pairs={{0,4},{4,0},{8,12},{12,8},{16,20},{20,16},{24,28},{28,24},{1,5},{5... | collective-permute-start | bytes 7077896 | tf_op jit(solution)/shard_map/ppermute | solution.py:45
  270.6 8.2 %collective-permute-start.32 = (bf16[384,3072]{1,0:T(8,128)(2,1)S(1)}, bf16[384,3072]{1,0:T(8,128)(2,1)S(1)}, u32[]{:S(2)}, u32[]{:S(2)}) collective-permute-start(bf16[384,3072]{1,0:T(8,128)(2,1)S(1)} %convolution_convert_fusion.2), channel_id=1, source_target_pairs={{0,4},{4,0},{8,12},{12,8},{16,20},{20,16},{24,28},{28,24},{1,5},{5... | collective-permute-start | bytes 7077896 | tf_op jit(solution)/shard_map/ppermute | solution.py:45
  280.9 31.6 %collective-permute-start.38 = (bf16[96,6912]{1,0:T(8,128)(2,1)}, bf16[96,6912]{1,0:T(8,128)(2,1)S(1)}, u32[]{:S(2)}, u32[]{:S(2)}) collective-permute-start(bf16[96,6912]{1,0:T(8,128)(2,1)} %pad_maximum_fusion.1), channel_id=1, source_target_pairs={{0,8},{4,12},{8,0},{12,4},{16,24},{20,28},{24,16},{28,20},{1,9},{5... | collective-permute-start | bytes 3981320 | tf_op jit(solution)/shard_map/ppermute | solution.py:45
  282.6 31.4 %collective-permute-start.39 = (bf16[96,6912]{1,0:T(8,128)(2,1)}, bf16[96,6912]{1,0:T(8,128)(2,1)}, u32[]{:S(2)}, u32[]{:S(2)}) collective-permute-start(bf16[96,6912]{1,0:T(8,128)(2,1)} %pad_maximum_fusion.2), channel_id=1, source_target_pairs={{0,16},{4,20},{8,24},{12,28},{16,0},{20,4},{24,8},{28,12},{1,17},{... | collective-permute-start | bytes 3981320 | tf_op jit(solution)/shard_map/ppermute | solution.py:45
  296.5 2.3 collective-permute-start.35
  311.5 5.2 %collective-permute-start.36 = (bf16[2,2,96,768]{3,2,1,0:T(8,128)(2,1)}, bf16[2,2,96,768]{3,2,1,0:T(8,128)(2,1)S(1)}, u32[]{:S(2)}, u32[]{:S(2)}) collective-permute-start(bf16[2,2,96,768]{3,2,1,0:T(8,128)(2,1)} %get-tuple-element.186), channel_id=1, source_target_pairs={{0,4},{4,0},{8,12},{12,8},{16,20},{20,16},{24,28},{28,24},{1,5},{5... | collective-permute-start | bytes 1769480 | tf_op jit(solution)/shard_map/ppermute | solution.py:45
  314.0 31.5 %collective-permute-start.40 = (bf16[96,6912]{1,0:T(8,128)(2,1)}, bf16[96,6912]{1,0:T(8,128)(2,1)}, u32[]{:S(2)}, u32[]{:S(2)}) collective-permute-start(bf16[96,6912]{1,0:T(8,128)(2,1)} %pad_maximum_fusion.3), channel_id=1, source_target_pairs={{0,24},{4,28},{8,16},{12,20},{16,8},{20,12},{24,0},{28,4},{1,25},{... | collective-permute-start | bytes 3981320 | tf_op jit(solution)/shard_map/ppermute | solution.py:45
  316.4 7.9 %collective-permute-start.37 = (bf16[2,96,768]{2,1,0:T(8,128)(2,1)S(1)}, bf16[2,96,768]{2,1,0:T(8,128)(2,1)S(1)}, u32[]{:S(2)}, u32[]{:S(2)}) collective-permute-start(bf16[2,96,768]{2,1,0:T(8,128)(2,1)S(1)} %fusion.9), channel_id=1, source_target_pairs={{0,1},{1,0},{2,3},{3,2},{4,5},{5,4},{6,7},{7,6},{8,9},{9,8},{10,11... | collective-permute-start | bytes 884744 | tf_op jit(solution)/shard_map/ppermute | solution.py:50
  336.7 2.3 collective-permute-start.42
  337.7 13.4 %collective-permute-start.41 = (bf16[2,96,768]{2,1,0:T(8,128)(2,1)}, bf16[2,96,768]{2,1,0:T(8,128)(2,1)}, u32[]{:S(2)}, u32[]{:S(2)}) collective-permute-start(bf16[2,96,768]{2,1,0:T(8,128)(2,1)} %fusion.10), channel_id=1, source_target_pairs={{0,1},{1,0},{2,3},{3,2},{4,5},{5,4},{6,7},{7,6},{8,9},{9,8},{10,11... | collective-permute-start | bytes 884744 | tf_op jit(solution)/shard_map/ppermute | solution.py:50
  340.9 12.8 %collective-permute-start.43 = (bf16[2,96,768]{2,1,0:T(8,128)(2,1)}, bf16[2,96,768]{2,1,0:T(8,128)(2,1)}, u32[]{:S(2)}, u32[]{:S(2)}) collective-permute-start(bf16[2,96,768]{2,1,0:T(8,128)(2,1)} %fusion.11), channel_id=1, source_target_pairs={{0,1},{1,0},{2,3},{3,2},{4,5},{5,4},{6,7},{7,6},{8,9},{9,8},{10,11... | collective-permute-start | bytes 884744 | tf_op jit(solution)/shard_map/ppermute | solution.py:50
  353.8 25.6 %copy-start.31 = (f32[2,2,768]{2,1,0:T(2,128)S(1)}, f32[2,2,768]{2,1,0:T(2,128)}, u32[]{:S(2)}) copy-start(f32[2,2,768]{2,1,0:T(2,128)} %get-tuple-element.205) | copy-start | bytes 36868
  353.8 25.6 %copy-start.32 = (f32[2,2,768]{2,1,0:T(2,128)S(1)}, f32[2,2,768]{2,1,0:T(2,128)}, u32[]{:S(2)}) copy-start(f32[2,2,768]{2,1,0:T(2,128)} %get-tuple-element.206) | copy-start | bytes 36868
  377.1 4.8 %collective-permute-start.44 = (bf16[384,2944]{1,0:T(8,128)(2,1)}, bf16[384,2944]{1,0:T(8,128)(2,1)}, u32[]{:S(2)}, u32[]{:S(2)}) collective-permute-start(bf16[384,2944]{1,0:T(8,128)(2,1)} %get-tuple-element.201), channel_id=1, source_target_pairs={{0,4},{4,0},{8,12},{12,8},{16,20},{20,16},{24,28},{28,24},{1,5},{5... | collective-permute-start | bytes 6782984 | tf_op jit(solution)/shard_map/ppermute | solution.py:45
  379.4 17.3 %collective-permute-start.48 = (bf16[96,3456]{1,0:T(8,128)(2,1)S(1)}, bf16[96,3456]{1,0:T(8,128)(2,1)S(1)}, u32[]{:S(2)}, u32[]{:S(2)}) collective-permute-start(bf16[96,3456]{1,0:T(8,128)(2,1)S(1)} %concatenate.170), channel_id=1, source_target_pairs={{0,1},{1,0},{2,3},{3,2},{4,5},{5,4},{6,7},{7,6},{8,9},{9,8},{10,11... | collective-permute-start | bytes 1990664 | tf_op jit(solution)/shard_map/ppermute | solution.py:50
  385.7 16.9 %collective-permute-start.47 = (bf16[96,2944]{1,0:T(8,128)(2,1)}, bf16[96,2944]{1,0:T(8,128)(2,1)}, u32[]{:S(2)}, u32[]{:S(2)}) collective-permute-start(bf16[96,2944]{1,0:T(8,128)(2,1)} %get-tuple-element.261), channel_id=1, source_target_pairs={{0,24},{4,28},{8,16},{12,20},{16,8},{20,12},{24,0},{28,4},{1,25},{... | collective-permute-start | bytes 1695752 | tf_op jit(solution)/shard_map/ppermute | solution.py:45
  386.1 27.0 %collective-permute-start.46 = (bf16[96,2944]{1,0:T(8,128)(2,1)}, bf16[96,2944]{1,0:T(8,128)(2,1)}, u32[]{:S(2)}, u32[]{:S(2)}) collective-permute-start(bf16[96,2944]{1,0:T(8,128)(2,1)} %get-tuple-element.260), channel_id=1, source_target_pairs={{0,16},{4,20},{8,24},{12,28},{16,0},{20,4},{24,8},{28,12},{1,17},{... | collective-permute-start | bytes 1695752 | tf_op jit(solution)/shard_map/ppermute | solution.py:45
  387.7 25.5 %collective-permute-start.45 = (bf16[96,2944]{1,0:T(8,128)(2,1)}, bf16[96,2944]{1,0:T(8,128)(2,1)}, u32[]{:S(2)}, u32[]{:S(2)}) collective-permute-start(bf16[96,2944]{1,0:T(8,128)(2,1)} %get-tuple-element.262), channel_id=1, source_target_pairs={{0,8},{4,12},{8,0},{12,4},{16,24},{20,28},{24,16},{28,20},{1,9},{5... | collective-permute-start | bytes 1695752 | tf_op jit(solution)/shard_map/ppermute | solution.py:45
  397.8 29.3 %collective-permute-start.53 = (bf16[96,1728]{1,0:T(8,128)(2,1)S(1)}, bf16[96,1728]{1,0:T(8,128)(2,1)S(1)}, u32[]{:S(2)}, u32[]{:S(2)}) collective-permute-start(bf16[96,1728]{1,0:T(8,128)(2,1)S(1)} %get-tuple-element.293), channel_id=1, source_target_pairs={{0,2},{1,3},{2,0},{3,1},{4,6},{5,7},{6,4},{7,5},{8,10},{9,11},{10,... | collective-permute-start | bytes 995336 | tf_op jit(solution)/shard_map/ppermute | solution.py:50
  415.1 4.9 %collective-permute-start.51 = (bf16[24,1280]{1,0:T(8,128)(2,1)S(1)}, bf16[24,1280]{1,0:T(8,128)(2,1)S(1)}, u32[]{:S(2)}, u32[]{:S(2)}) collective-permute-start(bf16[24,1280]{1,0:T(8,128)(2,1)S(1)} %pad_maximum_fusion.13), channel_id=1, source_target_pairs={{0,1},{1,0},{2,3},{3,2},{4,5},{5,4},{6,7},{7,6},{8,9},{9,8},{10,11... | collective-permute-start | bytes 184328 | tf_op jit(solution)/shard_map/ppermute | solution.py:50
  416.0 7.4 %collective-permute-start.49 = (bf16[96,1152]{1,0:T(8,128)(2,1)S(1)}, bf16[96,1152]{1,0:T(8,128)(2,1)S(1)}, u32[]{:S(2)}, u32[]{:S(2)}) collective-permute-start(bf16[96,1152]{1,0:T(8,128)(2,1)S(1)} %pad_maximum_fusion.9), channel_id=1, source_target_pairs={{0,1},{1,0},{2,3},{3,2},{4,5},{5,4},{6,7},{7,6},{8,9},{9,8},{10,11... | collective-permute-start | bytes 663560 | tf_op jit(solution)/shard_map/ppermute | solution.py:50
  420.7 6.4 %collective-permute-start.52 = (bf16[24,640]{1,0:T(8,128)(2,1)S(1)}, bf16[24,640]{1,0:T(8,128)(2,1)S(1)}, u32[]{:S(2)}, u32[]{:S(2)}) collective-permute-start(bf16[24,640]{1,0:T(8,128)(2,1)S(1)} %get-tuple-element.298), channel_id=1, source_target_pairs={{0,2},{1,3},{2,0},{3,1},{4,6},{5,7},{6,4},{7,5},{8,10},{9,11},{10,... | collective-permute-start | bytes 92168 | tf_op jit(solution)/shard_map/ppermute | solution.py:50
  424.4 7.1 %collective-permute-start.50 = (bf16[96,576]{1,0:T(8,128)(2,1)S(1)}, bf16[96,576]{1,0:T(8,128)(2,1)S(1)}, u32[]{:S(2)}, u32[]{:S(2)}) collective-permute-start(bf16[96,576]{1,0:T(8,128)(2,1)S(1)} %get-tuple-element.302), channel_id=1, source_target_pairs={{0,2},{1,3},{2,0},{3,1},{4,6},{5,7},{6,4},{7,5},{8,10},{9,11},{10,... | collective-permute-start | bytes 331784 | tf_op jit(solution)/shard_map/ppermute | solution.py:50
  434.6 1.5 collective-permute-start.54
  436.9 5.1 %collective-permute-start.57 = (f32[56,192]{1,0:T(8,128)S(1)}, f32[56,192]{1,0:T(8,128)S(1)}, u32[]{:S(2)}, u32[]{:S(2)}) collective-permute-start(f32[56,192]{1,0:T(8,128)S(1)} %add.706), channel_id=1, source_target_pairs={{0,24},{4,28},{8,16},{12,20},{16,8},{20,12},{24,0},{28,4},{1,25},{... | collective-permute-start | bytes 129032 | tf_op jit(solution)/shard_map/ppermute | solution.py:45
  439.3 4.7 %collective-permute-start.55 = (f32[56,192]{1,0:T(8,128)S(1)}, f32[56,192]{1,0:T(8,128)S(1)}, u32[]{:S(2)}, u32[]{:S(2)}) collective-permute-start(f32[56,192]{1,0:T(8,128)S(1)} %add.706), channel_id=1, source_target_pairs={{0,8},{4,12},{8,0},{12,4},{16,24},{20,28},{24,16},{28,20},{1,9},{5... | collective-permute-start | bytes 129032 | tf_op jit(solution)/shard_map/ppermute | solution.py:45
  440.8 4.2 collective-permute-start.56
  445.0 4.2 collective-permute-start.58
  449.3 5.2 %collective-permute-start.59 = (f32[56,192]{1,0:T(8,128)S(1)}, f32[56,192]{1,0:T(8,128)S(1)}, u32[]{:S(2)}, u32[]{:S(2)}) collective-permute-start(f32[56,192]{1,0:T(8,128)S(1)} %add.710.refs_1_), channel_id=1, source_target_pairs={{0,2},{1,3},{2,0},{3,1},{4,6},{5,7},{6,4},{7,5},{8,10},{9,11},{10,... | collective-permute-start | bytes 129032 | tf_op jit(solution)/shard_map/ppermute | solution.py:50
  (47 other events, 453.2 us)

commit v7 on v6

--- a/solution.py
+++ b/solution.py
@@ -127,9 +127,10 @@
     width = inputs.shape[1] // count
     order = [b for b in range(count) if b % 2 == 0] + [b for b in range(count) if b % 2]
     at = [order.index(b ^ 1) for b in order]
-    got = swap_dp(inputs, 1)
-    inputs = inputs + jnp.concatenate([got[:, p * width : (p + 1) * width] for p in at], axis=1)
-    return inputs + swap_mp(inputs, 1)
+    pairs = [(d * 4 + z, (d ^ 1) * 4 + (z ^ 1)) for d in range(count) for z in range(4)]
+    got = swap_dp(inputs, 1) + lax.ppermute(inputs, ("dp", "mp"), pairs)
+    inputs = inputs + swap_mp(inputs, 1)
+    return inputs + jnp.concatenate([got[:, p * width : (p + 1) * width] for p in at], axis=1)
 
 
 def call(
@@ -930,20 +931,22 @@
     )
 
 
-def update_kernel(rates, patch, odd_ref, one_ref, two_ref, *refs):
+def update_kernel(rates, patch, odd_ref, own_ref, one_ref, two_ref, three_ref, *refs):
     count = len(rates)
+    near = own_ref[...] + one_ref[...]
+    away = two_ref[...] + three_ref[...]
     attn_ref, small_ref, rest_ref = refs[:3]
     weights, moments, averages = (refs[3 + i * count : 3 + (i + 1) * count] for i in range(3))
     outs = refs[3 + 3 * count :]
     heads = weights[6].shape[0] * 3
     blocks = []
-    square = one_ref[52:53, 0:1] + two_ref[52:53, 0:1]
-    spot = lax.broadcasted_iota(jnp.int32, (13, one_ref.shape[1]), 1)
-    row = lax.broadcasted_iota(jnp.int32, (13, one_ref.shape[1]), 0)
+    square = near[52:53, 0:1] + away[52:53, 0:1]
+    spot = lax.broadcasted_iota(jnp.int32, (13, near.shape[1]), 1)
+    row = lax.broadcasted_iota(jnp.int32, (13, near.shape[1]), 0)
     counted = (row < 12) | (spot < heads)
     for c in range(4):
         far = 13 * (c ^ 2)
-        block = one_ref[13 * c : 13 * c + 13] + two_ref[far : far + 13]
+        block = near[13 * c : 13 * c + 13] + away[far : far + 13]
         kept = jnp.where(counted, block, 0.0)
         square = square + jnp.sum(kept * kept)
         blocks.append(block)
@@ -980,8 +983,8 @@
         step(6, slice(h, h + 1), mine[12:13, 3 * h : 3 * h + 3])
 
 
-def update(odd, one, two, grads, patch, weights, moments, averages, rates):
-    operands = (odd, one, two) + grads + weights + moments + averages
+def update(odd, parts, grads, patch, weights, moments, averages, rates):
+    operands = (odd,) + parts + grads + weights + moments + averages
     kept = [jax.ShapeDtypeStruct(w.shape, f32) for w in weights]
     shapes = kept * 3 + [jax.ShapeDtypeStruct(w.shape, bf16) for w in weights[:2]]
     shapes = shapes + [jax.ShapeDtypeStruct((1, 1), f32)] * 3
@@ -1377,8 +1380,7 @@
     )
     both = both + swap_dp(both, 1)
     both = both + sum(swap_dp(both, b) for b in range(2, dp_count, 2))
-    both = both + swap_mp(both, 1)
-    both_two = swap_mp(both, 2)
+    parts = (both,) + tuple(swap_mp(both, mask) for mask in (1, 2, 3))
 
     def turned(arrays):
         up, down, embed_part, head, vector, conv, position = arrays
@@ -1414,8 +1416,7 @@
     rates = (LEARNING,) * 4 + (VECTOR_LEARNING,) * 3
     made = update(
         across[None],
-        both,
-        both_two,
+        parts,
         (attn_mine, small_mine, rest_mine),
         patch,
         turned(masters),

time: 468 us -> 477 us (1.019)
  starting transfers between devices: 70.3 us -> 77.3 us
    ppermute x20 -> x21, starting transfers between devices: 27.3 us -> 36.4 us  [swap_mp(): return lax.ppermute(inputs, 'mp', [(i, i ^ mask) for i in range(size)])]
    ppermute x36, waiting for transfers between devices: 39.4 us -> 47.1 us  [swap_dp(): return lax.ppermute(inputs, 'dp', [(i, i ^ mask) for i in range(size)])]
    ppermute x20 -> x21, waiting for transfers between devices: 68.5 us -> 62.9 us  [swap_mp(): return lax.ppermute(inputs, 'mp', [(i, i ^ mask) for i in range(size)])]
    unnamed x110 -> x114, local copies, waits for them, and re-layouts: 9.62 us -> 9.35 us
  transfers between devices with their start and end apart: 60 -> 62, of which waited for: 28 -> 27; matrix products, arithmetic and copies ran while one was open for 14% -> 14% of each run, Pallas kernels for 25% -> 25%
where the time goes in v7:
time: 477 us; the launch traced here: 469 us
  Pallas kernels  183 us (38%)
  waiting for transfers between devices  110 us (23%)
  starting transfers between devices  77.3 us (16%)
  other arithmetic  37.9 us (8%)
  matrix products  23.1 us (5%)
  local copies, waits for them, and re-layouts  21.6 us (5%)
  between operations  16.5 us (3%)
    pallas_call x15, Pallas kernels, call(): pl.pallas_call(run, grid=grid, in_specs=list(in_specs) + [pl.BlockSpec(me...  183 us
    ppermute x21, waiting for transfers between devices, swap_mp(): return lax.ppermute(inputs, 'mp', [(i, i ^ mask) for i in range(size)])  62.9 us
    ppermute x36, waiting for transfers between devices, swap_dp(): return lax.ppermute(inputs, 'dp', [(i, i ^ mask) for i in range(size)])  47.1 us
    ppermute x21, starting transfers between devices, swap_mp(): return lax.ppermute(inputs, 'mp', [(i, i ^ mask) for i in range(size)])  36.4 us
    ppermute x36, starting transfers between devices, swap_dp(): return lax.ppermute(inputs, 'dp', [(i, i ^ mask) for i in range(size)])  21.9 us
    dot_general x7, matrix products, contract_rows(): lax.dot_general(first_operand, second_operand, (((0,), (0,)), ((), ())),...  21.2 us
    ppermute x4, starting transfers between devices, regroup(): return lax.ppermute(inputs, ('dp', 'mp'), pairs)  18 us
  transfers between devices with their start and end apart: 62, of which 27 were waited for; matrix products, arithmetic and copies ran while one was open for 14% of the time, Pallas kernels for 25%

profile of v7, /device:TPU:0, one launch (start us, length us, event | category | flops | bytes accessed | tf_op | source)
XLA Modules:
  0.0 469.2 jit_solution(11387587752910098587)
XLA Ops:
  6.9 3.1 collective-permute-start
  10.0 2.6 collective-permute-start.1
  15.6 1.5 collective-permute-done
  17.2 8.5 %collective-permute-done.1 = bf16[96,832]{1,0:T(8,128)(2,1)S(1)} collective-permute-done((bf16[96,832]{1,0:T(8,128)(2,1)S(1)}, bf16[96,832]{1,0:T(8,128)(2,1)S(1)}, u32[]{:S(2)}, u32[]{:S(2)}) %collective-permute-start.1) | collective-permute-done | bytes 159776 | tf_op jit(solution)/shard_map/ppermute | solution.py:50
  27.8 1.6 collective-permute-start.4
  29.4 9.4 %collective-permute-start.3 = (bf16[3,441,384]{2,1,0:T(8,128)(2,1)}, bf16[3,441,384]{2,1,0:T(8,128)(2,1)}, u32[]{:S(2)}, u32[]{:S(2)}) collective-permute-start(bf16[3,441,384]{2,1,0:T(8,128)(2,1)} %bitcast.1), channel_id=1, source_target_pairs={{0,0},{1,1},{2,4},{3,5},{4,2},{5,3},{6,6},{7,7},{8,8},{9,9},{10,12... | collective-permute-start | bytes 3048200 | tf_op jit(solution)/shard_map/ppermute | solution.py:64
  52.4 1.6 collective-permute-start.5
  59.4 16.4 %collective-permute-done.5.refs_5_.refs_22_ = bf16[96,2944]{1,0:T(8,128)(2,1)S(1)} collective-permute-done((bf16[96,2944]{1,0:T(8,128)(2,1)S(1)}, bf16[96,2944]{1,0:T(8,128)(2,1)S(1)}, u32[]{:S(2)}, u32[]{:S(2)}) %collective-permute-start.5) | collective-permute-done | bytes 565280 | tf_op jit(solution)/shard_map/ppermute | solution.py:45
  76.7 4.0 collective-permute-start.13
  81.5 1.5 reshape.676.refs_2_.refs_1_.refs_3_
  83.0 12.7 %shard_map.466 = (bf16[1152,441]{1,0:T(8,128)(2,1)}, f32[1152,768]{1,0:T(8,128)}, bf16[1152,768]{1,0:T(8,128)(2,1)}, bf16[1152,768]{1,0:T(8,128)(2,1)}, bf16[115...) custom-call(bf16[3,441,384]{2,1,0:T(8,128)(2,1)} %collective-permute, ...), custom_call_target="tpu_custom_call" | custom-call | flops 1000 | bytes 1000 | tf_op jit(solution)/shard_map/pallas_call | solution.py:144
  95.8 7.6 %collective-permute-done.12.refs_3_ = bf16[96,1728]{1,0:T(8,128)(2,1)} collective-permute-done((bf16[96,1728]{1,0:T(8,128)(2,1)}, bf16[96,1728]{1,0:T(8,128)(2,1)}, u32[]{:S(2)}, u32[]{:S(2)}) %collective-permute-start.12) | collective-permute-done | bytes 331808 | tf_op jit(solution)/shard_map/ppermute | solution.py:50
  103.4 2.5 shard_map.467.refs_4_.refs_6_
  106.4 1.5 collective-permute-start.15
  108.1 7.1 %collective-permute-start.18 = (bf16[3,2,96,768]{3,2,1,0:T(8,128)(2,1)S(1)}, bf16[3,2,96,768]{3,2,1,0:T(8,128)(2,1)S(1)}, u32[]{:S(2)}, u32[]{:S(2)}) collective-permute-start(bf16[3,2,96,768]{3,2,1,0:T(8,128)(2,1)S(1)} %copy-done), channel_id=1, source_target_pairs={{0,1},{1,0},{2,3},{3,2},{4,5},{5,4},{6,7},{7,6},{8,9},{9,8},{10,11... | collective-permute-start | bytes 2654216 | tf_op jit(solution)/shard_map/ppermute | solution.py:50
  115.7 6.2 %collective-permute-start.21 = (bf16[2,2,192,384]{3,2,1,0:T(8,128)(2,1)}, bf16[2,2,192,384]{3,2,1,0:T(8,128)(2,1)}, u32[]{:S(2)}, u32[]{:S(2)}) collective-permute-start(bf16[2,2,192,384]{3,2,1,0:T(8,128)(2,1)} %bitcast.17), channel_id=1, source_target_pairs={{0,0},{1,1},{2,4},{3,5},{4,2},{5,3},{6,6},{7,7},{8,8},{9,9},{10,12... | collective-permute-start | bytes 1769480 | tf_op jit(solution)/shard_map/ppermute | solution.py:64
  124.1 15.8 %collective-permute-done.18.refs_5_.refs_9_.refs_13_.refs_4_.refs_8_.refs_7_.refs_11_ = bf16[3,2,96,768]{3,2,1,0:T(8,128)(2,1)S(1)} collective-permute-done((bf16[3,2,96,768]{3,2,1,0:T(8,128)(2,1)S(1)}, bf16[3,2,96,768]{3,2,1,0:T(8,128)(2,1)S(1)}, u32[]{:S(2)}, u32[]{:S(2)}) %collective-permute-start.18) | collective-permute-done | bytes 884768 | tf_op jit(solution)/shard_map/ppermute | solution.py:50
  139.9 1.5 collective-permute-start.20
  141.5 4.8 %collective-permute-start.23 = (bf16[2,2,192,384]{3,2,1,0:T(8,128)(2,1)}, bf16[2,2,192,384]{3,2,1,0:T(8,128)(2,1)}, u32[]{:S(2)}, u32[]{:S(2)}) collective-permute-start(bf16[2,2,192,384]{3,2,1,0:T(8,128)(2,1)} %collective-permute-done.21.refs_2_), channel_id=1, source_target_pairs={{0,1},{1,0},{2,3},{3,2},{4,5},{5,4},{6,7},{7,6},{8,9},{9,8},{10,11... | collective-permute-start | bytes 1769480 | tf_op jit(solution)/shard_map/ppermute | solution.py:50
  148.1 10.1 %shard_map.468 = (bf16[1152,768]{1,0:T(8,128)(2,1)}, bf16[12,384,768]{2,1,0:T(8,128)(2,1)}, bf16[768,768]{1,0:T(8,128)(2,1)}, bf16[768,768]{1,0:T(8,128)(2,1)}) custom-call(bf16[1152,768]{1,0:T(8,128)(2,1)} %get-tuple-element.148.refs_0_, f32[2,6,768]{2,1,0:T(8,128)} %reshape.676.refs_2_.refs_1_.refs_3_, f32[3,4,768]{2,1,0:T(4,128)} %pad_maximum_fusion.16.refs_2_, ...), custom_call_target="tpu_custom_call" | custom-call | flops 1000 | bytes 1000 | tf_op jit(solution)/shard_map/pallas_call | solution.py:144
  162.4 5.5 %shard_map.469.refs_11_.refs_7_.refs_8_.refs_5_.refs_6_.refs_9_ = bf16[2,2,384,768]{3,2,1,0:T(8,128)(2,1)} custom-call(s32[4]{0:T(128)} %pad_add_fusion.2.refs_0_, bf16[384,384]{1,0:T(8,128)(2,1)} %fusion.7.refs_1_, bf16[2,2,192,384]{3,2,1,0:T(8,128)(2,1)} %collective-permute-done.21.refs_2_, bf16[2,2,192,384]{3,2,1,0:T(8,128)(2,1)} %copy-done.20, ...), custom_call_target="tpu_custom_call" | custom-call | flops 1000 | bytes 1000 | tf_op jit(solution)/shard_map/pallas_call | solution.py:144
  168.0 10.0 %shard_map.470 = (bf16[1152,768]{1,0:T(8,128)(2,1)}, bf16[12,384,768]{2,1,0:T(8,128)(2,1)}, bf16[768,768]{1,0:T(8,128)(2,1)}, bf16[768,768]{1,0:T(8,128)(2,1)}) custom-call(bf16[1152,768]{1,0:T(8,128)(2,1)} %get-tuple-element.148.refs_0_, f32[2,6,768]{2,1,0:T(8,128)} %reshape.676.refs_2_.refs_1_.refs_3_, ...), custom_call_target="tpu_custom_call", output_to_operand_aliasing={{0}: (12, {})} | custom-call | flops 1000 | bytes 1000 | tf_op jit(solution)/shard_map/pallas_call | solution.py:144
  180.9 9.9 %shard_map.471 = (bf16[1152,768]{1,0:T(8,128)(2,1)}, bf16[12,384,768]{2,1,0:T(8,128)(2,1)}, bf16[768,768]{1,0:T(8,128)(2,1)}, bf16[768,768]{1,0:T(8,128)(2,1)}) custom-call(bf16[1152,768]{1,0:T(8,128)(2,1)} %get-tuple-element.148.refs_0_, f32[2,6,768]{2,1,0:T(8,128)} %reshape.676.refs_2_.refs_1_.refs_3_, ...), custom_call_target="tpu_custom_call", output_to_operand_aliasing={{0}: (9, {})} | custom-call | flops 1000 | bytes 1000 | tf_op jit(solution)/shard_map/pallas_call | solution.py:144
  191.9 34.5 %shard_map.472 = (f32[1152,768]{1,0:T(8,128)}, bf16[1152,768]{1,0:T(8,128)(2,1)}, bf16[1152,3072]{1,0:T(8,128)(2,1)}, bf16[1152,3072]{1,0:T(8,128)(2,1)}, f32[1152,768]{1,0:T(8,128)}, /*index=5*/f32[3,8,768]{2,1,0:T(8,128)}) custom-call(bf16[1152,768]{1,0:T(8,128)(2,1)} %get-tuple-element.155.refs_0_, f32[1152,768]{1,0:T(8,128)} %get-tuple-element.156.refs_1_.refs_4_, ...), custom_call_target="tpu_custom_call" | custom-call | flops 1000 | bytes 1000 | tf_op jit(solution)/shard_map/pallas_call | solution.py:144
  228.8 4.3 shard_map.473.refs_14_
  233.1 1.7 collective-permute-start.32
  236.4 28.8 %shard_map.474 = (bf16[1152,768]{1,0:T(8,128)(2,1)}, bf16[1152,3072]{1,0:T(8,128)(2,1)}, bf16[1152,768]{1,0:T(8,128)(2,1)}, f32[1152,768]{1,0:T(8,128)}, bf16[1152,768]{1,0:T(8,128)(2,1)}, /*index=5*/f32[8,768]{1,0:T(8,128)}) custom-call(f32[3,8,768]{2,1,0:T(8,128)} %convolution_bitcast_fusion.refs_0_, f32[3,8,384]{2,1,0:T(8,128)} %convert_divide_fusion.refs_3_.refs_1_, ...), custom_call_target="tpu_custom_call" | custom-call | flops 1000 | bytes 1000 | tf_op jit(solution)/shard_map/pallas_call | solution.py:144
  265.2 2.3 convolution_convert_fusion.4
  267.5 1.7 collective-permute-start.35
  269.2 6.4 %convolution_convert_fusion = bf16[384,3072]{1,0:T(8,128)(2,1)S(1)} fusion(bf16[1152,3072]{1,0:T(8,128)(2,1)} %get-tuple-element.178, bf16[1152,768]{1,0:T(8,128)(2,1)S(1)} %copy-done.47), kind=kOutput, calls=%fused_computation | convolution fusion | flops 2719088640 | bytes 10321920 | tf_op jit(solution)/shard_map/dot_general | solution.py:38
  277.1 3.7 convolution_convert_fusion.2
  281.1 3.5 convolution_convert_fusion.1
  284.5 3.5 convolution_convert_fusion.3
  294.5 11.3 %shard_map.475 = (bf16[1152,768]{1,0:T(8,128)(2,1)}, bf16[2,2,96,768]{3,2,1,0:T(8,128)(2,1)}, bf16[2,2,96,768]{3,2,1,0:T(8,128)(2,1)}, f32[2,2,768]{2,1,0:T(2,128)}, f32[3,4,128]{2,1,0:T(4,128)}) custom-call(bf16[1152,768]{1,0:T(8,128)(2,1)} %get-tuple-element.148.refs_0_, bf16[768,768]{1,0:T(8,128)(2,1)} %get-tuple-element.171.refs_1_, ...), custom_call_target="tpu_custom_call" | custom-call | flops 1000 | bytes 1000 | tf_op jit(solution)/shard_map/pallas_call | solution.py:144
  305.9 2.2 collective-permute-done.36.refs_12_
  309.3 11.4 %shard_map.476 = (bf16[1152,768]{1,0:T(8,128)(2,1)}, bf16[2,2,96,768]{3,2,1,0:T(8,128)(2,1)}, bf16[2,2,96,768]{3,2,1,0:T(8,128)(2,1)}, f32[2,2,768]{2,1,0:T(2,128)}, f32[3,4,128]{2,1,0:T(4,128)}) custom-call(bf16[1152,768]{1,0:T(8,128)(2,1)} %get-tuple-element.148.refs_0_, ...), custom_call_target="tpu_custom_call", output_to_operand_aliasing={{0}: (10, {})} | custom-call | flops 1000 | bytes 1000 | tf_op jit(solution)/shard_map/pallas_call | solution.py:144
  320.9 1.8 collective-permute-done.39
  322.6 1.6 collective-permute-done.40
  326.7 1.9 fusion.10
  328.6 4.9 %collective-permute-done.38.refs_13_ = bf16[2,96,768]{2,1,0:T(8,128)(2,1)S(1)} collective-permute-done((bf16[2,96,768]{2,1,0:T(8,128)(2,1)S(1)}, bf16[2,96,768]{2,1,0:T(8,128)(2,1)S(1)}, u32[]{:S(2)}, u32[]{:S(2)}) %collective-permute-start.38) | collective-permute-done | bytes 294944 | tf_op jit(solution)/shard_map/ppermute | solution.py:50
  334.2 11.7 %shard_map.477 = (bf16[1152,768]{1,0:T(8,128)(2,1)}, bf16[2,2,96,768]{3,2,1,0:T(8,128)(2,1)}, bf16[2,2,96,768]{3,2,1,0:T(8,128)(2,1)}, f32[2,2,768]{2,1,0:T(2,128)}, f32[3,4,128]{2,1,0:T(4,128)}) custom-call(bf16[1152,768]{1,0:T(8,128)(2,1)} %get-tuple-element.148.refs_0_, ...), custom_call_target="tpu_custom_call", output_to_operand_aliasing={{0}: (13, {})} | custom-call | flops 1000 | bytes 1000 | tf_op jit(solution)/shard_map/pallas_call | solution.py:144
  348.2 1.9 fusion.11
  351.2 4.5 collective-permute-done.41
  355.7 2.8 fusion.67
  361.3 1.6 collective-permute-done.44.refs_19_
  363.0 23.3 %shard_map.478 = (bf16[384,2944]{1,0:T(8,128)(2,1)}, bf16[384,2944]{1,0:T(8,128)(2,1)}, f32[8,768]{1,0:T(8,128)}) custom-call(bf16[1152,768]{1,0:T(8,128)(2,1)} %get-tuple-element.191.refs_0_, bf16[1152,768]{1,0:T(8,128)(2,1)} %get-tuple-element.192.refs_1_, bf16[1152,768]{1,0:T(8,128)(2,1)} %get-tuple-element.193.refs_2_, ...), custom_call_target="tpu_custom_call" | custom-call | flops 1000 | bytes 1000 | tf_op jit(solution)/shard_map/pallas_call | solution.py:144
  391.1 3.8 add_convert_fusion.9
  394.9 1.5 collective-permute-start.48
  396.9 1.5 collective-permute-start.46
  398.5 7.5 %collective-permute-done.49 = bf16[96,3456]{1,0:T(8,128)(2,1)S(1)} collective-permute-done((bf16[96,3456]{1,0:T(8,128)(2,1)S(1)}, bf16[96,3456]{1,0:T(8,128)(2,1)S(1)}, u32[]{:S(2)}, u32[]{:S(2)}) %collective-permute-start.49) | collective-permute-done | bytes 663584 | tf_op jit(solution)/shard_map/ppermute | solution.py:50
  407.9 3.9 collective-permute-done.48
  411.8 11.3 %collective-permute-done.47 = bf16[96,2944]{1,0:T(8,128)(2,1)} collective-permute-done((bf16[96,2944]{1,0:T(8,128)(2,1)}, bf16[96,2944]{1,0:T(8,128)(2,1)}, u32[]{:S(2)}, u32[]{:S(2)}) %collective-permute-start.47) | collective-permute-done | bytes 565280 | tf_op jit(solution)/shard_map/ppermute | solution.py:45
  423.2 1.7 convert_add_fusion.1
  427.6 2.3 collective-permute-done.52
  431.2 3.2 collective-permute-done.50
  437.0 6.5 %collective-permute-done.51.refs_1_ = bf16[96,576]{1,0:T(8,128)(2,1)S(1)} collective-permute-done((bf16[96,576]{1,0:T(8,128)(2,1)S(1)}, bf16[96,576]{1,0:T(8,128)(2,1)S(1)}, u32[]{:S(2)}, u32[]{:S(2)}) %collective-permute-start.51) | collective-permute-done | bytes 110624 | tf_op jit(solution)/shard_map/ppermute | solution.py:50
  444.1 2.5 shard_map.479
  448.9 1.5 collective-permute-start.58
  450.3 2.0 collective-permute-start.57
  452.4 2.0 collective-permute-done.58
  455.1 1.8 collective-permute-start.60
  456.9 2.6 collective-permute-start.61
  459.5 2.5 collective-permute-done.60.refs_3_
  463.6 4.6 shard_map.480
  (341 shorter events, 73.8 us)
Async XLA Ops:
  6.9 10.2 %collective-permute-start = (bf16[96,832]{1,0:T(8,128)(2,1)S(1)}, bf16[96,832]{1,0:T(8,128)(2,1)S(1)}, u32[]{:S(2)}, u32[]{:S(2)}) collective-permute-start(bf16[96,832]{1,0:T(8,128)(2,1)S(1)} %maximum_maximum_fusion), channel_id=1, source_target_pairs={{0,1},{1,0},{2,3},{3,2},{4,5},{5,4},{6,7},{7,6},{8,9},{9,8},{10,11... | collective-permute-start | bytes 479240 | tf_op jit(solution)/shard_map/ppermute | solution.py:50
  10.0 15.7 %collective-permute-start.1 = (bf16[96,832]{1,0:T(8,128)(2,1)S(1)}, bf16[96,832]{1,0:T(8,128)(2,1)S(1)}, u32[]{:S(2)}, u32[]{:S(2)}) collective-permute-start(bf16[96,832]{1,0:T(8,128)(2,1)S(1)} %maximum_maximum_fusion), channel_id=1, source_target_pairs={{0,2},{1,3},{2,0},{3,1},{4,6},{5,7},{6,4},{7,5},{8,10},{9,11},{10,... | collective-permute-start | bytes 479240 | tf_op jit(solution)/shard_map/ppermute | solution.py:50
  12.6 13.2 %collective-permute-start.2 = (bf16[96,832]{1,0:T(8,128)(2,1)S(1)}, bf16[96,832]{1,0:T(8,128)(2,1)S(1)}, u32[]{:S(2)}, u32[]{:S(2)}) collective-permute-start(bf16[96,832]{1,0:T(8,128)(2,1)S(1)} %maximum_maximum_fusion), channel_id=1, source_target_pairs={{0,3},{1,2},{2,1},{3,0},{4,7},{5,6},{6,5},{7,4},{8,11},{9,10},{10,... | collective-permute-start | bytes 479240 | tf_op jit(solution)/shard_map/ppermute | solution.py:50
  13.0 25.9 %collective-permute-start.16 = (s32[16,128]{1,0:T(8,128)S(1)}, s32[16,128]{1,0:T(8,128)S(1)}, u32[]{:S(2)}, u32[]{:S(2)}) collective-permute-start(s32[16,128]{1,0:T(8,128)S(1)} %pad_bitcast_fusion), channel_id=1, source_target_pairs={{0,0},{1,1},{2,4},{3,5},{4,2},{5,3},{6,6},{7,7},{8,8},{9,9},{10,12... | collective-permute-start | bytes 24584 | tf_op jit(solution)/shard_map/ppermute | solution.py:64
  27.8 55.2 %copy-start.6 = (bf16[96,2944]{1,0:T(8,128)(2,1)}, bf16[96,2944]{1,0:T(8,128)(2,1)S(1)}, u32[]{:S(2)}) copy-start(bf16[96,2944]{1,0:T(8,128)(2,1)S(1)} %concatenate.155.refs_3_.refs_20_) | copy-start | bytes 1695748
  27.8 27.8 %collective-permute-start.4 = (bf16[96,2944]{1,0:T(8,128)(2,1)S(1)}, bf16[96,2944]{1,0:T(8,128)(2,1)S(1)}, u32[]{:S(2)}, u32[]{:S(2)}) collective-permute-start(bf16[96,2944]{1,0:T(8,128)(2,1)S(1)} %concatenate.155.refs_3_.refs_20_), channel_id=1, source_target_pairs={{0,8},{4,12},{8,0},{12,4},{16,24},{20,28},{24,16},{28,20},{1,9},{5... | collective-permute-start | bytes 1695752 | tf_op jit(solution)/shard_map/ppermute | solution.py:45
  29.4 46.9 %collective-permute-start.3 = (bf16[3,441,384]{2,1,0:T(8,128)(2,1)}, bf16[3,441,384]{2,1,0:T(8,128)(2,1)}, u32[]{:S(2)}, u32[]{:S(2)}) collective-permute-start(bf16[3,441,384]{2,1,0:T(8,128)(2,1)} %bitcast.1), channel_id=1, source_target_pairs={{0,0},{1,1},{2,4},{3,5},{4,2},{5,3},{6,6},{7,7},{8,8},{9,9},{10,12... | collective-permute-start | bytes 3048200 | tf_op jit(solution)/shard_map/ppermute | solution.py:64
  52.4 23.4 %collective-permute-start.5 = (bf16[96,2944]{1,0:T(8,128)(2,1)S(1)}, bf16[96,2944]{1,0:T(8,128)(2,1)S(1)}, u32[]{:S(2)}, u32[]{:S(2)}) collective-permute-start(bf16[96,2944]{1,0:T(8,128)(2,1)S(1)} %concatenate.155.refs_3_.refs_20_), channel_id=1, source_target_pairs={{0,16},{4,20},{8,24},{12,28},{16,0},{20,4},{24,8},{28,12},{1,17},{... | collective-permute-start | bytes 1695752 | tf_op jit(solution)/shard_map/ppermute | solution.py:45
  54.0 21.8 %collective-permute-start.6 = (bf16[96,2944]{1,0:T(8,128)(2,1)S(1)}, bf16[96,2944]{1,0:T(8,128)(2,1)S(1)}, u32[]{:S(2)}, u32[]{:S(2)}) collective-permute-start(bf16[96,2944]{1,0:T(8,128)(2,1)S(1)} %concatenate.155.refs_3_.refs_20_), channel_id=1, source_target_pairs={{0,24},{4,28},{8,16},{12,20},{16,8},{20,12},{24,0},{28,4},{1,25},{... | collective-permute-start | bytes 1695752 | tf_op jit(solution)/shard_map/ppermute | solution.py:45
  55.7 20.7 %collective-permute-start.7 = (bf16[96,2944]{1,0:T(8,128)(2,1)S(1)}, bf16[96,2944]{1,0:T(8,128)(2,1)S(1)}, u32[]{:S(2)}, u32[]{:S(2)}) collective-permute-start(bf16[96,2944]{1,0:T(8,128)(2,1)S(1)} %concatenate.155.refs_3_.refs_20_), channel_id=1, source_target_pairs={{0,4},{4,0},{8,12},{12,8},{16,20},{20,16},{24,28},{28,24},{1,5},{5... | collective-permute-start | bytes 1695752 | tf_op jit(solution)/shard_map/ppermute | solution.py:45
  55.7 21.1 %collective-permute-start.8 = (bf16[96,2944]{1,0:T(8,128)(2,1)S(1)}, bf16[96,2944]{1,0:T(8,128)(2,1)S(1)}, u32[]{:S(2)}, u32[]{:S(2)}) collective-permute-start(bf16[96,2944]{1,0:T(8,128)(2,1)S(1)} %collective-permute-done.4.refs_4_.refs_21_), channel_id=1, source_target_pairs={{0,4},{4,0},{8,12},{12,8},{16,20},{20,16},{24,28},{28,24},{1,5},{5... | collective-permute-start | bytes 1695752 | tf_op jit(solution)/shard_map/ppermute | solution.py:45
  75.8 7.2 %collective-permute-start.9 = (bf16[96,2944]{1,0:T(8,128)(2,1)S(1)}, bf16[96,2944]{1,0:T(8,128)(2,1)}, u32[]{:S(2)}, u32[]{:S(2)}) collective-permute-start(bf16[96,2944]{1,0:T(8,128)(2,1)S(1)} %collective-permute-done.5.refs_5_.refs_22_), channel_id=1, source_target_pairs={{0,4},{4,0},{8,12},{12,8},{16,20},{20,16},{24,28},{28,24},{1,5},{5... | collective-permute-start | bytes 1695752 | tf_op jit(solution)/shard_map/ppermute | solution.py:45
  75.8 7.2 %collective-permute-start.10 = (bf16[96,2944]{1,0:T(8,128)(2,1)S(1)}, bf16[96,2944]{1,0:T(8,128)(2,1)}, u32[]{:S(2)}, u32[]{:S(2)}) collective-permute-start(bf16[96,2944]{1,0:T(8,128)(2,1)S(1)} %collective-permute-done.6.refs_6_.refs_23_), channel_id=1, source_target_pairs={{0,4},{4,0},{8,12},{12,8},{16,20},{20,16},{24,28},{28,24},{1,5},{5... | collective-permute-start | bytes 1695752 | tf_op jit(solution)/shard_map/ppermute | solution.py:45
  76.3 19.5 %collective-permute-start.11 = (bf16[96,1728]{1,0:T(8,128)(2,1)}, bf16[96,1728]{1,0:T(8,128)(2,1)}, u32[]{:S(2)}, u32[]{:S(2)}) collective-permute-start(bf16[96,1728]{1,0:T(8,128)(2,1)} %pad_maximum_fusion.4.refs_1_), channel_id=1, source_target_pairs={{0,1},{1,0},{2,3},{3,2},{4,5},{5,4},{6,7},{7,6},{8,9},{9,8},{10,11... | collective-permute-start | bytes 995336 | tf_op jit(solution)/shard_map/ppermute | solution.py:50
  76.4 27.0 %collective-permute-start.12 = (bf16[96,1728]{1,0:T(8,128)(2,1)}, bf16[96,1728]{1,0:T(8,128)(2,1)}, u32[]{:S(2)}, u32[]{:S(2)}) collective-permute-start(bf16[96,1728]{1,0:T(8,128)(2,1)} %pad_maximum_fusion.4.refs_1_), channel_id=1, source_target_pairs={{0,2},{1,3},{2,0},{3,1},{4,6},{5,7},{6,4},{7,5},{8,10},{9,11},{10,... | collective-permute-start | bytes 995336 | tf_op jit(solution)/shard_map/ppermute | solution.py:50
  76.7 26.7 %collective-permute-start.13 = (bf16[96,1728]{1,0:T(8,128)(2,1)}, bf16[96,1728]{1,0:T(8,128)(2,1)}, u32[]{:S(2)}, u32[]{:S(2)}) collective-permute-start(bf16[96,1728]{1,0:T(8,128)(2,1)} %pad_maximum_fusion.4.refs_1_), channel_id=1, source_target_pairs={{0,3},{1,2},{2,1},{3,0},{4,7},{5,6},{6,5},{7,4},{8,11},{9,10},{10,... | collective-permute-start | bytes 995336 | tf_op jit(solution)/shard_map/ppermute | solution.py:50
  105.9 34.1 %collective-permute-start.14 = (bf16[96,6912]{1,0:T(8,128)(2,1)}, bf16[96,6912]{1,0:T(8,128)(2,1)}, u32[]{:S(2)}, u32[]{:S(2)}) collective-permute-start(bf16[96,6912]{1,0:T(8,128)(2,1)} %shard_map.467.refs_4_.refs_6_), channel_id=1, source_target_pairs={{0,8},{4,12},{8,0},{12,4},{16,24},{20,28},{24,16},{28,20},{1,9},{5... | collective-permute-start | bytes 3981320 | tf_op jit(solution)/shard_map/ppermute | solution.py:45
  106.4 33.5 %collective-permute-start.15 = (bf16[96,6912]{1,0:T(8,128)(2,1)}, bf16[96,6912]{1,0:T(8,128)(2,1)}, u32[]{:S(2)}, u32[]{:S(2)}) collective-permute-start(bf16[96,6912]{1,0:T(8,128)(2,1)} %shard_map.467.refs_4_.refs_6_), channel_id=1, source_target_pairs={{0,16},{4,20},{8,24},{12,28},{16,0},{20,4},{24,8},{28,12},{1,17},{... | collective-permute-start | bytes 3981320 | tf_op jit(solution)/shard_map/ppermute | solution.py:45
  108.1 31.9 %collective-permute-start.18 = (bf16[3,2,96,768]{3,2,1,0:T(8,128)(2,1)S(1)}, bf16[3,2,96,768]{3,2,1,0:T(8,128)(2,1)S(1)}, u32[]{:S(2)}, u32[]{:S(2)}) collective-permute-start(bf16[3,2,96,768]{3,2,1,0:T(8,128)(2,1)S(1)} %copy-done), channel_id=1, source_target_pairs={{0,1},{1,0},{2,3},{3,2},{4,5},{5,4},{6,7},{7,6},{8,9},{9,8},{10,11... | collective-permute-start | bytes 2654216 | tf_op jit(solution)/shard_map/ppermute | solution.py:50
  115.7 25.7 %collective-permute-start.21 = (bf16[2,2,192,384]{3,2,1,0:T(8,128)(2,1)}, bf16[2,2,192,384]{3,2,1,0:T(8,128)(2,1)}, u32[]{:S(2)}, u32[]{:S(2)}) collective-permute-start(bf16[2,2,192,384]{3,2,1,0:T(8,128)(2,1)} %bitcast.17), channel_id=1, source_target_pairs={{0,0},{1,1},{2,4},{3,5},{4,2},{5,3},{6,6},{7,7},{8,8},{9,9},{10,12... | collective-permute-start | bytes 1769480 | tf_op jit(solution)/shard_map/ppermute | solution.py:64
  124.1 22.2 %collective-permute-start.17 = (bf16[3,2,96,768]{3,2,1,0:T(8,128)(2,1)S(1)}, bf16[3,2,96,768]{3,2,1,0:T(8,128)(2,1)S(1)}, u32[]{:S(2)}, u32[]{:S(2)}) collective-permute-start(bf16[3,2,96,768]{3,2,1,0:T(8,128)(2,1)S(1)} %copy-done), channel_id=1, source_target_pairs={{0,4},{4,0},{8,12},{12,8},{16,20},{20,16},{24,28},{28,24},{1,5},{5... | collective-permute-start | bytes 2654216 | tf_op jit(solution)/shard_map/ppermute | solution.py:45
  139.9 6.3 %collective-permute-start.19 = (bf16[3,2,96,768]{3,2,1,0:T(8,128)(2,1)S(1)}, bf16[3,2,96,768]{3,2,1,0:T(8,128)(2,1)S(1)}, u32[]{:S(2)}, u32[]{:S(2)}) collective-permute-start(bf16[3,2,96,768]{3,2,1,0:T(8,128)(2,1)S(1)} %collective-permute-done.18.refs_5_.refs_9_.refs_13_.refs_4_.refs_8_.refs_7_.refs_11_), channel_id=1, source_target_pairs={{0,4},{4,0},{8,12},{12,8},{16,20},{20,16},{24,28},{28,24},{1,5},{5... | collective-permute-start | bytes 2654216 | tf_op jit(solution)/shard_map/ppermute | solution.py:45
  139.9 38.1 %collective-permute-start.20 = (bf16[96,6912]{1,0:T(8,128)(2,1)}, bf16[96,6912]{1,0:T(8,128)(2,1)}, u32[]{:S(2)}, u32[]{:S(2)}) collective-permute-start(bf16[96,6912]{1,0:T(8,128)(2,1)} %shard_map.467.refs_4_.refs_6_), channel_id=1, source_target_pairs={{0,24},{4,28},{8,16},{12,20},{16,8},{20,12},{24,0},{28,4},{1,25},{... | collective-permute-start | bytes 3981320 | tf_op jit(solution)/shard_map/ppermute | solution.py:45
  141.5 16.8 %collective-permute-start.23 = (bf16[2,2,192,384]{3,2,1,0:T(8,128)(2,1)}, bf16[2,2,192,384]{3,2,1,0:T(8,128)(2,1)}, u32[]{:S(2)}, u32[]{:S(2)}) collective-permute-start(bf16[2,2,192,384]{3,2,1,0:T(8,128)(2,1)} %collective-permute-done.21.refs_2_), channel_id=1, source_target_pairs={{0,1},{1,0},{2,3},{3,2},{4,5},{5,4},{6,7},{7,6},{8,9},{9,8},{10,11... | collective-permute-start | bytes 1769480 | tf_op jit(solution)/shard_map/ppermute | solution.py:50
  158.2 2.6 collective-permute-start.22
  158.2 3.0 collective-permute-start.24
  160.2 30.6 %collective-permute-start.25 = (bf16[96,6912]{1,0:T(8,128)(2,1)}, bf16[96,6912]{1,0:T(8,128)(2,1)S(1)}, u32[]{:S(2)}, u32[]{:S(2)}) collective-permute-start(bf16[96,6912]{1,0:T(8,128)(2,1)} %shard_map.467.refs_4_.refs_6_), channel_id=1, source_target_pairs={{0,4},{4,0},{8,12},{12,8},{16,20},{20,16},{24,28},{28,24},{1,5},{5... | collective-permute-start | bytes 3981320 | tf_op jit(solution)/shard_map/ppermute | solution.py:45
  160.3 30.5 %collective-permute-start.26 = (bf16[96,6912]{1,0:T(8,128)(2,1)}, bf16[96,6912]{1,0:T(8,128)(2,1)}, u32[]{:S(2)}, u32[]{:S(2)}) collective-permute-start(bf16[96,6912]{1,0:T(8,128)(2,1)} %collective-permute-done.14.refs_5_.refs_7_), channel_id=1, source_target_pairs={{0,4},{4,0},{8,12},{12,8},{16,20},{20,16},{24,28},{28,24},{1,5},{5... | collective-permute-start | bytes 3981320 | tf_op jit(solution)/shard_map/ppermute | solution.py:45
  167.9 22.9 %collective-permute-start.27 = (bf16[96,6912]{1,0:T(8,128)(2,1)}, bf16[96,6912]{1,0:T(8,128)(2,1)}, u32[]{:S(2)}, u32[]{:S(2)}) collective-permute-start(bf16[96,6912]{1,0:T(8,128)(2,1)} %collective-permute-done.15.refs_6_.refs_8_), channel_id=1, source_target_pairs={{0,4},{4,0},{8,12},{12,8},{16,20},{20,16},{24,28},{28,24},{1,5},{5... | collective-permute-start | bytes 3981320 | tf_op jit(solution)/shard_map/ppermute | solution.py:45
  178.1 12.7 %collective-permute-start.28 = (bf16[96,6912]{1,0:T(8,128)(2,1)}, bf16[96,6912]{1,0:T(8,128)(2,1)}, u32[]{:S(2)}, u32[]{:S(2)}) collective-permute-start(bf16[96,6912]{1,0:T(8,128)(2,1)} %collective-permute-done.20.refs_7_.refs_9_), channel_id=1, source_target_pairs={{0,4},{4,0},{8,12},{12,8},{16,20},{20,16},{24,28},{28,24},{1,5},{5... | collective-permute-start | bytes 3981320 | tf_op jit(solution)/shard_map/ppermute | solution.py:45
  226.3 8.5 %collective-permute-start.30 = (f32[24,768]{1,0:T(8,128)}, f32[24,768]{1,0:T(8,128)S(1)}, u32[]{:S(2)}, u32[]{:S(2)}) collective-permute-start(f32[24,768]{1,0:T(8,128)} %bitcast.90), channel_id=1, source_target_pairs={{0,4},{4,0},{8,12},{12,8},{16,20},{20,16},{24,28},{28,24},{1,5},{5... | collective-permute-start | bytes 221192 | tf_op jit(solution)/shard_map/ppermute | solution.py:45
  226.5 8.3 %collective-permute-start.31 = (f32[24,768]{1,0:T(8,128)}, f32[24,768]{1,0:T(8,128)S(1)}, u32[]{:S(2)}, u32[]{:S(2)}) collective-permute-start(f32[24,768]{1,0:T(8,128)} %bitcast.91), channel_id=1, source_target_pairs={{0,5},{1,4},{2,7},{3,6},{4,1},{5,0},{6,3},{7,2},{8,13},{9,12},{10,... | collective-permute-start | bytes 221192 | tf_op jit(solution)/shard_map/ppermute | solution.py:131
  227.6 7.2 %collective-permute-start.29 = (f32[24,768]{1,0:T(8,128)}, f32[24,768]{1,0:T(8,128)S(1)}, u32[]{:S(2)}, u32[]{:S(2)}) collective-permute-start(f32[24,768]{1,0:T(8,128)} %bitcast.92), channel_id=1, source_target_pairs={{0,1},{1,0},{2,3},{3,2},{4,5},{5,4},{6,7},{7,6},{8,9},{9,8},{10,11... | collective-permute-start | bytes 221192 | tf_op jit(solution)/shard_map/ppermute | solution.py:50
  233.1 43.7 %collective-permute-start.32 = (bf16[2,2,192,384]{3,2,1,0:T(8,128)(2,1)}, bf16[2,2,192,384]{3,2,1,0:T(8,128)(2,1)S(1)}, u32[]{:S(2)}, u32[]{:S(2)}) collective-permute-start(bf16[2,2,192,384]{3,2,1,0:T(8,128)(2,1)} %shard_map.473.refs_14_), channel_id=1, source_target_pairs={{0,0},{1,1},{2,4},{3,5},{4,2},{5,3},{6,6},{7,7},{8,8},{9,9},{10,12... | collective-permute-start | bytes 1769480 | tf_op jit(solution)/shard_map/ppermute | solution.py:64
  236.4 28.8 %copy-start.4 = (bf16[1152,768]{1,0:T(8,128)(2,1)S(1)}, bf16[1152,768]{1,0:T(8,128)(2,1)}, u32[]{:S(2)}) copy-start(bf16[1152,768]{1,0:T(8,128)(2,1)} %get-tuple-element.155.refs_0_) | copy-start | bytes 5308420
  267.5 20.5 %collective-permute-start.35 = (bf16[384,768]{1,0:T(8,128)(2,1)S(1)}, bf16[384,768]{1,0:T(8,128)(2,1)S(1)}, u32[]{:S(2)}, u32[]{:S(2)}) collective-permute-start(bf16[384,768]{1,0:T(8,128)(2,1)S(1)} %convolution_convert_fusion.4), channel_id=1, source_target_pairs={{0,4},{4,0},{8,12},{12,8},{16,20},{20,16},{24,28},{28,24},{1,5},{5... | collective-permute-start | bytes 1769480 | tf_op jit(solution)/shard_map/ppermute | solution.py:45
  275.7 12.5 %collective-permute-start.34 = (bf16[384,3072]{1,0:T(8,128)(2,1)S(1)}, bf16[384,3072]{1,0:T(8,128)(2,1)S(1)}, u32[]{:S(2)}, u32[]{:S(2)}) collective-permute-start(bf16[384,3072]{1,0:T(8,128)(2,1)S(1)} %convolution_convert_fusion), channel_id=1, source_target_pairs={{0,4},{4,0},{8,12},{12,8},{16,20},{20,16},{24,28},{28,24},{1,5},{5... | collective-permute-start | bytes 7077896 | tf_op jit(solution)/shard_map/ppermute | solution.py:45
  280.8 8.2 %collective-permute-start.33 = (bf16[384,3072]{1,0:T(8,128)(2,1)S(1)}, bf16[384,3072]{1,0:T(8,128)(2,1)S(1)}, u32[]{:S(2)}, u32[]{:S(2)}) collective-permute-start(bf16[384,3072]{1,0:T(8,128)(2,1)S(1)} %convolution_convert_fusion.2), channel_id=1, source_target_pairs={{0,4},{4,0},{8,12},{12,8},{16,20},{20,16},{24,28},{28,24},{1,5},{5... | collective-permute-start | bytes 7077896 | tf_op jit(solution)/shard_map/ppermute | solution.py:45
  291.0 31.6 %collective-permute-start.39 = (bf16[96,6912]{1,0:T(8,128)(2,1)}, bf16[96,6912]{1,0:T(8,128)(2,1)S(1)}, u32[]{:S(2)}, u32[]{:S(2)}) collective-permute-start(bf16[96,6912]{1,0:T(8,128)(2,1)} %pad_maximum_fusion.1), channel_id=1, source_target_pairs={{0,8},{4,12},{8,0},{12,4},{16,24},{20,28},{24,16},{28,20},{1,9},{5... | collective-permute-start | bytes 3981320 | tf_op jit(solution)/shard_map/ppermute | solution.py:45
  292.8 31.4 %collective-permute-start.40 = (bf16[96,6912]{1,0:T(8,128)(2,1)}, bf16[96,6912]{1,0:T(8,128)(2,1)}, u32[]{:S(2)}, u32[]{:S(2)}) collective-permute-start(bf16[96,6912]{1,0:T(8,128)(2,1)} %pad_maximum_fusion.2), channel_id=1, source_target_pairs={{0,16},{4,20},{8,24},{12,28},{16,0},{20,4},{24,8},{28,12},{1,17},{... | collective-permute-start | bytes 3981320 | tf_op jit(solution)/shard_map/ppermute | solution.py:45
  305.8 2.3 collective-permute-start.36
  320.7 6.0 %collective-permute-start.37 = (bf16[2,2,96,768]{3,2,1,0:T(8,128)(2,1)}, bf16[2,2,96,768]{3,2,1,0:T(8,128)(2,1)S(1)}, u32[]{:S(2)}, u32[]{:S(2)}) collective-permute-start(bf16[2,2,96,768]{3,2,1,0:T(8,128)(2,1)} %get-tuple-element.186), channel_id=1, source_target_pairs={{0,4},{4,0},{8,12},{12,8},{16,20},{20,16},{24,28},{28,24},{1,5},{5... | collective-permute-start | bytes 1769480 | tf_op jit(solution)/shard_map/ppermute | solution.py:45
  324.2 31.5 %collective-permute-start.41 = (bf16[96,6912]{1,0:T(8,128)(2,1)}, bf16[96,6912]{1,0:T(8,128)(2,1)}, u32[]{:S(2)}, u32[]{:S(2)}) collective-permute-start(bf16[96,6912]{1,0:T(8,128)(2,1)} %pad_maximum_fusion.3), channel_id=1, source_target_pairs={{0,24},{4,28},{8,16},{12,20},{16,8},{20,12},{24,0},{28,4},{1,25},{... | collective-permute-start | bytes 3981320 | tf_op jit(solution)/shard_map/ppermute | solution.py:45
  325.6 7.9 %collective-permute-start.38 = (bf16[2,96,768]{2,1,0:T(8,128)(2,1)S(1)}, bf16[2,96,768]{2,1,0:T(8,128)(2,1)S(1)}, u32[]{:S(2)}, u32[]{:S(2)}) collective-permute-start(bf16[2,96,768]{2,1,0:T(8,128)(2,1)S(1)} %fusion.9), channel_id=1, source_target_pairs={{0,1},{1,0},{2,3},{3,2},{4,5},{5,4},{6,7},{7,6},{8,9},{9,8},{10,11... | collective-permute-start | bytes 884744 | tf_op jit(solution)/shard_map/ppermute | solution.py:50
  345.9 2.3 collective-permute-start.43
  346.9 14.4 %collective-permute-start.42 = (bf16[2,96,768]{2,1,0:T(8,128)(2,1)}, bf16[2,96,768]{2,1,0:T(8,128)(2,1)}, u32[]{:S(2)}, u32[]{:S(2)}) collective-permute-start(bf16[2,96,768]{2,1,0:T(8,128)(2,1)} %fusion.10), channel_id=1, source_target_pairs={{0,1},{1,0},{2,3},{3,2},{4,5},{5,4},{6,7},{7,6},{8,9},{9,8},{10,11... | collective-permute-start | bytes 884744 | tf_op jit(solution)/shard_map/ppermute | solution.py:50
  350.2 12.8 %collective-permute-start.44 = (bf16[2,96,768]{2,1,0:T(8,128)(2,1)}, bf16[2,96,768]{2,1,0:T(8,128)(2,1)}, u32[]{:S(2)}, u32[]{:S(2)}) collective-permute-start(bf16[2,96,768]{2,1,0:T(8,128)(2,1)} %fusion.11), channel_id=1, source_target_pairs={{0,1},{1,0},{2,3},{3,2},{4,5},{5,4},{6,7},{7,6},{8,9},{9,8},{10,11... | collective-permute-start | bytes 884744 | tf_op jit(solution)/shard_map/ppermute | solution.py:50
  386.3 4.8 %collective-permute-start.45 = (bf16[384,2944]{1,0:T(8,128)(2,1)}, bf16[384,2944]{1,0:T(8,128)(2,1)}, u32[]{:S(2)}, u32[]{:S(2)}) collective-permute-start(bf16[384,2944]{1,0:T(8,128)(2,1)} %get-tuple-element.201), channel_id=1, source_target_pairs={{0,4},{4,0},{8,12},{12,8},{16,20},{20,16},{24,28},{28,24},{1,5},{5... | collective-permute-start | bytes 6782984 | tf_op jit(solution)/shard_map/ppermute | solution.py:45
  388.6 17.3 %collective-permute-start.49 = (bf16[96,3456]{1,0:T(8,128)(2,1)S(1)}, bf16[96,3456]{1,0:T(8,128)(2,1)S(1)}, u32[]{:S(2)}, u32[]{:S(2)}) collective-permute-start(bf16[96,3456]{1,0:T(8,128)(2,1)S(1)} %concatenate.170), channel_id=1, source_target_pairs={{0,1},{1,0},{2,3},{3,2},{4,5},{5,4},{6,7},{7,6},{8,9},{9,8},{10,11... | collective-permute-start | bytes 1990664 | tf_op jit(solution)/shard_map/ppermute | solution.py:50
  394.9 16.9 %collective-permute-start.48 = (bf16[96,2944]{1,0:T(8,128)(2,1)}, bf16[96,2944]{1,0:T(8,128)(2,1)}, u32[]{:S(2)}, u32[]{:S(2)}) collective-permute-start(bf16[96,2944]{1,0:T(8,128)(2,1)} %get-tuple-element.261), channel_id=1, source_target_pairs={{0,24},{4,28},{8,16},{12,20},{16,8},{20,12},{24,0},{28,4},{1,25},{... | collective-permute-start | bytes 1695752 | tf_op jit(solution)/shard_map/ppermute | solution.py:45
  396.4 26.6 %collective-permute-start.47 = (bf16[96,2944]{1,0:T(8,128)(2,1)}, bf16[96,2944]{1,0:T(8,128)(2,1)}, u32[]{:S(2)}, u32[]{:S(2)}) collective-permute-start(bf16[96,2944]{1,0:T(8,128)(2,1)} %get-tuple-element.260), channel_id=1, source_target_pairs={{0,16},{4,20},{8,24},{12,28},{16,0},{20,4},{24,8},{28,12},{1,17},{... | collective-permute-start | bytes 1695752 | tf_op jit(solution)/shard_map/ppermute | solution.py:45
  396.9 26.2 %collective-permute-start.46 = (bf16[96,2944]{1,0:T(8,128)(2,1)}, bf16[96,2944]{1,0:T(8,128)(2,1)}, u32[]{:S(2)}, u32[]{:S(2)}) collective-permute-start(bf16[96,2944]{1,0:T(8,128)(2,1)} %get-tuple-element.262), channel_id=1, source_target_pairs={{0,8},{4,12},{8,0},{12,4},{16,24},{20,28},{24,16},{28,20},{1,9},{5... | collective-permute-start | bytes 1695752 | tf_op jit(solution)/shard_map/ppermute | solution.py:45
  407.0 29.9 %collective-permute-start.54 = (bf16[96,1728]{1,0:T(8,128)(2,1)S(1)}, bf16[96,1728]{1,0:T(8,128)(2,1)S(1)}, u32[]{:S(2)}, u32[]{:S(2)}) collective-permute-start(bf16[96,1728]{1,0:T(8,128)(2,1)S(1)} %get-tuple-element.293), channel_id=1, source_target_pairs={{0,2},{1,3},{2,0},{3,1},{4,6},{5,7},{6,4},{7,5},{8,10},{9,11},{10,... | collective-permute-start | bytes 995336 | tf_op jit(solution)/shard_map/ppermute | solution.py:50
  425.1 4.8 %collective-permute-start.52 = (bf16[24,1280]{1,0:T(8,128)(2,1)S(1)}, bf16[24,1280]{1,0:T(8,128)(2,1)S(1)}, u32[]{:S(2)}, u32[]{:S(2)}) collective-permute-start(bf16[24,1280]{1,0:T(8,128)(2,1)S(1)} %pad_maximum_fusion.13), channel_id=1, source_target_pairs={{0,1},{1,0},{2,3},{3,2},{4,5},{5,4},{6,7},{7,6},{8,9},{9,8},{10,11... | collective-permute-start | bytes 184328 | tf_op jit(solution)/shard_map/ppermute | solution.py:50
  426.6 7.9 %collective-permute-start.50 = (bf16[96,1152]{1,0:T(8,128)(2,1)S(1)}, bf16[96,1152]{1,0:T(8,128)(2,1)S(1)}, u32[]{:S(2)}, u32[]{:S(2)}) collective-permute-start(bf16[96,1152]{1,0:T(8,128)(2,1)S(1)} %pad_maximum_fusion.9), channel_id=1, source_target_pairs={{0,1},{1,0},{2,3},{3,2},{4,5},{5,4},{6,7},{7,6},{8,9},{9,8},{10,11... | collective-permute-start | bytes 663560 | tf_op jit(solution)/shard_map/ppermute | solution.py:50
  430.6 6.4 %collective-permute-start.53 = (bf16[24,640]{1,0:T(8,128)(2,1)S(1)}, bf16[24,640]{1,0:T(8,128)(2,1)S(1)}, u32[]{:S(2)}, u32[]{:S(2)}) collective-permute-start(bf16[24,640]{1,0:T(8,128)(2,1)S(1)} %get-tuple-element.298), channel_id=1, source_target_pairs={{0,2},{1,3},{2,0},{3,1},{4,6},{5,7},{6,4},{7,5},{8,10},{9,11},{10,... | collective-permute-start | bytes 92168 | tf_op jit(solution)/shard_map/ppermute | solution.py:50
  435.4 8.0 %collective-permute-start.51 = (bf16[96,576]{1,0:T(8,128)(2,1)S(1)}, bf16[96,576]{1,0:T(8,128)(2,1)S(1)}, u32[]{:S(2)}, u32[]{:S(2)}) collective-permute-start(bf16[96,576]{1,0:T(8,128)(2,1)S(1)} %get-tuple-element.302), channel_id=1, source_target_pairs={{0,2},{1,3},{2,0},{3,1},{4,6},{5,7},{6,4},{7,5},{8,10},{9,11},{10,... | collective-permute-start | bytes 331784 | tf_op jit(solution)/shard_map/ppermute | solution.py:50
  446.6 1.5 collective-permute-start.55
  448.9 5.5 %collective-permute-start.58 = (f32[56,192]{1,0:T(8,128)S(1)}, f32[56,192]{1,0:T(8,128)S(1)}, u32[]{:S(2)}, u32[]{:S(2)}) collective-permute-start(f32[56,192]{1,0:T(8,128)S(1)} %add.707), channel_id=1, source_target_pairs={{0,24},{4,28},{8,16},{12,20},{16,8},{20,12},{24,0},{28,4},{1,25},{... | collective-permute-start | bytes 129032 | tf_op jit(solution)/shard_map/ppermute | solution.py:45
  450.3 4.2 collective-permute-start.56
  450.3 4.6 collective-permute-start.57
  455.0 4.5 collective-permute-start.59
  455.1 6.9 %collective-permute-start.60 = (f32[56,192]{1,0:T(8,128)S(1)}, f32[56,192]{1,0:T(8,128)S(1)}, u32[]{:S(2)}, u32[]{:S(2)}) collective-permute-start(f32[56,192]{1,0:T(8,128)S(1)} %add_add_fusion.refs_1_), channel_id=1, source_target_pairs={{0,2},{1,3},{2,0},{3,1},{4,6},{5,7},{6,4},{7,5},{8,10},{9,11},{10,... | collective-permute-start | bytes 129032 | tf_op jit(solution)/shard_map/ppermute | solution.py:50
  456.9 6.1 %collective-permute-start.61 = (f32[56,192]{1,0:T(8,128)S(1)}, f32[56,192]{1,0:T(8,128)S(1)}, u32[]{:S(2)}, u32[]{:S(2)}) collective-permute-start(f32[56,192]{1,0:T(8,128)S(1)} %add_add_fusion.refs_1_), channel_id=1, source_target_pairs={{0,3},{1,2},{2,1},{3,0},{4,7},{5,6},{6,5},{7,4},{8,11},{9,10},{10,... | collective-permute-start | bytes 129032 | tf_op jit(solution)/shard_map/ppermute | solution.py:50
  (51 other events, 530.1 us)
